TPU v7x, 32 devices: a whole 2x2x4 slice. The times are simulated.
32 devices in a mesh: fsdp: 16 (over z, x, core), tp: 2 (over y).
Axes of the slice: x: 2, y: 2, z: 4, core: 2. Of those that a mesh axis runs over, the one named last changes fastest.
Arguments:
- inputs: bfloat16 [10240, 2048], P(('fsdp', 'tp')), may hold values from -12 to 12
- cotangent: bfloat16 [10240, 2048], P(('fsdp', 'tp')), may hold values from -12 to 12
- lengths: int32 [16], replicated, may hold values from 384 to 640, as said below
- owners: int32 [16], replicated, may hold values from 0 to 15, each once
- qkv_weight: float32 [2048, 4096], P('fsdp', 'tp'), may hold values from -0.125 to 0.125
- out_weight: float32 [2048, 2048], P('tp', 'fsdp'), may hold values from -0.5 to 0.5
- gate_up_weight: float32 [2048, 12288], P('fsdp', 'tp'), may hold values from -0.125 to 0.125
- down_weight: float32 [6144, 2048], P('tp', 'fsdp'), may hold values from -0.12757759 to 0.12757759
- norm_gains: float32 [4352], replicated, may hold values from 0.3 to 3
- qkv_moment: float32 [2048, 4096], P('fsdp', 'tp'), may hold values from -9.1552734e-05 to 9.1552734e-05
- out_moment: float32 [2048, 2048], P('tp', 'fsdp'), may hold values from -9.1552734e-05 to 9.1552734e-05
- gate_up_moment: float32 [2048, 12288], P('fsdp', 'tp'), may hold values from -9.1552734e-05 to 9.1552734e-05
- down_moment: float32 [6144, 2048], P('tp', 'fsdp'), may hold values from -9.1552734e-05 to 9.1552734e-05
- gains_moment: float32 [4352], replicated, may hold values from -0.00036621094 to 0.00036621094
- qkv_square: float32 [2048, 4096], P('fsdp', 'tp'), may hold values from 1.9866497e-11 to 7.946599e-11
- out_square: float32 [2048, 2048], P('tp', 'fsdp'), may hold values from 1.9866497e-11 to 7.946599e-11
- gate_up_square: float32 [2048, 12288], P('fsdp', 'tp'), may hold values from 1.9866497e-11 to 7.946599e-11
- down_square: float32 [6144, 2048], P('tp', 'fsdp'), may hold values from 1.9866497e-11 to 7.946599e-11
- gains_square: float32 [4352], replicated, may hold values from 3.1786396e-10 to 1.2714558e-09
Outputs:
- output: bfloat16 [10240, 2048], P(('fsdp', 'tp'))
- input_grad: bfloat16 [10240, 2048], P(('fsdp', 'tp'))
- grad_norm: float32 [], replicated
- new_qkv: float32 [2048, 4096], P('fsdp', 'tp')
- new_qkv_moment: float32 [2048, 4096], P('fsdp', 'tp')
- new_qkv_square: float32 [2048, 4096], P('fsdp', 'tp')
- qkv_copy: bfloat16 [2048, 4096], P('fsdp', 'tp')
- new_out: float32 [2048, 2048], P('tp', 'fsdp')
- new_out_moment: float32 [2048, 2048], P('tp', 'fsdp')
- new_out_square: float32 [2048, 2048], P('tp', 'fsdp')
- out_copy: bfloat16 [2048, 2048], P('tp', 'fsdp')
- new_gate_up: float32 [2048, 12288], P('fsdp', 'tp')
- new_gate_up_moment: float32 [2048, 12288], P('fsdp', 'tp')
- new_gate_up_square: float32 [2048, 12288], P('fsdp', 'tp')
- gate_up_copy: bfloat16 [2048, 12288], P('fsdp', 'tp')
- new_down: float32 [6144, 2048], P('tp', 'fsdp')
- new_down_moment: float32 [6144, 2048], P('tp', 'fsdp')
- new_down_square: float32 [6144, 2048], P('tp', 'fsdp')
- down_copy: bfloat16 [6144, 2048], P('tp', 'fsdp')
- new_gains: float32 [4352], replicated
- new_gains_moment: float32 [4352], replicated
- new_gains_square: float32 [4352], replicated
Inputs may be any that keep to these rules, and one draw needn't show every extreme that they name: `lengths`: every length is a multiple of 128; one sequence has exactly 640 tokens and one exactly 384.
All inputs are finite; a program needn't handle non-finite values.
Results may differ from a plain program's by a relative error of at most 0.019.
Values may be sent and summed in bfloat16 or wider, within the bound.
A program may use at most 384 MiB of HBM per device.

v0:
```python
from functools import partial

import jax
import jax.numpy as jnp
from jax import lax
from jax.sharding import PartitionSpec as P

D = 2048
H = 16
KV = 8
HD = 128
FF = 6144
STEP = 10


norm_epsilon = 1e-06
rope_base = 1000000.0
clip_norm = 1.0
learn_rate = 0.04
gain_rate = 0.8
beta_first = 0.9
beta_second = 0.999
adam_epsilon = 1e-08
weight_decay = 0.1
masked_score = -1e30


def rms_scale(values):
    return lax.rsqrt(jnp.mean(values * values, axis=-1, keepdims=True) + norm_epsilon)


def norm_apply(values, gain):
    return values * rms_scale(values) * gain


def rotary(positions, width):
    half_width = width // 2
    frequency = rope_base ** (-(jnp.arange(half_width, dtype=jnp.float32) * 2.0 / width))
    angles = positions.astype(jnp.float32)[:, None] * frequency[None, :]
    return (jnp.cos(angles), jnp.sin(angles))


def rotate(values, cos_table, sin_table):
    half_width = values.shape[-1] // 2
    first_half = values[..., :half_width]
    second_half = values[..., half_width:]
    cosine = cos_table[:, None, :]
    sine_part = sin_table[:, None, :]
    return jnp.concatenate(
        [
            first_half * cosine - second_half * sine_part,
            second_half * cosine + first_half * sine_part,
        ],
        axis=-1,
    )


def head_prepare(raw, gain, cos_table, sin_table):
    return rotate(norm_apply(raw, gain), cos_table, sin_table)


def swish_product(gate_part, up_part):
    return jax.nn.silu(gate_part) * up_part


def score_block(queries, key_heads, key_mask, score_scale):
    scores = (
        jnp.einsum("qgrd,kgd->grqk", queries, key_heads, preferred_element_type=jnp.float32)
        * score_scale
    )
    return jnp.where(key_mask[None, None], scores, masked_score)


def gather_rows(values):
    return lax.all_gather(values, "tp", axis=0, tiled=True)


def sum_rows(values):
    return lax.psum_scatter(
        values.astype(jnp.bfloat16), "tp", scatter_dimension=0, tiled=True
    ).astype(jnp.float32)


def gather_grads(values):
    return lax.all_gather(values, "tp", axis=0, tiled=True)


def sum_grads(values):
    return lax.psum_scatter(
        values.astype(jnp.bfloat16), "tp", scatter_dimension=0, tiled=True
    ).astype(jnp.float32)


def adam_update(weight, gradient, moment_one, moment_two, factor, decay_rate, rate_value):
    clipped = gradient * factor
    moment_one = beta_first * moment_one + (1.0 - beta_first) * clipped
    moment_two = beta_second * moment_two + (1.0 - beta_second) * clipped * clipped
    first_fixed = moment_one / (1.0 - beta_first**STEP)
    second_fixed = moment_two / (1.0 - beta_second**STEP)
    weight = weight - rate_value * (
        first_fixed / (jnp.sqrt(second_fixed) + adam_epsilon) + decay_rate * weight
    )
    return (weight, moment_one, moment_two)


def local(
    inputs,
    cotangent,
    lengths,
    owners,
    qkv_weight,
    out_weight,
    gate_up_weight,
    down_weight,
    norm_gains,
    qkv_moment,
    out_moment,
    gate_up_moment,
    down_moment,
    gains_moment,
    qkv_square,
    out_square,
    gate_up_square,
    down_square,
    gains_square,
):
    tp_count = lax.axis_size("tp")
    local_heads = H // tp_count
    local_groups = KV // tp_count
    local_hidden = FF // tp_count
    repeat = H // KV
    half_rows = inputs.shape[0]
    row_count = half_rows * tp_count
    group_rank = lax.axis_index("fsdp")
    length = jnp.sum(jnp.where(owners == group_rank, lengths, 0))
    positions = jnp.arange(row_count)
    key_mask = (positions[None, :] <= positions[:, None]) & (positions[None, :] < length)
    own_rows = lax.axis_index("tp") * half_rows + jnp.arange(half_rows)
    valid_rows = (own_rows < length).astype(jnp.float32)[:, None]
    cos_table, sin_table = rotary(positions, HD)
    score_scale = HD ** (-0.5)
    attn_gain = norm_gains[:D]
    mlp_gain = norm_gains[D : 2 * D]
    query_gain = norm_gains[2 * D : 2 * D + HD]
    key_gain = norm_gains[2 * D + HD :]
    head_apply = partial(head_prepare, cos_table=cos_table, sin_table=sin_table)
    qkv_shard = qkv_weight.astype(jnp.bfloat16)
    out_shard = out_weight.astype(jnp.bfloat16)
    gate_up_shard = gate_up_weight.astype(jnp.bfloat16)
    down_shard = down_weight.astype(jnp.bfloat16)
    qkv_full, out_full, gate_up_full, down_full = (
        lax.all_gather(qkv_shard, "fsdp", axis=0, tiled=True),
        lax.all_gather(out_shard, "fsdp", axis=1, tiled=True),
        lax.all_gather(gate_up_shard, "fsdp", axis=0, tiled=True),
        lax.all_gather(down_shard, "fsdp", axis=1, tiled=True),
    )
    residual_in = inputs.astype(jnp.float32)
    normed_attn = gather_rows(norm_apply(residual_in, attn_gain).astype(jnp.bfloat16))
    projected = jnp.dot(normed_attn, qkv_full, preferred_element_type=jnp.float32)
    query_raw = projected[:, : local_heads * HD].reshape(row_count, local_heads, HD)
    key_raw = projected[:, local_heads * HD : (local_heads + local_groups) * HD].reshape(
        row_count, local_groups, HD
    )
    value_raw = projected[:, (local_heads + local_groups) * HD :].reshape(
        row_count, local_groups, HD
    )
    queries = (
        head_apply(query_raw, query_gain)
        .astype(jnp.bfloat16)
        .reshape(row_count, local_groups, repeat, HD)
    )
    key_heads = head_apply(key_raw, key_gain).astype(jnp.bfloat16)
    value_heads = value_raw.astype(jnp.bfloat16)
    scores = score_block(queries, key_heads, key_mask, score_scale)
    row_max = jnp.max(scores, axis=-1, keepdims=True)
    exponent = jnp.exp(scores - row_max)
    row_total = jnp.sum(exponent, axis=-1, keepdims=True)
    log_total = row_max + jnp.log(row_total)
    attention = exponent / row_total
    attended = (
        jnp.einsum(
            "grqk,kgd->qgrd",
            attention.astype(jnp.bfloat16),
            value_heads,
            preferred_element_type=jnp.float32,
        )
        .reshape(row_count, local_heads * HD)
        .astype(jnp.bfloat16)
    )
    attn_branch = sum_rows(jnp.dot(attended, out_full, preferred_element_type=jnp.float32))
    hidden = residual_in + attn_branch
    normed_mlp = gather_rows(norm_apply(hidden, mlp_gain).astype(jnp.bfloat16))
    gate_up = jnp.dot(normed_mlp, gate_up_full, preferred_element_type=jnp.float32)
    gate_part = gate_up[:, :local_hidden]
    up_part = gate_up[:, local_hidden:]
    activated = swish_product(gate_part, up_part).astype(jnp.bfloat16)
    mlp_branch = sum_rows(jnp.dot(activated, down_full, preferred_element_type=jnp.float32))
    output = (hidden + mlp_branch).astype(jnp.bfloat16)
    grad_output = cotangent.astype(jnp.float32) * valid_rows
    grad_low = gather_grads(grad_output.astype(jnp.bfloat16))
    qkv_later, out_later, gate_up_later, down_later, grad_low = lax.optimization_barrier(
        (qkv_shard, out_shard, gate_up_shard, down_shard, grad_low)
    )
    qkv_full, out_full, gate_up_full, down_full = (
        lax.all_gather(qkv_later, "fsdp", axis=0, tiled=True),
        lax.all_gather(out_later, "fsdp", axis=1, tiled=True),
        lax.all_gather(gate_up_later, "fsdp", axis=0, tiled=True),
        lax.all_gather(down_later, "fsdp", axis=1, tiled=True),
    )
    grad_activated = jnp.einsum(
        "td,fd->tf", grad_low, down_full, preferred_element_type=jnp.float32
    )
    swish_pull = jax.vjp(swish_product, gate_part, up_part)[1]
    grad_gate, grad_up = swish_pull(grad_activated)
    grad_gate_up = jnp.concatenate([grad_gate, grad_up], axis=1).astype(jnp.bfloat16)
    grad_normed_mlp = sum_grads(
        jnp.einsum("tf,df->td", grad_gate_up, gate_up_full, preferred_element_type=jnp.float32)
    )
    mlp_pull = jax.vjp(norm_apply, hidden, mlp_gain)[1]
    grad_hidden_norm, grad_mlp_gain = mlp_pull(grad_normed_mlp)
    grad_hidden = grad_output + grad_hidden_norm
    grad_attn = gather_grads(grad_hidden.astype(jnp.bfloat16))
    grad_attended = jnp.einsum("td,cd->tc", grad_attn, out_full, preferred_element_type=jnp.float32)
    grad_attended = grad_attended.astype(jnp.bfloat16).reshape(row_count, local_groups, repeat, HD)
    attention = jnp.exp(score_block(queries, key_heads, key_mask, score_scale) - log_total)
    grad_probs = jnp.einsum(
        "qgrd,kgd->grqk", grad_attended, value_heads, preferred_element_type=jnp.float32
    )
    grad_values = jnp.einsum(
        "grqk,qgrd->kgd",
        attention.astype(jnp.bfloat16),
        grad_attended,
        preferred_element_type=jnp.float32,
    )
    inner_sum = jnp.sum(attention * grad_probs, axis=-1, keepdims=True)
    grad_scores = (attention * (grad_probs - inner_sum)).astype(jnp.bfloat16)
    grad_queries = (
        jnp.einsum("grqk,kgd->qgrd", grad_scores, key_heads, preferred_element_type=jnp.float32)
        * score_scale
    )
    grad_keys = (
        jnp.einsum("grqk,qgrd->kgd", grad_scores, queries, preferred_element_type=jnp.float32)
        * score_scale
    )
    query_pull = jax.vjp(head_apply, query_raw, query_gain)[1]
    grad_query_raw, grad_query_gain = query_pull(grad_queries.reshape(row_count, local_heads, HD))
    key_pull = jax.vjp(head_apply, key_raw, key_gain)[1]
    grad_key_raw, grad_key_gain = key_pull(grad_keys)
    grad_projected = jnp.concatenate(
        [
            grad_query_raw.reshape(row_count, local_heads * HD),
            grad_key_raw.reshape(row_count, local_groups * HD),
            grad_values.reshape(row_count, local_groups * HD),
        ],
        axis=1,
    ).astype(jnp.bfloat16)
    grad_down = jnp.einsum("tf,td->fd", activated, grad_low, preferred_element_type=jnp.float32)
    grad_gate_up_weight = jnp.einsum(
        "td,tf->df", normed_mlp, grad_gate_up, preferred_element_type=jnp.float32
    )
    grad_out_weight = jnp.einsum(
        "tc,td->cd", attended, grad_attn, preferred_element_type=jnp.float32
    )
    grad_qkv_weight = jnp.einsum(
        "td,tc->dc", normed_attn, grad_projected, preferred_element_type=jnp.float32
    )
    qkv_sum, out_sum, gate_up_sum, down_sum = (
        lax.psum_scatter(grad_qkv_weight, "fsdp", scatter_dimension=0, tiled=True),
        lax.psum_scatter(grad_out_weight, "fsdp", scatter_dimension=1, tiled=True),
        lax.psum_scatter(grad_gate_up_weight, "fsdp", scatter_dimension=0, tiled=True),
        lax.psum_scatter(grad_down, "fsdp", scatter_dimension=1, tiled=True),
    )
    grad_normed_attn = sum_grads(
        jnp.einsum("tc,dc->td", grad_projected, qkv_full, preferred_element_type=jnp.float32)
    )
    attn_pull = jax.vjp(norm_apply, residual_in, attn_gain)[1]
    grad_input_norm, grad_attn_gain = attn_pull(grad_normed_attn)
    input_grad = (grad_hidden + grad_input_norm).astype(jnp.bfloat16)
    gain_part = jnp.concatenate([grad_attn_gain, grad_mlp_gain, grad_query_gain, grad_key_gain])
    square_part = sum(
        (jnp.sum(member * member) for member in (qkv_sum, out_sum, gate_up_sum, down_sum))
    )
    gain_grad, square_total = lax.psum((gain_part, square_part), ("fsdp", "tp"))
    grad_norm = jnp.sqrt(square_total + jnp.sum(gain_grad * gain_grad))
    factor = jnp.minimum(1.0, clip_norm / (grad_norm + 1e-06))
    new_qkv, new_qkv_one, new_qkv_two = adam_update(
        qkv_weight, qkv_sum, qkv_moment, qkv_square, factor, weight_decay, learn_rate
    )
    new_out, new_out_one, new_out_two = adam_update(
        out_weight, out_sum, out_moment, out_square, factor, weight_decay, learn_rate
    )
    new_gate_up, new_gate_up_one, new_gate_up_two = adam_update(
        gate_up_weight,
        gate_up_sum,
        gate_up_moment,
        gate_up_square,
        factor,
        weight_decay,
        learn_rate,
    )
    new_down, new_down_one, new_down_two = adam_update(
        down_weight, down_sum, down_moment, down_square, factor, weight_decay, learn_rate
    )
    new_gains, new_gains_one, new_gains_two = adam_update(
        norm_gains, gain_grad, gains_moment, gains_square, factor, 0.0, gain_rate
    )
    return (
        output,
        input_grad,
        grad_norm,
        new_qkv,
        new_qkv_one,
        new_qkv_two,
        new_qkv.astype(jnp.bfloat16),
        new_out,
        new_out_one,
        new_out_two,
        new_out.astype(jnp.bfloat16),
        new_gate_up,
        new_gate_up_one,
        new_gate_up_two,
        new_gate_up.astype(jnp.bfloat16),
        new_down,
        new_down_one,
        new_down_two,
        new_down.astype(jnp.bfloat16),
        new_gains,
        new_gains_one,
        new_gains_two,
    )


def solution(mesh):
    return jax.shard_map(
        local,
        mesh=mesh,
        in_specs=(
            P(("fsdp", "tp"), None),
            P(("fsdp", "tp"), None),
            P(),
            P(),
            P("fsdp", "tp"),
            P("tp", "fsdp"),
            P("fsdp", "tp"),
            P("tp", "fsdp"),
            P(),
            P("fsdp", "tp"),
            P("tp", "fsdp"),
            P("fsdp", "tp"),
            P("tp", "fsdp"),
            P(),
            P("fsdp", "tp"),
            P("tp", "fsdp"),
            P("fsdp", "tp"),
            P("tp", "fsdp"),
            P(),
        ),
        out_specs=(
            P(("fsdp", "tp"), None),
            P(("fsdp", "tp"), None),
            P(),
            P("fsdp", "tp"),
            P("fsdp", "tp"),
            P("fsdp", "tp"),
            P("fsdp", "tp"),
            P("tp", "fsdp"),
            P("tp", "fsdp"),
            P("tp", "fsdp"),
            P("tp", "fsdp"),
            P("fsdp", "tp"),
            P("fsdp", "tp"),
            P("fsdp", "tp"),
            P("fsdp", "tp"),
            P("tp", "fsdp"),
            P("tp", "fsdp"),
            P("tp", "fsdp"),
            P("tp", "fsdp"),
            P(),
            P(),
            P(),
        ),
        check_vma=False,
    )
```

profile of v0, /device:TPU:0, one launch (start us, length us, event | category | flops | bytes accessed | tf_op | source)
XLA Modules:
  0.0 2181.6 jit_solution(5927913070004142553)
XLA Ops:
  10.3 2.8 fusion.21
  16.5 2.0 multiply_cosine_fusion
  19.3 35.7 %all-gather.13.cloned.1.call-done = bf16[640,2048]{1,0:T(8,128)(2,1)} async-done(((bf16[320,2048]{1,0:T(8,128)(2,1)}), bf16[640,2048]{1,0:T(8,128)(2,1)}) %all-gather.13.cloned.1.call-update) | async-done | bytes 2621456 | tf_op jit(solution)/shard_map/all_gather | solution.py:75
  55.0 77.7 %all-gather.15.cloned.1.call-done = bf16[2048,2048]{1,0:T(8,128)(2,1)} async-done(((bf16[128,2048]{1,0:T(8,128)(2,1)}), bf16[2048,2048]{1,0:T(8,128)(2,1)}) %all-gather.15.cloned.1.call-update) | async-done | bytes 8388624 | tf_op jit(solution)/shard_map/all_gather | solution.py:152
  132.7 8.8 fusion.81
  152.7 2.7 fusion.76
  155.4 3.1 reshape.263
  158.5 2.8 multiply_reduce_fusion.7
  162.5 2.8 convert_element_type.152
  167.7 3.5 fusion.80
  173.0 3.0 copy-done
  176.0 2.9 fusion.33
  178.9 8.1 all-gather.17.cloned.1.call-done
  186.9 6.6 convolution_convert_fusion.2
  196.3 33.2 %reduce-scatter.9.cloned.1.call-done = bf16[320,2048]{1,0:T(8,128)(2,1)} async-done(((bf16[640,2048]{1,0:T(8,128)(2,1)}), bf16[320,2048]{1,0:T(8,128)(2,1)}) %reduce-scatter.9.cloned.1.call-update) | async-done | bytes 1310736 | tf_op jit(solution)/shard_map/reduce_scatter | solution.py:79
  229.5 1.9 multiply_reduce_fusion.3
  233.2 3.2 convert_element_type.162
  236.5 2.5 convert_element_type.164
  239.0 31.6 %all-gather.25.cloned.1.call-done = bf16[640,2048]{1,0:T(8,128)(2,1)} async-done(((bf16[320,2048]{1,0:T(8,128)(2,1)}), bf16[640,2048]{1,0:T(8,128)(2,1)}) %all-gather.25.cloned.1.call-update) | async-done | bytes 2621456 | tf_op jit(solution)/shard_map/all_gather | solution.py:85
  271.6 40.1 %all-gather.19.cloned.1.call-done = bf16[640,2048]{1,0:T(8,128)(2,1)} async-done(((bf16[320,2048]{1,0:T(8,128)(2,1)}), bf16[640,2048]{1,0:T(8,128)(2,1)}) %all-gather.19.cloned.1.call-update) | async-done | bytes 2621456 | tf_op jit(solution)/shard_map/all_gather | solution.py:75
  311.7 130.9 %all-gather.21.cloned.1.call-done = bf16[2048,6144]{1,0:T(8,128)(2,1)} async-done(((bf16[128,6144]{1,0:T(8,128)(2,1)}), bf16[2048,6144]{1,0:T(8,128)(2,1)}) %all-gather.21.cloned.1.call-update) | async-done | bytes 25165840 | tf_op jit(solution)/shard_map/all_gather | solution.py:154
  442.6 23.3 %fusion.82 = f32[640,6144]{1,0:T(8,128)} fusion(bf16[640,2048]{1,0:T(8,128)(2,1)} %all-gather.19.cloned.1.call-done, bf16[2048,6144]{1,0:T(8,128)(2,1)} %all-gather.21.cloned.1.call-done), kind=kOutput, calls=%fused_computation.170 | convolution fusion | flops 16106127360 | bytes 43515904 | tf_op jit(solution)/shard_map/dot_general | solution.py:193
  465.9 83.6 %all-gather.27.cloned.1.call-done = bf16[3072,2048]{1,0:T(8,128)(2,1)} async-done(((bf16[3072,128]{1,0:T(8,128)(2,1)}), bf16[3072,2048]{1,0:T(8,128)(2,1)}) %all-gather.27.cloned.1.call-update) | async-done | bytes 12582928 | tf_op jit(solution)/shard_map/all_gather | solution.py:208
  549.5 21.0 fusion.7
  570.5 108.1 %all-gather.29.cloned.1.call-done = bf16[2048,6144]{1,0:T(8,128)(2,1)} async-done(((bf16[128,6144]{1,0:T(8,128)(2,1)}), bf16[2048,6144]{1,0:T(8,128)(2,1)}) %all-gather.29.cloned.1.call-update) | async-done | bytes 25165840 | tf_op jit(solution)/shard_map/all_gather | solution.py:207
  678.6 23.2 %fusion.15 = bf16[640,2048]{1,0:T(8,128)(2,1)} fusion(bf16[2048,6144]{1,0:T(8,128)(2,1)} %all-gather.29.cloned.1.call-done, bf16[640,3072]{1,0:T(8,128)(2,1)} %get-tuple-element.62, bf16[640,3072]{1,0:T(8,128)(2,1)} %get-tuple-element.61), kind=kOutput, calls=%fused_computation.38 | convolution fusion | flops 16123166720 | bytes 35651584 | tf_op jit(solution)/shard_map/tf,df->td/dot_general | solution.py:217
  702.6 36.9 %reduce-scatter.13.cloned.1.call-done = bf16[320,2048]{1,0:T(8,128)(2,1)} async-done(((bf16[640,2048]{1,0:T(8,128)(2,1)}), bf16[320,2048]{1,0:T(8,128)(2,1)}) %reduce-scatter.13.cloned.1.call-update) | async-done | bytes 1310736 | tf_op jit(solution)/shard_map/reduce_scatter | solution.py:89
  739.5 3.2 fusion.23
  742.7 2.1 fusion.66
  746.3 49.2 %all-gather.33.cloned.1.call-done = bf16[1024,2048]{1,0:T(8,128)(2,1)} async-done(((bf16[1024,128]{1,0:T(8,128)(2,1)}), bf16[1024,2048]{1,0:T(8,128)(2,1)}) %all-gather.33.cloned.1.call-update) | async-done | bytes 4194320 | tf_op jit(solution)/shard_map/all_gather | solution.py:206
  795.5 39.2 %all-gather.31.cloned.1.call-done = bf16[640,2048]{1,0:T(8,128)(2,1)} async-done(((bf16[320,2048]{1,0:T(8,128)(2,1)}), bf16[640,2048]{1,0:T(8,128)(2,1)}) %all-gather.31.cloned.1.call-update) | async-done | bytes 2621456 | tf_op jit(solution)/shard_map/all_gather | solution.py:85
  834.7 5.9 convolution_convert_fusion.3
  841.8 11.9 fusion
  855.8 6.5 fusion.2
  865.3 2.1 copy.197
  867.4 2.1 copy.198
  869.5 4.2 multiply_add_fusion.2
  873.9 3.3 multiply_reduce_fusion.1
  879.2 4.7 fusion.26
  886.1 4.8 fusion.36
  896.3 7.2 fusion.40
  903.7 8.6 all-gather.35.cloned.1.call-done
  912.4 10.4 convolution_convert_fusion
  922.8 8.9 fusion.83
  932.9 12.3 fusion.46
  946.9 15.9 fusion.84
  964.6 28.5 %fusion.13 = f32[2048,6144]{1,0:T(8,128)} fusion(bf16[640,2048]{1,0:T(8,128)(2,1)S(1)} %copy-done.39, bf16[640,3072]{1,0:T(8,128)(2,1)} %get-tuple-element.62, bf16[640,3072]{1,0:T(8,128)(2,1)} %get-tuple-element.61), kind=kOutput, calls=%fused_computation.28 | convolution fusion | flops 16121856000 | bytes 60817408 | tf_op jit(solution)/shard_map/td,tf->df/dot_general | solution.py:258
  993.2 24.0 %all-gather.23.cloned.1.call-done = bf16[3072,2048]{1,0:T(8,128)(2,1)} async-done(((bf16[3072,128]{1,0:T(8,128)(2,1)}), bf16[3072,2048]{1,0:T(8,128)(2,1)}) %all-gather.23.cloned.1.call-update) | async-done | bytes 12582928 | tf_op jit(solution)/shard_map/all_gather | solution.py:155
  1017.2 13.7 convolution_convert_fusion.1
  1030.9 24.7 %reduce-scatter.15.cloned.1.call-done = bf16[320,2048]{1,0:T(8,128)(2,1)} async-done(((bf16[640,2048]{1,0:T(8,128)(2,1)}), bf16[320,2048]{1,0:T(8,128)(2,1)}) %reduce-scatter.15.cloned.1.call-update) | async-done | bytes 1310736 | tf_op jit(solution)/shard_map/reduce_scatter | solution.py:89
  1055.7 2.4 fusion.24
  1058.1 107.0 %reduce-scatter.19.cloned.1.call-done = f32[1024,128]{1,0:T(8,128)} async-done(((f32[1024,2048]{1,0:T(8,128)}), f32[1024,128]{1,0:T(8,128)}) %reduce-scatter.19.cloned.1.call-update) | async-done | bytes 524304 | tf_op jit(solution)/shard_map/reduce_scatter | solution.py:269
  1166.9 181.1 %reduce-scatter.17.cloned.1.call-done = f32[128,2048]{1,0:T(8,128)} async-done(((f32[2048,2048]{1,0:T(8,128)}), f32[128,2048]{1,0:T(8,128)}) %reduce-scatter.17.cloned.1.call-update) | async-done | bytes 1048592 | tf_op jit(solution)/shard_map/reduce_scatter | solution.py:268
  1348.0 2.1 multiply_reduce_fusion.8
  1351.5 243.9 %reduce-scatter.23.cloned.1.call-done = f32[3072,128]{1,0:T(8,128)} async-done(((f32[3072,2048]{1,0:T(8,128)}), f32[3072,128]{1,0:T(8,128)}) %reduce-scatter.23.cloned.1.call-update) | async-done | bytes 1572880 | tf_op jit(solution)/shard_map/reduce_scatter | solution.py:271
  1595.4 2.4 multiply_reduce_fusion.5
  1597.9 469.4 %reduce-scatter.21.cloned.1.call-done = f32[128,6144]{1,0:T(8,128)} async-done(((f32[2048,6144]{1,0:T(8,128)}), f32[128,6144]{1,0:T(8,128)}) %reduce-scatter.21.cloned.1.call-update) | async-done | bytes 3145744 | tf_op jit(solution)/shard_map/reduce_scatter | solution.py:270
  2067.2 3.3 multiply_reduce_fusion
  2071.8 34.9 %reduce-scatter.11.cloned.1.call-done = bf16[320,2048]{1,0:T(8,128)(2,1)} async-done(((bf16[640,2048]{1,0:T(8,128)(2,1)}), bf16[320,2048]{1,0:T(8,128)(2,1)}) %reduce-scatter.11.cloned.1.call-update) | async-done | bytes 1310736 | tf_op jit(solution)/shard_map/reduce_scatter | solution.py:79
  2106.7 5.1 fusion.28
  2111.8 39.7 %all-reduce.4 = (f32[]{:T(128)}, f32[4352]{0:T(1024)S(1)}) all-reduce(f32[]{:T(128)S(6)} %add.220, f32[4352]{0:T(1024)S(1)} %pad_maximum_fusion.11), channel_id=1, replica_groups=mesh['fsdp'=16,'tp'=2] {'fsdp','tp'}, use_global_device_ids=true, to_apply=%region_24.25 | all-reduce | flops 4353 | bytes 34824 | tf_op jit(solution)/shard_map/psum | solution.py:283
  2154.1 6.3 fusion.68
  2161.8 6.5 fusion.70
  2170.8 2.4 fusion.74
  (263 shorter events, 58.7 us)
Async XLA Ops:
  7.2 47.8 %all-gather.13.cloned.1.call-start = ((), (), s32[]{:S(2)}) async-start(), calls=%async_computation.8 | async-start | bytes 3932160 | tf_op jit(solution)/shard_map/all_gather | solution.py:75
  8.0 5.2 copy-start.55
  8.0 734.7 %copy-start.49 = (f32[2048]{0:T(1024)}, f32[2048]{0:T(1024)S(1)}, u32[]{:S(2)}) copy-start(f32[2048]{0:T(1024)S(1)} %get-tuple-element.78) | copy-start | bytes 24580
  8.0 5.2 copy-start.33
  13.1 119.5 %all-gather.15.cloned.1.call-start = ((), (), s32[]{:S(2)}) async-start(), calls=%async_computation.9 | async-start | bytes 8912896 | tf_op jit(solution)/shard_map/all_gather | solution.py:152
  14.1 172.8 %all-gather.17.cloned.1.call-start = ((), (), s32[]{:S(2)}) async-start(), calls=%async_computation.10 | async-start | bytes 4456448 | tf_op jit(solution)/shard_map/all_gather | solution.py:153
  14.9 214.6 %reduce-scatter.9.cloned.1.call-start = ((), (), s32[]{:S(2)}) async-start(), calls=%async_computation.11 | async-start | bytes 3932160 | tf_op jit(solution)/shard_map/reduce_scatter | solution.py:79
  18.5 147.8 %copy-start.23 = (f32[640,64]{1,0:T(8,128)}, f32[640,64]{1,0:T(8,128)S(1)}, u32[]{:S(2)}) copy-start(f32[640,64]{1,0:T(8,128)S(1)} %get-tuple-element.82) | copy-start | bytes 491524
  19.3 129.0 %copy-start.75 = (f32[128]{0:T(128)}, f32[128]{0:T(128)S(1)}, u32[]{:S(2)}) copy-start(f32[128]{0:T(128)S(1)} %get-tuple-element.81) | copy-start | bytes 1540
  19.3 146.1 %copy-start.73 = (f32[128]{0:T(128)}, f32[128]{0:T(128)S(1)}, u32[]{:S(2)}) copy-start(f32[128]{0:T(128)S(1)} %get-tuple-element.80) | copy-start | bytes 1540
  144.6 5.4 copy-start.1
  151.2 15.7 copy-start.16
  155.4 10.0 copy-start.10
  171.2 4.7 copy-start
  171.2 4.7 copy-start.38
  178.8 8.1 copy-start.80
  193.6 35.9 %copy-start.3 = (bf16[320,2048]{1,0:T(8,128)(2,1)S(1)}, bf16[320,2048]{1,0:T(8,128)(2,1)}, u32[]{:S(2)}) copy-start(bf16[320,2048]{1,0:T(8,128)(2,1)} %param.19) | copy-start | bytes 3932164
  193.6 77.0 %all-gather.25.cloned.1.call-start = ((), (), s32[]{:S(2)}) async-start(), calls=%async_computation.16 | async-start | bytes 3932160 | tf_op jit(solution)/shard_map/all_gather | solution.py:85
  194.9 547.8 %copy-start.65 = (f32[320]{0:T(512)}, f32[320]{0:T(512)S(1)}, u32[]{:S(2)}) copy-start(f32[320]{0:T(512)S(1)} %fusion.55) | copy-start | bytes 3844
  196.2 115.5 %all-gather.19.cloned.1.call-start = ((), (), s32[]{:S(2)}) async-start(), calls=%async_computation.12 | async-start | bytes 3932160 | tf_op jit(solution)/shard_map/all_gather | solution.py:75
  231.5 511.2 %copy-start.60 = (f32[320]{0:T(512)}, f32[320]{0:T(512)S(1)}, u32[]{:S(2)}) copy-start(f32[320]{0:T(512)S(1)} %fusion.57) | copy-start | bytes 3844
  233.1 209.4 %all-gather.21.cloned.1.call-start = ((), (), s32[]{:S(2)}) async-start(), calls=%async_computation.13 | async-start | bytes 26738688 | tf_op jit(solution)/shard_map/all_gather | solution.py:154
  236.4 313.1 %all-gather.27.cloned.1.call-start = ((), (), s32[]{:S(2)}) async-start(), calls=%async_computation.17 | async-start | bytes 13369344 | tf_op jit(solution)/shard_map/all_gather | solution.py:208
  270.6 407.9 %all-gather.29.cloned.1.call-start = ((), (), s32[]{:S(2)}) async-start(), calls=%async_computation.18 | async-start | bytes 26738688 | tf_op jit(solution)/shard_map/all_gather | solution.py:207
  271.4 468.1 %reduce-scatter.13.cloned.1.call-start = ((), (), s32[]{:S(2)}) async-start(), calls=%async_computation.19 | async-start | bytes 3932160 | tf_op jit(solution)/shard_map/reduce_scatter | solution.py:89
  701.8 93.7 %all-gather.33.cloned.1.call-start = ((), (), s32[]{:S(2)}) async-start(), calls=%async_computation.21 | async-start | bytes 4456448 | tf_op jit(solution)/shard_map/all_gather | solution.py:206
  702.5 132.2 %all-gather.31.cloned.1.call-start = ((), (), s32[]{:S(2)}) async-start(), calls=%async_computation.20 | async-start | bytes 3932160 | tf_op jit(solution)/shard_map/all_gather | solution.py:85
  744.9 167.5 %all-gather.35.cloned.1.call-start = ((), (), s32[]{:S(2)}) async-start(), calls=%async_computation.22 | async-start | bytes 8912896 | tf_op jit(solution)/shard_map/all_gather | solution.py:205
  745.7 271.5 %all-gather.23.cloned.1.call-start = ((), (), s32[]{:S(2)}) async-start(), calls=%async_computation.14 | async-start | bytes 13369344 | tf_op jit(solution)/shard_map/all_gather | solution.py:155
  746.2 309.4 %reduce-scatter.15.cloned.1.call-start = ((), (), s32[]{:S(2)}) async-start(), calls=%async_computation.23 | async-start | bytes 3932160 | tf_op jit(solution)/shard_map/reduce_scatter | solution.py:89
  841.7 12.0 copy-start.14
  841.7 12.0 slice-start
  841.8 12.4 slice-start.1
  841.8 14.0 slice-start.2
  841.8 14.0 slice-start.3
  855.8 6.6 copy-start.29
  855.8 6.6 copy-start.31
  896.3 16.1 copy-start.43
  922.8 242.3 %reduce-scatter.19.cloned.1.call-start = ((), (), s32[]{:S(2)}) async-start(), calls=%async_computation.25 | async-start | bytes 8912896 | tf_op jit(solution)/shard_map/reduce_scatter | solution.py:269
  931.8 416.2 %reduce-scatter.17.cloned.1.call-start = ((), (), s32[]{:S(2)}) async-start(), calls=%async_computation.24 | async-start | bytes 17825792 | tf_op jit(solution)/shard_map/reduce_scatter | solution.py:268
  945.2 650.2 %reduce-scatter.23.cloned.1.call-start = ((), (), s32[]{:S(2)}) async-start(), calls=%async_computation.27 | async-start | bytes 26738688 | tf_op jit(solution)/shard_map/reduce_scatter | solution.py:271
  962.8 1104.4 %reduce-scatter.21.cloned.1.call-start = ((), (), s32[]{:S(2)}) async-start(), calls=%async_computation.26 | async-start | bytes 53477376 | tf_op jit(solution)/shard_map/reduce_scatter | solution.py:270
  993.1 1113.6 %reduce-scatter.11.cloned.1.call-start = ((), (), s32[]{:S(2)}) async-start(), calls=%async_computation.15 | async-start | bytes 3932160 | tf_op jit(solution)/shard_map/reduce_scatter | solution.py:79
  1030.9 24.8 %copy-start.4 = (bf16[320,2048]{1,0:T(8,128)(2,1)S(1)}, bf16[320,2048]{1,0:T(8,128)(2,1)}, u32[]{:S(2)}) copy-start(bf16[320,2048]{1,0:T(8,128)(2,1)} %param.19) | copy-start | bytes 3932164
  1030.9 24.8 %copy-start.56 = (f32[2048]{0:T(1024)S(1)}, f32[2048]{0:T(1024)}, u32[]{:S(2)}) copy-start(f32[2048]{0:T(1024)} %copy-done.55) | copy-start | bytes 24580
  1030.9 24.8 %copy-start.64 = (f32[320]{0:T(512)S(1)}, f32[320]{0:T(512)}, u32[]{:S(2)}) copy-start(f32[320]{0:T(512)} %copy-done.63) | copy-start | bytes 3844
  1030.9 27.2 %copy-start.62 = (f32[2048]{0:T(1024)S(1)}, f32[2048]{0:T(1024)}, u32[]{:S(2)}) copy-start(f32[2048]{0:T(1024)} %get-tuple-element.34) | copy-start | bytes 24580
  1030.9 27.2 %copy-start.72 = (f32[320]{0:T(512)S(1)}, f32[320]{0:T(512)}, u32[]{:S(2)}) copy-start(f32[320]{0:T(512)} %copy-done.71) | copy-start | bytes 3844
  1350.1 756.6 %copy-start.7 = (bf16[320,2048]{1,0:T(8,128)(2,1)S(1)}, bf16[320,2048]{1,0:T(8,128)(2,1)}, u32[]{:S(2)}) copy-start(bf16[320,2048]{1,0:T(8,128)(2,1)} %reduce-scatter.9.cloned.1.call-done) | copy-start | bytes 3932164
  1350.1 756.6 %copy-start.50 = (f32[2048]{0:T(1024)S(1)}, f32[2048]{0:T(1024)}, u32[]{:S(2)}) copy-start(f32[2048]{0:T(1024)} %copy-done.49) | copy-start | bytes 24580
  1350.1 756.6 %copy-start.61 = (f32[320]{0:T(512)S(1)}, f32[320]{0:T(512)}, u32[]{:S(2)}) copy-start(f32[320]{0:T(512)} %copy-done.60) | copy-start | bytes 3844
  1350.1 756.6 %copy-start.66 = (f32[320]{0:T(512)S(1)}, f32[320]{0:T(512)}, u32[]{:S(2)}) copy-start(f32[320]{0:T(512)} %copy-done.65) | copy-start | bytes 3844
  1350.1 756.6 %copy-start.70 = (f32[320]{0:T(512)S(1)}, f32[320]{0:T(512)}, u32[]{:S(2)}) copy-start(f32[320]{0:T(512)} %copy-done.69) | copy-start | bytes 3844
  2071.8 81.7 %copy-start.59 = (f32[4352]{0:T(1024)S(1)}, f32[4352]{0:T(1024)}, u32[]{:S(2)}) copy-start(f32[4352]{0:T(1024)} %param.27) | copy-start | bytes 52228
  2071.8 81.7 %copy-start.67 = (f32[4352]{0:T(1024)S(1)}, f32[4352]{0:T(1024)}, u32[]{:S(2)}) copy-start(f32[4352]{0:T(1024)} %param.32) | copy-start | bytes 52228
  2071.8 81.7 %copy-start.68 = (f32[4352]{0:T(1024)S(1)}, f32[4352]{0:T(1024)}, u32[]{:S(2)}) copy-start(f32[4352]{0:T(1024)} %param.37) | copy-start | bytes 52228
  2154.1 6.3 copy-start.12
  2154.1 6.3 copy-start.13
  2154.1 7.6 copy-start.37
  2161.7 6.5 copy-start.41
  2161.7 6.5 copy-start.42
  2161.7 6.5 copy-start.47
  2161.7 6.5 copy-start.48
  2161.7 8.1 copy-start.45
  (41 other events, 101.4 us)
Sparse Core Ops, SparseCore 0:
  13.2 41.7 all-gather.12
  57.7 74.8 all-gather.14
  135.4 51.4 all-gather.16
  193.7 35.7 reduce-scatter.8
  231.6 39.0 all-gather.24
  272.7 39.0 all-gather.18
  314.0 128.5 all-gather.20
  445.5 103.9 all-gather.26
  551.8 126.7 all-gather.28
  701.9 37.5 reduce-scatter.12
  742.2 53.2 all-gather.32
  797.5 37.1 all-gather.30
  837.4 74.8 all-gather.34
  915.0 102.1 all-gather.22
  1019.8 35.7 reduce-scatter.14
  1060.1 104.9 reduce-scatter.18
  1169.6 178.3 reduce-scatter.16
  1352.5 242.8 reduce-scatter.22
  1600.3 466.9 reduce-scatter.20
  2070.0 36.6 reduce-scatter.10
where the time goes:
time: 2190 us; the launch traced here: 2180 us
  waiting for transfers between devices  1770 us (81%)
  matrix products  210 us (10%)
  other arithmetic  93.2 us (4%)
  local copies, waits for them, and re-layouts  45.8 us (2%)
  blocking collectives  39.7 us (2%)
    reduce_scatter x1, waiting for transfers between devices, local(): lax.psum_scatter(grad_gate_up_weight, 'fsdp', scatter_dimension=0, tiled=...  469 us
    reduce_scatter x1, waiting for transfers between devices, local(): lax.psum_scatter(grad_down, 'fsdp', scatter_dimension=1, tiled=True)  244 us
    reduce_scatter x1, waiting for transfers between devices, local(): lax.psum_scatter(grad_qkv_weight, 'fsdp', scatter_dimension=0, tiled=True)  181 us
    all_gather x1, waiting for transfers between devices, local(): lax.all_gather(gate_up_shard, 'fsdp', axis=0, tiled=True)  131 us
    all_gather x1, waiting for transfers between devices, local(): lax.all_gather(gate_up_later, 'fsdp', axis=0, tiled=True)  108 us
    reduce_scatter x1, waiting for transfers between devices, local(): lax.psum_scatter(grad_out_weight, 'fsdp', scatter_dimension=1, tiled=True)  107 us
    all_gather x1, waiting for transfers between devices, local(): lax.all_gather(down_later, 'fsdp', axis=1, tiled=True)  83.6 us
    all_gather x1, waiting for transfers between devices, local(): lax.all_gather(qkv_shard, 'fsdp', axis=0, tiled=True)  77.7 us
  transfers between devices with their start and end apart: 20, of which 20 were waited for; matrix products, arithmetic and copies ran while one was open for 12% of the time, Pallas kernels for 0%

commit v1 on v0

--- a/solution.py
+++ b/solution.py
@@ -88,6 +88,12 @@
 def sum_grads(values):
     return lax.psum_scatter(
         values.astype(jnp.bfloat16), "tp", scatter_dimension=0, tiled=True
+    ).astype(jnp.float32)
+
+
+def sum_weight(values, axis):
+    return lax.psum_scatter(
+        values.astype(jnp.bfloat16), "fsdp", scatter_dimension=axis, tiled=True
     ).astype(jnp.float32)
 
 
@@ -198,15 +204,6 @@
     output = (hidden + mlp_branch).astype(jnp.bfloat16)
     grad_output = cotangent.astype(jnp.float32) * valid_rows
     grad_low = gather_grads(grad_output.astype(jnp.bfloat16))
-    qkv_later, out_later, gate_up_later, down_later, grad_low = lax.optimization_barrier(
-        (qkv_shard, out_shard, gate_up_shard, down_shard, grad_low)
-    )
-    qkv_full, out_full, gate_up_full, down_full = (
-        lax.all_gather(qkv_later, "fsdp", axis=0, tiled=True),
-        lax.all_gather(out_later, "fsdp", axis=1, tiled=True),
-        lax.all_gather(gate_up_later, "fsdp", axis=0, tiled=True),
-        lax.all_gather(down_later, "fsdp", axis=1, tiled=True),
-    )
     grad_activated = jnp.einsum(
         "td,fd->tf", grad_low, down_full, preferred_element_type=jnp.float32
     )
@@ -265,10 +262,10 @@
         "td,tc->dc", normed_attn, grad_projected, preferred_element_type=jnp.float32
     )
     qkv_sum, out_sum, gate_up_sum, down_sum = (
-        lax.psum_scatter(grad_qkv_weight, "fsdp", scatter_dimension=0, tiled=True),
-        lax.psum_scatter(grad_out_weight, "fsdp", scatter_dimension=1, tiled=True),
-        lax.psum_scatter(grad_gate_up_weight, "fsdp", scatter_dimension=0, tiled=True),
-        lax.psum_scatter(grad_down, "fsdp", scatter_dimension=1, tiled=True),
+        sum_weight(grad_qkv_weight, 0),
+        sum_weight(grad_out_weight, 1),
+        sum_weight(grad_gate_up_weight, 0),
+        sum_weight(grad_down, 1),
     )
     grad_normed_attn = sum_grads(
         jnp.einsum("tc,dc->td", grad_projected, qkv_full, preferred_element_type=jnp.float32)

time: 2190 us -> 1470 us (0.67)
  waiting for transfers between devices: 1770 us -> 1050 us
    reduce_scatter x4 -> x2, waiting for transfers between devices: 1000 us -> 350 us  [sum_weight(): lax.psum_scatter(values.astype(jnp.bfloat16), 'fsdp', scatter_dimension=a...]
    all_gather x4 -> x0, waiting for transfers between devices: 250 us -> none  [the longest x1 108 us: local(): lax.all_gather(gate_up_later, 'fsdp', axis=0, tiled=True)]
    unnamed x20 -> x18, waiting for transfers between devices: 2.84 us -> 147 us
    all_gather x1, waiting for transfers between devices: 24 us -> 107 us  [local(): lax.all_gather(down_shard, 'fsdp', axis=1, tiled=True)]
    reduce_scatter x2, waiting for transfers between devices: 61.7 us -> 35.9 us  [sum_grads(): lax.psum_scatter(values.astype(jnp.bfloat16), 'tp', scatter_dimension=0,...]
    unnamed x175 -> x169, local copies, waits for them, and re-layouts: 24.9 us -> 47.4 us
  transfers between devices with their start and end apart: 20 -> 16, of which waited for: 20 -> 15; matrix products, arithmetic and copies ran while one was open for 12% -> 13% of each run, Pallas kernels for 0% -> 0%
where the time goes in v1:
time: 1470 us
  waiting for transfers between devices  1050 us (71%)
  matrix products  202 us (14%)
  other arithmetic  88 us (6%)
  local copies, waits for them, and re-layouts  66.8 us (5%)
  blocking collectives  40 us (3%)
  between operations  20.4 us (1%)
    reduce_scatter x2, waiting for transfers between devices, sum_weight(): lax.psum_scatter(values.astype(jnp.bfloat16), 'fsdp', scatter_dimension=a...  350 us
    unnamed x18, waiting for transfers between devices  147 us
    all_gather x1, waiting for transfers between devices, local(): lax.all_gather(gate_up_shard, 'fsdp', axis=0, tiled=True)  131 us
    all_gather x1, waiting for transfers between devices, local(): lax.all_gather(down_shard, 'fsdp', axis=1, tiled=True)  107 us
    all_gather x1, waiting for transfers between devices, local(): lax.all_gather(qkv_shard, 'fsdp', axis=0, tiled=True)  77.7 us
    reduce_scatter x2, waiting for transfers between devices, sum_rows(): lax.psum_scatter(values.astype(jnp.bfloat16), 'tp', scatter_dimension=0,...  70.9 us
    all_gather x2, waiting for transfers between devices, gather_rows(): return lax.all_gather(values, 'tp', axis=0, tiled=True)  65.5 us
    all_gather x2, waiting for transfers between devices, gather_grads(): return lax.all_gather(values, 'tp', axis=0, tiled=True)  57.2 us
  transfers between devices with their start and end apart: 16, of which 15 were waited for; matrix products, arithmetic and copies ran while one was open for 13% of the time, Pallas kernels for 0%

profile of v1, /device:TPU:0, one launch (start us, length us, event | category | flops | bytes accessed | tf_op | source)
XLA Modules:
  0.0 1467.3 jit_solution(2184326137695413605)
XLA Ops:
  9.8 2.8 fusion.23
  15.9 2.0 multiply_cosine_fusion
  18.7 35.7 %all-gather.9.cloned.1.call-done = bf16[640,2048]{1,0:T(8,128)(2,1)} async-done(((bf16[320,2048]{1,0:T(8,128)(2,1)}), bf16[640,2048]{1,0:T(8,128)(2,1)}) %all-gather.9.cloned.1.call-update) | async-done | bytes 2621456 | tf_op jit(solution)/shard_map/all_gather | solution.py:75
  54.5 77.7 %all-gather.11.cloned.1.call-done = bf16[2048,2048]{1,0:T(8,128)(2,1)} async-done(((bf16[128,2048]{1,0:T(8,128)(2,1)}), bf16[2048,2048]{1,0:T(8,128)(2,1)}) %all-gather.11.cloned.1.call-update) | async-done | bytes 8388624 | tf_op jit(solution)/shard_map/all_gather | solution.py:158
  132.1 8.8 fusion.95
  140.9 2.3 copy-done.32
  146.9 4.1 fusion.90
  151.0 2.6 reshape.263
  153.6 2.8 multiply_reduce_fusion.5
  161.1 2.0 multiply_multiply_fusion.1
  166.9 3.5 fusion.94
  172.2 2.9 copy-done
  175.1 2.9 fusion.36
  178.0 8.3 all-gather.13.cloned.1.call-done
  186.4 6.6 convolution_convert_fusion.6
  193.3 35.7 %reduce-scatter.13.cloned.1.call-done = bf16[320,2048]{1,0:T(8,128)(2,1)} async-done(((bf16[640,2048]{1,0:T(8,128)(2,1)}), bf16[320,2048]{1,0:T(8,128)(2,1)}) %reduce-scatter.13.cloned.1.call-update) | async-done | bytes 1310736 | tf_op jit(solution)/shard_map/reduce_scatter | solution.py:79
  229.0 1.9 multiply_reduce_fusion.2
  232.7 3.2 convert_element_type.186
  236.6 2.7 fusion.33
  239.4 2.6 convert_element_type.188
  242.0 29.8 %all-gather.15.cloned.1.call-done = bf16[640,2048]{1,0:T(8,128)(2,1)} async-done(((bf16[320,2048]{1,0:T(8,128)(2,1)}), bf16[640,2048]{1,0:T(8,128)(2,1)}) %all-gather.15.cloned.1.call-update) | async-done | bytes 2621456 | tf_op jit(solution)/shard_map/all_gather | solution.py:75
  271.8 130.7 %all-gather.17.cloned.1.call-done = bf16[2048,6144]{1,0:T(8,128)(2,1)} async-done(((bf16[128,6144]{1,0:T(8,128)(2,1)}), bf16[2048,6144]{1,0:T(8,128)(2,1)}) %all-gather.17.cloned.1.call-update) | async-done | bytes 25165840 | tf_op jit(solution)/shard_map/all_gather | solution.py:160
  402.5 23.2 %fusion.96 = f32[640,6144]{1,0:T(8,128)} fusion(bf16[640,2048]{1,0:T(8,128)(2,1)} %all-gather.15.cloned.1.call-done, bf16[2048,6144]{1,0:T(8,128)(2,1)} %all-gather.17.cloned.1.call-done), kind=kOutput, calls=%fused_computation.184 | convolution fusion | flops 16106127360 | bytes 43515904 | tf_op jit(solution)/shard_map/dot_general | solution.py:199
  425.7 18.1 %all-gather.21.cloned.1.call-done = bf16[640,2048]{1,0:T(8,128)(2,1)} async-done(((bf16[320,2048]{1,0:T(8,128)(2,1)}), bf16[640,2048]{1,0:T(8,128)(2,1)}) %all-gather.21.cloned.1.call-update) | async-done | bytes 2621456 | tf_op jit(solution)/shard_map/all_gather | solution.py:85
  443.7 106.9 %all-gather.19.cloned.1.call-done = bf16[3072,2048]{1,0:T(8,128)(2,1)} async-done(((bf16[3072,128]{1,0:T(8,128)(2,1)}), bf16[3072,2048]{1,0:T(8,128)(2,1)}) %all-gather.19.cloned.1.call-update) | async-done | bytes 12582928 | tf_op jit(solution)/shard_map/all_gather | solution.py:161
  550.7 21.1 %fusion.7 = (bf16[640,3072]{1,0:T(8,128)(2,1)}, bf16[640,3072]{1,0:T(8,128)(2,1)}, bf16[640,3072]{1,0:T(8,128)(2,1)}) fusion(f32[640,6144]{1,0:T(8,128)} %fusion.96, bf16[640,2048]{1,0:T(8,128)(2,1)} %all-gather.21.cloned.1.call-done, bf16[3072,2048]{1,0:T(8,128)(2,1)} %all-gather.19.cloned.1.call-done), kind=kOutput, calls=%fused_computation.16 | convolution fusion | flops 8084520960 | bytes 42729472 | tf_op jit(solution)/shard_map/td,fd->tf/dot_general | solution.py:207
  571.8 23.4 %fusion.15 = bf16[640,2048]{1,0:T(8,128)(2,1)} fusion(bf16[2048,6144]{1,0:T(8,128)(2,1)} %all-gather.17.cloned.1.call-done, bf16[640,3072]{1,0:T(8,128)(2,1)} %get-tuple-element.52, bf16[640,3072]{1,0:T(8,128)(2,1)} %get-tuple-element.51), kind=kOutput, calls=%fused_computation.44 | convolution fusion | flops 16123166720 | bytes 35651584 | tf_op jit(solution)/shard_map/tf,df->td/dot_general | solution.py:214
  595.2 35.9 %reduce-scatter.17.cloned.1.call-done = bf16[320,2048]{1,0:T(8,128)(2,1)} async-done(((bf16[640,2048]{1,0:T(8,128)(2,1)}), bf16[320,2048]{1,0:T(8,128)(2,1)}) %reduce-scatter.17.cloned.1.call-update) | async-done | bytes 1310736 | tf_op jit(solution)/shard_map/reduce_scatter | solution.py:89
  631.1 3.2 fusion.25
  634.3 2.1 fusion.76
  636.6 39.1 %all-gather.23.cloned.1.call-done = bf16[640,2048]{1,0:T(8,128)(2,1)} async-done(((bf16[320,2048]{1,0:T(8,128)(2,1)}), bf16[640,2048]{1,0:T(8,128)(2,1)}) %all-gather.23.cloned.1.call-update) | async-done | bytes 2621456 | tf_op jit(solution)/shard_map/all_gather | solution.py:85
  675.7 5.9 convolution_convert_fusion.7
  682.5 7.0 fusion.45
  689.5 9.4 fusion
  699.0 6.7 fusion.2
  705.7 2.0 fusion.41
  707.7 2.9 convolution_multiply_fusion
  711.7 3.0 fusion.91
  714.7 3.2 copy.201
  723.0 2.3 copy.202
  725.3 3.3 multiply_add_fusion.1
  728.7 2.6 multiply_reduce_fusion
  731.6 4.4 fusion.28
  737.4 10.3 convolution_convert_fusion.4
  747.7 7.6 convolution_convert_fusion.3
  755.3 6.4 copy.197
  761.7 15.9 %convolution_convert_fusion.1 = bf16[3072,2048]{1,0:T(8,128)(2,1)} fusion(bf16[640,3072]{1,0:T(8,128)(2,1)} %get-tuple-element.53, bf16[640,2048]{1,0:T(8,128)(2,1)} %all-gather.21.cloned.1.call-done), kind=kOutput, calls=%fused_computation.12 | convolution fusion | flops 8059355136 | bytes 19136512 | tf_op jit(solution)/shard_map/tf,td->fd/dot_general | solution.py:254
  777.6 16.7 %copy.199 = bf16[3072,2048]{0,1:T(8,128)(2,1)} copy(bf16[3072,2048]{1,0:T(8,128)(2,1)} %convolution_convert_fusion.1) | data formatting | bytes 25165824
  794.4 11.1 convolution_convert_fusion.2
  807.3 27.0 %convolution_convert_fusion = bf16[2048,6144]{1,0:T(8,128)(2,1)} fusion(bf16[640,2048]{1,0:T(8,128)(2,1)S(1)} %copy-done.74, bf16[640,3072]{1,0:T(8,128)(2,1)} %get-tuple-element.52, bf16[640,3072]{1,0:T(8,128)(2,1)} %get-tuple-element.51), kind=kOutput, calls=%fused_computation | convolution fusion | flops 16134438912 | bytes 35651584 | tf_op jit(solution)/shard_map/td,tf->df/dot_general | solution.py:255
  834.3 13.6 convolution_convert_fusion.5
  849.2 2.4 fusion.26
  851.7 10.4 reduce-scatter.25.cloned.1.call-done
  864.0 135.9 %reduce-scatter.27.cloned.1.call-done = bf16[128,3072]{1,0:T(8,128)(2,1)} async-done(((bf16[2048,3072]{1,0:T(8,128)(2,1)}), bf16[128,3072]{1,0:T(8,128)(2,1)}) %reduce-scatter.27.cloned.1.call-update) | async-done | bytes 786448
  1002.5 105.2 %reduce-scatter.21.cloned.1.call-done = bf16[128,2048]{1,0:T(8,128)(2,1)} async-done(((bf16[2048,2048]{1,0:T(8,128)(2,1)}), bf16[128,2048]{1,0:T(8,128)(2,1)}) %reduce-scatter.21.cloned.1.call-update) | async-done | bytes 524304 | tf_op jit(solution)/shard_map/reduce_scatter | solution.py:95
  1110.9 244.4 %reduce-scatter.23.cloned.1.call-done = bf16[128,6144]{1,0:T(8,128)(2,1)} async-done(((bf16[2048,6144]{1,0:T(8,128)(2,1)}), bf16[128,6144]{1,0:T(8,128)(2,1)}) %reduce-scatter.23.cloned.1.call-update) | async-done | bytes 1572880 | tf_op jit(solution)/shard_map/reduce_scatter | solution.py:95
  1355.3 2.8 fusion.17
  1359.4 35.2 %reduce-scatter.15.cloned.1.call-done = bf16[320,2048]{1,0:T(8,128)(2,1)} async-done(((bf16[640,2048]{1,0:T(8,128)(2,1)}), bf16[320,2048]{1,0:T(8,128)(2,1)}) %reduce-scatter.15.cloned.1.call-update) | async-done | bytes 1310736 | tf_op jit(solution)/shard_map/reduce_scatter | solution.py:79
  1394.7 5.1 fusion.30
  1399.7 40.0 %all-reduce.4 = (f32[]{:T(128)}, f32[4352]{0:T(1024)S(1)}) all-reduce(f32[]{:T(128)S(6)} %add.220, f32[4352]{0:T(1024)S(1)} %pad_maximum_fusion.11), channel_id=1, replica_groups=mesh['fsdp'=16,'tp'=2] {'fsdp','tp'}, use_global_device_ids=true, to_apply=%region_24.25 | all-reduce | flops 4353 | bytes 34824 | tf_op jit(solution)/shard_map/psum | solution.py:280
  1442.4 2.9 fusion.84
  1445.4 4.9 fusion.78
  1450.4 2.4 fusion.87
  1454.5 5.0 fusion.81
  (245 shorter events, 44.6 us)
Async XLA Ops:
  7.2 5.5 copy-start.30
  7.2 47.3 %all-gather.9.cloned.1.call-start = ((), (), s32[]{:S(2)}) async-start(), calls=%async_computation.8 | async-start | bytes 3932160 | tf_op jit(solution)/shard_map/all_gather | solution.py:75
  9.0 4.5 copy-start.58
  9.7 3.8 copy-start.50
  9.7 624.5 %copy-start.44 = (f32[2048]{0:T(1024)}, f32[2048]{0:T(1024)S(1)}, u32[]{:S(2)}) copy-start(f32[2048]{0:T(1024)S(1)} %get-tuple-element.68) | copy-start | bytes 24580
  9.8 3.8 copy-start.37
  12.6 119.5 %all-gather.11.cloned.1.call-start = ((), (), s32[]{:S(2)}) async-start(), calls=%async_computation.9 | async-start | bytes 8912896 | tf_op jit(solution)/shard_map/all_gather | solution.py:158
  13.5 172.8 %all-gather.13.cloned.1.call-start = ((), (), s32[]{:S(2)}) async-start(), calls=%async_computation.10 | async-start | bytes 4456448 | tf_op jit(solution)/shard_map/all_gather | solution.py:159
  14.4 214.6 %reduce-scatter.13.cloned.1.call-start = ((), (), s32[]{:S(2)}) async-start(), calls=%async_computation.11 | async-start | bytes 3932160 | tf_op jit(solution)/shard_map/reduce_scatter | solution.py:79
  18.0 148.4 %copy-start.18 = (f32[640,64]{1,0:T(8,128)}, f32[640,64]{1,0:T(8,128)S(1)}, u32[]{:S(2)}) copy-start(f32[640,64]{1,0:T(8,128)S(1)} %get-tuple-element.72) | copy-start | bytes 491524
  18.7 142.4 %copy-start.68 = (f32[128]{0:T(128)}, f32[128]{0:T(128)S(1)}, u32[]{:S(2)}) copy-start(f32[128]{0:T(128)S(1)} %get-tuple-element.71) | copy-start | bytes 1540
  18.7 145.8 %copy-start.70 = (f32[128]{0:T(128)}, f32[128]{0:T(128)S(1)}, u32[]{:S(2)}) copy-start(f32[128]{0:T(128)S(1)} %get-tuple-element.70) | copy-start | bytes 1540
  146.9 14.2 copy-start.1
  157.6 6.9 copy-start.52
  166.8 3.6 copy-start.24
  166.9 3.6 copy-start.26
  170.4 4.7 copy-start
  170.4 4.7 copy-start.35
  178.0 8.3 copy-start.75
  193.0 36.0 %copy-start.3 = (bf16[320,2048]{1,0:T(8,128)(2,1)S(1)}, bf16[320,2048]{1,0:T(8,128)(2,1)}, u32[]{:S(2)}) copy-start(bf16[320,2048]{1,0:T(8,128)(2,1)} %param.19) | copy-start | bytes 3932164
  193.0 78.7 %all-gather.15.cloned.1.call-start = ((), (), s32[]{:S(2)}) async-start(), calls=%async_computation.12 | async-start | bytes 3932160 | tf_op jit(solution)/shard_map/all_gather | solution.py:75
  230.9 403.4 %copy-start.55 = (f32[320]{0:T(512)}, f32[320]{0:T(512)S(1)}, u32[]{:S(2)}) copy-start(f32[320]{0:T(512)S(1)} %fusion.67) | copy-start | bytes 3844
  232.6 169.9 %all-gather.17.cloned.1.call-start = ((), (), s32[]{:S(2)}) async-start(), calls=%async_computation.13 | async-start | bytes 26738688 | tf_op jit(solution)/shard_map/all_gather | solution.py:160
  235.9 207.8 %all-gather.21.cloned.1.call-start = ((), (), s32[]{:S(2)}) async-start(), calls=%async_computation.16 | async-start | bytes 3932160 | tf_op jit(solution)/shard_map/all_gather | solution.py:85
  236.6 397.7 %copy-start.60 = (f32[320]{0:T(512)}, f32[320]{0:T(512)S(1)}, u32[]{:S(2)}) copy-start(f32[320]{0:T(512)S(1)} %fusion.65) | copy-start | bytes 3844
  239.3 311.4 %all-gather.19.cloned.1.call-start = ((), (), s32[]{:S(2)}) async-start(), calls=%async_computation.14 | async-start | bytes 13369344 | tf_op jit(solution)/shard_map/all_gather | solution.py:161
  242.0 389.2 %reduce-scatter.17.cloned.1.call-start = ((), (), s32[]{:S(2)}) async-start(), calls=%async_computation.17 | async-start | bytes 3932160 | tf_op jit(solution)/shard_map/reduce_scatter | solution.py:89
  595.2 80.5 %all-gather.23.cloned.1.call-start = ((), (), s32[]{:S(2)}) async-start(), calls=%async_computation.18 | async-start | bytes 3932160 | tf_op jit(solution)/shard_map/all_gather | solution.py:85
  636.5 211.5 %reduce-scatter.19.cloned.1.call-start = ((), (), s32[]{:S(2)}) async-start(), calls=%async_computation.19 | async-start | bytes 3932160 | tf_op jit(solution)/shard_map/reduce_scatter | solution.py:89
  682.5 16.4 %slice-start = ((s8[13107200]{0:T(1024)(128)(4,1)}), s8[4194304]{0:T(1024)(128)(4,1)S(1)}, s32[]{:S(2)}) async-start(s8[13107200]{0:T(1024)(128)(4,1)} %bitcast.105), calls=%async_computation.24 | async-start | bytes 8388608
  682.5 16.4 %slice-start.1 = ((s8[13107200]{0:T(1024)(128)(4,1)}), s8[4194304]{0:T(1024)(128)(4,1)S(1)}, s32[]{:S(2)}) async-start(s8[13107200]{0:T(1024)(128)(4,1)} %bitcast.105), calls=%async_computation.25 | async-start | bytes 8388608
  689.5 9.4 slice-start.2
  689.5 9.4 slice-start.3
  699.0 6.7 copy-start.13
  699.0 6.7 copy-start.15
  725.3 3.3 copy-start.2
  725.3 3.3 copy-start.28
  725.3 3.3 copy-start.69
  747.7 114.4 %reduce-scatter.25.cloned.1.call-start = ((), (), s32[]{:S(2)}) async-start(), calls=%async_computation.22 | async-start | bytes 4456448
  761.7 238.3 %reduce-scatter.27.cloned.1.call-start = ((), (), s32[]{:S(2)}) async-start(), calls=%async_computation.23 | async-start | bytes 13369344
  794.3 313.3 %reduce-scatter.21.cloned.1.call-start = ((), (), s32[]{:S(2)}) async-start(), calls=%async_computation.20 | async-start | bytes 8912896 | tf_op jit(solution)/shard_map/reduce_scatter | solution.py:95
  805.5 549.8 %reduce-scatter.23.cloned.1.call-start = ((), (), s32[]{:S(2)}) async-start(), calls=%async_computation.21 | async-start | bytes 26738688 | tf_op jit(solution)/shard_map/reduce_scatter | solution.py:95
  834.3 560.4 %reduce-scatter.15.cloned.1.call-start = ((), (), s32[]{:S(2)}) async-start(), calls=%async_computation.15 | async-start | bytes 3932160 | tf_op jit(solution)/shard_map/reduce_scatter | solution.py:79
  847.9 3.7 copy-start.57
  847.9 3.7 copy-start.67
  862.0 532.6 %copy-start.6 = (bf16[320,2048]{1,0:T(8,128)(2,1)S(1)}, bf16[320,2048]{1,0:T(8,128)(2,1)}, u32[]{:S(2)}) copy-start(bf16[320,2048]{1,0:T(8,128)(2,1)} %reduce-scatter.13.cloned.1.call-done) | copy-start | bytes 3932164
  862.0 532.6 %copy-start.45 = (f32[2048]{0:T(1024)S(1)}, f32[2048]{0:T(1024)}, u32[]{:S(2)}) copy-start(f32[2048]{0:T(1024)} %copy-done.44) | copy-start | bytes 24580
  862.0 532.6 %copy-start.56 = (f32[320]{0:T(512)S(1)}, f32[320]{0:T(512)}, u32[]{:S(2)}) copy-start(f32[320]{0:T(512)} %copy-done.55) | copy-start | bytes 3844
  862.0 532.6 %copy-start.61 = (f32[320]{0:T(512)S(1)}, f32[320]{0:T(512)}, u32[]{:S(2)}) copy-start(f32[320]{0:T(512)} %copy-done.60) | copy-start | bytes 3844
  862.0 532.6 %copy-start.65 = (f32[320]{0:T(512)S(1)}, f32[320]{0:T(512)}, u32[]{:S(2)}) copy-start(f32[320]{0:T(512)} %copy-done.64) | copy-start | bytes 3844
  863.3 136.7 %copy-start.36 = (bf16[1024,128]{1,0:T(8,128)(2,1)}, bf16[1024,128]{1,0:T(8,128)(2,1)S(1)}, u32[]{:S(2)}) copy-start(bf16[1024,128]{1,0:T(8,128)(2,1)S(1)} %copy.198) | copy-start | bytes 786436
  1359.4 82.3 %copy-start.54 = (f32[4352]{0:T(1024)S(1)}, f32[4352]{0:T(1024)}, u32[]{:S(2)}) copy-start(f32[4352]{0:T(1024)} %param.27) | copy-start | bytes 52228
  1359.4 82.3 %copy-start.62 = (f32[4352]{0:T(1024)S(1)}, f32[4352]{0:T(1024)}, u32[]{:S(2)}) copy-start(f32[4352]{0:T(1024)} %param.32) | copy-start | bytes 52228
  1359.4 82.3 %copy-start.63 = (f32[4352]{0:T(1024)S(1)}, f32[4352]{0:T(1024)}, u32[]{:S(2)}) copy-start(f32[4352]{0:T(1024)} %param.37) | copy-start | bytes 52228
  1399.7 45.6 %copy-start.23 = (f32[3072,128]{1,0:T(8,128)S(1)}, f32[3072,128]{1,0:T(8,128)}, u32[]{:S(2)}) copy-start(f32[3072,128]{1,0:T(8,128)} %param.26) | copy-start | bytes 4718596
  1441.8 3.6 copy-start.39
  1445.4 5.0 copy-start.31
  1445.4 5.0 copy-start.38
  1445.4 5.0 copy-start.40
  1445.4 5.0 copy-start.41
  1445.4 7.4 copy-start.33
  1445.4 7.4 copy-start.34
  1450.4 3.7 copy-start.11
  1450.4 4.1 copy-start.22
  (32 other events, 65.2 us)
Sparse Core Ops, SparseCore 0:
  12.7 41.7 all-gather.8
  57.2 74.8 all-gather.10
  134.9 51.4 all-gather.12
  193.1 35.7 reduce-scatter.12
  232.7 38.9 all-gather.14
  273.9 128.5 all-gather.16
  404.7 39.0 all-gather.20
  446.7 103.9 all-gather.18
  595.3 35.7 reduce-scatter.16
  636.6 39.0 all-gather.22
  747.8 37.5 reduce-scatter.18
  789.6 72.3 reduce-scatter.24
  866.1 133.8 reduce-scatter.26
  1003.9 103.7 reduce-scatter.20
  1111.6 243.6 reduce-scatter.22
  1357.9 36.6 reduce-scatter.14

commit v2 on v1

v2 whole, which is shorter than its diff:
```python
from functools import partial

import jax
import jax.numpy as jnp
from jax import lax
from jax.sharding import Mesh, PartitionSpec as P

D = 2048
H = 16
KV = 8
HD = 128
FF = 6144
STEP = 10


norm_epsilon = 1e-06
rope_base = 1000000.0
clip_norm = 1.0
learn_rate = 0.04
gain_rate = 0.8
beta_first = 0.9
beta_second = 0.999
adam_epsilon = 1e-08
weight_decay = 0.1
masked_score = -1e30

NEAR = 2
CORE = 2
TEAM = NEAR * CORE
LAYER = ("near", "core", "tp")


def rms_scale(values):
    return lax.rsqrt(jnp.mean(values * values, axis=-1, keepdims=True) + norm_epsilon)


def norm_apply(values, gain):
    return values * rms_scale(values) * gain


def rotary(positions, width):
    half_width = width // 2
    frequency = rope_base ** (-(jnp.arange(half_width, dtype=jnp.float32) * 2.0 / width))
    angles = positions.astype(jnp.float32)[:, None] * frequency[None, :]
    return (jnp.cos(angles), jnp.sin(angles))


def rotate(values, cos_table, sin_table):
    half_width = values.shape[-1] // 2
    first_half = values[..., :half_width]
    second_half = values[..., half_width:]
    cosine = cos_table[:, None, :]
    sine_part = sin_table[:, None, :]
    return jnp.concatenate(
        [
            first_half * cosine - second_half * sine_part,
            second_half * cosine + first_half * sine_part,
        ],
        axis=-1,
    )


def head_prepare(raw, gain, cos_table, sin_table):
    return rotate(norm_apply(raw, gain), cos_table, sin_table)


def swish_product(gate_part, up_part):
    return jax.nn.silu(gate_part) * up_part


def score_block(queries, key_heads, key_mask, score_scale):
    scores = (
        jnp.einsum("sqrd,skd->srqk", queries, key_heads, preferred_element_type=jnp.float32)
        * score_scale
    )
    return jnp.where(key_mask[:, None], scores, masked_score)


def swap(values, axis):
    return lax.ppermute(values, axis, [(0, 1), (1, 0)])


def pick(values, index):
    return lax.dynamic_index_in_dim(values, index, 0, keepdims=False)


def put(buffer, values, *index):
    zero = jnp.zeros((), jnp.int32)
    start = tuple(index) + (zero,) * (buffer.ndim - len(index))
    return lax.dynamic_update_slice(buffer, values[(None,) * len(index)], start)


def gather_rows(values):
    near, core, tp = (lax.axis_index(name) for name in LAYER)
    half = values.shape[0] // 2
    buffer = jnp.zeros((NEAR, CORE, 2) + values.shape, values.dtype)
    by_near = swap(values, "near")
    by_tp = swap(values, "tp")
    far_top = swap(by_tp[:half], "near")
    far_low = swap(by_near[half:], "tp")
    by_both = jnp.concatenate([far_top, far_low], axis=0)
    for where_near, where_tp, block in (
        (near, tp, values),
        (1 - near, tp, by_near),
        (near, 1 - tp, by_tp),
        (1 - near, 1 - tp, by_both),
    ):
        buffer = put(buffer, block, where_near, core, where_tp)
        buffer = put(buffer, swap(block, "core"), where_near, 1 - core, where_tp)
    return buffer.reshape(-1, values.shape[1])


def sum_rows(values, multiply):
    near, core, tp = (lax.axis_index(name) for name in LAYER)
    blocks = values.reshape(NEAR, CORE, 2, -1, values.shape[1])

    def part(which):
        chosen = lax.dynamic_index_in_dim(blocks, which, 1, keepdims=False)
        flat = chosen.reshape(-1, values.shape[1])
        return multiply(flat).reshape(NEAR, 2, -1, D)

    theirs = swap(part(1 - core).astype(jnp.bfloat16), "core")
    ours = part(core) + theirs.astype(jnp.float32)

    def block(where_near, where_tp):
        return pick(pick(ours, where_near), where_tp)

    far = block(1 - near, 1 - tp).astype(jnp.bfloat16)
    half = far.shape[0] // 2
    top = swap(far[:half], "near").astype(jnp.float32)
    low = swap(far[half:], "tp").astype(jnp.float32)
    to_tp = block(near, 1 - tp)
    to_tp = jnp.concatenate([to_tp[:half] + top, to_tp[half:]], axis=0)
    to_near = block(1 - near, tp)
    to_near = jnp.concatenate([to_near[:half], to_near[half:] + low], axis=0)
    from_tp = swap(to_tp.astype(jnp.bfloat16), "tp").astype(jnp.float32)
    from_near = swap(to_near.astype(jnp.bfloat16), "near").astype(jnp.float32)
    return block(near, tp) + from_tp + from_near


def team_swap(values, offset):
    pairs = [(member, member ^ offset) for member in range(TEAM)]
    return lax.ppermute(values, ("near", "core"), pairs)


def team_exchange(pieces):
    own = lax.axis_index("near") * CORE + lax.axis_index("core")
    buffer = jnp.zeros_like(pieces)
    buffer = put(buffer, pick(pieces, own), own)
    for offset in range(1, TEAM):
        there = own ^ offset
        buffer = put(buffer, team_swap(pick(pieces, there), offset), there)
    return buffer


def split_columns(values, widths):
    members = []
    for member in range(TEAM):
        start, parts = 0, []
        for width in widths:
            share = width // TEAM
            first = start + member * share
            parts.append(values[:, first : first + share])
            start += width
        members.append(jnp.concatenate(parts, axis=1))
    return jnp.stack(members)


def join_columns(pieces, widths):
    parts, start = [], 0
    for width in widths:
        share = width // TEAM
        parts += [pieces[member, :, start : start + share] for member in range(TEAM)]
        start += share
    return jnp.concatenate(parts, axis=1)


def gather_weight(shard, widths):
    mixed = team_exchange(split_columns(shard, widths))
    mixed = mixed.reshape(-1, mixed.shape[-1])
    return lax.all_gather(mixed, "outer", axis=0, tiled=True)


def sum_weight(gradient):
    return lax.psum_scatter(
        gradient.astype(jnp.bfloat16), "outer", scatter_dimension=0, tiled=True
    )


def return_weight(summed, widths):
    pieces = summed.reshape(TEAM, -1, summed.shape[-1])
    return join_columns(team_exchange(pieces), widths).astype(jnp.float32)


def adam_update(weight, gradient, moment_one, moment_two, factor, decay_rate, rate_value):
    clipped = gradient * factor
    moment_one = beta_first * moment_one + (1.0 - beta_first) * clipped
    moment_two = beta_second * moment_two + (1.0 - beta_second) * clipped * clipped
    first_fixed = moment_one / (1.0 - beta_first**STEP)
    second_fixed = moment_two / (1.0 - beta_second**STEP)
    weight = weight - rate_value * (
        first_fixed / (jnp.sqrt(second_fixed) + adam_epsilon) + decay_rate * weight
    )
    return (weight, moment_one, moment_two)


def dot(left, right, contract):
    return lax.dot_general(
        left, right, ((contract[0], contract[1]), ((), ())), preferred_element_type=jnp.float32
    )


def times(left, right):
    return dot(left, right, ((1,), (0,)))


def times_across(left, right):
    return dot(left, right, ((1,), (1,)))


def over_rows(left, right):
    return dot(left, right, ((0,), (0,)))


def local(
    inputs,
    cotangent,
    lengths,
    owners,
    qkv_weight,
    out_weight,
    gate_up_weight,
    down_weight,
    norm_gains,
    qkv_moment,
    out_moment,
    gate_up_moment,
    down_moment,
    gains_moment,
    qkv_square,
    out_square,
    gate_up_square,
    down_square,
    gains_square,
):
    tp_count = lax.axis_size("tp")
    half_rows = inputs.shape[0]
    row_count = half_rows * tp_count
    heads = H // tp_count // TEAM
    hidden_units = FF // tp_count // TEAM
    qkv_widths = (H * HD // tp_count, KV * HD // tp_count, KV * HD // tp_count)
    out_widths = (H * HD // tp_count,)
    gate_up_widths = (FF // tp_count, FF // tp_count)
    down_widths = (FF // tp_count,)

    first_group = lax.axis_index("outer") * TEAM
    group_ids = first_group + jnp.arange(TEAM)
    group_length = jnp.sum(
        jnp.where(owners[None, :] == group_ids[:, None], lengths[None, :], 0), axis=1
    )
    own_group = lax.axis_index("near") * CORE + lax.axis_index("core")
    positions = jnp.arange(row_count)
    key_mask = (positions[None, None, :] <= positions[None, :, None]) & (
        positions[None, None, :] < group_length[:, None, None]
    )
    own_rows = lax.axis_index("tp") * half_rows + jnp.arange(half_rows)
    valid_rows = (own_rows < pick(group_length, own_group)).astype(jnp.float32)[:, None]
    cos_table, sin_table = rotary(jnp.tile(positions, TEAM), HD)
    score_scale = HD ** (-0.5)
    attn_gain = norm_gains[:D]
    mlp_gain = norm_gains[D : 2 * D]
    query_gain = norm_gains[2 * D : 2 * D + HD]
    key_gain = norm_gains[2 * D + HD :]
    head_apply = partial(head_prepare, cos_table=cos_table, sin_table=sin_table)

    qkv_full = gather_weight(qkv_weight.astype(jnp.bfloat16), qkv_widths)
    out_full = gather_weight(out_weight.astype(jnp.bfloat16).T, out_widths)
    gate_up_full = gather_weight(gate_up_weight.astype(jnp.bfloat16), gate_up_widths)
    down_full = gather_weight(down_weight.astype(jnp.bfloat16).T, down_widths)

    residual_in = inputs.astype(jnp.float32)
    normed_attn = gather_rows(norm_apply(residual_in, attn_gain).astype(jnp.bfloat16))
    projected = times(normed_attn, qkv_full)
    all_rows = projected.shape[0]
    query_raw = projected[:, : heads * HD].reshape(all_rows, heads, HD)
    key_raw = projected[:, heads * HD : (heads + 1) * HD].reshape(all_rows, 1, HD)
    value_heads = projected[:, (heads + 1) * HD :].astype(jnp.bfloat16)
    value_heads = value_heads.reshape(TEAM, row_count, HD)
    queries = head_apply(query_raw, query_gain).astype(jnp.bfloat16)
    queries = queries.reshape(TEAM, row_count, heads, HD)
    key_heads = head_apply(key_raw, key_gain).astype(jnp.bfloat16)
    key_heads = key_heads.reshape(TEAM, row_count, HD)
    scores = score_block(queries, key_heads, key_mask, score_scale)
    row_max = jnp.max(scores, axis=-1, keepdims=True)
    exponent = jnp.exp(scores - row_max)
    row_total = jnp.sum(exponent, axis=-1, keepdims=True)
    log_total = row_max + jnp.log(row_total)
    attention = exponent / row_total
    attended = (
        jnp.einsum(
            "srqk,skd->sqrd",
            attention.astype(jnp.bfloat16),
            value_heads,
            preferred_element_type=jnp.float32,
        )
        .reshape(all_rows, heads * HD)
        .astype(jnp.bfloat16)
    )
    attn_branch = sum_rows(attended, lambda rows: times_across(rows, out_full))
    hidden = residual_in + attn_branch
    normed_mlp = gather_rows(norm_apply(hidden, mlp_gain).astype(jnp.bfloat16))
    gate_up = times(normed_mlp, gate_up_full)
    gate_part = gate_up[:, :hidden_units]
    up_part = gate_up[:, hidden_units:]
    activated = swish_product(gate_part, up_part).astype(jnp.bfloat16)
    mlp_branch = sum_rows(activated, lambda rows: times_across(rows, down_full))
    output = (hidden + mlp_branch).astype(jnp.bfloat16)

    grad_output = cotangent.astype(jnp.float32) * valid_rows
    grad_low = gather_rows(grad_output.astype(jnp.bfloat16))
    grad_activated = times(grad_low, down_full)
    swish_pull = jax.vjp(swish_product, gate_part, up_part)[1]
    grad_gate, grad_up = swish_pull(grad_activated)
    grad_gate_up = jnp.concatenate([grad_gate, grad_up], axis=1).astype(jnp.bfloat16)
    grad_normed_mlp = sum_rows(grad_gate_up, lambda rows: times_across(rows, gate_up_full))
    down_sum = sum_weight(over_rows(grad_low, activated))
    gate_up_sum = sum_weight(over_rows(normed_mlp, grad_gate_up))
    mlp_pull = jax.vjp(norm_apply, hidden, mlp_gain)[1]
    grad_hidden_norm, grad_mlp_gain = mlp_pull(grad_normed_mlp)
    grad_hidden = grad_output + grad_hidden_norm
    grad_attn = gather_rows(grad_hidden.astype(jnp.bfloat16))
    grad_attended = times(grad_attn, out_full).astype(jnp.bfloat16)
    grad_attended = grad_attended.reshape(TEAM, row_count, heads, HD)
    out_sum = sum_weight(over_rows(grad_attn, attended))
    attention = jnp.exp(score_block(queries, key_heads, key_mask, score_scale) - log_total)
    grad_probs = jnp.einsum(
        "sqrd,skd->srqk", grad_attended, value_heads, preferred_element_type=jnp.float32
    )
    grad_values = jnp.einsum(
        "srqk,sqrd->skd",
        attention.astype(jnp.bfloat16),
        grad_attended,
        preferred_element_type=jnp.float32,
    )
    inner_sum = jnp.sum(attention * grad_probs, axis=-1, keepdims=True)
    grad_scores = (attention * (grad_probs - inner_sum)).astype(jnp.bfloat16)
    grad_queries = (
        jnp.einsum("srqk,skd->sqrd", grad_scores, key_heads, preferred_element_type=jnp.float32)
        * score_scale
    )
    grad_keys = (
        jnp.einsum("srqk,sqrd->skd", grad_scores, queries, preferred_element_type=jnp.float32)
        * score_scale
    )
    query_pull = jax.vjp(head_apply, query_raw, query_gain)[1]
    grad_query_raw, grad_query_gain = query_pull(grad_queries.reshape(all_rows, heads, HD))
    key_pull = jax.vjp(head_apply, key_raw, key_gain)[1]
    grad_key_raw, grad_key_gain = key_pull(grad_keys.reshape(all_rows, 1, HD))
    grad_projected = jnp.concatenate(
        [
            grad_query_raw.reshape(all_rows, heads * HD),
            grad_key_raw.reshape(all_rows, HD),
            grad_values.reshape(all_rows, HD),
        ],
        axis=1,
    ).astype(jnp.bfloat16)
    qkv_sum = sum_weight(over_rows(normed_attn, grad_projected))
    grad_normed_attn = sum_rows(grad_projected, lambda rows: times_across(rows, qkv_full))
    attn_pull = jax.vjp(norm_apply, residual_in, attn_gain)[1]
    grad_input_norm, grad_attn_gain = attn_pull(grad_normed_attn)
    input_grad = (grad_hidden + grad_input_norm).astype(jnp.bfloat16)
    gain_part = jnp.concatenate([grad_attn_gain, grad_mlp_gain, grad_query_gain, grad_key_gain])
    square_part = sum(
        jnp.sum(jnp.square(member.astype(jnp.float32)))
        for member in (qkv_sum, out_sum, gate_up_sum, down_sum)
    )
    gain_grad, square_total = lax.psum((gain_part, square_part), ("outer",) + LAYER)
    down_grad = return_weight(down_sum, down_widths).T
    gate_up_grad = return_weight(gate_up_sum, gate_up_widths)
    out_grad = return_weight(out_sum, out_widths).T
    qkv_grad = return_weight(qkv_sum, qkv_widths)
    grad_norm = jnp.sqrt(square_total + jnp.sum(gain_grad * gain_grad))
    factor = jnp.minimum(1.0, clip_norm / (grad_norm + 1e-06))
    new_qkv, new_qkv_one, new_qkv_two = adam_update(
        qkv_weight, qkv_grad, qkv_moment, qkv_square, factor, weight_decay, learn_rate
    )
    new_out, new_out_one, new_out_two = adam_update(
        out_weight, out_grad, out_moment, out_square, factor, weight_decay, learn_rate
    )
    new_gate_up, new_gate_up_one, new_gate_up_two = adam_update(
        gate_up_weight,
        gate_up_grad,
        gate_up_moment,
        gate_up_square,
        factor,
        weight_decay,
        learn_rate,
    )
    new_down, new_down_one, new_down_two = adam_update(
        down_weight, down_grad, down_moment, down_square, factor, weight_decay, learn_rate
    )
    new_gains, new_gains_one, new_gains_two = adam_update(
        norm_gains, gain_grad, gains_moment, gains_square, factor, 0.0, gain_rate
    )
    return (
        output,
        input_grad,
        grad_norm,
        new_qkv,
        new_qkv_one,
        new_qkv_two,
        new_qkv.astype(jnp.bfloat16),
        new_out,
        new_out_one,
        new_out_two,
        new_out.astype(jnp.bfloat16),
        new_gate_up,
        new_gate_up_one,
        new_gate_up_two,
        new_gate_up.astype(jnp.bfloat16),
        new_down,
        new_down_one,
        new_down_two,
        new_down.astype(jnp.bfloat16),
        new_gains,
        new_gains_one,
        new_gains_two,
    )


def solution(mesh):
    fsdp_count, tp_count = mesh.shape["fsdp"], mesh.shape["tp"]
    cut = mesh.devices.reshape(fsdp_count // TEAM, NEAR, CORE, tp_count)
    cut_mesh = Mesh(cut, ("outer",) + LAYER)
    fsdp = ("outer", "near", "core")
    rows = P(fsdp + ("tp",), None)
    wide = P(fsdp, "tp")
    tall = P("tp", fsdp)
    weights = (wide, tall, wide, tall, P())
    return jax.shard_map(
        local,
        mesh=cut_mesh,
        in_specs=(rows, rows, P(), P()) + weights * 3,
        out_specs=(rows, rows, P()) + (wide,) * 4 + (tall,) * 4 + (wide,) * 4 + (tall,) * 4 + (P(),) * 3,
        check_vma=False,
    )
```

time: 1470 us -> 936 us (0.64)
  waiting for transfers between devices: 1050 us -> 315 us
  local copies, waits for them, and re-layouts: 66.8 us -> 186 us
  starting transfers between devices: 0.88 us -> 60.1 us
    all_gather x8 -> x4, waiting for transfers between devices: 446 us -> 0.03 us  [gather_weight(): return lax.all_gather(mixed, 'outer', axis=0, tiled=True)]
    reduce_scatter x6 -> x4, waiting for transfers between devices: 456 us -> 15.8 us  [sum_weight(): lax.psum_scatter(gradient.astype(jnp.bfloat16), 'outer', scatter_dimensio...]
    ppermute x0 -> x76, waiting for transfers between devices: none -> 299 us  [the longest x52 177 us: swap(): return lax.ppermute(values, axis, [(0, 1), (1, 0)])]
    unnamed x18 -> x8, waiting for transfers between devices: 147 us -> 0.13 us
    ppermute x0 -> x76, starting transfers between devices: none -> 59.3 us  [the longest x52 43.3 us: swap(): return lax.ppermute(values, axis, [(0, 1), (1, 0)])]
    dynamic_update_slice x0 -> x56, local copies, waits for them, and re-layouts: none -> 54.7 us  [put(): return lax.dynamic_update_slice(buffer, values[(None,) * len(index)], start)]
    another operation x3 -> x17, local copies, waits for them, and re-layouts: 0.65 us -> 28.2 us
    convert_element_type x1 -> x7, local copies, waits for them, and re-layouts: 0.99 us -> 18.5 us  [the longest x2 15.3 us: local(): attended = jnp.einsum('srqk,skd->sqrd', attention.astype(jnp.bfloat16), v...]
  transfers between devices with their start and end apart: 16 -> 84, of which waited for: 15 -> 34; matrix products, arithmetic and copies ran while one was open for 13% -> 43% of each run, Pallas kernels for 0% -> 0%
where the time goes in v2:
time: 936 us; the launch traced here: 928 us
  waiting for transfers between devices  315 us (34%)
  matrix products  203 us (22%)
  local copies, waits for them, and re-layouts  186 us (20%)
  other arithmetic  101 us (11%)
  starting transfers between devices  60.1 us (6%)
  blocking collectives  40.2 us (4%)
  between operations  22 us (2%)
    ppermute x52, waiting for transfers between devices, swap(): return lax.ppermute(values, axis, [(0, 1), (1, 0)])  177 us
    dot_general x16, matrix products, dot(): lax.dot_general(left, right, ((contract[0], contract[1]), ((), ())), pref...  175 us
    ppermute x24, waiting for transfers between devices, team_swap(): return lax.ppermute(values, ('near', 'core'), pairs)  122 us
    dynamic_update_slice x56, local copies, waits for them, and re-layouts, put(): return lax.dynamic_update_slice(buffer, values[(None,) * len(index)], start)  54.7 us
    ppermute x52, starting transfers between devices, swap(): return lax.ppermute(values, axis, [(0, 1), (1, 0)])  43.3 us
    psum x1, blocking collectives, local(): lax.psum((gain_part, square_part), ('outer',) + LAYER)  40.2 us
    unnamed x294, local copies, waits for them, and re-layouts  32.9 us
    another operation x15, local copies, waits for them, and re-layouts  28.2 us
  transfers between devices with their start and end apart: 84, of which 34 were waited for; matrix products, arithmetic and copies ran while one was open for 43% of the time, Pallas kernels for 0%

profile of v2, /device:TPU:0, one launch (start us, length us, event | category | flops | bytes accessed | tf_op | source)
XLA Modules:
  0.0 927.8 jit_solution(6454326609702208751)
XLA Ops:
  13.6 3.9 copy-done.18
  30.6 22.3 %collective-permute-done.9 = bf16[128,512]{1,0:T(8,128)(2,1)S(1)} collective-permute-done((bf16[128,512]{1,0:T(8,128)(2,1)S(1)}, bf16[128,512]{1,0:T(8,128)(2,1)S(1)}, u32[]{:S(2)}, u32[]{:S(2)}) %collective-permute-start.9) | collective-permute-done | bytes 131104 | tf_op jit(solution)/shard_map/ppermute | solution.py:143
  54.6 3.8 collective-permute-done.10
  63.4 6.2 multiply_cosine_fusion
  71.7 3.2 collective-permute-done.13
  78.1 8.7 collective-permute-done.28
  86.8 6.8 collective-permute-done.29
  105.3 8.4 collective-permute-done.5
  122.8 9.9 %fusion.198 = f32[2560,512]{0,1:T(8,128)S(1)} fusion(bf16[2560,2048]{1,0:T(8,128)(2,1)} %bitcast.586, bf16[2048,512]{1,0:T(8,128)(2,1)} %all-gather.5.cloned.1.call-done), kind=kOutput, calls=%fused_computation.472 | convolution fusion | flops 5368709120 | bytes 17825792 | tf_op jit(solution)/shard_map/dot_general | solution.py:208
  142.7 3.4 fusion.128
  154.9 2.8 subtract_convert_fusion
  157.8 3.7 fusion.197
  163.3 2.9 copy-done
  167.0 2.9 fusion.75
  169.9 12.6 %reshape.558 = bf16[2,2,2,320,256]{3,2,4,1,0:T(2,128)(2,1)S(1)} reshape(bf16[4,640,2,128]{1,3,2,0:T(8,128)(2,1)S(1)} %fusion.75) | data formatting | bytes 2621440 | tf_op jit(solution)/shard_map/convert_element_type | solution.py:307
  187.1 5.1 convolution_convert_fusion.2
  193.8 5.3 broadcast.307.clone.2
  206.8 29.8 %collective-permute-done.31 = bf16[128,768]{0,1:T(8,128)(2,1)S(1)} collective-permute-done((bf16[128,768]{0,1:T(8,128)(2,1)S(1)}, bf16[128,768]{0,1:T(8,128)(2,1)S(1)}, u32[]{:S(2)}, u32[]{:S(2)}) %collective-permute-start.31) | collective-permute-done | bytes 196640 | tf_op jit(solution)/shard_map/ppermute | solution.py:143
  237.5 6.3 collective-permute-done.32
  255.8 4.1 convert_add_fusion.3
  264.0 14.2 %collective-permute-done.15 = bf16[160,2048]{1,0:T(8,128)(2,1)S(1)} collective-permute-done((bf16[160,2048]{1,0:T(8,128)(2,1)S(1)}, bf16[160,2048]{1,0:T(8,128)(2,1)S(1)}, u32[]{:S(2)}, u32[]{:S(2)}) %collective-permute-start.15) | collective-permute-done | bytes 655392 | tf_op jit(solution)/shard_map/ppermute | solution.py:80
  278.3 3.1 collective-permute-done.17
  285.7 2.6 bitcast_dynamic-update-slice_fusion.12
  290.8 21.1 %collective-permute-done.18 = bf16[320,2048]{1,0:T(8,128)(2,1)S(1)} collective-permute-done((bf16[320,2048]{1,0:T(8,128)(2,1)S(1)}, bf16[320,2048]{1,0:T(8,128)(2,1)S(1)}, u32[]{:S(2)}, u32[]{:S(2)}) %collective-permute-start.18) | collective-permute-done | bytes 1310752 | tf_op jit(solution)/shard_map/ppermute | solution.py:80
  314.1 5.2 broadcast.307.clone.1
  327.1 25.9 %collective-permute-done.22 = bf16[320,2048]{1,0:T(8,128)(2,1)S(1)} collective-permute-done((bf16[320,2048]{1,0:T(8,128)(2,1)S(1)}, bf16[320,2048]{1,0:T(8,128)(2,1)S(1)}, u32[]{:S(2)}, u32[]{:S(2)}) %collective-permute-start.22) | collective-permute-done | bytes 1310752 | tf_op jit(solution)/shard_map/ppermute | solution.py:80
  358.3 10.8 %collective-permute-done.24 = bf16[160,2048]{1,0:T(8,128)(2,1)S(1)} collective-permute-done((bf16[160,2048]{1,0:T(8,128)(2,1)S(1)}, bf16[160,2048]{1,0:T(8,128)(2,1)S(1)}, u32[]{:S(2)}, u32[]{:S(2)}) %collective-permute-start.24) | collective-permute-done | bytes 655392 | tf_op jit(solution)/shard_map/ppermute | solution.py:80
  376.0 22.4 %fusion.199 = f32[2560,1536]{1,0:T(8,128)} fusion(bf16[2560,2048]{1,0:T(8,128)(2,1)} %bitcast.63, bf16[2048,1536]{1,0:T(8,128)(2,1)} %all-gather.9.cloned.1.call-done), kind=kOutput, calls=%fused_computation.473 | convolution fusion | flops 16106127360 | bytes 32505856 | tf_op jit(solution)/shard_map/dot_general | solution.py:208
  398.4 21.2 %multiply_convert_fusion = (bf16[2560,768]{1,0:T(8,128)(2,1)}, bf16[2560,768]{1,0:T(8,128)(2,1)}, bf16[2560,768]{1,0:T(8,128)(2,1)}) fusion(f32[2560,1536]{1,0:T(8,128)} %fusion.199, bf16[2560,2048]{1,0:T(8,128)(2,1)} %bitcast.109, bf16[2048,768]{1,0:T(8,128)(2,1)} %all-gather.11.cloned.1.call-done), kind=kOutput, calls=%fused_computation.27 | convolution fusion | flops 8084520960 | bytes 41156608 | tf_op jit(solution)/shard_map/dot_general | solution.py:208
  419.6 11.7 %fusion.26 = bf16[2,2,320,2048]{3,2,1,0:T(8,128)(2,1)} fusion(bf16[2048,1536]{1,0:T(8,128)(2,1)S(1)} %copy-done.117, s32[]{:T(128)S(6)} %select_n.123, bf16[2,2,2,320,768]{4,3,2,1,0:T(8,128)(2,1)} %bitcast.622, bf16[2,2,2,320,768]{4,3,2,1,0:T(8,128)(2,1)} %bitcast.620), kind=kOutput, calls=%fused_computation.45 | convolution fusion | flops 8063549440 | bytes 19398660 | tf_op jit(solution)/shard_map/dot_general | solution.py:208
  431.8 6.1 convolution_convert_fusion.1
  437.9 2.8 copy.159
  440.7 13.6 %convolution_convert_fusion.4 = bf16[2048,768]{1,0:T(8,128)(2,1)} fusion(bf16[2560,2048]{1,0:T(8,128)(2,1)} %bitcast.109, bf16[2560,768]{1,0:T(8,128)(2,1)} %get-tuple-element.66), kind=kOutput, calls=%fused_computation.57 | convolution fusion | flops 8054636544 | bytes 17563648 | tf_op jit(solution)/shard_map/dot_general | solution.py:208
  454.4 13.1 %convert_add_fusion.1 = f32[2,2,320,2048]{3,2,1,0:T(8,128)S(1)} fusion(bf16[2,2,320,2048]{3,2,1,0:T(8,128)(2,1)} %collective-permute-done.46, bf16[2048,1536]{1,0:T(8,128)(2,1)} %all-gather.9.cloned.1.call-done, s32[]{:T(128)S(6)} %select_n.121, bf16[2,2,2,320,768]{4,3,2,1,0:T(8,128)(2,1)} %bitcast.623, bf16[2,2,2,320,768]{4,3,2,1,0:T(8,128)(2,1)} %bitcast.621), kind=kOutput, calls=%fused_computation.12 | convolution fusion | flops 8066170880 | bytes 29884420 | tf_op jit(solution)/shard_map/dot_general | solution.py:208
  471.7 9.0 convert_add_fusion.2
  491.7 8.6 collective-permute-done.34
  508.4 20.4 %fusion.13 = bf16[2048,1536]{1,0:T(8,128)(2,1)} fusion(bf16[2560,2048]{1,0:T(8,128)(2,1)} %bitcast.63, bf16[2560,768]{1,0:T(8,128)(2,1)S(1)} %copy-done.121, bf16[2560,768]{1,0:T(8,128)(2,1)S(1)} %copy-done.122), kind=kOutput, calls=%fused_computation.31 | convolution fusion | flops 16125001728 | bytes 24641536 | tf_op jit(solution)/shard_map/dot_general | solution.py:208
  529.9 26.3 %collective-permute-done.37 = bf16[320,2048]{1,0:T(8,128)(2,1)} collective-permute-done((bf16[320,2048]{1,0:T(8,128)(2,1)}, bf16[320,2048]{1,0:T(8,128)(2,1)}, u32[]{:S(2)}, u32[]{:S(2)}) %collective-permute-start.37) | collective-permute-done | bytes 1310752 | tf_op jit(solution)/shard_map/ppermute | solution.py:80
  557.3 6.7 multiply_reduce_fusion.2
  565.4 5.0 bitcast_dynamic-update-slice_fusion.7
  570.4 4.0 copy-done.17
  583.2 27.3 %collective-permute-done.74 = bf16[128,768]{0,1:T(8,128)(2,1)} collective-permute-done((bf16[128,768]{0,1:T(8,128)(2,1)S(1)}, bf16[128,768]{0,1:T(8,128)(2,1)}, u32[]{:S(2)}, u32[]{:S(2)}) %collective-permute-start.74) | collective-permute-done | bytes 196640 | tf_op jit(solution)/shard_map/ppermute | solution.py:143
  623.8 8.3 collective-permute-done.56
  639.9 6.9 convolution_convert_fusion.3
  647.9 12.0 %fusion = (f32[4,2,640]{2,1,0:T(2,128)S(1)}, f32[4,640,640,2]{2,1,3,0:T(8,128)}) fusion(f32[4,2,640,640]{2,3,1,0:T(8,128)} %copy-done, f32[4,2,640]{2,1,0:T(2,128)S(1)} %bitcast.610, bf16[4,640,128,1]{2,1,3,0:T(8,128)(2,1)S(1)} %copy-done.44, bf16[4,640,2,128]{3,2,1,0:T(2,128)(2,1)S(1)} %reshape.537), kind=kOutput, calls=%fused_computation.2 | convolution fusion | flops 848686080 | bytes 28221440 | tf_op jit(solution)/shard_map/sqrd,skd->srqk/dot_general | solution.py:336
  660.6 6.6 fusion.2
  672.8 6.0 multiply_bitcast_fusion
  681.1 4.1 fusion.131
  696.0 8.1 convolution_convert_fusion.6
  704.3 2.6 fusion.83
  706.9 11.8 %copy.153 = bf16[2560,2,128]{2,1,0:T(2,128)(2,1)} copy(bf16[2560,2,128]{2,0,1:T(8,128)(2,1)S(1)} %fusion.46) | data formatting | bytes 2621440 | tf_op jit(solution)/shard_map/convert.21
  720.4 3.4 concatenate.156
  725.5 4.6 convolution_convert_fusion
  731.7 12.2 %convolution_convert_fusion.5 = bf16[2048,512]{1,0:T(8,128)(2,1)} fusion(bf16[2560,2048]{1,0:T(8,128)(2,1)} %bitcast.587, bf16[2560,128]{0,1:T(8,128)(2,1)} %copy.158, bf16[2560,128]{0,1:T(8,128)(2,1)S(1)} %bitcast.604, bf16[2560,256]{0,1:T(8,128)(2,1)S(1)} %bitcast.607), kind=kOutput, calls=%fused_computation.69 | convolution fusion | flops 5377622016 | bytes 15204352 | tf_op jit(solution)/shard_map/dot_general | solution.py:208
  762.6 4.9 collective-permute-done.68
  768.4 3.7 collective-permute-done.69
  773.1 15.8 %reduce-scatter.5.cloned.1.call-done = bf16[512,512]{1,0:T(8,128)(2,1)} async-done(((bf16[2048,512]{1,0:T(8,128)(2,1)}), bf16[512,512]{1,0:T(8,128)(2,1)}) %reduce-scatter.5.cloned.1.call-update) | async-done | bytes 524304 | tf_op jit(solution)/shard_map/reduce_scatter | solution.py:185
  798.5 6.5 convert_add_fusion
  808.5 13.7 %collective-permute-done.60 = bf16[160,2048]{1,0:T(8,128)(2,1)S(1)} collective-permute-done((bf16[160,2048]{1,0:T(8,128)(2,1)S(1)}, bf16[160,2048]{1,0:T(8,128)(2,1)S(1)}, u32[]{:S(2)}, u32[]{:S(2)}) %collective-permute-start.60) | collective-permute-done | bytes 655392 | tf_op jit(solution)/shard_map/ppermute | solution.py:80
  826.5 27.5 %collective-permute-done.63 = bf16[320,2048]{1,0:T(8,128)(2,1)S(1)} collective-permute-done((bf16[320,2048]{1,0:T(8,128)(2,1)S(1)}, bf16[320,2048]{1,0:T(8,128)(2,1)S(1)}, u32[]{:S(2)}, u32[]{:S(2)}) %collective-permute-start.63) | collective-permute-done | bytes 1310752 | tf_op jit(solution)/shard_map/ppermute | solution.py:80
  857.1 40.2 %all-reduce.4 = (f32[]{:T(128)}, f32[4352]{0:T(1024)S(1)}) all-reduce(f32[]{:T(128)S(6)} %add.626, f32[4352]{0:T(1024)S(1)} %pad_maximum_fusion.16), channel_id=1, replica_groups=mesh['outer'=4,'near'=2,'core'=2,'tp'=2] {'outer','near','core','tp'}, use_global_device_ids=true, to_apply=%region_20.21 | all-reduce | flops 4353 | bytes 34824 | tf_op jit(solution)/shard_map/psum | solution.py:377
  899.4 4.5 fusion.48
  908.8 5.0 fusion.179
  916.4 3.3 fusion.176
  (645 shorter events, 261.4 us)
Async XLA Ops:
  7.2 115.6 %all-gather.5.cloned.1.call-start = ((), (), s32[]{:S(2)}) async-start(), calls=%async_computation.4 | async-start | bytes 2621440 | tf_op jit(solution)/shard_map/all_gather | solution.py:181
  17.5 82.7 %collective-permute-start = (bf16[320,2048]{1,0:T(8,128)(2,1)}, bf16[320,2048]{1,0:T(8,128)(2,1)}, u32[]{:S(2)}, u32[]{:S(2)}) collective-permute-start(bf16[320,2048]{1,0:T(8,128)(2,1)} %get-tuple-element.63), channel_id=1, source_target_pairs={{0,2},{2,0},{1,3},{3,1},{4,6},{6,4},{5,7},{7,5},{8,10},{10,8},{9,1... | collective-permute-start | bytes 3932168 | tf_op jit(solution)/shard_map/ppermute | solution.py:80
  17.9 78.8 %collective-permute-start.1 = (bf16[320,2048]{1,0:T(8,128)(2,1)}, bf16[320,2048]{1,0:T(8,128)(2,1)}, u32[]{:S(2)}, u32[]{:S(2)}) collective-permute-start(bf16[320,2048]{1,0:T(8,128)(2,1)} %get-tuple-element.63), channel_id=1, source_target_pairs={{0,4},{4,0},{1,5},{5,1},{2,6},{6,2},{3,7},{7,3},{8,12},{12,8},{9,1... | collective-permute-start | bytes 3932168 | tf_op jit(solution)/shard_map/ppermute | solution.py:80
  20.4 74.4 %collective-permute-start.3 = (bf16[320,2048]{1,0:T(8,128)(2,1)}, bf16[320,2048]{1,0:T(8,128)(2,1)}, u32[]{:S(2)}, u32[]{:S(2)}) collective-permute-start(bf16[320,2048]{1,0:T(8,128)(2,1)} %get-tuple-element.63), channel_id=1, source_target_pairs={{0,1},{1,0},{2,3},{3,2},{4,5},{5,4},{6,7},{7,6},{8,9},{9,8},{10,11... | collective-permute-start | bytes 3932168 | tf_op jit(solution)/shard_map/ppermute | solution.py:80
  22.8 47.7 %collective-permute-start.11 = (bf16[128,256]{0,1:T(8,128)(2,1)}, bf16[128,256]{0,1:T(8,128)(2,1)}, u32[]{:S(2)}, u32[]{:S(2)}) collective-permute-start(bf16[128,256]{0,1:T(8,128)(2,1)} %get-tuple-element.166), channel_id=1, source_target_pairs={{0,2},{2,0},{4,6},{6,4},{1,3},{3,1},{5,7},{7,5},{8,10},{10,8},{12,... | collective-permute-start | bytes 196616 | tf_op jit(solution)/shard_map/ppermute | solution.py:143
  29.3 23.5 %collective-permute-start.9 = (bf16[128,512]{1,0:T(8,128)(2,1)S(1)}, bf16[128,512]{1,0:T(8,128)(2,1)S(1)}, u32[]{:S(2)}, u32[]{:S(2)}) collective-permute-start(bf16[128,512]{1,0:T(8,128)(2,1)S(1)} %copy-done.82), channel_id=1, source_target_pairs={{0,4},{2,6},{4,0},{6,2},{1,5},{3,7},{5,1},{7,3},{8,12},{10,14},{12... | collective-permute-start | bytes 393224 | tf_op jit(solution)/shard_map/ppermute | solution.py:143
  61.0 126.0 %all-gather.7.cloned.1.call-start = ((), (), s32[]{:S(2)}) async-start(), calls=%async_computation.5 | async-start | bytes 1310720 | tf_op jit(solution)/shard_map/all_gather | solution.py:181
  75.7 300.3 %all-gather.9.cloned.1.call-start = ((), (), s32[]{:S(2)}) async-start(), calls=%async_computation.6 | async-start | bytes 7864320 | tf_op jit(solution)/shard_map/all_gather | solution.py:181
  76.6 17.0 %collective-permute-start.29 = (bf16[128,1536]{1,0:T(8,128)(2,1)S(1)}, bf16[128,1536]{1,0:T(8,128)(2,1)S(1)}, u32[]{:S(2)}, u32[]{:S(2)}) collective-permute-start(bf16[128,1536]{1,0:T(8,128)(2,1)S(1)} %get-tuple-element.92), channel_id=1, source_target_pairs={{0,6},{2,4},{4,2},{6,0},{1,7},{3,5},{5,3},{7,1},{8,14},{10,12},{12... | collective-permute-start | bytes 1179656 | tf_op jit(solution)/shard_map/ppermute | solution.py:143
  94.8 303.6 %all-gather.11.cloned.1.call-start = ((), (), s32[]{:S(2)}) async-start(), calls=%async_computation.7 | async-start | bytes 3932160 | tf_op jit(solution)/shard_map/all_gather | solution.py:181
  96.0 17.6 %collective-permute-start.5 = (bf16[160,2048]{1,0:T(8,128)(2,1)S(1)}, bf16[160,2048]{1,0:T(8,128)(2,1)S(1)}, u32[]{:S(2)}, u32[]{:S(2)}) collective-permute-start(bf16[160,2048]{1,0:T(8,128)(2,1)S(1)} %slice.509), channel_id=1, source_target_pairs={{0,4},{4,0},{1,5},{5,1},{2,6},{6,2},{3,7},{7,3},{8,12},{12,8},{9,1... | collective-permute-start | bytes 1966088 | tf_op jit(solution)/shard_map/ppermute | solution.py:80
  97.8 17.4 %collective-permute-start.6 = (bf16[160,2048]{1,0:T(8,128)(2,1)S(1)}, bf16[160,2048]{1,0:T(8,128)(2,1)S(1)}, u32[]{:S(2)}, u32[]{:S(2)}) collective-permute-start(bf16[160,2048]{1,0:T(8,128)(2,1)S(1)} %slice.510), channel_id=1, source_target_pairs={{0,1},{1,0},{2,3},{3,2},{4,5},{5,4},{6,7},{7,6},{8,9},{9,8},{10,11... | collective-permute-start | bytes 1966088 | tf_op jit(solution)/shard_map/ppermute | solution.py:80
  100.1 19.1 %collective-permute-start.4 = (bf16[320,2048]{1,0:T(8,128)(2,1)}, bf16[320,2048]{1,0:T(8,128)(2,1)S(1)}, u32[]{:S(2)}, u32[]{:S(2)}) collective-permute-start(bf16[320,2048]{1,0:T(8,128)(2,1)} %collective-permute-done.3), channel_id=1, source_target_pairs={{0,2},{2,0},{1,3},{3,1},{4,6},{6,4},{5,7},{7,5},{8,10},{10,8},{9,1... | collective-permute-start | bytes 3932168 | tf_op jit(solution)/shard_map/ppermute | solution.py:80
  192.1 63.7 %collective-permute-start.14 = (bf16[2,2,320,2048]{3,2,1,0:T(8,128)(2,1)}, bf16[2,2,320,2048]{3,2,1,0:T(8,128)(2,1)}, u32[]{:S(2)}, u32[]{:S(2)}) collective-permute-start(bf16[2,2,320,2048]{3,2,1,0:T(8,128)(2,1)} %convolution_convert_fusion.2), channel_id=1, source_target_pairs={{0,2},{2,0},{1,3},{3,1},{4,6},{6,4},{5,7},{7,5},{8,10},{10,8},{9,1... | collective-permute-start | bytes 15728648 | tf_op jit(solution)/shard_map/ppermute | solution.py:80
  201.0 51.1 %collective-permute-start.38 = (bf16[320,2048]{1,0:T(8,128)(2,1)}, bf16[320,2048]{1,0:T(8,128)(2,1)}, u32[]{:S(2)}, u32[]{:S(2)}) collective-permute-start(bf16[320,2048]{1,0:T(8,128)(2,1)} %get-tuple-element.57), channel_id=1, source_target_pairs={{0,2},{2,0},{1,3},{3,1},{4,6},{6,4},{5,7},{7,5},{8,10},{10,8},{9,1... | collective-permute-start | bytes 3932168 | tf_op jit(solution)/shard_map/ppermute | solution.py:80
  201.0 47.6 %collective-permute-start.39 = (bf16[320,2048]{1,0:T(8,128)(2,1)}, bf16[320,2048]{1,0:T(8,128)(2,1)}, u32[]{:S(2)}, u32[]{:S(2)}) collective-permute-start(bf16[320,2048]{1,0:T(8,128)(2,1)} %get-tuple-element.57), channel_id=1, source_target_pairs={{0,4},{4,0},{1,5},{5,1},{2,6},{6,2},{3,7},{7,3},{8,12},{12,8},{9,1... | collective-permute-start | bytes 3932168 | tf_op jit(solution)/shard_map/ppermute | solution.py:80
  202.5 42.6 %collective-permute-start.41 = (bf16[320,2048]{1,0:T(8,128)(2,1)}, bf16[320,2048]{1,0:T(8,128)(2,1)}, u32[]{:S(2)}, u32[]{:S(2)}) collective-permute-start(bf16[320,2048]{1,0:T(8,128)(2,1)} %get-tuple-element.57), channel_id=1, source_target_pairs={{0,1},{1,0},{2,3},{3,2},{4,5},{5,4},{6,7},{7,6},{8,9},{9,8},{10,11... | collective-permute-start | bytes 3932168 | tf_op jit(solution)/shard_map/ppermute | solution.py:80
  206.0 30.6 %collective-permute-start.31 = (bf16[128,768]{0,1:T(8,128)(2,1)S(1)}, bf16[128,768]{0,1:T(8,128)(2,1)S(1)}, u32[]{:S(2)}, u32[]{:S(2)}) collective-permute-start(bf16[128,768]{0,1:T(8,128)(2,1)S(1)} %get-tuple-element.129), channel_id=1, source_target_pairs={{0,4},{2,6},{4,0},{6,2},{1,5},{3,7},{5,1},{7,3},{8,12},{10,14},{12... | collective-permute-start | bytes 589832 | tf_op jit(solution)/shard_map/ppermute | solution.py:143
  245.0 331.5 %reduce-scatter.11.cloned.1.call-start = ((), (), s32[]{:S(2)}) async-start(), calls=%async_computation.11 | async-start | bytes 3932160 | tf_op jit(solution)/shard_map/reduce_scatter | solution.py:185
  247.1 35.7 %collective-permute-start.43 = (bf16[160,2048]{1,0:T(8,128)(2,1)}, bf16[160,2048]{1,0:T(8,128)(2,1)S(1)}, u32[]{:S(2)}, u32[]{:S(2)}) collective-permute-start(bf16[160,2048]{1,0:T(8,128)(2,1)} %slice.554), channel_id=1, source_target_pairs={{0,4},{4,0},{1,5},{5,1},{2,6},{6,2},{3,7},{7,3},{8,12},{12,8},{9,1... | collective-permute-start | bytes 1966088 | tf_op jit(solution)/shard_map/ppermute | solution.py:80
  250.6 33.9 %collective-permute-start.44 = (bf16[160,2048]{1,0:T(8,128)(2,1)}, bf16[160,2048]{1,0:T(8,128)(2,1)}, u32[]{:S(2)}, u32[]{:S(2)}) collective-permute-start(bf16[160,2048]{1,0:T(8,128)(2,1)} %slice.555), channel_id=1, source_target_pairs={{0,1},{1,0},{2,3},{3,2},{4,5},{5,4},{6,7},{7,6},{8,9},{9,8},{10,11... | collective-permute-start | bytes 1966088 | tf_op jit(solution)/shard_map/ppermute | solution.py:80
  252.1 33.6 %collective-permute-start.40 = (bf16[320,2048]{1,0:T(8,128)(2,1)}, bf16[320,2048]{1,0:T(8,128)(2,1)}, u32[]{:S(2)}, u32[]{:S(2)}) collective-permute-start(bf16[320,2048]{1,0:T(8,128)(2,1)} %collective-permute-done.39), channel_id=1, source_target_pairs={{0,2},{2,0},{1,3},{3,1},{4,6},{6,4},{5,7},{7,5},{8,10},{10,8},{9,1... | collective-permute-start | bytes 3932168 | tf_op jit(solution)/shard_map/ppermute | solution.py:80
  260.2 18.1 %collective-permute-start.15 = (bf16[160,2048]{1,0:T(8,128)(2,1)S(1)}, bf16[160,2048]{1,0:T(8,128)(2,1)S(1)}, u32[]{:S(2)}, u32[]{:S(2)}) collective-permute-start(bf16[160,2048]{1,0:T(8,128)(2,1)S(1)} %get-tuple-element.118), channel_id=1, source_target_pairs={{0,4},{4,0},{1,5},{5,1},{2,6},{6,2},{3,7},{7,3},{8,12},{12,8},{9,1... | collective-permute-start | bytes 1966088 | tf_op jit(solution)/shard_map/ppermute | solution.py:80
  260.8 20.6 %collective-permute-start.17 = (bf16[160,2048]{1,0:T(8,128)(2,1)S(1)}, bf16[160,2048]{1,0:T(8,128)(2,1)S(1)}, u32[]{:S(2)}, u32[]{:S(2)}) collective-permute-start(bf16[160,2048]{1,0:T(8,128)(2,1)S(1)} %get-tuple-element.119), channel_id=1, source_target_pairs={{0,1},{1,0},{2,3},{3,2},{4,5},{5,4},{6,7},{7,6},{8,9},{9,8},{10,11... | collective-permute-start | bytes 1966088 | tf_op jit(solution)/shard_map/ppermute | solution.py:80
  278.3 45.3 %collective-permute-start.42 = (bf16[320,2048]{1,0:T(8,128)(2,1)}, bf16[320,2048]{1,0:T(8,128)(2,1)S(1)}, u32[]{:S(2)}, u32[]{:S(2)}) collective-permute-start(bf16[320,2048]{1,0:T(8,128)(2,1)} %collective-permute-done.41), channel_id=1, source_target_pairs={{0,2},{2,0},{1,3},{3,1},{4,6},{6,4},{5,7},{7,5},{8,10},{10,8},{9,1... | collective-permute-start | bytes 3932168 | tf_op jit(solution)/shard_map/ppermute | solution.py:80
  282.0 29.9 %collective-permute-start.18 = (bf16[320,2048]{1,0:T(8,128)(2,1)S(1)}, bf16[320,2048]{1,0:T(8,128)(2,1)S(1)}, u32[]{:S(2)}, u32[]{:S(2)}) collective-permute-start(bf16[320,2048]{1,0:T(8,128)(2,1)S(1)} %pad_maximum_fusion.4), channel_id=1, source_target_pairs={{0,4},{4,0},{1,5},{5,1},{2,6},{6,2},{3,7},{7,3},{8,12},{12,8},{9,1... | collective-permute-start | bytes 3932168 | tf_op jit(solution)/shard_map/ppermute | solution.py:80
  282.8 29.7 %collective-permute-start.16 = (bf16[320,2048]{1,0:T(8,128)(2,1)S(1)}, bf16[320,2048]{1,0:T(8,128)(2,1)S(1)}, u32[]{:S(2)}, u32[]{:S(2)}) collective-permute-start(bf16[320,2048]{1,0:T(8,128)(2,1)S(1)} %pad_maximum_fusion.3), channel_id=1, source_target_pairs={{0,1},{1,0},{2,3},{3,2},{4,5},{5,4},{6,7},{7,6},{8,9},{9,8},{10,11... | collective-permute-start | bytes 3932168 | tf_op jit(solution)/shard_map/ppermute | solution.py:80
  285.6 40.4 %collective-permute-start.45 = (bf16[320,2048]{1,0:T(8,128)(2,1)S(1)}, bf16[320,2048]{1,0:T(8,128)(2,1)S(1)}, u32[]{:S(2)}, u32[]{:S(2)}) collective-permute-start(bf16[320,2048]{1,0:T(8,128)(2,1)S(1)} %constant_dynamic-update-slice_fusion.4), channel_id=1, source_target_pairs={{0,2},{2,0},{1,3},{3,1},{4,6},{6,4},{5,7},{7,5},{8,10},{10,8},{9,1... | collective-permute-start | bytes 3932168 | tf_op jit(solution)/shard_map/ppermute | solution.py:80
  320.8 35.1 %collective-permute-start.19 = (bf16[320,2048]{1,0:T(8,128)(2,1)S(1)}, bf16[320,2048]{1,0:T(8,128)(2,1)S(1)}, u32[]{:S(2)}, u32[]{:S(2)}) collective-permute-start(bf16[320,2048]{1,0:T(8,128)(2,1)S(1)} %get-tuple-element.59), channel_id=1, source_target_pairs={{0,2},{2,0},{1,3},{3,1},{4,6},{6,4},{5,7},{7,5},{8,10},{10,8},{9,1... | collective-permute-start | bytes 3932168 | tf_op jit(solution)/shard_map/ppermute | solution.py:80
  320.8 33.1 %collective-permute-start.20 = (bf16[320,2048]{1,0:T(8,128)(2,1)S(1)}, bf16[320,2048]{1,0:T(8,128)(2,1)S(1)}, u32[]{:S(2)}, u32[]{:S(2)}) collective-permute-start(bf16[320,2048]{1,0:T(8,128)(2,1)S(1)} %get-tuple-element.59), channel_id=1, source_target_pairs={{0,4},{4,0},{1,5},{5,1},{2,6},{6,2},{3,7},{7,3},{8,12},{12,8},{9,1... | collective-permute-start | bytes 3932168 | tf_op jit(solution)/shard_map/ppermute | solution.py:80
  322.1 30.9 %collective-permute-start.22 = (bf16[320,2048]{1,0:T(8,128)(2,1)S(1)}, bf16[320,2048]{1,0:T(8,128)(2,1)S(1)}, u32[]{:S(2)}, u32[]{:S(2)}) collective-permute-start(bf16[320,2048]{1,0:T(8,128)(2,1)S(1)} %get-tuple-element.59), channel_id=1, source_target_pairs={{0,1},{1,0},{2,3},{3,2},{4,5},{5,4},{6,7},{7,6},{8,9},{9,8},{10,11... | collective-permute-start | bytes 3932168 | tf_op jit(solution)/shard_map/ppermute | solution.py:80
  353.0 16.1 %collective-permute-start.24 = (bf16[160,2048]{1,0:T(8,128)(2,1)S(1)}, bf16[160,2048]{1,0:T(8,128)(2,1)S(1)}, u32[]{:S(2)}, u32[]{:S(2)}) collective-permute-start(bf16[160,2048]{1,0:T(8,128)(2,1)S(1)} %slice.536), channel_id=1, source_target_pairs={{0,4},{4,0},{1,5},{5,1},{2,6},{6,2},{3,7},{7,3},{8,12},{12,8},{9,1... | collective-permute-start | bytes 1966088 | tf_op jit(solution)/shard_map/ppermute | solution.py:80
  353.9 15.8 %collective-permute-start.25 = (bf16[160,2048]{1,0:T(8,128)(2,1)S(1)}, bf16[160,2048]{1,0:T(8,128)(2,1)S(1)}, u32[]{:S(2)}, u32[]{:S(2)}) collective-permute-start(bf16[160,2048]{1,0:T(8,128)(2,1)S(1)} %slice.537), channel_id=1, source_target_pairs={{0,1},{1,0},{2,3},{3,2},{4,5},{5,4},{6,7},{7,6},{8,9},{9,8},{10,11... | collective-permute-start | bytes 1966088 | tf_op jit(solution)/shard_map/ppermute | solution.py:80
  355.3 17.0 %collective-permute-start.23 = (bf16[320,2048]{1,0:T(8,128)(2,1)S(1)}, bf16[320,2048]{1,0:T(8,128)(2,1)S(1)}, u32[]{:S(2)}, u32[]{:S(2)}) collective-permute-start(bf16[320,2048]{1,0:T(8,128)(2,1)S(1)} %collective-permute-done.22), channel_id=1, source_target_pairs={{0,2},{2,0},{1,3},{3,1},{4,6},{6,4},{5,7},{7,5},{8,10},{10,8},{9,1... | collective-permute-start | bytes 3932168 | tf_op jit(solution)/shard_map/ppermute | solution.py:80
  431.3 23.1 %collective-permute-start.46 = (bf16[2,2,320,2048]{3,2,1,0:T(8,128)(2,1)}, bf16[2,2,320,2048]{3,2,1,0:T(8,128)(2,1)}, u32[]{:S(2)}, u32[]{:S(2)}) collective-permute-start(bf16[2,2,320,2048]{3,2,1,0:T(8,128)(2,1)} %fusion.26), channel_id=1, source_target_pairs={{0,2},{2,0},{1,3},{3,1},{4,6},{6,4},{5,7},{7,5},{8,10},{10,8},{9,1... | collective-permute-start | bytes 15728648 | tf_op jit(solution)/shard_map/ppermute | solution.py:80
  437.9 32.8 %collective-permute-start.33 = (bf16[2,2,320,2048]{3,2,1,0:T(8,128)(2,1)}, bf16[2,2,320,2048]{3,2,1,0:T(8,128)(2,1)}, u32[]{:S(2)}, u32[]{:S(2)}) collective-permute-start(bf16[2,2,320,2048]{3,2,1,0:T(8,128)(2,1)} %convolution_convert_fusion.1), channel_id=1, source_target_pairs={{0,2},{2,0},{1,3},{3,1},{4,6},{6,4},{5,7},{7,5},{8,10},{10,8},{9,1... | collective-permute-start | bytes 15728648 | tf_op jit(solution)/shard_map/ppermute | solution.py:80
  454.3 289.6 %reduce-scatter.9.cloned.1.call-start = ((), (), s32[]{:S(2)}) async-start(), calls=%async_computation.10 | async-start | bytes 7864320 | tf_op jit(solution)/shard_map/reduce_scatter | solution.py:185
  467.8 20.0 %collective-permute-start.47 = (bf16[160,2048]{1,0:T(8,128)(2,1)S(1)}, bf16[160,2048]{1,0:T(8,128)(2,1)S(1)}, u32[]{:S(2)}, u32[]{:S(2)}) collective-permute-start(bf16[160,2048]{1,0:T(8,128)(2,1)S(1)} %get-tuple-element.114), channel_id=1, source_target_pairs={{0,4},{4,0},{1,5},{5,1},{2,6},{6,2},{3,7},{7,3},{8,12},{12,8},{9,1... | collective-permute-start | bytes 1966088 | tf_op jit(solution)/shard_map/ppermute | solution.py:80
  469.2 18.6 %collective-permute-start.49 = (bf16[160,2048]{1,0:T(8,128)(2,1)S(1)}, bf16[160,2048]{1,0:T(8,128)(2,1)S(1)}, u32[]{:S(2)}, u32[]{:S(2)}) collective-permute-start(bf16[160,2048]{1,0:T(8,128)(2,1)S(1)} %get-tuple-element.115), channel_id=1, source_target_pairs={{0,1},{1,0},{2,3},{3,2},{4,5},{5,4},{6,7},{7,6},{8,9},{9,8},{10,11... | collective-permute-start | bytes 1966088 | tf_op jit(solution)/shard_map/ppermute | solution.py:80
  482.7 17.6 %collective-permute-start.34 = (bf16[160,2048]{1,0:T(8,128)(2,1)S(1)}, bf16[160,2048]{1,0:T(8,128)(2,1)S(1)}, u32[]{:S(2)}, u32[]{:S(2)}) collective-permute-start(bf16[160,2048]{1,0:T(8,128)(2,1)S(1)} %get-tuple-element.116), channel_id=1, source_target_pairs={{0,4},{4,0},{1,5},{5,1},{2,6},{6,2},{3,7},{7,3},{8,12},{12,8},{9,1... | collective-permute-start | bytes 1966088 | tf_op jit(solution)/shard_map/ppermute | solution.py:80
  484.1 17.6 %collective-permute-start.36 = (bf16[160,2048]{1,0:T(8,128)(2,1)S(1)}, bf16[160,2048]{1,0:T(8,128)(2,1)S(1)}, u32[]{:S(2)}, u32[]{:S(2)}) collective-permute-start(bf16[160,2048]{1,0:T(8,128)(2,1)S(1)} %get-tuple-element.117), channel_id=1, source_target_pairs={{0,1},{1,0},{2,3},{3,2},{4,5},{5,4},{6,7},{7,6},{8,9},{9,8},{10,11... | collective-permute-start | bytes 1966088 | tf_op jit(solution)/shard_map/ppermute | solution.py:80
  489.4 39.9 %collective-permute-start.50 = (bf16[320,2048]{1,0:T(8,128)(2,1)}, bf16[320,2048]{1,0:T(8,128)(2,1)}, u32[]{:S(2)}, u32[]{:S(2)}) collective-permute-start(bf16[320,2048]{1,0:T(8,128)(2,1)} %pad_maximum_fusion.8), channel_id=1, source_target_pairs={{0,4},{4,0},{1,5},{5,1},{2,6},{6,2},{3,7},{7,3},{8,12},{12,8},{9,1... | collective-permute-start | bytes 3932168 | tf_op jit(solution)/shard_map/ppermute | solution.py:80
  491.1 38.8 %collective-permute-start.48 = (bf16[320,2048]{1,0:T(8,128)(2,1)}, bf16[320,2048]{1,0:T(8,128)(2,1)}, u32[]{:S(2)}, u32[]{:S(2)}) collective-permute-start(bf16[320,2048]{1,0:T(8,128)(2,1)} %pad_maximum_fusion.7), channel_id=1, source_target_pairs={{0,1},{1,0},{2,3},{3,2},{4,5},{5,4},{6,7},{7,6},{8,9},{9,8},{10,11... | collective-permute-start | bytes 3932168 | tf_op jit(solution)/shard_map/ppermute | solution.py:80
  505.2 51.0 %collective-permute-start.37 = (bf16[320,2048]{1,0:T(8,128)(2,1)}, bf16[320,2048]{1,0:T(8,128)(2,1)}, u32[]{:S(2)}, u32[]{:S(2)}) collective-permute-start(bf16[320,2048]{1,0:T(8,128)(2,1)} %pad_maximum_fusion.6), channel_id=1, source_target_pairs={{0,4},{4,0},{1,5},{5,1},{2,6},{6,2},{3,7},{7,3},{8,12},{12,8},{9,1... | collective-permute-start | bytes 3932168 | tf_op jit(solution)/shard_map/ppermute | solution.py:80
  507.0 50.3 %collective-permute-start.35 = (bf16[320,2048]{1,0:T(8,128)(2,1)}, bf16[320,2048]{1,0:T(8,128)(2,1)}, u32[]{:S(2)}, u32[]{:S(2)}) collective-permute-start(bf16[320,2048]{1,0:T(8,128)(2,1)} %pad_maximum_fusion.5), channel_id=1, source_target_pairs={{0,1},{1,0},{2,3},{3,2},{4,5},{5,4},{6,7},{7,6},{8,9},{9,8},{10,11... | collective-permute-start | bytes 3932168 | tf_op jit(solution)/shard_map/ppermute | solution.py:80
  528.8 220.6 %reduce-scatter.7.cloned.1.call-start = ((), (), s32[]{:S(2)}) async-start(), calls=%async_computation.9 | async-start | bytes 1310720 | tf_op jit(solution)/shard_map/reduce_scatter | solution.py:185
  574.4 44.4 %collective-permute-start.51 = (bf16[320,2048]{1,0:T(8,128)(2,1)}, bf16[320,2048]{1,0:T(8,128)(2,1)}, u32[]{:S(2)}, u32[]{:S(2)}) collective-permute-start(bf16[320,2048]{1,0:T(8,128)(2,1)} %get-tuple-element.53), channel_id=1, source_target_pairs={{0,2},{2,0},{1,3},{3,1},{4,6},{6,4},{5,7},{7,5},{8,10},{10,8},{9,1... | collective-permute-start | bytes 3932168 | tf_op jit(solution)/shard_map/ppermute | solution.py:80
  574.4 41.2 %collective-permute-start.52 = (bf16[320,2048]{1,0:T(8,128)(2,1)}, bf16[320,2048]{1,0:T(8,128)(2,1)}, u32[]{:S(2)}, u32[]{:S(2)}) collective-permute-start(bf16[320,2048]{1,0:T(8,128)(2,1)} %get-tuple-element.53), channel_id=1, source_target_pairs={{0,4},{4,0},{1,5},{5,1},{2,6},{6,2},{3,7},{7,3},{8,12},{12,8},{9,1... | collective-permute-start | bytes 3932168 | tf_op jit(solution)/shard_map/ppermute | solution.py:80
  575.1 39.7 %collective-permute-start.54 = (bf16[320,2048]{1,0:T(8,128)(2,1)}, bf16[320,2048]{1,0:T(8,128)(2,1)S(1)}, u32[]{:S(2)}, u32[]{:S(2)}) collective-permute-start(bf16[320,2048]{1,0:T(8,128)(2,1)} %get-tuple-element.53), channel_id=1, source_target_pairs={{0,1},{1,0},{2,3},{3,2},{4,5},{5,4},{6,7},{7,6},{8,9},{9,8},{10,11... | collective-permute-start | bytes 3932168 | tf_op jit(solution)/shard_map/ppermute | solution.py:80
  579.0 31.5 %collective-permute-start.74 = (bf16[128,768]{0,1:T(8,128)(2,1)S(1)}, bf16[128,768]{0,1:T(8,128)(2,1)}, u32[]{:S(2)}, u32[]{:S(2)}) collective-permute-start(bf16[128,768]{0,1:T(8,128)(2,1)S(1)} %bitcast.613), channel_id=1, source_target_pairs={{0,4},{2,6},{4,0},{6,2},{1,5},{3,7},{5,1},{7,3},{8,12},{10,14},{12... | collective-permute-start | bytes 589832 | tf_op jit(solution)/shard_map/ppermute | solution.py:143
  581.8 32.0 %collective-permute-start.75 = (bf16[128,768]{0,1:T(8,128)(2,1)S(1)}, bf16[128,768]{0,1:T(8,128)(2,1)S(1)}, u32[]{:S(2)}, u32[]{:S(2)}) collective-permute-start(bf16[128,768]{0,1:T(8,128)(2,1)S(1)} %bitcast.614), channel_id=1, source_target_pairs={{0,6},{2,4},{4,2},{6,0},{1,7},{3,5},{5,3},{7,1},{8,14},{10,12},{12... | collective-permute-start | bytes 589832 | tf_op jit(solution)/shard_map/ppermute | solution.py:143
  614.8 17.3 %collective-permute-start.56 = (bf16[160,2048]{1,0:T(8,128)(2,1)S(1)}, bf16[160,2048]{1,0:T(8,128)(2,1)S(1)}, u32[]{:S(2)}, u32[]{:S(2)}) collective-permute-start(bf16[160,2048]{1,0:T(8,128)(2,1)S(1)} %slice.558), channel_id=1, source_target_pairs={{0,4},{4,0},{1,5},{5,1},{2,6},{6,2},{3,7},{7,3},{8,12},{12,8},{9,1... | collective-permute-start | bytes 1966088 | tf_op jit(solution)/shard_map/ppermute | solution.py:80
  616.7 17.0 %collective-permute-start.57 = (bf16[160,2048]{1,0:T(8,128)(2,1)S(1)}, bf16[160,2048]{1,0:T(8,128)(2,1)S(1)}, u32[]{:S(2)}, u32[]{:S(2)}) collective-permute-start(bf16[160,2048]{1,0:T(8,128)(2,1)S(1)} %slice.559), channel_id=1, source_target_pairs={{0,1},{1,0},{2,3},{3,2},{4,5},{5,4},{6,7},{7,6},{8,9},{9,8},{10,11... | collective-permute-start | bytes 1966088 | tf_op jit(solution)/shard_map/ppermute | solution.py:80
  618.2 15.7 %collective-permute-start.53 = (bf16[320,2048]{1,0:T(8,128)(2,1)}, bf16[320,2048]{1,0:T(8,128)(2,1)S(1)}, u32[]{:S(2)}, u32[]{:S(2)}) collective-permute-start(bf16[320,2048]{1,0:T(8,128)(2,1)} %collective-permute-done.52), channel_id=1, source_target_pairs={{0,2},{2,0},{1,3},{3,1},{4,6},{6,4},{5,7},{7,5},{8,10},{10,8},{9,1... | collective-permute-start | bytes 3932168 | tf_op jit(solution)/shard_map/ppermute | solution.py:80
  618.3 18.0 %collective-permute-start.55 = (bf16[320,2048]{1,0:T(8,128)(2,1)S(1)}, bf16[320,2048]{1,0:T(8,128)(2,1)S(1)}, u32[]{:S(2)}, u32[]{:S(2)}) collective-permute-start(bf16[320,2048]{1,0:T(8,128)(2,1)S(1)} %collective-permute-done.54), channel_id=1, source_target_pairs={{0,2},{2,0},{1,3},{3,1},{4,6},{6,4},{5,7},{7,5},{8,10},{10,8},{9,1... | collective-permute-start | bytes 3932168 | tf_op jit(solution)/shard_map/ppermute | solution.py:80
  704.2 84.7 %reduce-scatter.5.cloned.1.call-start = ((), (), s32[]{:S(2)}) async-start(), calls=%async_computation.8 | async-start | bytes 2621440 | tf_op jit(solution)/shard_map/reduce_scatter | solution.py:185
  730.1 68.4 %collective-permute-start.59 = (bf16[2,2,320,2048]{3,2,1,0:T(8,128)(2,1)}, bf16[2,2,320,2048]{3,2,1,0:T(8,128)(2,1)}, u32[]{:S(2)}, u32[]{:S(2)}) collective-permute-start(bf16[2,2,320,2048]{3,2,1,0:T(8,128)(2,1)} %convolution_convert_fusion), channel_id=1, source_target_pairs={{0,2},{2,0},{1,3},{3,1},{4,6},{6,4},{5,7},{7,5},{8,10},{10,8},{9,1... | collective-permute-start | bytes 15728648 | tf_op jit(solution)/shard_map/ppermute | solution.py:80
  746.1 26.7 %collective-permute-start.70 = (bf16[128,1536]{1,0:T(8,128)(2,1)}, bf16[128,1536]{1,0:T(8,128)(2,1)S(1)}, u32[]{:S(2)}, u32[]{:S(2)}) collective-permute-start(bf16[128,1536]{1,0:T(8,128)(2,1)} %get-tuple-element.90), channel_id=1, source_target_pairs={{0,2},{2,0},{4,6},{6,4},{1,3},{3,1},{5,7},{7,5},{8,10},{10,8},{12,... | collective-permute-start | bytes 1179656 | tf_op jit(solution)/shard_map/ppermute | solution.py:143
  746.2 26.7 %collective-permute-start.71 = (bf16[128,1536]{1,0:T(8,128)(2,1)S(1)}, bf16[128,1536]{1,0:T(8,128)(2,1)S(1)}, u32[]{:S(2)}, u32[]{:S(2)}) collective-permute-start(bf16[128,1536]{1,0:T(8,128)(2,1)S(1)} %get-tuple-element.89), channel_id=1, source_target_pairs={{0,4},{2,6},{4,0},{6,2},{1,5},{3,7},{5,1},{7,3},{8,12},{10,14},{12... | collective-permute-start | bytes 1179656 | tf_op jit(solution)/shard_map/ppermute | solution.py:143
  747.6 25.3 %collective-permute-start.72 = (bf16[128,1536]{1,0:T(8,128)(2,1)S(1)}, bf16[128,1536]{1,0:T(8,128)(2,1)S(1)}, u32[]{:S(2)}, u32[]{:S(2)}) collective-permute-start(bf16[128,1536]{1,0:T(8,128)(2,1)S(1)} %get-tuple-element.88), channel_id=1, source_target_pairs={{0,6},{2,4},{4,2},{6,0},{1,7},{3,5},{5,3},{7,1},{8,14},{10,12},{12... | collective-permute-start | bytes 1179656 | tf_op jit(solution)/shard_map/ppermute | solution.py:143
  805.3 17.0 %collective-permute-start.60 = (bf16[160,2048]{1,0:T(8,128)(2,1)S(1)}, bf16[160,2048]{1,0:T(8,128)(2,1)S(1)}, u32[]{:S(2)}, u32[]{:S(2)}) collective-permute-start(bf16[160,2048]{1,0:T(8,128)(2,1)S(1)} %get-tuple-element.110), channel_id=1, source_target_pairs={{0,4},{4,0},{1,5},{5,1},{2,6},{6,2},{3,7},{7,3},{8,12},{12,8},{9,1... | collective-permute-start | bytes 1966088 | tf_op jit(solution)/shard_map/ppermute | solution.py:80
  806.8 16.6 %collective-permute-start.62 = (bf16[160,2048]{1,0:T(8,128)(2,1)S(1)}, bf16[160,2048]{1,0:T(8,128)(2,1)S(1)}, u32[]{:S(2)}, u32[]{:S(2)}) collective-permute-start(bf16[160,2048]{1,0:T(8,128)(2,1)S(1)} %get-tuple-element.111), channel_id=1, source_target_pairs={{0,1},{1,0},{2,3},{3,2},{4,5},{5,4},{6,7},{7,6},{8,9},{9,8},{10,11... | collective-permute-start | bytes 1966088 | tf_op jit(solution)/shard_map/ppermute | solution.py:80
  824.1 29.9 %collective-permute-start.63 = (bf16[320,2048]{1,0:T(8,128)(2,1)S(1)}, bf16[320,2048]{1,0:T(8,128)(2,1)S(1)}, u32[]{:S(2)}, u32[]{:S(2)}) collective-permute-start(bf16[320,2048]{1,0:T(8,128)(2,1)S(1)} %pad_maximum_fusion.10), channel_id=1, source_target_pairs={{0,4},{4,0},{1,5},{5,1},{2,6},{6,2},{3,7},{7,3},{8,12},{12,8},{9,1... | collective-permute-start | bytes 3932168 | tf_op jit(solution)/shard_map/ppermute | solution.py:80
  824.8 29.7 %collective-permute-start.61 = (bf16[320,2048]{1,0:T(8,128)(2,1)S(1)}, bf16[320,2048]{1,0:T(8,128)(2,1)S(1)}, u32[]{:S(2)}, u32[]{:S(2)}) collective-permute-start(bf16[320,2048]{1,0:T(8,128)(2,1)S(1)} %pad_maximum_fusion.9), channel_id=1, source_target_pairs={{0,1},{1,0},{2,3},{3,2},{4,5},{5,4},{6,7},{7,6},{8,9},{9,8},{10,11... | collective-permute-start | bytes 3932168 | tf_op jit(solution)/shard_map/ppermute | solution.py:80
  (153 other events, 1356.5 us)
Sparse Core Ops, SparseCore 0:
  61.2 46.2 all-gather.4
  109.6 26.6 all-gather.6
  138.4 114.8 all-gather.8
  255.3 61.7 all-gather.10
  454.4 61.3 reduce-scatter.10
  528.9 110.9 reduce-scatter.8
  704.3 28.3 reduce-scatter.6
  744.0 44.8 reduce-scatter.4

commit v3 on v2

v3 whole, which is shorter than its diff:
```python
import jax
import jax.numpy as jnp
from jax import lax
from jax.experimental import pallas as pl
from jax.experimental.pallas import tpu as pltpu
from jax.sharding import Mesh, PartitionSpec as P

D = 2048
H = 16
KV = 8
HD = 128
FF = 6144
STEP = 10


norm_epsilon = 1e-06
rope_base = 1000000.0
clip_norm = 1.0
learn_rate = 0.04
gain_rate = 0.8
beta_first = 0.9
beta_second = 0.999
adam_epsilon = 1e-08
weight_decay = 0.1
masked_score = -1e30

NEAR = 2
CORE = 2
TEAM = NEAR * CORE
LAYER = ("near", "core", "tp")
BLOCK = 128
PAD = 128


def rms_scale(values):
    return lax.rsqrt(jnp.mean(values * values, axis=-1, keepdims=True) + norm_epsilon)


def swish_product(gate_part, up_part):
    return jax.nn.silu(gate_part) * up_part


def swap(values, axis):
    return lax.ppermute(values, axis, [(0, 1), (1, 0)])


def pick(values, index):
    return lax.dynamic_index_in_dim(values, index, 0, keepdims=False)


def put(buffer, values, *index):
    zero = jnp.zeros((), jnp.int32)
    start = tuple(index) + (zero,) * (buffer.ndim - len(index))
    return lax.dynamic_update_slice(buffer, values[(None,) * len(index)], start)


def by_twin(values, multiply):
    core = lax.axis_index("core")
    blocks = values.reshape(NEAR, CORE, 2, -1, values.shape[1])

    def part(which):
        chosen = lax.dynamic_index_in_dim(blocks, which, 1, keepdims=False)
        return multiply(chosen.reshape(-1, values.shape[1])).reshape(NEAR, 2, -1, D)

    return part(1 - core), part(core)


def sum_rows(values, multiply):
    near, _, tp = (lax.axis_index(name) for name in LAYER)
    theirs, ours = by_twin(values, multiply)
    ours = ours + swap(theirs.astype(jnp.bfloat16), "core").astype(jnp.float32)

    def block(where_near, where_tp):
        return pick(pick(ours, where_near), where_tp)

    far = block(1 - near, 1 - tp).astype(jnp.bfloat16)
    half = far.shape[0] // 2
    top = swap(far[:half], "near").astype(jnp.float32)
    low = swap(far[half:], "tp").astype(jnp.float32)
    to_tp = block(near, 1 - tp)
    to_tp = jnp.concatenate([to_tp[:half] + top, to_tp[half:]], axis=0)
    to_near = block(1 - near, tp)
    to_near = jnp.concatenate([to_near[:half], to_near[half:] + low], axis=0)
    from_tp = swap(to_tp.astype(jnp.bfloat16), "tp").astype(jnp.float32)
    from_near = swap(to_near.astype(jnp.bfloat16), "near").astype(jnp.float32)
    return block(near, tp) + from_tp + from_near


MESH_ID = pl.DeviceIdType.MESH
VMEM_LIMIT = 48 * 1024 * 1024
CHUNK = 16
GATHER_COPIES = 13
SUM_COPIES = 10


def spots():
    return tuple(lax.axis_index(name) for name in LAYER)


def greet():
    barrier = pltpu.get_barrier_semaphore()
    for name, spot in zip(LAYER, spots()):
        pl.semaphore_signal(
            barrier, inc=1, device_id={name: 1 - spot}, device_id_type=MESH_ID
        )
    pl.semaphore_wait(barrier, len(LAYER))


def link(source, target, send_sem, recv_sem, name):
    spot = lax.axis_index(name)
    return pltpu.make_async_remote_copy(
        src_ref=source,
        dst_ref=target,
        send_sem=send_sem,
        recv_sem=recv_sem,
        device_id={name: 1 - spot},
        device_id_type=MESH_ID,
    )


def run_gather(own, out, send, recv, own_sem):
    near, core, tp = spots()
    rows = own.shape[0]
    low, high = pl.ds(0, rows // 2), pl.ds(rows // 2, rows // 2)

    def go(number, source, target, name):
        copy = link(source, target, send.at[number], recv.at[number], name)
        copy.start()
        return copy

    def pass_on(number, block, part, name):
        ref = out.at[block[0], block[1], block[2], part]
        return go(number, ref, ref, name)

    here = (near, core, tp)
    beside = (1 - near, core, tp)
    across = (near, core, 1 - tp)
    far = (1 - near, core, 1 - tp)
    tp_low = go(0, own.at[low], out.at[near, core, tp, low], "tp")
    near_high = go(1, own.at[high], out.at[near, core, tp, high], "near")
    tp_high = go(2, own.at[high], out.at[near, core, tp, high], "tp")
    near_low = go(3, own.at[low], out.at[near, core, tp, low], "near")
    twin = [go(4, own, out.at[near, core, tp], "core")]
    keep = pltpu.make_async_copy(own, out.at[near, core, tp], own_sem)
    keep.start()
    tp_low.wait_recv()
    far_low = pass_on(5, across, low, "near")
    twin.append(pass_on(6, across, low, "core"))
    near_high.wait_recv()
    far_high = pass_on(7, beside, high, "tp")
    twin.append(pass_on(8, beside, high, "core"))
    tp_high.wait_recv()
    twin.append(pass_on(9, across, high, "core"))
    near_low.wait_recv()
    twin.append(pass_on(10, beside, low, "core"))
    far_low.wait_recv()
    twin.append(pass_on(11, far, low, "core"))
    far_high.wait_recv()
    twin.append(pass_on(12, far, high, "core"))
    for copy in twin:
        copy.wait_recv()
    for copy in [tp_low, near_high, tp_high, near_low, far_low, far_high] + twin:
        copy.wait_send()
    keep.wait()


def add_rows(target, start, count, *sources):
    @pl.loop(0, count // CHUNK)
    def _(step):
        at = pl.ds(pl.multiple_of(start + step * CHUNK, CHUNK), CHUNK)
        total = None
        for source, shift in sources:
            where = pl.ds(pl.multiple_of(start - shift + step * CHUNK, CHUNK), CHUNK)
            value = source[where].astype(jnp.float32)
            total = value if total is None else total + value
        target[at] = total.astype(target.dtype)


def run_sum(part, total, held, send, recv, local_sem):
    mine, theirs, far, to_tp, to_near, way_near, way_tp, from_tp, from_near = held
    near, core, tp = spots()
    rows = total.shape[0]
    half = rows // 2
    low, high = pl.ds(0, half), pl.ds(half, half)
    order = [(1 - near, 1 - tp), (near, 1 - tp), (1 - near, tp), (near, tp)]
    twin, keep = [], []
    for number, (a, b) in enumerate(order):
        copy = link(
            part.at[a, 1 - core, b], theirs.at[number], send.at[number], recv.at[number], "core"
        )
        copy.start()
        twin.append(copy)
        copy = pltpu.make_async_copy(part.at[a, core, b], mine.at[number], local_sem.at[number])
        copy.start()
        keep.append(copy)

    def ready(number):
        keep[number].wait()
        twin[number].wait_recv()
        return (mine.at[number], 0), (theirs.at[number], 0)

    def go(number, source, target, name):
        copy = link(source, target, send.at[number], recv.at[number], name)
        copy.start()
        return copy

    pair = ready(0)
    add_rows(far, 0, half, *pair)
    far_low = go(4, far.at[low], way_near, "near")
    add_rows(far, half, half, *pair)
    far_high = go(5, far.at[high], way_tp, "tp")
    pair = ready(1)
    add_rows(to_tp, half, half, *pair)
    tp_high = go(6, to_tp.at[high], from_tp.at[high], "tp")
    other = ready(2)
    add_rows(to_near, 0, half, *other)
    near_low = go(7, to_near.at[low], from_near.at[low], "near")
    far_low.wait_recv()
    add_rows(to_tp, 0, half, *pair, (way_near, 0))
    tp_low = go(8, to_tp.at[low], from_tp.at[low], "tp")
    far_high.wait_recv()
    add_rows(to_near, half, half, *other, (way_tp, half))
    near_high = go(9, to_near.at[high], from_near.at[high], "near")
    pair = ready(3)
    add_rows(total, 0, rows, *pair)
    tp_high.wait_recv()
    near_low.wait_recv()
    tp_low.wait_recv()
    near_high.wait_recv()
    for copy in twin + [far_low, far_high, tp_high, near_low, tp_low, near_high]:
        copy.wait_send()
    return from_tp, from_near


def sum_scratch(rows, width):
    low = jnp.bfloat16
    return [
        pltpu.VMEM((4, rows, width), low),
        pltpu.VMEM((4, rows, width), low),
        pltpu.VMEM((rows, width), low),
        pltpu.VMEM((rows, width), low),
        pltpu.VMEM((rows, width), low),
        pltpu.VMEM((rows // 2, width), low),
        pltpu.VMEM((rows // 2, width), low),
        pltpu.VMEM((rows, width), low),
        pltpu.VMEM((rows, width), low),
        pltpu.SemaphoreType.DMA((SUM_COPIES,)),
        pltpu.SemaphoreType.DMA((SUM_COPIES,)),
        pltpu.SemaphoreType.DMA((4,)),
    ]


def gather_scratch():
    return [
        pltpu.SemaphoreType.DMA((GATHER_COPIES,)),
        pltpu.SemaphoreType.DMA((GATHER_COPIES,)),
        pltpu.SemaphoreType.DMA,
    ]


def params(number):
    return pltpu.CompilerParams(
        collective_id=number, has_side_effects=True, vmem_limit_bytes=VMEM_LIMIT
    )


def link_cost(rows, width, exchanges):
    return pl.CostEstimate(
        flops=0, bytes_accessed=exchanges * rows * width * 240, transcendentals=0
    )


def in_vmem():
    return pl.BlockSpec(memory_space=pltpu.VMEM)


def anywhere():
    return pl.BlockSpec(memory_space=pl.ANY)


def gather_rows(values, number, name):
    rows, width = values.shape

    def kernel(own, out, send, recv, own_sem):
        greet()
        run_gather(own, out, send, recv, own_sem)

    full = pl.pallas_call(
        kernel,
        name=name,
        out_shape=jax.ShapeDtypeStruct((NEAR, CORE, 2, rows, width), values.dtype),
        in_specs=[anywhere()],
        out_specs=anywhere(),
        scratch_shapes=gather_scratch(),
        compiler_params=params(number),
        cost_estimate=link_cost(rows, width, 1),
    )(values)
    return full.reshape(-1, width)


def row_loop(rows, body):
    @pl.loop(0, rows // CHUNK)
    def _(step):
        body(pl.ds(pl.multiple_of(step * CHUNK, CHUNK), CHUNK))


def spread(part, rows):
    return part.reshape(NEAR, CORE, 2, rows, part.shape[-1])


def branch_and_norm(part, residual, gain, number, name):
    rows, width = residual.shape

    def kernel(part, residual, gain, hidden, out, *scratch):
        held, (send, recv, local_sem, normed, g_send, g_recv, own_sem) = scratch[:9], scratch[9:]
        greet()
        from_tp, from_near = run_sum(part, hidden, held, send, recv, local_sem)

        def finish(at):
            value = hidden[at] + from_tp[at].astype(jnp.float32)
            value = value + from_near[at].astype(jnp.float32)
            value = residual[at].astype(jnp.float32) + value
            hidden[at] = value
            normed[at] = (value * rms_scale(value) * gain[...]).astype(jnp.bfloat16)

        row_loop(rows, finish)
        run_gather(normed, out, g_send, g_recv, own_sem)

    hidden, full = pl.pallas_call(
        kernel,
        name=name,
        out_shape=(
            jax.ShapeDtypeStruct((rows, width), jnp.float32),
            jax.ShapeDtypeStruct((NEAR, CORE, 2, rows, width), jnp.bfloat16),
        ),
        in_specs=[anywhere(), in_vmem(), in_vmem()],
        out_specs=(in_vmem(), anywhere()),
        scratch_shapes=sum_scratch(rows, width)
        + [pltpu.VMEM((rows, width), jnp.bfloat16)]
        + gather_scratch(),
        compiler_params=params(number),
        cost_estimate=link_cost(rows, width, 2),
    )(spread(part, rows), residual, gain.reshape(1, width))
    return hidden, full.reshape(-1, width)


def norm_back(value, gain, grad):
    scale = rms_scale(value)
    scaled = grad * gain
    inner = jnp.mean(scaled * value, axis=-1, keepdims=True)
    return scale * scaled - value * (scale * scale * scale * inner), grad * value * scale


def norm_back_rows(part, values, upstream, gain, number, name, gather):
    rows, width = values.shape

    def kernel(part, values, upstream, gain, *rest):
        outs, scratch = rest[: 3 if gather else 2], rest[3 if gather else 2 :]
        result, gain_grad = outs[0], outs[1]
        held, (send, recv, local_sem, total) = scratch[:9], scratch[9:13]
        greet()
        from_tp, from_near = run_sum(part, total, held, send, recv, local_sem)
        gain_grad[...] = jnp.zeros_like(gain_grad)
        if gather:
            low, g_send, g_recv, own_sem = scratch[13:]

        def finish(at):
            grad = total[at] + from_tp[at].astype(jnp.float32)
            grad = grad + from_near[at].astype(jnp.float32)
            back, by_gain = norm_back(values[at].astype(jnp.float32), gain[...], grad)
            gain_grad[...] += by_gain.reshape(CHUNK // 8, 8, width).sum(axis=0)
            value = upstream[at].astype(jnp.float32) + back
            result[at] = value.astype(result.dtype)
            if gather:
                low[at] = value.astype(jnp.bfloat16)

        row_loop(rows, finish)
        if gather:
            run_gather(low, outs[2], g_send, g_recv, own_sem)

    out_shape = [
        jax.ShapeDtypeStruct((rows, width), jnp.float32 if gather else jnp.bfloat16),
        jax.ShapeDtypeStruct((8, width), jnp.float32),
    ]
    out_specs = [in_vmem(), in_vmem()]
    scratch_shapes = sum_scratch(rows, width) + [pltpu.VMEM((rows, width), jnp.float32)]
    if gather:
        out_shape.append(jax.ShapeDtypeStruct((NEAR, CORE, 2, rows, width), jnp.bfloat16))
        out_specs.append(anywhere())
        scratch_shapes += [pltpu.VMEM((rows, width), jnp.bfloat16)] + gather_scratch()
    outs = pl.pallas_call(
        kernel,
        name=name,
        out_shape=tuple(out_shape),
        in_specs=[anywhere()] + [in_vmem()] * 3,
        out_specs=tuple(out_specs),
        scratch_shapes=scratch_shapes,
        compiler_params=params(number),
        cost_estimate=link_cost(rows, width, 2 if gather else 1),
    )(spread(part, rows), values, upstream, gain.reshape(1, width))
    gain_grad = outs[1].sum(axis=0)
    if gather:
        return outs[0], gain_grad, outs[2].reshape(-1, width)
    return outs[0], gain_grad


def total_everywhere(values, outer_count, number, name):
    shape = values.shape

    def kernel(values, out, layer, outers, send, recv):
        near, core, tp = spots()
        outer = lax.axis_index("outer")
        partners = [
            {
                "near": 1 - near if a else near,
                "core": 1 - core if b else core,
                "tp": 1 - tp if c else tp,
            }
            for a in range(NEAR)
            for b in range(CORE)
            for c in range(2)
            if a + b + c
        ]
        partners += [{"outer": (outer + step) % outer_count} for step in range(1, outer_count)]
        barrier = pltpu.get_barrier_semaphore()
        for partner in partners:
            pl.semaphore_signal(barrier, inc=1, device_id=partner, device_id_type=MESH_ID)
        pl.semaphore_wait(barrier, len(partners))

        def share(slots, mine, first, count):
            copies = []
            for number in range(first, first + count):
                copy = pltpu.make_async_remote_copy(
                    src_ref=slots.at[mine],
                    dst_ref=slots.at[mine],
                    send_sem=send.at[number],
                    recv_sem=recv.at[number],
                    device_id=partners[number],
                    device_id_type=MESH_ID,
                )
                copy.start()
                copies.append(copy)
            for copy in copies:
                copy.wait()

        mine = near * (CORE * 2) + core * 2 + tp
        layer[mine] = values[...]
        share(layer, mine, 0, 7)
        total = layer[0]
        for slot in range(1, 8):
            total = total + layer[slot]
        outers[outer] = total
        share(outers, outer, 7, outer_count - 1)
        total = outers[0]
        for slot in range(1, outer_count):
            total = total + outers[slot]
        out[...] = total

    return pl.pallas_call(
        kernel,
        name=name,
        out_shape=jax.ShapeDtypeStruct(shape, jnp.float32),
        in_specs=[in_vmem()],
        out_specs=in_vmem(),
        scratch_shapes=[
            pltpu.VMEM((8,) + shape, jnp.float32),
            pltpu.VMEM((outer_count,) + shape, jnp.float32),
            pltpu.SemaphoreType.DMA((6 + outer_count,)),
            pltpu.SemaphoreType.DMA((6 + outer_count,)),
        ],
        compiler_params=params(number),
    )(values)


def head_scale(raw, gain, cos_full, sin_full):
    normed = raw * rms_scale(raw) * gain
    return (normed * cos_full + pltpu.roll(normed, HD // 2, 1) * sin_full).astype(jnp.bfloat16)


def head_back(raw, gain, grad, cos_full, sin_full):
    grad = grad * cos_full - pltpu.roll(grad, HD // 2, 1) * sin_full
    return norm_back(raw, gain, grad)


def columns(index):
    return pl.ds(index * HD, HD)


def head_inputs(proj, gains, cos_ref, sin_ref, queries, keys, values, heads):
    for head in range(heads):
        queries[head] = head_scale(
            proj[0, :, columns(head)], gains[0:1, :], cos_ref[...], sin_ref[...]
        )
    keys[...] = head_scale(
        proj[0, :, columns(heads)], gains[1:2, :], cos_ref[...], sin_ref[...]
    )
    values[...] = proj[0, :, columns(heads + 1)].astype(jnp.bfloat16)


def masked_scores(stacked, keys, step, length):
    scores = lax.dot_general(
        stacked, keys, (((1,), (1,)), ((), ())), preferred_element_type=jnp.float32
    ) * (HD ** (-0.5))
    row = lax.broadcasted_iota(jnp.int32, scores.shape, 0) % BLOCK + step * BLOCK
    column = lax.broadcasted_iota(jnp.int32, scores.shape, 1)
    return jnp.where((column <= row) & (column < length), scores, masked_score)


def stack_heads(ref, at, heads):
    return jnp.concatenate([ref[head, at] for head in range(heads)], axis=0)


def attend(projected, group_length, cos_full, sin_full, gains, heads):
    count, rows, width = projected.shape

    def kernel(lengths, proj, cos_ref, sin_ref, gains, out, logs, queries, keys, values):
        length = lengths[pl.program_id(0)]
        head_inputs(proj, gains, cos_ref, sin_ref, queries, keys, values, heads)
        lane = lax.broadcasted_iota(jnp.int32, (BLOCK, HD), 1)
        for step in range(rows // BLOCK):
            at = pl.ds(step * BLOCK, BLOCK)
            seen = pl.ds(0, (step + 1) * BLOCK)
            scores = masked_scores(stack_heads(queries, at, heads), keys[seen], step, length)
            top = jnp.max(scores, axis=-1, keepdims=True)
            exponent = jnp.exp(scores - top)
            total = jnp.sum(exponent, axis=-1, keepdims=True)
            probs = (exponent / total).astype(jnp.bfloat16)
            mixed = jnp.dot(probs, values[seen], preferred_element_type=jnp.float32)
            log_total = top + jnp.log(total)
            kept = jnp.zeros((BLOCK, HD), jnp.float32)
            for head in range(heads):
                mine = slice(head * BLOCK, (head + 1) * BLOCK)
                out[0, at, columns(head)] = mixed[mine].astype(jnp.bfloat16)
                kept = jnp.where(lane == head, log_total[mine], kept)
            logs[0, at] = kept

    return pl.pallas_call(
        kernel,
        name="attend",
        grid=(count,),
        out_shape=(
            jax.ShapeDtypeStruct((count, rows, heads * HD), jnp.bfloat16),
            jax.ShapeDtypeStruct((count, rows, HD), jnp.float32),
        ),
        in_specs=[
            pl.BlockSpec(memory_space=pltpu.SMEM),
            pl.BlockSpec((1, rows, width), lambda s: (s, 0, 0)),
            pl.BlockSpec((rows, HD), lambda s: (0, 0)),
            pl.BlockSpec((rows, HD), lambda s: (0, 0)),
            pl.BlockSpec((2, HD), lambda s: (0, 0)),
        ],
        out_specs=(
            pl.BlockSpec((1, rows, heads * HD), lambda s: (s, 0, 0)),
            pl.BlockSpec((1, rows, HD), lambda s: (s, 0, 0)),
        ),
        scratch_shapes=[
            pltpu.VMEM((heads, rows, HD), jnp.bfloat16),
            pltpu.VMEM((rows, HD), jnp.bfloat16),
            pltpu.VMEM((rows, HD), jnp.bfloat16),
        ],
        compiler_params=pltpu.CompilerParams(vmem_limit_bytes=VMEM_LIMIT),
        cost_estimate=pl.CostEstimate(flops=0, bytes_accessed=80 * 2**20, transcendentals=0),
    )(group_length, projected, cos_full, sin_full, gains)


def attend_back(projected, grad_attended, logs, group_length, cos_full, sin_full, gains, heads):
    count, rows, width = projected.shape

    def kernel(
        lengths, proj, grad, logs, cos_ref, sin_ref, gains, out, gain_grad, queries, keys, values, grad_q, grad_k, grad_v
    ):
        sequence = pl.program_id(0)
        length = lengths[sequence]
        head_inputs(proj, gains, cos_ref, sin_ref, queries, keys, values, heads)
        grad_k[...] = jnp.zeros_like(grad_k)
        grad_v[...] = jnp.zeros_like(grad_v)

        @pl.when(sequence == 0)
        def _():
            gain_grad[...] = jnp.zeros_like(gain_grad)

        for step in range(rows // BLOCK):
            at = pl.ds(step * BLOCK, BLOCK)
            seen = pl.ds(0, (step + 1) * BLOCK)
            stacked = stack_heads(queries, at, heads)
            above = jnp.concatenate([grad[0, at, columns(head)] for head in range(heads)], axis=0)
            log_total = jnp.concatenate(
                [logs[0, at, head : head + 1] for head in range(heads)], axis=0
            )
            probs = jnp.exp(masked_scores(stacked, keys[seen], step, length) - log_total)
            grad_probs = lax.dot_general(
                above, values[seen], (((1,), (1,)), ((), ())), preferred_element_type=jnp.float32
            )
            inner = jnp.sum(probs * grad_probs, axis=-1, keepdims=True)
            grad_scores = (probs * (grad_probs - inner)).astype(jnp.bfloat16)
            by_query = jnp.dot(grad_scores, keys[seen], preferred_element_type=jnp.float32)
            for head in range(heads):
                grad_q[head, at] = by_query[head * BLOCK : (head + 1) * BLOCK] * (HD ** (-0.5))
            grad_k[seen] += lax.dot_general(
                grad_scores, stacked, (((0,), (0,)), ((), ())), preferred_element_type=jnp.float32
            )
            grad_v[seen] += lax.dot_general(
                probs.astype(jnp.bfloat16),
                above,
                (((0,), (0,)), ((), ())),
                preferred_element_type=jnp.float32,
            )

        def finish(column, gain, value):
            back, by_gain = head_back(
                proj[0, :, columns(column)], gains[gain : gain + 1, :], value, cos_ref[...], sin_ref[...]
            )
            out[0, :, columns(column)] = back.astype(jnp.bfloat16)
            gain_grad[gain] += by_gain.reshape(rows // 8, 8, HD).sum(axis=0)

        for head in range(heads):
            finish(head, 0, grad_q[head])
        finish(heads, 1, grad_k[...] * (HD ** (-0.5)))
        out[0, :, columns(heads + 1)] = grad_v[...].astype(jnp.bfloat16)

    return pl.pallas_call(
        kernel,
        name="attend_back",
        grid=(count,),
        out_shape=(
            jax.ShapeDtypeStruct((count, rows, width), jnp.bfloat16),
            jax.ShapeDtypeStruct((2, 8, HD), jnp.float32),
        ),
        in_specs=[
            pl.BlockSpec(memory_space=pltpu.SMEM),
            pl.BlockSpec((1, rows, width), lambda s: (s, 0, 0)),
            pl.BlockSpec((1, rows, heads * HD), lambda s: (s, 0, 0)),
            pl.BlockSpec((1, rows, HD), lambda s: (s, 0, 0)),
            pl.BlockSpec((rows, HD), lambda s: (0, 0)),
            pl.BlockSpec((rows, HD), lambda s: (0, 0)),
            pl.BlockSpec((2, HD), lambda s: (0, 0)),
        ],
        out_specs=(
            pl.BlockSpec((1, rows, width), lambda s: (s, 0, 0)),
            pl.BlockSpec((2, 8, HD), lambda s: (0, 0, 0)),
        ),
        scratch_shapes=[
            pltpu.VMEM((heads, rows, HD), jnp.bfloat16),
            pltpu.VMEM((rows, HD), jnp.bfloat16),
            pltpu.VMEM((rows, HD), jnp.bfloat16),
            pltpu.VMEM((heads, rows, HD), jnp.float32),
            pltpu.VMEM((rows, HD), jnp.float32),
            pltpu.VMEM((rows, HD), jnp.float32),
        ],
        compiler_params=pltpu.CompilerParams(vmem_limit_bytes=VMEM_LIMIT),
        cost_estimate=pl.CostEstimate(flops=0, bytes_accessed=120 * 2**20, transcendentals=0),
    )(group_length, projected, grad_attended, logs, cos_full, sin_full, gains)


def team_swap(values, offset):
    pairs = [(member, member ^ offset) for member in range(TEAM)]
    return lax.ppermute(values, ("near", "core"), pairs)


def team_exchange(pieces):
    own = lax.axis_index("near") * CORE + lax.axis_index("core")
    buffer = jnp.zeros_like(pieces)
    buffer = put(buffer, pick(pieces, own), own)
    for offset in range(1, TEAM):
        there = own ^ offset
        buffer = put(buffer, team_swap(pick(pieces, there), offset), there)
    return buffer


def split_columns(values, widths):
    members = []
    for member in range(TEAM):
        start, parts = 0, []
        for width in widths:
            share = width // TEAM
            first = start + member * share
            parts.append(values[:, first : first + share])
            start += width
        members.append(jnp.concatenate(parts, axis=1))
    return jnp.stack(members)


def join_columns(pieces, widths):
    parts, start = [], 0
    for width in widths:
        share = width // TEAM
        parts += [pieces[member, :, start : start + share] for member in range(TEAM)]
        start += share
    return jnp.concatenate(parts, axis=1)


def gather_weight(shard, widths):
    mixed = team_exchange(split_columns(shard, widths))
    mixed = mixed.reshape(-1, mixed.shape[-1])
    return lax.all_gather(mixed, "outer", axis=0, tiled=True)


def sum_weight(gradient):
    return lax.psum_scatter(
        gradient.astype(jnp.bfloat16), "outer", scatter_dimension=0, tiled=True
    )


def return_weight(summed, widths):
    pieces = summed.reshape(TEAM, -1, summed.shape[-1])
    return join_columns(team_exchange(pieces), widths).astype(jnp.float32)


def adam_update(weight, gradient, moment_one, moment_two, factor, decay_rate, rate_value):
    clipped = gradient * factor
    moment_one = beta_first * moment_one + (1.0 - beta_first) * clipped
    moment_two = beta_second * moment_two + (1.0 - beta_second) * clipped * clipped
    first_fixed = moment_one / (1.0 - beta_first**STEP)
    second_fixed = moment_two / (1.0 - beta_second**STEP)
    weight = weight - rate_value * (
        first_fixed / (jnp.sqrt(second_fixed) + adam_epsilon) + decay_rate * weight
    )
    return (weight, moment_one, moment_two)


def dot(left, right, contract):
    return lax.dot_general(
        left, right, ((contract[0], contract[1]), ((), ())), preferred_element_type=jnp.float32
    )


def times(left, right):
    return dot(left, right, ((1,), (0,)))


def times_across(left, right):
    return dot(left, right, ((1,), (1,)))


def over_rows(left, right):
    return dot(left, right, ((0,), (0,)))


def local(
    inputs,
    cotangent,
    lengths,
    owners,
    qkv_weight,
    out_weight,
    gate_up_weight,
    down_weight,
    norm_gains,
    qkv_moment,
    out_moment,
    gate_up_moment,
    down_moment,
    gains_moment,
    qkv_square,
    out_square,
    gate_up_square,
    down_square,
    gains_square,
):
    tp_count = lax.axis_size("tp")
    half_rows = inputs.shape[0]
    row_count = half_rows * tp_count
    heads = H // tp_count // TEAM
    hidden_units = FF // tp_count // TEAM
    qkv_widths = (H * HD // tp_count, KV * HD // tp_count, KV * HD // tp_count)
    out_widths = (H * HD // tp_count,)
    gate_up_widths = (FF // tp_count, FF // tp_count)
    down_widths = (FF // tp_count,)

    first_group = lax.axis_index("outer") * TEAM
    group_ids = first_group + jnp.arange(TEAM)
    group_length = jnp.sum(
        jnp.where(owners[None, :] == group_ids[:, None], lengths[None, :], 0), axis=1
    )
    own_group = lax.axis_index("near") * CORE + lax.axis_index("core")
    own_rows = lax.axis_index("tp") * half_rows + jnp.arange(half_rows)
    valid_rows = (own_rows < pick(group_length, own_group))[:, None]
    half_width = HD // 2
    frequency = rope_base ** (-(jnp.arange(half_width, dtype=jnp.float32) * 2.0 / HD))
    angles = jnp.arange(row_count, dtype=jnp.float32)[:, None] * frequency[None, :]
    cosine, sine = jnp.cos(angles), jnp.sin(angles)
    cos_full = jnp.concatenate([cosine, cosine], axis=1)
    sin_full = jnp.concatenate([-sine, sine], axis=1)
    attn_gain = norm_gains[:D]
    mlp_gain = norm_gains[D : 2 * D]
    head_gains = norm_gains[2 * D :].reshape(2, HD)

    qkv_full = gather_weight(qkv_weight.astype(jnp.bfloat16), qkv_widths)
    out_full = gather_weight(out_weight.astype(jnp.bfloat16).T, out_widths)
    gate_up_full = gather_weight(gate_up_weight.astype(jnp.bfloat16), gate_up_widths)
    down_full = gather_weight(down_weight.astype(jnp.bfloat16).T, down_widths)

    residual_in = inputs.astype(jnp.float32)
    normed_attn = residual_in * rms_scale(residual_in) * attn_gain
    normed_attn = gather_rows(normed_attn.astype(jnp.bfloat16), 0, "gather_inputs")
    grad_low = jnp.where(valid_rows, cotangent, jnp.zeros_like(cotangent))
    grad_all = gather_rows(grad_low, 1, "gather_cotangent")
    projected = times(normed_attn, qkv_full)
    projected = projected.reshape(TEAM, row_count, projected.shape[1])
    attended, logs = attend(projected, group_length, cos_full, sin_full, head_gains, heads)
    attended = attended.reshape(-1, heads * HD)
    attn_branch = times_across(attended, out_full).astype(jnp.bfloat16)
    hidden, normed_mlp = branch_and_norm(attn_branch, inputs, mlp_gain, 2, "branch_and_norm")
    gate_up = times(normed_mlp, gate_up_full)
    gate_part = gate_up[:, :hidden_units]
    up_part = gate_up[:, hidden_units:]
    activated = swish_product(gate_part, up_part).astype(jnp.bfloat16)
    mlp_branch = sum_rows(activated, lambda rows: times_across(rows, down_full))
    output = (hidden + mlp_branch).astype(jnp.bfloat16)

    grad_activated = times(grad_all, down_full)
    swish_pull = jax.vjp(swish_product, gate_part, up_part)[1]
    grad_gate, grad_up = swish_pull(grad_activated)
    grad_gate_up = jnp.concatenate([grad_gate, grad_up], axis=1).astype(jnp.bfloat16)
    grad_normed_mlp = times_across(grad_gate_up, gate_up_full).astype(jnp.bfloat16)
    down_sum = sum_weight(over_rows(grad_all, activated))
    gate_up_sum = sum_weight(over_rows(normed_mlp, grad_gate_up))
    grad_hidden, grad_mlp_gain, grad_attn = norm_back_rows(
        grad_normed_mlp, hidden, grad_low, mlp_gain, 3, "norm_back_mlp", True
    )
    grad_attended = times(grad_attn, out_full).astype(jnp.bfloat16)
    grad_attended = grad_attended.reshape(TEAM, row_count, heads * HD)
    out_sum = sum_weight(over_rows(grad_attn, attended))
    grad_projected, grad_head_gains = attend_back(
        projected, grad_attended, logs, group_length, cos_full, sin_full, head_gains, heads
    )
    grad_projected = grad_projected.reshape(-1, projected.shape[2])
    qkv_sum = sum_weight(over_rows(normed_attn, grad_projected))
    grad_normed_attn = times_across(grad_projected, qkv_full).astype(jnp.bfloat16)
    input_grad, grad_attn_gain = norm_back_rows(
        grad_normed_attn, inputs, grad_hidden, attn_gain, 4, "norm_back_attn", False
    )
    gain_part = jnp.concatenate(
        [grad_attn_gain, grad_mlp_gain, grad_head_gains.sum(axis=1).reshape(-1)]
    )
    square_part = sum(
        jnp.sum(jnp.square(member.astype(jnp.float32)))
        for member in (qkv_sum, out_sum, gate_up_sum, down_sum)
    )
    gain_count = gain_part.shape[0]
    packed = jnp.concatenate([gain_part, square_part[None], jnp.zeros(PAD - 1, jnp.float32)])
    packed = packed.reshape(-1, HD)
    packed = jnp.pad(packed, ((0, -packed.shape[0] % 8), (0, 0)))
    packed = total_everywhere(packed, lax.axis_size("outer"), 5, "total_everywhere").reshape(-1)
    gain_grad, square_total = packed[:gain_count], packed[gain_count]
    down_grad = return_weight(down_sum, down_widths).T
    gate_up_grad = return_weight(gate_up_sum, gate_up_widths)
    out_grad = return_weight(out_sum, out_widths).T
    qkv_grad = return_weight(qkv_sum, qkv_widths)
    grad_norm = jnp.sqrt(square_total + jnp.sum(gain_grad * gain_grad))
    factor = jnp.minimum(1.0, clip_norm / (grad_norm + 1e-06))
    new_qkv, new_qkv_one, new_qkv_two = adam_update(
        qkv_weight, qkv_grad, qkv_moment, qkv_square, factor, weight_decay, learn_rate
    )
    new_out, new_out_one, new_out_two = adam_update(
        out_weight, out_grad, out_moment, out_square, factor, weight_decay, learn_rate
    )
    new_gate_up, new_gate_up_one, new_gate_up_two = adam_update(
        gate_up_weight,
        gate_up_grad,
        gate_up_moment,
        gate_up_square,
        factor,
        weight_decay,
        learn_rate,
    )
    new_down, new_down_one, new_down_two = adam_update(
        down_weight, down_grad, down_moment, down_square, factor, weight_decay, learn_rate
    )
    new_gains, new_gains_one, new_gains_two = adam_update(
        norm_gains, gain_grad, gains_moment, gains_square, factor, 0.0, gain_rate
    )
    return (
        output,
        input_grad,
        grad_norm,
        new_qkv,
        new_qkv_one,
        new_qkv_two,
        new_qkv.astype(jnp.bfloat16),
        new_out,
        new_out_one,
        new_out_two,
        new_out.astype(jnp.bfloat16),
        new_gate_up,
        new_gate_up_one,
        new_gate_up_two,
        new_gate_up.astype(jnp.bfloat16),
        new_down,
        new_down_one,
        new_down_two,
        new_down.astype(jnp.bfloat16),
        new_gains,
        new_gains_one,
        new_gains_two,
    )


def solution(mesh):
    fsdp_count, tp_count = mesh.shape["fsdp"], mesh.shape["tp"]
    cut = mesh.devices.reshape(fsdp_count // TEAM, NEAR, CORE, tp_count)
    cut_mesh = Mesh(cut, ("outer",) + LAYER)
    fsdp = ("outer", "near", "core")
    rows = P(fsdp + ("tp",), None)
    wide = P(fsdp, "tp")
    tall = P("tp", fsdp)
    weights = (wide, tall, wide, tall, P())
    return jax.shard_map(
        local,
        mesh=cut_mesh,
        in_specs=(rows, rows, P(), P()) + weights * 3,
        out_specs=(rows, rows, P()) + (wide,) * 4 + (tall,) * 4 + (wide,) * 4 + (tall,) * 4 + (P(),) * 3,
        check_vma=False,
    )
```

time: 936 us -> 820 us (0.88)
  Pallas kernels: 0 us -> 404 us
  waiting for transfers between devices: 315 us -> 104 us
  local copies, waits for them, and re-layouts: 186 us -> 51.8 us
  other arithmetic: 101 us -> 38.9 us
  blocking collectives: 40.2 us -> 0 us
  starting transfers between devices: 60.1 us -> 22.4 us
  matrix products: 203 us -> 172 us
    pallas_call x0 -> x8, Pallas kernels: none -> 404 us  [the longest x2 153 us: norm_back_rows(): pl.pallas_call(kernel, name=name, out_shape=tuple(out_shape), in_specs=[a...]
    ppermute x52 -> x5, waiting for transfers between devices: 177 us -> 16 us  [swap(): return lax.ppermute(values, axis, [(0, 1), (1, 0)])]
    ppermute x24, waiting for transfers between devices: 122 us -> 67 us  [team_swap(): return lax.ppermute(values, ('near', 'core'), pairs)]
    dynamic_update_slice x56 -> x26, local copies, waits for them, and re-layouts: 54.7 us -> 14.4 us  [put(): return lax.dynamic_update_slice(buffer, values[(None,) * len(index)], start)]
    psum x1 -> x0, blocking collectives: 40.2 us -> none  [local(): lax.psum((gain_part, square_part), ('outer',) + LAYER)]
    ppermute x52 -> x5, starting transfers between devices: 43.3 us -> 4.56 us  [swap(): return lax.ppermute(values, axis, [(0, 1), (1, 0)])]
    dot_general x6 -> x0, matrix products: 28.5 us -> none  [the longest x1 12 us: local(): jnp.einsum('sqrd,skd->srqk', grad_attended, value_heads, preferred_elemen...]
    another operation x15 -> x8, local copies, waits for them, and re-layouts: 28.2 us -> 2.24 us
  transfers between devices with their start and end apart: 84 -> 37, of which waited for: 34 -> 17; matrix products, arithmetic and copies ran while one was open for 43% -> 23% of each run, Pallas kernels for 0% -> 36%
where the time goes in v3:
time: 820 us; the launch traced here: 814 us
  Pallas kernels  404 us (49%)
  matrix products  172 us (21%)
  waiting for transfers between devices  104 us (13%)
  local copies, waits for them, and re-layouts  51.8 us (6%)
  other arithmetic  38.9 us (5%)
  starting transfers between devices  22.4 us (3%)
  between operations  20.7 us (3%)
    dot_general x13, matrix products, dot(): lax.dot_general(left, right, ((contract[0], contract[1]), ((), ())), pref...  172 us
    pallas_call x2, Pallas kernels, norm_back_rows(): pl.pallas_call(kernel, name=name, out_shape=tuple(out_shape), in_specs=[a...  153 us
    pallas_call x2, Pallas kernels, gather_rows(): pl.pallas_call(kernel, name=name, out_shape=jax.ShapeDtypeStruct((NEAR, C...  104 us
    pallas_call x1, Pallas kernels, branch_and_norm(): pl.pallas_call(kernel, name=name, out_shape=(jax.ShapeDtypeStruct((rows,...  98.7 us
    ppermute x24, waiting for transfers between devices, team_swap(): return lax.ppermute(values, ('near', 'core'), pairs)  67 us
    pallas_call x1, Pallas kernels, attend_back(): pl.pallas_call(kernel, name='attend_back', grid=(count,), out_shape=(jax....  22.1 us
    reduce_scatter x4, waiting for transfers between devices, sum_weight(): lax.psum_scatter(gradient.astype(jnp.bfloat16), 'outer', scatter_dimensio...  21.1 us
    unnamed x121, local copies, waits for them, and re-layouts  20.6 us
  transfers between devices with their start and end apart: 37, of which 17 were waited for; matrix products, arithmetic and copies ran while one was open for 23% of the time, Pallas kernels for 36%

profile of v3, /device:TPU:0, one launch (start us, length us, event | category | flops | bytes accessed | tf_op | source)
XLA Modules:
  0.0 814.0 jit_solution(7735791611604622310)
XLA Ops:
  7.2 1.3 convert_element_type.113
  10.8 2.5 collective-permute-start.1
  14.1 3.5 collective-permute-done.1
  18.3 1.8 collective-permute-done.2
  20.8 2.0 copy.68
  24.2 1.6 collective-permute-start.4
  28.6 1.4 collective-permute-done.5
  33.4 9.7 %collective-permute-done.7 = bf16[128,1536]{1,0:T(8,128)(2,1)S(1)} collective-permute-done((bf16[128,1536]{1,0:T(8,128)(2,1)}, bf16[128,1536]{1,0:T(8,128)(2,1)S(1)}, u32[]{:S(2)}, u32[]{:S(2)}) %collective-permute-start.7) | collective-permute-done | bytes 393248 | tf_op jit(solution)/shard_map/ppermute | solution.py:657
  43.1 6.7 collective-permute-done.8
  49.9 1.1 copy-done.17
  54.2 1.2 collective-permute-start.10
  56.4 54.6 %gather_inputs.1 = bf16[2,2,2,320,2048]{4,3,2,1,0:T(8,128)(2,1)} custom-call(bf16[320,2048]{1,0:T(8,128)(2,1)S(1)} %fusion.12.own), custom_call_target="tpu_custom_call" | custom-call | bytes 157286400 | tf_op jit(solution)/shard_map/gather_inputs/pallas_call | solution.py:288
  112.4 1.5 broadcast_select_fusion.own.upstream
  113.9 49.2 %gather_cotangent.1 = bf16[2,2,2,320,2048]{4,3,2,1,0:T(8,128)(2,1)} custom-call(bf16[320,2048]{1,0:T(8,128)(2,1)S(1)} %broadcast_select_fusion.own.upstream), custom_call_target="tpu_custom_call" | custom-call | bytes 157286400 | tf_op jit(solution)/shard_map/gather_cotangent/pallas_call | solution.py:288
  163.2 1.2 fusion.43
  164.7 1.6 bitcast_dynamic-update-slice_fusion.11
  166.3 1.6 bitcast_dynamic-update-slice_fusion.10
  167.9 1.6 bitcast_dynamic-update-slice_fusion.9
  169.6 2.3 copy.69
  172.2 10.6 %fusion.16.proj = f32[4,640,512]{2,1,0:T(8,128)} fusion(bf16[4,640,2048]{2,1,0:T(8,128)(2,1)} %bitcast.351, bf16[2048,512]{1,0:T(8,128)(2,1)} %all-gather.5.cloned.1.call-done), kind=kOutput, calls=%fused_computation.39 | convolution fusion | flops 5368709120 | bytes 17825792 | tf_op jit(solution)/shard_map/dot_general | solution.py:722
  182.8 15.3 %attend.1 = (bf16[4,640,256]{2,1,0:T(8,128)(2,1)S(1)}, f32[4,640,128]{2,1,0:T(8,128)S(1)}) custom-call(s32[4]{0:T(128)S(1)} %select_reduce_fusion.lengths, f32[4,640,512]{2,1,0:T(8,128)} %fusion.16.proj, f32[640,128]{1,0:T(8,128)S(1)} %get-tuple-element.193.cos_ref, f32[640,128]{1,0:T(8,128)S(1)} %get-tuple-element.194.sin_ref, ...), custom_call_target="tpu_custom_call" | custom-call | bytes 83886080 | tf_op jit(solution)/shard_map/attend/pallas_call | solution.py:537
  200.2 8.5 %convolution_convert_fusion.2 = bf16[2560,2048]{1,0:T(8,128)(2,1)} fusion(bf16[2560,256]{1,0:T(8,128)(2,1)} %bitcast.341, bf16[2048,256]{1,0:T(8,128)(2,1)} %all-gather.7.cloned.1.call-done), kind=kOutput, calls=%fused_computation.3 | convolution fusion | flops 2689597440 | bytes 12845056 | tf_op jit(solution)/shard_map/dot_general | solution.py:722
  208.7 98.7 %branch_and_norm.1 = (f32[320,2048]{1,0:T(8,128)S(1)}, bf16[2,2,2,320,2048]{4,3,2,1,0:T(8,128)(2,1)}) custom-call(bf16[2,2,2,320,2048]{4,3,2,1,0:T(8,128)(2,1)} %bitcast.350, bf16[320,2048]{1,0:T(8,128)(2,1)S(1)} %copy-done, f32[1,2048]{1,0:T(1,128)S(1)} %bitcast.346), custom_call_target="tpu_custom_call" | custom-call | bytes 314572800 | tf_op jit(solution)/shard_map/branch_and_norm/pallas_call | solution.py:329
  307.5 1.5 copy-done.1
  309.0 22.4 %fusion.70 = f32[2560,1536]{1,0:T(8,128)} fusion(bf16[2560,2048]{1,0:T(8,128)(2,1)} %bitcast.368, bf16[2048,1536]{1,0:T(8,128)(2,1)} %all-gather.9.cloned.1.call-done), kind=kOutput, calls=%fused_computation.238 | convolution fusion | flops 16106127360 | bytes 32505856 | tf_op jit(solution)/shard_map/dot_general | solution.py:722
  331.3 21.5 %fusion.2 = (bf16[2560,768]{1,0:T(8,128)(2,1)}, bf16[2560,768]{1,0:T(8,128)(2,1)}, bf16[2560,768]{1,0:T(8,128)(2,1)}) fusion(f32[2560,1536]{1,0:T(8,128)} %fusion.70, bf16[2560,2048]{1,0:T(8,128)(2,1)} %bitcast.353, bf16[2048,768]{1,0:T(8,128)(2,1)} %all-gather.11.cloned.1.call-done), kind=kOutput, calls=%fused_computation.7 | convolution fusion | flops 8084520960 | bytes 41156608 | tf_op jit(solution)/shard_map/dot_general | solution.py:722
  352.9 20.5 %convolution_convert_fusion.1 = bf16[2560,2048]{1,0:T(8,128)(2,1)} fusion(bf16[2048,1536]{1,0:T(8,128)(2,1)S(1)} %copy-done.45, bf16[2560,768]{1,0:T(8,128)(2,1)} %get-tuple-element.108, bf16[2560,768]{1,0:T(8,128)(2,1)} %get-tuple-element.107), kind=kOutput, calls=%fused_computation.2 | convolution fusion | flops 16127098880 | bytes 24641536 | tf_op jit(solution)/shard_map/dot_general | solution.py:722
  373.4 100.9 %norm_back_mlp.1 = (f32[320,2048]{1,0:T(8,128)S(1)}, f32[8,2048]{1,0:T(8,128)S(1)}, bf16[2,2,2,320,2048]{4,3,2,1,0:T(8,128)(2,1)}) custom-call(bf16[2,2,2,320,2048]{4,3,2,1,0:T(8,128)(2,1)} %bitcast.355, f32[320,2048]{1,0:T(8,128)} %copy-done.1, bf16[320,2048]{1,0:T(8,128)(2,1)S(1)} %broadcast_select_fusion.own.upstream, f32[1,2048]{1,0:T(1,128)S(1)} %bitcast.347), custom_call_target="tpu_custom_call" | custom-call | bytes 314572800 | tf_op jit(solution)/shard_map/norm_back_mlp/pallas_call | solution.py:391
  474.4 1.5 copy-done.3
  475.9 8.1 convolution_convert_fusion.8
  484.0 7.2 convolution_convert_fusion.5
  491.2 22.1 %attend_back.1 = (bf16[4,640,512]{2,1,0:T(8,128)(2,1)S(1)}, f32[2,8,128]{2,1,0:T(8,128)S(1)}) custom-call(s32[4]{0:T(128)S(1)} %select_reduce_fusion.lengths, f32[4,640,512]{2,1,0:T(8,128)} %fusion.16.proj, bf16[4,640,256]{2,1,0:T(8,128)(2,1)S(1)} %bitcast.343, f32[4,640,128]{2,1,0:T(8,128)S(1)} %copy-done.8, f32[640,128]{1,0:T(8,128)S(1)} %get-tuple-element.193.cos_ref, ...), custom_call_target="tpu_custom_call" | custom-call | bytes 125829120 | tf_op jit(solution)/shard_map/attend_back/pallas_call | solution.py:621
  513.4 1.5 copy-done.13
  514.9 11.2 %convolution_convert_fusion.7 = bf16[2048,512]{1,0:T(8,128)(2,1)} fusion(bf16[2560,2048]{1,0:T(8,128)(2,1)} %bitcast.352, bf16[2560,512]{1,0:T(8,128)(2,1)S(1)} %bitcast.348), kind=kOutput, calls=%fused_computation.28 | convolution fusion | flops 5369757696 | bytes 15204352 | tf_op jit(solution)/shard_map/dot_general | solution.py:722
  526.2 13.6 %convolution_convert_fusion.6 = bf16[2048,768]{1,0:T(8,128)(2,1)} fusion(bf16[2560,2048]{1,0:T(8,128)(2,1)} %bitcast.354, bf16[2560,768]{1,0:T(8,128)(2,1)} %get-tuple-element.109), kind=kOutput, calls=%fused_computation.17 | convolution fusion | flops 8054636544 | bytes 17563648 | tf_op jit(solution)/shard_map/dot_general | solution.py:722
  539.8 22.7 %convolution_convert_fusion.3 = bf16[2048,1536]{1,0:T(8,128)(2,1)} fusion(bf16[2560,2048]{1,0:T(8,128)(2,1)} %bitcast.369, bf16[2560,768]{1,0:T(8,128)(2,1)} %get-tuple-element.108, bf16[2560,768]{1,0:T(8,128)(2,1)} %get-tuple-element.107), kind=kOutput, calls=%fused_computation.13 | convolution fusion | flops 16125001728 | bytes 24641536 | tf_op jit(solution)/shard_map/dot_general | solution.py:722
  565.5 9.3 %convolution_convert_fusion.4 = bf16[2,2,320,2048]{3,2,1,0:T(8,128)(2,1)} fusion(bf16[2048,768]{1,0:T(8,128)(2,1)} %all-gather.11.cloned.1.call-done, bf16[2,2,2,320,768]{4,3,2,1,0:T(8,128)(2,1)} %bitcast.372, s32[]{:T(128)S(6)} %select_n.125), kind=kOutput, calls=%fused_computation.15 | convolution fusion | flops 4029153280 | bytes 10354692 | tf_op jit(solution)/shard_map/dot_general | solution.py:722
  575.2 8.2 %convolution_convert_fusion = bf16[2560,2048]{1,0:T(8,128)(2,1)} fusion(bf16[2560,512]{1,0:T(8,128)(2,1)S(1)} %bitcast.349, bf16[2048,512]{1,0:T(8,128)(2,1)S(1)} %copy-done.46), kind=kOutput, calls=%fused_computation.1 | convolution fusion | flops 5373952000 | bytes 15204352 | tf_op jit(solution)/shard_map/dot_general | solution.py:722
  583.4 52.0 %norm_back_attn.1 = (bf16[320,2048]{1,0:T(8,128)(2,1)S(1)}, f32[8,2048]{1,0:T(8,128)S(1)}) custom-call(bf16[2,2,2,320,2048]{4,3,2,1,0:T(8,128)(2,1)} %bitcast.356, bf16[320,2048]{1,0:T(8,128)(2,1)S(1)} %copy-done, f32[320,2048]{1,0:T(8,128)S(1)} %copy-done.4, f32[1,2048]{1,0:T(1,128)S(1)} %bitcast.345), custom_call_target="tpu_custom_call" | custom-call | bytes 157286400 | tf_op jit(solution)/shard_map/norm_back_attn/pallas_call | solution.py:391
  639.6 1.7 multiply_reduce_fusion.3
  641.3 1.4 collective-permute-done.21
  643.8 1.1 dynamic-slice_bitcast_fusion.11
  646.9 1.9 multiply_reduce_fusion.2
  650.2 1.5 collective-permute-done.18
  651.7 1.3 collective-permute-done.19
  653.3 8.3 %convert_add_fusion = f32[2,2,320,2048]{3,2,1,0:T(8,128)S(1)} fusion(bf16[2,2,320,2048]{3,2,1,0:T(8,128)(2,1)} %collective-permute-done.12, bf16[2048,768]{1,0:T(8,128)(2,1)} %all-gather.11.cloned.1.call-done, bf16[2,2,2,320,768]{4,3,2,1,0:T(8,128)(2,1)} %bitcast.373, s32[]{:T(128)S(6)} %select_n.124), kind=kOutput, calls=%fused_computation.4 | convolution fusion | flops 4031774720 | bytes 20840452 | tf_op jit(solution)/shard_map/dot_general | solution.py:722
  661.9 1.3 collective-permute-start.13
  664.3 15.3 %collective-permute-done.13 = bf16[160,2048]{1,0:T(8,128)(2,1)S(1)} collective-permute-done((bf16[160,2048]{1,0:T(8,128)(2,1)S(1)}, bf16[160,2048]{1,0:T(8,128)(2,1)S(1)}, u32[]{:S(2)}, u32[]{:S(2)}) %collective-permute-start.13) | collective-permute-done | bytes 655392 | tf_op jit(solution)/shard_map/ppermute | solution.py:44
  680.7 1.1 pad_maximum_fusion.5
  682.8 1.1 pad_maximum_fusion.4
  685.0 2.0 constant_dynamic-slice_fusion.3
  690.5 1.7 copy.79
  696.1 21.9 %collective-permute-done.27 = bf16[128,768]{0,1:T(8,128)(2,1)} collective-permute-done((bf16[128,768]{0,1:T(8,128)(2,1)}, bf16[128,768]{0,1:T(8,128)(2,1)}, u32[]{:S(2)}, u32[]{:S(2)}) %collective-permute-start.27) | collective-permute-done | bytes 196640 | tf_op jit(solution)/shard_map/ppermute | solution.py:657
  720.5 4.4 fusion.15
  724.9 21.1 %reduce-scatter.9.cloned.1.call-done = bf16[512,1536]{1,0:T(8,128)(2,1)} async-done(((bf16[2048,1536]{1,0:T(8,128)(2,1)}), bf16[512,1536]{1,0:T(8,128)(2,1)}) %reduce-scatter.9.cloned.1.call-update) | async-done | bytes 1572880 | tf_op jit(solution)/shard_map/reduce_scatter | solution.py:699
  746.1 2.9 multiply_reduce_fusion
  750.4 10.9 %total_everywhere.1 = f32[40,128]{1,0:T(8,128)S(1)} custom-call(f32[40,128]{1,0:T(8,128)S(1)} %pad.4.values), custom_call_target="tpu_custom_call" | custom-call | tf_op jit(solution)/shard_map/total_everywhere/pallas_call | solution.py:459
  765.1 4.6 fusion.64
  769.8 3.3 fusion.56
  777.6 1.4 collective-permute-start.24
  780.3 1.2 bitcast_dynamic-update-slice_fusion.2
  781.5 8.4 %collective-permute-done.24 = bf16[128,1536]{1,0:T(8,128)(2,1)S(1)} collective-permute-done((bf16[128,1536]{1,0:T(8,128)(2,1)}, bf16[128,1536]{1,0:T(8,128)(2,1)S(1)}, u32[]{:S(2)}, u32[]{:S(2)}) %collective-permute-start.24) | collective-permute-done | bytes 393248 | tf_op jit(solution)/shard_map/ppermute | solution.py:657
  789.9 7.8 collective-permute-done.25
  797.9 6.9 fusion.59
  (263 shorter events, 54.7 us)
Async XLA Ops:
  7.2 165.0 %all-gather.5.cloned.1.call-start = ((), (), s32[]{:S(2)}) async-start(), calls=%async_computation.4 | async-start | bytes 2621440 | tf_op jit(solution)/shard_map/all_gather | solution.py:695
  10.3 15.7 %copy-start.15 = (f32[128,6144]{1,0:T(8,128)S(1)}, f32[128,6144]{1,0:T(8,128)}, u32[]{:S(2)}) copy-start(f32[128,6144]{1,0:T(8,128)} %param.25) | copy-start | bytes 9437188
  10.3 3.1 collective-permute-start
  10.8 6.8 collective-permute-start.1
  13.3 6.8 collective-permute-start.2
  20.7 179.5 %all-gather.7.cloned.1.call-start = ((), (), s32[]{:S(2)}) async-start(), calls=%async_computation.5 | async-start | bytes 1310720 | tf_op jit(solution)/shard_map/all_gather | solution.py:695
  24.0 4.2 collective-permute-start.3
  24.2 4.4 collective-permute-start.4
  25.9 4.2 collective-permute-start.5
  27.8 23.3 %copy-start.19 = (f32[3072,128]{1,0:T(8,128)S(1)}, f32[3072,128]{1,0:T(8,128)}, u32[]{:S(2)}) copy-start(f32[3072,128]{1,0:T(8,128)} %param.26) | copy-start | bytes 4718596
  27.8 4.6 collective-permute-start.6
  30.8 278.2 %all-gather.9.cloned.1.call-start = ((), (), s32[]{:S(2)}) async-start(), calls=%async_computation.6 | async-start | bytes 7864320 | tf_op jit(solution)/shard_map/all_gather | solution.py:695
  30.8 12.2 %collective-permute-start.7 = (bf16[128,1536]{1,0:T(8,128)(2,1)}, bf16[128,1536]{1,0:T(8,128)(2,1)S(1)}, u32[]{:S(2)}, u32[]{:S(2)}) collective-permute-start(bf16[128,1536]{1,0:T(8,128)(2,1)} %get-tuple-element.119), channel_id=1, source_target_pairs={{0,4},{2,6},{4,0},{6,2},{1,5},{3,7},{5,1},{7,3},{8,12},{10,14},{12... | collective-permute-start | bytes 1179656 | tf_op jit(solution)/shard_map/ppermute | solution.py:657
  31.8 18.1 %collective-permute-start.8 = (bf16[128,1536]{1,0:T(8,128)(2,1)}, bf16[128,1536]{1,0:T(8,128)(2,1)S(1)}, u32[]{:S(2)}, u32[]{:S(2)}) collective-permute-start(bf16[128,1536]{1,0:T(8,128)(2,1)} %get-tuple-element.118), channel_id=1, source_target_pairs={{0,6},{2,4},{4,2},{6,0},{1,7},{3,5},{5,3},{7,1},{8,14},{10,12},{12... | collective-permute-start | bytes 1179656 | tf_op jit(solution)/shard_map/ppermute | solution.py:657
  51.0 280.3 %all-gather.11.cloned.1.call-start = ((), (), s32[]{:S(2)}) async-start(), calls=%async_computation.7 | async-start | bytes 3932160 | tf_op jit(solution)/shard_map/all_gather | solution.py:695
  51.3 4.7 copy-start.39
  53.2 111.5 %collective-permute-start.9 = (bf16[128,768]{0,1:T(8,128)(2,1)}, bf16[128,768]{0,1:T(8,128)(2,1)}, u32[]{:S(2)}, u32[]{:S(2)}) collective-permute-start(bf16[128,768]{0,1:T(8,128)(2,1)} %get-tuple-element.142), channel_id=1, source_target_pairs={{0,2},{2,0},{4,6},{6,4},{1,3},{3,1},{5,7},{7,5},{8,10},{10,8},{12,... | collective-permute-start | bytes 589832 | tf_op jit(solution)/shard_map/ppermute | solution.py:657
  54.2 112.1 %collective-permute-start.10 = (bf16[128,768]{0,1:T(8,128)(2,1)}, bf16[128,768]{0,1:T(8,128)(2,1)}, u32[]{:S(2)}, u32[]{:S(2)}) collective-permute-start(bf16[128,768]{0,1:T(8,128)(2,1)} %get-tuple-element.141), channel_id=1, source_target_pairs={{0,4},{2,6},{4,0},{6,2},{1,5},{3,7},{5,1},{7,3},{8,12},{10,14},{12... | collective-permute-start | bytes 589832 | tf_op jit(solution)/shard_map/ppermute | solution.py:657
  55.5 112.5 %collective-permute-start.11 = (bf16[128,768]{0,1:T(8,128)(2,1)S(1)}, bf16[128,768]{0,1:T(8,128)(2,1)}, u32[]{:S(2)}, u32[]{:S(2)}) collective-permute-start(bf16[128,768]{0,1:T(8,128)(2,1)S(1)} %get-tuple-element.140), channel_id=1, source_target_pairs={{0,6},{2,4},{4,2},{6,0},{1,7},{3,5},{5,3},{7,1},{8,14},{10,12},{12... | collective-permute-start | bytes 589832 | tf_op jit(solution)/shard_map/ppermute | solution.py:657
  56.0 55.0 %copy-start.11 = (f32[2048]{0:T(1024)}, f32[2048]{0:T(1024)S(1)}, u32[]{:S(2)}) copy-start(f32[2048]{0:T(1024)S(1)} %get-tuple-element.185) | copy-start | bytes 24580
  56.4 54.6 %copy-start.43 = (s32[16]{0:T(128)S(1)}, s32[16]{0:T(128)}, u32[]{:S(2)}) copy-start(s32[16]{0:T(128)} %param.21) | copy-start | bytes 196
  56.4 54.6 %copy-start.44 = (s32[16]{0:T(128)S(1)}, s32[16]{0:T(128)}, u32[]{:S(2)}) copy-start(s32[16]{0:T(128)} %param.22) | copy-start | bytes 196
  171.9 464.7 %reduce-scatter.7.cloned.1.call-start = ((), (), s32[]{:S(2)}) async-start(), calls=%async_computation.9 | async-start | bytes 1310720 | tf_op jit(solution)/shard_map/reduce_scatter | solution.py:699
  331.3 21.5 %copy-start.45 = (bf16[2048,1536]{1,0:T(8,128)(2,1)S(1)}, bf16[2048,1536]{1,0:T(8,128)(2,1)}, u32[]{:S(2)}) copy-start(bf16[2048,1536]{1,0:T(8,128)(2,1)} %all-gather.9.cloned.1.call-done) | copy-start | bytes 18874372
  373.4 102.4 %copy-start.6 = (bf16[4,640,256]{2,1,0:T(8,128)(2,1)S(1)}, bf16[4,640,256]{2,1,0:T(8,128)(2,1)}, u32[]{:S(2)}) copy-start(bf16[4,640,256]{2,1,0:T(8,128)(2,1)} %copy-done.5) | copy-start | bytes 3932164
  483.9 7.3 copy-start.8
  484.0 159.8 %reduce-scatter.5.cloned.1.call-start = ((), (), s32[]{:S(2)}) async-start(), calls=%async_computation.8 | async-start | bytes 2621440 | tf_op jit(solution)/shard_map/reduce_scatter | solution.py:699
  526.1 158.9 %reduce-scatter.11.cloned.1.call-start = ((), (), s32[]{:S(2)}) async-start(), calls=%async_computation.11 | async-start | bytes 3932160 | tf_op jit(solution)/shard_map/reduce_scatter | solution.py:699
  539.8 206.3 %reduce-scatter.9.cloned.1.call-start = ((), (), s32[]{:S(2)}) async-start(), calls=%async_computation.10 | async-start | bytes 7864320 | tf_op jit(solution)/shard_map/reduce_scatter | solution.py:699
  565.5 9.7 %copy-start.14 = (bf16[4,640,512]{2,1,0:T(8,128)(2,1)S(1)}, bf16[4,640,512]{2,1,0:T(8,128)(2,1)}, u32[]{:S(2)}) copy-start(bf16[4,640,512]{2,1,0:T(8,128)(2,1)} %copy-done.13) | copy-start | bytes 7864324
  565.5 9.7 %copy-start.46 = (bf16[2048,512]{1,0:T(8,128)(2,1)S(1)}, bf16[2048,512]{1,0:T(8,128)(2,1)}, u32[]{:S(2)}) copy-start(bf16[2048,512]{1,0:T(8,128)(2,1)} %all-gather.5.cloned.1.call-done) | copy-start | bytes 6291460
  574.8 8.6 %copy-start.4 = (f32[320,2048]{1,0:T(8,128)S(1)}, f32[320,2048]{1,0:T(8,128)}, u32[]{:S(2)}) copy-start(f32[320,2048]{1,0:T(8,128)} %copy-done.3) | copy-start | bytes 7864324
  574.8 8.6 %copy-start.12 = (f32[2048]{0:T(1024)S(1)}, f32[2048]{0:T(1024)}, u32[]{:S(2)}) copy-start(f32[2048]{0:T(1024)} %copy-done.11) | copy-start | bytes 24580
  574.8 78.5 %collective-permute-start.12 = (bf16[2,2,320,2048]{3,2,1,0:T(8,128)(2,1)}, bf16[2,2,320,2048]{3,2,1,0:T(8,128)(2,1)}, u32[]{:S(2)}, u32[]{:S(2)}) collective-permute-start(bf16[2,2,320,2048]{3,2,1,0:T(8,128)(2,1)} %convolution_convert_fusion.4), channel_id=1, source_target_pairs={{0,2},{2,0},{1,3},{3,1},{4,6},{6,4},{5,7},{7,5},{8,10},{10,8},{9,1... | collective-permute-start | bytes 15728648 | tf_op jit(solution)/shard_map/ppermute | solution.py:44
  637.6 3.6 collective-permute-start.20
  637.8 4.9 collective-permute-start.21
  638.7 4.5 collective-permute-start.22
  645.0 5.1 collective-permute-start.17
  645.4 6.3 collective-permute-start.18
  646.2 6.8 collective-permute-start.19
  661.6 20.2 %copy-start.21 = (f32[2,2,320,2048]{3,2,1,0:T(8,128)}, f32[2,2,320,2048]{3,2,1,0:T(8,128)S(1)}, u32[]{:S(2)}) copy-start(f32[2,2,320,2048]{3,2,1,0:T(8,128)S(1)} %convert_add_fusion) | copy-start | bytes 31457284
  661.9 17.6 %collective-permute-start.13 = (bf16[160,2048]{1,0:T(8,128)(2,1)S(1)}, bf16[160,2048]{1,0:T(8,128)(2,1)S(1)}, u32[]{:S(2)}, u32[]{:S(2)}) collective-permute-start(bf16[160,2048]{1,0:T(8,128)(2,1)S(1)} %get-tuple-element.130), channel_id=1, source_target_pairs={{0,4},{4,0},{1,5},{5,1},{2,6},{6,2},{3,7},{7,3},{8,12},{12,8},{9,1... | collective-permute-start | bytes 1966088 | tf_op jit(solution)/shard_map/ppermute | solution.py:44
  663.2 17.1 %collective-permute-start.15 = (bf16[160,2048]{1,0:T(8,128)(2,1)S(1)}, bf16[160,2048]{1,0:T(8,128)(2,1)S(1)}, u32[]{:S(2)}, u32[]{:S(2)}) collective-permute-start(bf16[160,2048]{1,0:T(8,128)(2,1)S(1)} %get-tuple-element.131), channel_id=1, source_target_pairs={{0,1},{1,0},{2,3},{3,2},{4,5},{5,4},{6,7},{7,6},{8,9},{9,8},{10,11... | collective-permute-start | bytes 1966088 | tf_op jit(solution)/shard_map/ppermute | solution.py:44
  664.1 16.6 %copy-start.32 = (bf16[128,2048]{1,0:T(8,128)(2,1)}, bf16[128,2048]{1,0:T(8,128)(2,1)S(1)}, u32[]{:S(2)}) copy-start(bf16[128,2048]{1,0:T(8,128)(2,1)S(1)} %constant_dynamic-update-slice_fusion) | copy-start | bytes 1572868
  681.8 38.7 %collective-permute-start.16 = (bf16[320,2048]{1,0:T(8,128)(2,1)}, bf16[320,2048]{1,0:T(8,128)(2,1)}, u32[]{:S(2)}, u32[]{:S(2)}) collective-permute-start(bf16[320,2048]{1,0:T(8,128)(2,1)} %pad_maximum_fusion.5), channel_id=1, source_target_pairs={{0,4},{4,0},{1,5},{5,1},{2,6},{6,2},{3,7},{7,3},{8,12},{12,8},{9,1... | collective-permute-start | bytes 3932168 | tf_op jit(solution)/shard_map/ppermute | solution.py:44
  684.0 36.5 %collective-permute-start.14 = (bf16[320,2048]{1,0:T(8,128)(2,1)}, bf16[320,2048]{1,0:T(8,128)(2,1)}, u32[]{:S(2)}, u32[]{:S(2)}) collective-permute-start(bf16[320,2048]{1,0:T(8,128)(2,1)} %pad_maximum_fusion.4), channel_id=1, source_target_pairs={{0,1},{1,0},{2,3},{3,2},{4,5},{5,4},{6,7},{7,6},{8,9},{9,8},{10,11... | collective-permute-start | bytes 3932168 | tf_op jit(solution)/shard_map/ppermute | solution.py:44
  685.0 9.2 %copy-start.23 = (bf16[512,768]{1,0:T(8,128)(2,1)S(1)}, bf16[512,768]{1,0:T(8,128)(2,1)}, u32[]{:S(2)}) copy-start(bf16[512,768]{1,0:T(8,128)(2,1)} %reduce-scatter.11.cloned.1.call-done) | copy-start | bytes 2359300
  688.7 6.5 collective-permute-start.26
  689.5 31.0 %copy-start.2 = (f32[320,2048]{1,0:T(8,128)S(1)}, f32[320,2048]{1,0:T(8,128)}, u32[]{:S(2)}) copy-start(f32[320,2048]{1,0:T(8,128)} %copy-done.1) | copy-start | bytes 7864324
  689.5 28.6 %collective-permute-start.27 = (bf16[128,768]{0,1:T(8,128)(2,1)}, bf16[128,768]{0,1:T(8,128)(2,1)}, u32[]{:S(2)}, u32[]{:S(2)}) collective-permute-start(bf16[128,768]{0,1:T(8,128)(2,1)} %bitcast.364), channel_id=1, source_target_pairs={{0,4},{2,6},{4,0},{6,2},{1,5},{3,7},{5,1},{7,3},{8,12},{10,14},{12... | collective-permute-start | bytes 589832 | tf_op jit(solution)/shard_map/ppermute | solution.py:657
  692.2 27.4 %collective-permute-start.28 = (bf16[128,768]{0,1:T(8,128)(2,1)}, bf16[128,768]{0,1:T(8,128)(2,1)S(1)}, u32[]{:S(2)}, u32[]{:S(2)}) collective-permute-start(bf16[128,768]{0,1:T(8,128)(2,1)} %bitcast.365), channel_id=1, source_target_pairs={{0,6},{2,4},{4,2},{6,0},{1,7},{3,5},{5,3},{7,1},{8,14},{10,12},{12... | collective-permute-start | bytes 589832 | tf_op jit(solution)/shard_map/ppermute | solution.py:657
  746.1 17.9 %copy-start.18 = (bf16[512,1536]{1,0:T(8,128)(2,1)S(1)}, bf16[512,1536]{1,0:T(8,128)(2,1)}, u32[]{:S(2)}) copy-start(bf16[512,1536]{1,0:T(8,128)(2,1)} %reduce-scatter.9.cloned.1.call-done) | copy-start | bytes 4718596
  765.0 4.7 copy-start.27
  765.0 4.7 copy-start.29
  765.0 4.7 copy-start.30
  765.0 4.7 copy-start.31
  765.0 15.3 %collective-permute-start.23 = (bf16[128,1536]{1,0:T(8,128)(2,1)}, bf16[128,1536]{1,0:T(8,128)(2,1)}, u32[]{:S(2)}, u32[]{:S(2)}) collective-permute-start(bf16[128,1536]{1,0:T(8,128)(2,1)} %get-tuple-element.116), channel_id=1, source_target_pairs={{0,2},{2,0},{4,6},{6,4},{1,3},{3,1},{5,7},{7,5},{8,10},{10,8},{12,... | collective-permute-start | bytes 1179656 | tf_op jit(solution)/shard_map/ppermute | solution.py:657
  773.8 5.9 copy-start.40
  773.8 5.9 copy-start.41
  773.8 5.9 copy-start.42
  777.6 12.2 %collective-permute-start.24 = (bf16[128,1536]{1,0:T(8,128)(2,1)}, bf16[128,1536]{1,0:T(8,128)(2,1)S(1)}, u32[]{:S(2)}, u32[]{:S(2)}) collective-permute-start(bf16[128,1536]{1,0:T(8,128)(2,1)} %get-tuple-element.115), channel_id=1, source_target_pairs={{0,4},{2,6},{4,0},{6,2},{1,5},{3,7},{5,1},{7,3},{8,12},{10,14},{12... | collective-permute-start | bytes 1179656 | tf_op jit(solution)/shard_map/ppermute | solution.py:657
  779.0 18.7 %collective-permute-start.25 = (bf16[128,1536]{1,0:T(8,128)(2,1)S(1)}, bf16[128,1536]{1,0:T(8,128)(2,1)S(1)}, u32[]{:S(2)}, u32[]{:S(2)}) collective-permute-start(bf16[128,1536]{1,0:T(8,128)(2,1)S(1)} %copy-done.35), channel_id=1, source_target_pairs={{0,6},{2,4},{4,2},{6,0},{1,7},{3,5},{5,3},{7,1},{8,14},{10,12},{12... | collective-permute-start | bytes 1179656 | tf_op jit(solution)/shard_map/ppermute | solution.py:657
  780.3 17.6 %copy-start.16 = (f32[128,6144]{1,0:T(8,128)S(1)}, f32[128,6144]{1,0:T(8,128)}, u32[]{:S(2)}) copy-start(f32[128,6144]{1,0:T(8,128)} %param.25) | copy-start | bytes 9437188
  797.9 6.9 copy-start.10
  (20 other events, 50.8 us)
Sparse Core Ops, SparseCore 0:
  20.9 47.2 all-gather.4
  70.3 26.6 all-gather.6
  99.1 114.8 all-gather.8
  216.0 61.7 all-gather.10
  484.1 27.4 reduce-scatter.6
  526.2 44.1 reduce-scatter.4
  573.3 59.5 reduce-scatter.10
  635.2 110.7 reduce-scatter.8

commit v4 on v3

v4 whole, which is shorter than its diff:
```python
import jax
import jax.numpy as jnp
from jax import lax
from jax.experimental import pallas as pl
from jax.experimental.pallas import tpu as pltpu
from jax.sharding import Mesh, PartitionSpec as P

D = 2048
H = 16
KV = 8
HD = 128
FF = 6144
STEP = 10


norm_epsilon = 1e-06
rope_base = 1000000.0
clip_norm = 1.0
learn_rate = 0.04
gain_rate = 0.8
beta_first = 0.9
beta_second = 0.999
adam_epsilon = 1e-08
weight_decay = 0.1
masked_score = -1e30

NEAR = 2
CORE = 2
TEAM = NEAR * CORE
LAYER = ("near", "core", "tp")
BLOCK = 128
PAD = 8 * 128


def rms_scale(values):
    return lax.rsqrt(jnp.mean(values * values, axis=-1, keepdims=True) + norm_epsilon)


def swish_product(gate_part, up_part):
    return jax.nn.silu(gate_part) * up_part


def pick(values, index):
    return lax.dynamic_index_in_dim(values, index, 0, keepdims=False)


MESH_ID = pl.DeviceIdType.MESH
VMEM_LIMIT = 60 * 1024 * 1024
CHUNK = 16
GATHER_COPIES = 13
SUM_COPIES = 10
NEIGHBOURS = ((1, 0, 0), (0, 1, 0), (0, 0, 1))
MATES = ((0, 1, 0), (1, 0, 0), (1, 1, 0))
EVERYONE_NEAR = NEIGHBOURS + ((1, 1, 0),)


def spots():
    return tuple(lax.axis_index(name) for name in LAYER)


def flipped(near_flip, core_flip, tp_flip):
    return {
        name: 1 - spot if flip else spot
        for name, spot, flip in zip(LAYER, spots(), (near_flip, core_flip, tp_flip))
    }


def greet(flips):
    barrier = pltpu.get_barrier_semaphore()
    for flip in flips:
        pl.semaphore_signal(barrier, inc=1, device_id=flipped(*flip), device_id_type=MESH_ID)
    pl.semaphore_wait(barrier, len(flips))


def link(source, target, send_sem, recv_sem, flip):
    return pltpu.make_async_remote_copy(
        src_ref=source,
        dst_ref=target,
        send_sem=send_sem,
        recv_sem=recv_sem,
        device_id=flipped(*flip),
        device_id_type=MESH_ID,
    )


TO_NEAR, TO_CORE, TO_TP = NEIGHBOURS


def plan_exchange(pieces, out, send, recv, own_sem):
    near, core, _ = spots()
    own = near * CORE + core
    copies = []
    for number, flip in enumerate(MATES):
        there = (1 - near if flip[0] else near) * CORE + (1 - core if flip[1] else core)
        copies.append(
            link(pieces.at[there], out.at[own], send.at[number], recv.at[number], flip)
        )
    copies.append(pltpu.make_async_copy(pieces.at[own], out.at[own], own_sem))
    return copies


def exchange_scratch():
    return [
        pltpu.SemaphoreType.DMA((len(MATES),)),
        pltpu.SemaphoreType.DMA((len(MATES),)),
        pltpu.SemaphoreType.DMA,
    ]


def plan_exchanges(pieces, mixed, sems):
    copies = []
    for place, (piece, result) in enumerate(zip(pieces, mixed)):
        copies += plan_exchange(piece, result, *sems[3 * place : 3 * place + 3])
    return copies


def plan_gather(own, out, send, recv, own_sem, cut):
    near, core, tp = spots()
    rows = own.shape[0]
    low, high = pl.ds(0, cut), pl.ds(cut, rows - cut)

    def make(number, source, target, flip):
        return link(source, target, send.at[number], recv.at[number], flip)

    def give(number, part, flip):
        return make(number, own.at[part], out.at[near, core, tp, part], flip)

    def relay(number, where_near, where_tp, part, flip):
        ref = out.at[where_near, core, where_tp, part]
        return make(number, ref, ref, flip)

    keep = pltpu.make_async_copy(own, out.at[near, core, tp], own_sem)
    twin_own = make(4, own, out.at[near, core, tp], TO_CORE)
    near_high = give(1, high, TO_NEAR)
    tp_high = give(2, high, TO_TP)
    far_high = relay(7, 1 - near, tp, high, TO_TP)
    twin_beside = relay(8, 1 - near, tp, high, TO_CORE)
    twin_across = relay(9, near, 1 - tp, high, TO_CORE)
    twin_far = relay(12, 1 - near, 1 - tp, high, TO_CORE)
    twins = [twin_own, twin_beside, twin_across, twin_far]
    ways = [near_high, tp_high, far_high]
    if cut:
        tp_low = give(0, low, TO_TP)
        near_low = give(3, low, TO_NEAR)
        far_low = relay(5, near, 1 - tp, low, TO_NEAR)
        twin_across_low = relay(6, near, 1 - tp, low, TO_CORE)
        twin_beside_low = relay(10, 1 - near, tp, low, TO_CORE)
        twin_far_low = relay(11, 1 - near, 1 - tp, low, TO_CORE)
        twins += [twin_across_low, twin_beside_low, twin_far_low]
        ways += [tp_low, near_low, far_low]

    def begin():
        if cut:
            tp_low.start()
        near_high.start()
        tp_high.start()
        if cut:
            near_low.start()
        twin_own.start()
        keep.start()

    def middle():
        if cut:
            tp_low.wait_recv()
            far_low.start()
            twin_across_low.start()
        near_high.wait_recv()
        far_high.start()
        twin_beside.start()

    def later():
        tp_high.wait_recv()
        twin_across.start()
        if cut:
            near_low.wait_recv()
            twin_beside_low.start()

    def finish():
        if cut:
            far_low.wait_recv()
            twin_far_low.start()
        far_high.wait_recv()
        twin_far.start()
        for copy in twins:
            copy.wait_recv()
        for copy in ways + twins:
            copy.wait_send()
        keep.wait()

    return [begin, middle, later, finish]


def gather_scratch():
    return [
        pltpu.SemaphoreType.DMA((GATHER_COPIES,)),
        pltpu.SemaphoreType.DMA((GATHER_COPIES,)),
        pltpu.SemaphoreType.DMA,
    ]


def add_rows(target, start, count, *sources):
    @pl.loop(0, count // CHUNK)
    def _(step):
        at = pl.ds(pl.multiple_of(start + step * CHUNK, CHUNK), CHUNK)
        total = None
        for source, shift in sources:
            where = pl.ds(pl.multiple_of(start - shift + step * CHUNK, CHUNK), CHUNK)
            value = source[where].astype(jnp.float32)
            total = value if total is None else total + value
        target[at] = total.astype(target.dtype)


def plan_sum(part, total, scratch, cut):
    mine, theirs, way_near, way_tp, from_tp, from_near, send, recv, local_sem = scratch
    near, core, tp = spots()
    rows = total.shape[0]
    low, high = pl.ds(0, cut), pl.ds(cut, rows - cut)
    order = [(1 - near, 1 - tp), (near, 1 - tp), (1 - near, tp), (near, tp)]
    twin, keep = [], []
    for number, (a, b) in enumerate(order):
        twin.append(
            link(
                part.at[a, 1 - core, b],
                theirs.at[number],
                send.at[number],
                recv.at[number],
                TO_CORE,
            )
        )
        keep.append(
            pltpu.make_async_copy(part.at[a, core, b], mine.at[number], local_sem.at[number])
        )

    def make(number, source, target, flip):
        return link(source, target, send.at[number], recv.at[number], flip)

    far, to_tp, to_near = mine.at[0], mine.at[1], mine.at[2]
    far_high = make(5, far.at[high], way_tp, TO_TP)
    tp_high = make(6, to_tp.at[high], from_tp.at[high], TO_TP)
    near_high = make(9, to_near.at[high], from_near.at[high], TO_NEAR)
    ways = [far_high, tp_high, near_high]
    if cut:
        far_low = make(4, far.at[low], way_near, TO_NEAR)
        near_low = make(7, to_near.at[low], from_near.at[low], TO_NEAR)
        tp_low = make(8, to_tp.at[low], from_tp.at[low], TO_TP)
        ways += [far_low, near_low, tp_low]

    def ready(number):
        keep[number].wait()
        twin[number].wait_recv()

    def both(number):
        return (mine.at[number], 0), (theirs.at[number], 0)

    def begin():
        for number in range(4):
            twin[number].start()
            keep[number].start()

    def first():
        ready(0)
        if cut:
            add_rows(far, 0, cut, *both(0))
            far_low.start()
        add_rows(far, cut, rows - cut, *both(0))
        far_high.start()
        ready(1)
        add_rows(to_tp, cut, rows - cut, *both(1))
        tp_high.start()
        ready(2)
        if cut:
            add_rows(to_near, 0, cut, *both(2))
            near_low.start()

    def second():
        if cut:
            far_low.wait_recv()
            add_rows(to_tp, 0, cut, *both(1), (way_near, 0))
            tp_low.start()
        far_high.wait_recv()
        add_rows(to_near, cut, rows - cut, *both(2), (way_tp, cut))
        near_high.start()
        ready(3)
        add_rows(total, 0, rows, *both(3))

    def finish():
        for copy in ways[1:]:
            if not cut or copy is not far_low:
                copy.wait_recv()
        for copy in twin + ways:
            copy.wait_send()

    return [begin, first, second, finish], from_tp, from_near


def sum_scratch(rows, width, cut):
    low = jnp.bfloat16
    return [
        pltpu.VMEM((4, rows, width), low),
        pltpu.VMEM((4, rows, width), low),
        pltpu.VMEM((max(cut, CHUNK), width), low),
        pltpu.VMEM((rows - cut, width), low),
        pltpu.VMEM((rows, width), low),
        pltpu.VMEM((rows, width), low),
        pltpu.SemaphoreType.DMA((SUM_COPIES,)),
        pltpu.SemaphoreType.DMA((SUM_COPIES,)),
        pltpu.SemaphoreType.DMA((4,)),
    ]


SUM_SCRATCH = 9


def params(number):
    return pltpu.CompilerParams(
        collective_id=number, has_side_effects=True, vmem_limit_bytes=VMEM_LIMIT
    )


def cost_of(microseconds):
    return pl.CostEstimate(
        flops=0, bytes_accessed=int(microseconds * 3.4e6), transcendentals=0
    )


def in_vmem():
    return pl.BlockSpec(memory_space=pltpu.VMEM)


def anywhere():
    return pl.BlockSpec(memory_space=pl.ANY)


def like(array):
    return jax.ShapeDtypeStruct(array.shape, array.dtype)


def layer_rows(rows, width):
    return jax.ShapeDtypeStruct((NEAR, CORE, 2, rows, width), jnp.bfloat16)


def exchange(pieces, number, name):
    def kernel(pieces, out, *sems):
        greet(MATES)
        copies = plan_exchange(pieces, out, *sems)
        for copy in copies:
            copy.start()
        for copy in copies:
            copy.wait()

    return pl.pallas_call(
        kernel,
        name=name,
        out_shape=like(pieces),
        in_specs=[anywhere()],
        out_specs=anywhere(),
        scratch_shapes=exchange_scratch(),
        compiler_params=params(number),
        cost_estimate=cost_of(12),
    )(pieces)


def gather_rows(values, extra, number, name):
    rows, width = values.shape
    extras = len(extra)

    def kernel(own, *rest):
        pieces, out, mixed = rest[:extras], rest[extras], rest[extras + 1 : 2 * extras + 1]
        sems = rest[2 * extras + 1 :]
        begin, *steps = plan_gather(own, out, *sems[:3], cut=0)
        copies = plan_exchanges(pieces, mixed, sems[3:])
        greet(EVERYONE_NEAR)
        begin()
        for copy in copies:
            copy.start()
        for step in steps:
            step()
        for copy in copies:
            copy.wait()

    outs = pl.pallas_call(
        kernel,
        name=name,
        out_shape=(layer_rows(rows, width),) + tuple(like(piece) for piece in extra),
        in_specs=[anywhere()] * (1 + extras),
        out_specs=(anywhere(),) * (1 + extras),
        scratch_shapes=gather_scratch() + exchange_scratch() * extras,
        compiler_params=params(number),
        cost_estimate=cost_of(60),
    )(values, *extra)
    return (outs[0].reshape(-1, width),) + tuple(outs[1:])


def row_loop(rows, body):
    @pl.loop(0, rows // CHUNK)
    def _(step):
        body(pl.ds(pl.multiple_of(step * CHUNK, CHUNK), CHUNK))


def spread(part, rows):
    return part.reshape(NEAR, CORE, 2, rows, part.shape[-1])


def read(ref, at):
    return ref[at].astype(jnp.float32)


def branch_and_norm(part, residual, gain, number, name):
    rows, width = residual.shape
    cut = rows // 2

    def kernel(part, residual, gain, hidden, out, *scratch):
        normed, sems = scratch[SUM_SCRATCH], scratch[SUM_SCRATCH + 1 :]
        steps, from_tp, from_near = plan_sum(part, hidden, scratch[:SUM_SCRATCH], cut)
        onward = plan_gather(normed, out, *sems, cut=cut)
        greet(NEIGHBOURS)
        for step in steps:
            step()

        def finish(at):
            value = hidden[at] + read(from_tp, at) + read(from_near, at)
            value = read(residual, at) + value
            hidden[at] = value
            normed[at] = (value * rms_scale(value) * gain[...]).astype(jnp.bfloat16)

        row_loop(rows, finish)
        for step in onward:
            step()

    hidden, full = pl.pallas_call(
        kernel,
        name=name,
        out_shape=(jax.ShapeDtypeStruct((rows, width), jnp.float32), layer_rows(rows, width)),
        in_specs=[anywhere(), in_vmem(), in_vmem()],
        out_specs=(in_vmem(), anywhere()),
        scratch_shapes=sum_scratch(rows, width, cut)
        + [pltpu.VMEM((rows, width), jnp.bfloat16)]
        + gather_scratch(),
        compiler_params=params(number),
        cost_estimate=cost_of(95),
    )(spread(part, rows), residual, gain.reshape(1, width))
    return hidden, full.reshape(-1, width)


def norm_back(value, gain, grad):
    scale = rms_scale(value)
    scaled = grad * gain
    inner = jnp.mean(scaled * value, axis=-1, keepdims=True)
    return scale * scaled - value * (scale * scale * scale * inner), grad * value * scale


def norm_back_gather(part, values, upstream, gain, number, name):
    rows, width = values.shape
    cut = rows // 2

    def kernel(part, values, upstream, gain, result, gain_grad, out, *scratch):
        (total, low), sems = (
            scratch[SUM_SCRATCH : SUM_SCRATCH + 2],
            scratch[SUM_SCRATCH + 2 :],
        )
        steps, from_tp, from_near = plan_sum(part, total, scratch[:SUM_SCRATCH], cut)
        onward = plan_gather(low, out, *sems, cut=cut)
        greet(NEIGHBOURS)
        for step in steps:
            step()
        gain_grad[...] = jnp.zeros_like(gain_grad)

        def finish(at):
            grad = total[at] + read(from_tp, at) + read(from_near, at)
            back, by_gain = norm_back(read(values, at), gain[...], grad)
            gain_grad[...] += by_gain.reshape(CHUNK // 8, 8, width).sum(axis=0)
            value = read(upstream, at) + back
            result[at] = value
            low[at] = value.astype(jnp.bfloat16)

        row_loop(rows, finish)
        for step in onward:
            step()

    result, gain_grad, full = pl.pallas_call(
        kernel,
        name=name,
        out_shape=(
            jax.ShapeDtypeStruct((rows, width), jnp.float32),
            jax.ShapeDtypeStruct((8, width), jnp.float32),
            layer_rows(rows, width),
        ),
        in_specs=[anywhere()] + [in_vmem()] * 3,
        out_specs=(in_vmem(), in_vmem(), anywhere()),
        scratch_shapes=sum_scratch(rows, width, cut)
        + [pltpu.VMEM((rows, width), jnp.float32), pltpu.VMEM((rows, width), jnp.bfloat16)]
        + gather_scratch(),
        compiler_params=params(number),
        cost_estimate=cost_of(100),
    )(spread(part, rows), values, upstream, gain.reshape(1, width))
    return result, gain_grad.sum(axis=0), full.reshape(-1, width)


def norm_back_last(part, values, upstream, gain, extra, number, name):
    rows, width = values.shape
    extras = len(extra)

    def kernel(part, values, upstream, gain, *rest):
        pieces, (result, gain_grad) = rest[:extras], rest[extras : extras + 2]
        mixed, rest = rest[extras + 2 : 2 * extras + 2], rest[2 * extras + 2 :]
        total, sems = rest[SUM_SCRATCH], rest[SUM_SCRATCH + 1 :]
        steps, from_tp, from_near = plan_sum(part, total, rest[:SUM_SCRATCH], 0)
        copies = plan_exchanges(pieces, mixed, sems)
        greet(EVERYONE_NEAR)
        steps[0]()
        for copy in copies:
            copy.start()
        for step in steps[1:]:
            step()
        gain_grad[...] = jnp.zeros_like(gain_grad)

        def finish(at):
            grad = total[at] + read(from_tp, at) + read(from_near, at)
            back, by_gain = norm_back(read(values, at), gain[...], grad)
            gain_grad[...] += by_gain.reshape(CHUNK // 8, 8, width).sum(axis=0)
            result[at] = (read(upstream, at) + back).astype(jnp.bfloat16)

        row_loop(rows, finish)
        for copy in copies:
            copy.wait()

    outs = pl.pallas_call(
        kernel,
        name=name,
        out_shape=(
            jax.ShapeDtypeStruct((rows, width), jnp.bfloat16),
            jax.ShapeDtypeStruct((8, width), jnp.float32),
        )
        + tuple(like(piece) for piece in extra),
        in_specs=[anywhere()] + [in_vmem()] * 3 + [anywhere()] * extras,
        out_specs=(in_vmem(), in_vmem()) + (anywhere(),) * extras,
        scratch_shapes=sum_scratch(rows, width, 0)
        + [pltpu.VMEM((rows, width), jnp.float32)]
        + exchange_scratch() * extras,
        compiler_params=params(number),
        cost_estimate=cost_of(65),
    )(spread(part, rows), values, upstream, gain.reshape(1, width), *extra)
    return (outs[0], outs[1].sum(axis=0)) + tuple(outs[2:])


def total_everywhere(values, pieces, outer_count, number, name):
    shape = values.shape

    def kernel(values, pieces, out, norm, factor, mixed, layer, outers, send, recv, *sems):
        near, core, tp = spots()
        outer = lax.axis_index("outer")
        partners = [
            flipped(a, b, c)
            for a in range(NEAR)
            for b in range(CORE)
            for c in range(2)
            if a + b + c
        ]
        partners += [{"outer": (outer + step) % outer_count} for step in range(1, outer_count)]
        barrier = pltpu.get_barrier_semaphore()
        for partner in partners:
            pl.semaphore_signal(barrier, inc=1, device_id=partner, device_id_type=MESH_ID)
        pl.semaphore_wait(barrier, len(partners))

        def share(slots, mine, first, count):
            copies = []
            for number in range(first, first + count):
                copy = pltpu.make_async_remote_copy(
                    src_ref=slots.at[mine],
                    dst_ref=slots.at[mine],
                    send_sem=send.at[number],
                    recv_sem=recv.at[number],
                    device_id=partners[number],
                    device_id_type=MESH_ID,
                )
                copy.start()
                copies.append(copy)
            return copies

        mine = near * (CORE * 2) + core * 2 + tp
        layer[mine] = values[...]
        copies = share(layer, mine, 0, 7)
        others = plan_exchange(pieces, mixed, *sems)
        for copy in others:
            copy.start()
        for copy in copies:
            copy.wait()
        total = layer[0]
        for slot in range(1, 8):
            total = total + layer[slot]
        outers[outer] = total
        for copy in share(outers, outer, 7, outer_count - 1):
            copy.wait()
        total = outers[0]
        for slot in range(1, outer_count):
            total = total + outers[slot]
        out[...] = total
        row = lax.broadcasted_iota(jnp.int32, shape, 0)
        squares = jnp.sum(jnp.where(row < shape[0] - 8, total * total, total), keepdims=True)
        root = jnp.sqrt(squares)
        norm[...] = jnp.broadcast_to(root, norm.shape)
        factor[...] = jnp.broadcast_to(
            jnp.minimum(1.0, clip_norm / (root + 1e-06)), factor.shape
        )
        for copy in others:
            copy.wait()

    tile = jax.ShapeDtypeStruct((8, HD), jnp.float32)
    return pl.pallas_call(
        kernel,
        name=name,
        out_shape=(jax.ShapeDtypeStruct(shape, jnp.float32), tile, tile, like(pieces)),
        in_specs=[in_vmem(), anywhere()],
        out_specs=(in_vmem(), in_vmem(), in_vmem(), anywhere()),
        scratch_shapes=[
            pltpu.VMEM((8,) + shape, jnp.float32),
            pltpu.VMEM((outer_count,) + shape, jnp.float32),
            pltpu.SemaphoreType.DMA((6 + outer_count,)),
            pltpu.SemaphoreType.DMA((6 + outer_count,)),
        ]
        + exchange_scratch(),
        compiler_params=params(number),
    )(values, pieces)


def head_scale(raw, gain, cos_full, sin_full):
    normed = raw * rms_scale(raw) * gain
    return (normed * cos_full + pltpu.roll(normed, HD // 2, 1) * sin_full).astype(jnp.bfloat16)


def head_back(raw, gain, grad, cos_full, sin_full):
    grad = grad * cos_full - pltpu.roll(grad, HD // 2, 1) * sin_full
    return norm_back(raw, gain, grad)


def columns(index):
    return pl.ds(index * HD, HD)


def head_inputs(proj, gains, cos_ref, sin_ref, queries, keys, values, heads):
    for head in range(heads):
        queries[head] = head_scale(
            proj[0, :, columns(head)], gains[0:1, :], cos_ref[...], sin_ref[...]
        )
    keys[...] = head_scale(
        proj[0, :, columns(heads)], gains[1:2, :], cos_ref[...], sin_ref[...]
    )
    values[...] = proj[0, :, columns(heads + 1)].astype(jnp.bfloat16)


def masked_scores(stacked, keys, step, length):
    scores = lax.dot_general(
        stacked, keys, (((1,), (1,)), ((), ())), preferred_element_type=jnp.float32
    ) * (HD ** (-0.5))
    row = lax.broadcasted_iota(jnp.int32, scores.shape, 0) % BLOCK + step * BLOCK
    column = lax.broadcasted_iota(jnp.int32, scores.shape, 1)
    return jnp.where((column <= row) & (column < length), scores, masked_score)


def stack_heads(ref, at, heads):
    return jnp.concatenate([ref[head, at] for head in range(heads)], axis=0)


def per_sequence(*shape):
    return pl.BlockSpec((1,) + shape, lambda s: (s,) + (0,) * len(shape))


def whole(*shape):
    return pl.BlockSpec(shape, lambda s: (0,) * len(shape), pipeline_mode=pl.Buffered(1))


def across_columns(left, weights, first, width, out):
    total = weights.shape[0]
    for start in range(0, total, 512):
        at = pl.ds(start, 512)
        out[0, :, at] = lax.dot_general(
            left,
            weights[at, first : first + width],
            (((1,), (1,)), ((), ())),
            preferred_element_type=jnp.float32,
        ).astype(out.dtype)


def attend(normed, weights, cotangent, extra, group_length, cos_full, sin_full, gains, heads, number):
    count, rows, width = normed.shape
    wide = (heads + 2) * HD
    extras = len(extra)
    own_rows = cotangent.shape[0]

    def kernel(lengths, normed, weights, cos_ref, sin_ref, gains, own, *rest):
        pieces, rest = rest[:extras], rest[extras:]
        (proj, out, logs, branch, gathered), rest = rest[:5], rest[5:]
        mixed, (queries, keys, values), sems = rest[:extras], rest[extras : extras + 3], rest[extras + 3 :]
        sequence = pl.program_id(0)
        steps = plan_gather(own, gathered, *sems[:3], cut=own_rows // 2)
        copies = plan_exchanges(pieces, mixed, sems[3:])

        @pl.when(sequence == 0)
        def _():
            greet(EVERYONE_NEAR)
            steps[0]()
            for copy in copies:
                copy.start()

        length = lengths[sequence]
        proj[0] = jnp.dot(
            normed[0], weights[:, :wide], preferred_element_type=jnp.float32
        )
        head_inputs(proj, gains, cos_ref, sin_ref, queries, keys, values, heads)
        lane = lax.broadcasted_iota(jnp.int32, (BLOCK, HD), 1)
        for step in range(rows // BLOCK):
            at = pl.ds(step * BLOCK, BLOCK)
            seen = pl.ds(0, (step + 1) * BLOCK)
            scores = masked_scores(stack_heads(queries, at, heads), keys[seen], step, length)
            top = jnp.max(scores, axis=-1, keepdims=True)
            exponent = jnp.exp(scores - top)
            total = jnp.sum(exponent, axis=-1, keepdims=True)
            probs = (exponent / total).astype(jnp.bfloat16)
            mixed_values = jnp.dot(probs, values[seen], preferred_element_type=jnp.float32)
            log_total = top + jnp.log(total)
            kept = jnp.zeros((BLOCK, HD), jnp.float32)
            for head in range(heads):
                mine = slice(head * BLOCK, (head + 1) * BLOCK)
                out[0, at, columns(head)] = mixed_values[mine].astype(jnp.bfloat16)
                kept = jnp.where(lane == head, log_total[mine], kept)
            logs[0, at] = kept
        across_columns(out[0], weights, wide, heads * HD, branch)

        @pl.when(sequence == 1)
        def _():
            steps[1]()

        @pl.when(sequence == 2)
        def _():
            steps[2]()

        @pl.when(sequence == count - 1)
        def _():
            steps[3]()
            for copy in copies:
                copy.wait()

    outs = pl.pallas_call(
        kernel,
        name="attend",
        grid=(count,),
        out_shape=(
            jax.ShapeDtypeStruct((count, rows, wide), jnp.float32),
            jax.ShapeDtypeStruct((count, rows, heads * HD), jnp.bfloat16),
            jax.ShapeDtypeStruct((count, rows, HD), jnp.float32),
            jax.ShapeDtypeStruct((count, rows, width), jnp.bfloat16),
            layer_rows(own_rows, width),
        )
        + tuple(like(piece) for piece in extra),
        in_specs=[
            pl.BlockSpec(memory_space=pltpu.SMEM),
            per_sequence(rows, width),
            whole(width, wide + heads * HD),
            whole(rows, HD),
            whole(rows, HD),
            whole(2, HD),
            anywhere(),
        ]
        + [anywhere()] * extras,
        out_specs=(
            per_sequence(rows, wide),
            per_sequence(rows, heads * HD),
            per_sequence(rows, HD),
            per_sequence(rows, width),
            anywhere(),
        )
        + (anywhere(),) * extras,
        scratch_shapes=[
            pltpu.VMEM((heads, rows, HD), jnp.bfloat16),
            pltpu.VMEM((rows, HD), jnp.bfloat16),
            pltpu.VMEM((rows, HD), jnp.bfloat16),
        ]
        + gather_scratch()
        + exchange_scratch() * extras,
        compiler_params=params(number),
        cost_estimate=cost_of(50),
    )(group_length, normed, weights, cos_full, sin_full, gains, cotangent, *extra)
    return outs[:4] + (outs[4].reshape(-1, width),) + tuple(outs[5:])


def attend_back(
    projected, grad_attn, logs, weights, part, hidden, group_length, cos_full, sin_full, gains, heads, number
):
    count, rows, wide = projected.shape
    own_rows, width = hidden.shape
    cut = own_rows // 2

    def kernel(
        lengths, proj, grad, logs, weights, cos_ref, sin_ref, gains, part, hidden, *rest
    ):
        (out, gain_grad, back_part, output), rest = rest[:4], rest[4:]
        (queries, keys, values, grad_att, grad_q, grad_k, grad_v, total, held, held_sem), rest = (
            rest[:10],
            rest[10:],
        )
        sequence = pl.program_id(0)
        steps, from_tp, from_near = plan_sum(part, total, rest, cut)
        fetch = pltpu.make_async_copy(hidden, held, held_sem)

        @pl.when(sequence == 0)
        def _():
            greet(NEIGHBOURS)
            steps[0]()
            fetch.start()
            gain_grad[...] = jnp.zeros_like(gain_grad)

        length = lengths[sequence]
        grad_att[...] = jnp.dot(
            grad[0], weights[:, wide:], preferred_element_type=jnp.float32
        ).astype(jnp.bfloat16)
        head_inputs(proj, gains, cos_ref, sin_ref, queries, keys, values, heads)
        grad_k[...] = jnp.zeros_like(grad_k)
        grad_v[...] = jnp.zeros_like(grad_v)

        @pl.when(sequence == 0)
        def _():
            steps[1]()

        for step in range(rows // BLOCK):
            at = pl.ds(step * BLOCK, BLOCK)
            seen = pl.ds(0, (step + 1) * BLOCK)
            stacked = stack_heads(queries, at, heads)
            above = jnp.concatenate([grad_att[at, columns(head)] for head in range(heads)], axis=0)
            log_total = jnp.concatenate(
                [logs[0, at, head : head + 1] for head in range(heads)], axis=0
            )
            probs = jnp.exp(masked_scores(stacked, keys[seen], step, length) - log_total)
            grad_probs = lax.dot_general(
                above, values[seen], (((1,), (1,)), ((), ())), preferred_element_type=jnp.float32
            )
            inner = jnp.sum(probs * grad_probs, axis=-1, keepdims=True)
            grad_scores = (probs * (grad_probs - inner)).astype(jnp.bfloat16)
            by_query = jnp.dot(grad_scores, keys[seen], preferred_element_type=jnp.float32)
            for head in range(heads):
                grad_q[head, at] = by_query[head * BLOCK : (head + 1) * BLOCK] * (HD ** (-0.5))
            grad_k[seen] += lax.dot_general(
                grad_scores, stacked, (((0,), (0,)), ((), ())), preferred_element_type=jnp.float32
            )
            grad_v[seen] += lax.dot_general(
                probs.astype(jnp.bfloat16),
                above,
                (((0,), (0,)), ((), ())),
                preferred_element_type=jnp.float32,
            )

        def settle(column, gain, value):
            back, by_gain = head_back(
                proj[0, :, columns(column)], gains[gain : gain + 1, :], value, cos_ref[...], sin_ref[...]
            )
            out[0, :, columns(column)] = back.astype(jnp.bfloat16)
            gain_grad[gain] += by_gain.reshape(rows // 8, 8, HD).sum(axis=0)

        for head in range(heads):
            settle(head, 0, grad_q[head])
        settle(heads, 1, grad_k[...] * (HD ** (-0.5)))
        out[0, :, columns(heads + 1)] = grad_v[...].astype(jnp.bfloat16)

        @pl.when(sequence == 2)
        def _():
            steps[2]()

        across_columns(out[0], weights, 0, wide, back_part)

        @pl.when(sequence == count - 1)
        def _():
            fetch.wait()
            steps[3]()

            def finish(at):
                value = total[at] + read(from_tp, at) + read(from_near, at)
                output[at] = (held[at] + value).astype(jnp.bfloat16)

            row_loop(own_rows, finish)

    return pl.pallas_call(
        kernel,
        name="attend_back",
        grid=(count,),
        out_shape=(
            jax.ShapeDtypeStruct((count, rows, wide), jnp.bfloat16),
            jax.ShapeDtypeStruct((2, 8, HD), jnp.float32),
            jax.ShapeDtypeStruct((count, rows, width), jnp.bfloat16),
            jax.ShapeDtypeStruct((own_rows, width), jnp.bfloat16),
        ),
        in_specs=[
            pl.BlockSpec(memory_space=pltpu.SMEM),
            per_sequence(rows, wide),
            per_sequence(rows, width),
            per_sequence(rows, HD),
            whole(width, wide + heads * HD),
            whole(rows, HD),
            whole(rows, HD),
            whole(2, HD),
            anywhere(),
            anywhere(),
        ],
        out_specs=(
            per_sequence(rows, wide),
            pl.BlockSpec((2, 8, HD), lambda s: (0, 0, 0)),
            per_sequence(rows, width),
            pl.BlockSpec((own_rows, width), lambda s: (0, 0)),
        ),
        scratch_shapes=[
            pltpu.VMEM((heads, rows, HD), jnp.bfloat16),
            pltpu.VMEM((rows, HD), jnp.bfloat16),
            pltpu.VMEM((rows, HD), jnp.bfloat16),
            pltpu.VMEM((rows, heads * HD), jnp.bfloat16),
            pltpu.VMEM((heads, rows, HD), jnp.float32),
            pltpu.VMEM((rows, HD), jnp.float32),
            pltpu.VMEM((rows, HD), jnp.float32),
            pltpu.VMEM((own_rows, width), jnp.float32),
            pltpu.VMEM((own_rows, width), jnp.float32),
            pltpu.SemaphoreType.DMA,
        ]
        + sum_scratch(own_rows, width, cut),
        compiler_params=params(number),
        cost_estimate=cost_of(50),
    )(
        group_length, projected, grad_attn, logs, weights, cos_full, sin_full, gains, spread(part, own_rows), hidden
    )


def adam_rows(weight, moment, square, pieces, factor, widths):
    rows, total = weight.shape
    height = 16

    def kernel(weight, moment, square, pieces, factor, new, one, two, low):
        scale = factor[0:1, 0:1]
        for member in range(TEAM):
            first, inside = 0, 0
            for width in widths:
                share = width // TEAM
                at = pl.ds(first + member * share, share)
                gradient = pieces[member, :, inside : inside + share].astype(jnp.float32)
                value, one[:, at], two[:, at] = adam_update(
                    weight[:, at], gradient, moment[:, at], square[:, at], scale, weight_decay, learn_rate
                )
                new[:, at] = value
                low[:, at] = value.astype(jnp.bfloat16)
                first += width
                inside += share

    block = pl.BlockSpec((height, total), lambda s: (s, 0))
    return pl.pallas_call(
        kernel,
        name="adam_rows",
        grid=(rows // height,),
        out_shape=(like(weight),) * 3 + (jax.ShapeDtypeStruct(weight.shape, jnp.bfloat16),),
        in_specs=[
            block,
            block,
            block,
            pl.BlockSpec((TEAM, height, pieces.shape[2]), lambda s: (0, s, 0)),
            whole(8, HD),
        ],
        out_specs=(block,) * 4,
        compiler_params=pltpu.CompilerParams(vmem_limit_bytes=VMEM_LIMIT),
        cost_estimate=cost_of(rows * total * 28 / 3.4e6),
    )(weight, moment, square, pieces, factor)


def adam_columns(weight, moment, square, pieces, factor):
    rows, total = weight.shape
    share = rows // TEAM

    def kernel(weight, moment, square, pieces, factor, new, one, two, low):
        gradient = pieces[0].astype(jnp.float32).T
        value, one[...], two[...] = adam_update(
            weight[...], gradient, moment[...], square[...], factor[0:1, 0:1], weight_decay, learn_rate
        )
        new[...] = value
        low[...] = value.astype(jnp.bfloat16)

    block = pl.BlockSpec((share, total), lambda s: (s, 0))
    return pl.pallas_call(
        kernel,
        name="adam_columns",
        grid=(TEAM,),
        out_shape=(like(weight),) * 3 + (jax.ShapeDtypeStruct(weight.shape, jnp.bfloat16),),
        in_specs=[block, block, block, per_sequence(*pieces.shape[1:]), whole(8, HD)],
        out_specs=(block,) * 4,
        compiler_params=pltpu.CompilerParams(vmem_limit_bytes=VMEM_LIMIT),
        cost_estimate=cost_of(rows * total * 28 / 3.4e6),
    )(weight, moment, square, pieces, factor)


def split_columns(values, widths):
    members = []
    for member in range(TEAM):
        start, parts = 0, []
        for width in widths:
            share = width // TEAM
            first = start + member * share
            parts.append(values[:, first : first + share])
            start += width
        members.append(jnp.concatenate(parts, axis=1))
    return jnp.stack(members)


def gather_outer(mixed):
    return lax.all_gather(mixed.reshape(-1, mixed.shape[2]), "outer", axis=0, tiled=True)


def team_pieces(summed):
    return summed.reshape(TEAM, -1, summed.shape[-1])


def sum_weight(gradient):
    return lax.psum_scatter(gradient, "outer", scatter_dimension=0, tiled=True)


def after(values, earlier):
    return lax.optimization_barrier((values, earlier))


def adam_update(weight, gradient, moment_one, moment_two, factor, decay_rate, rate_value):
    clipped = gradient * factor
    moment_one = beta_first * moment_one + (1.0 - beta_first) * clipped
    moment_two = beta_second * moment_two + (1.0 - beta_second) * clipped * clipped
    first_fixed = moment_one / (1.0 - beta_first**STEP)
    second_fixed = moment_two / (1.0 - beta_second**STEP)
    weight = weight - rate_value * (
        first_fixed / (jnp.sqrt(second_fixed) + adam_epsilon) + decay_rate * weight
    )
    return (weight, moment_one, moment_two)


def dot(left, right, contract):
    return lax.dot_general(
        left, right, ((contract[0], contract[1]), ((), ())), preferred_element_type=jnp.float32
    )


def times(left, right):
    return dot(left, right, ((1,), (0,)))


def times_across(left, right):
    return dot(left, right, ((1,), (1,)))


def over_rows(left, right):
    return dot(left, right, ((0,), (0,)))


def local(
    inputs,
    cotangent,
    lengths,
    owners,
    qkv_weight,
    out_weight,
    gate_up_weight,
    down_weight,
    norm_gains,
    qkv_moment,
    out_moment,
    gate_up_moment,
    down_moment,
    gains_moment,
    qkv_square,
    out_square,
    gate_up_square,
    down_square,
    gains_square,
):
    tp_count = lax.axis_size("tp")
    half_rows = inputs.shape[0]
    row_count = half_rows * tp_count
    heads = H // tp_count // TEAM
    hidden_units = FF // tp_count // TEAM
    qkv_widths = (H * HD // tp_count, KV * HD // tp_count, KV * HD // tp_count)
    out_widths = (H * HD // tp_count,)
    gate_up_widths = (FF // tp_count, FF // tp_count)
    down_widths = (FF // tp_count,)

    first_group = lax.axis_index("outer") * TEAM
    group_ids = first_group + jnp.arange(TEAM)
    group_length = jnp.sum(
        jnp.where(owners[None, :] == group_ids[:, None], lengths[None, :], 0), axis=1
    )
    own_group = lax.axis_index("near") * CORE + lax.axis_index("core")
    own_rows = lax.axis_index("tp") * half_rows + jnp.arange(half_rows)
    valid_rows = (own_rows < pick(group_length, own_group))[:, None]
    half_width = HD // 2
    frequency = rope_base ** (-(jnp.arange(half_width, dtype=jnp.float32) * 2.0 / HD))
    angles = jnp.arange(row_count, dtype=jnp.float32)[:, None] * frequency[None, :]
    cosine, sine = jnp.cos(angles), jnp.sin(angles)
    cos_full = jnp.concatenate([cosine, cosine], axis=1)
    sin_full = jnp.concatenate([-sine, sine], axis=1)
    attn_gain = norm_gains[:D]
    mlp_gain = norm_gains[D : 2 * D]
    head_gains = norm_gains[2 * D :].reshape(2, HD)

    first_pieces = jnp.concatenate(
        [
            split_columns(qkv_weight.astype(jnp.bfloat16), qkv_widths),
            split_columns(out_weight.astype(jnp.bfloat16).T, out_widths),
        ],
        axis=2,
    )
    gate_up_pieces = split_columns(gate_up_weight.astype(jnp.bfloat16), gate_up_widths)
    down_pieces = split_columns(down_weight.astype(jnp.bfloat16).T, down_widths)
    first_mixed = exchange(first_pieces, 6, "exchange_first")
    first_full = gather_outer(first_mixed)
    qkv_full = first_full[:, : (heads + 2) * HD]

    residual_in = inputs.astype(jnp.float32)
    normed_attn = residual_in * rms_scale(residual_in) * attn_gain
    normed_attn, first_mixed = lax.optimization_barrier(
        (normed_attn.astype(jnp.bfloat16), first_mixed)
    )
    normed_attn, gate_up_mixed = gather_rows(
        normed_attn, (gate_up_pieces,), 0, "gather_inputs"
    )
    gate_up_full = gather_outer(gate_up_mixed)
    grad_low = jnp.where(valid_rows, cotangent, jnp.zeros_like(cotangent))
    projected, attended, logs, attn_branch, grad_all, down_mixed = attend(
        normed_attn.reshape(TEAM, row_count, D),
        first_full,
        grad_low,
        (down_pieces,),
        group_length,
        cos_full,
        sin_full,
        head_gains,
        heads,
        1,
    )
    down_full = gather_outer(down_mixed)
    attended = attended.reshape(-1, heads * HD)
    hidden, normed_mlp = branch_and_norm(attn_branch, inputs, mlp_gain, 2, "branch_and_norm")
    gate_up = times(normed_mlp, gate_up_full)
    gate_part = gate_up[:, :hidden_units]
    up_part = gate_up[:, hidden_units:]
    activated = swish_product(gate_part, up_part).astype(jnp.bfloat16)
    mlp_part = times_across(activated, down_full).astype(jnp.bfloat16)

    grad_down = over_rows(grad_all, activated).astype(jnp.bfloat16)
    grad_all, grad_down = after(grad_all, grad_down)
    down_sum = sum_weight(grad_down)
    grad_activated = times(grad_all, down_full)
    swish_pull = jax.vjp(swish_product, gate_part, up_part)[1]
    grad_gate, grad_up = swish_pull(grad_activated)
    grad_gate_up = jnp.concatenate([grad_gate, grad_up], axis=1).astype(jnp.bfloat16)
    grad_normed_mlp = times_across(grad_gate_up, gate_up_full).astype(jnp.bfloat16)
    grad_gate_up_weight = over_rows(normed_mlp, grad_gate_up).astype(jnp.bfloat16)
    grad_normed_mlp, grad_gate_up_weight, down_sum = lax.optimization_barrier(
        (grad_normed_mlp, grad_gate_up_weight, down_sum)
    )
    gate_up_sum = sum_weight(grad_gate_up_weight)
    grad_hidden, grad_mlp_gain, grad_attn = norm_back_gather(
        grad_normed_mlp, hidden, grad_low, mlp_gain, 3, "norm_back_mlp"
    )
    grad_out_weight = over_rows(grad_attn, attended).astype(jnp.bfloat16)
    grad_out_weight, gate_up_sum = after(grad_out_weight, gate_up_sum)
    out_sum = sum_weight(grad_out_weight)
    grad_projected, grad_head_gains, grad_normed_attn, output = attend_back(
        projected,
        grad_attn.reshape(TEAM, row_count, D),
        logs,
        first_full,
        mlp_part,
        hidden,
        group_length,
        cos_full,
        sin_full,
        head_gains,
        heads,
        7,
    )
    grad_projected = grad_projected.reshape(-1, projected.shape[2])
    grad_qkv_weight = over_rows(normed_attn, grad_projected).astype(jnp.bfloat16)
    grad_qkv_weight, out_sum = after(grad_qkv_weight, out_sum)
    qkv_sum = sum_weight(grad_qkv_weight)
    input_grad, grad_attn_gain, down_mixed, gate_up_mixed, out_mixed = norm_back_last(
        grad_normed_attn,
        inputs,
        grad_hidden,
        attn_gain,
        (team_pieces(down_sum), team_pieces(gate_up_sum), team_pieces(out_sum)),
        4,
        "norm_back_attn",
    )
    gain_part = jnp.concatenate(
        [grad_attn_gain, grad_mlp_gain, grad_head_gains.sum(axis=1).reshape(-1)]
    )
    square_part = sum(
        jnp.sum(jnp.square(member.astype(jnp.float32)))
        for member in (qkv_sum, out_sum, gate_up_sum, down_sum)
    )
    gain_count = gain_part.shape[0]
    packed = jnp.pad(gain_part, (0, -gain_count % PAD))
    packed = jnp.concatenate([packed, jnp.pad(square_part[None], (0, PAD - 1))])
    packed, norm_tile, factor_tile, qkv_mixed = total_everywhere(
        packed.reshape(-1, HD), team_pieces(qkv_sum), lax.axis_size("outer"), 5, "total_everywhere"
    )
    gain_grad = packed.reshape(-1)[:gain_count]
    grad_norm, factor = norm_tile[0, 0], factor_tile[0, 0]
    new_qkv, new_qkv_one, new_qkv_two, qkv_copy = adam_rows(
        qkv_weight, qkv_moment, qkv_square, qkv_mixed, factor_tile, qkv_widths
    )
    new_out, new_out_one, new_out_two, out_copy = adam_columns(
        out_weight, out_moment, out_square, out_mixed, factor_tile
    )
    new_gate_up, new_gate_up_one, new_gate_up_two, gate_up_copy = adam_rows(
        gate_up_weight, gate_up_moment, gate_up_square, gate_up_mixed, factor_tile, gate_up_widths
    )
    new_down, new_down_one, new_down_two, down_copy = adam_columns(
        down_weight, down_moment, down_square, down_mixed, factor_tile
    )
    new_gains, new_gains_one, new_gains_two = adam_update(
        norm_gains, gain_grad, gains_moment, gains_square, factor, 0.0, gain_rate
    )
    return (
        output,
        input_grad,
        grad_norm,
        new_qkv,
        new_qkv_one,
        new_qkv_two,
        qkv_copy,
        new_out,
        new_out_one,
        new_out_two,
        out_copy,
        new_gate_up,
        new_gate_up_one,
        new_gate_up_two,
        gate_up_copy,
        new_down,
        new_down_one,
        new_down_two,
        down_copy,
        new_gains,
        new_gains_one,
        new_gains_two,
    )


def solution(mesh):
    fsdp_count, tp_count = mesh.shape["fsdp"], mesh.shape["tp"]
    cut = mesh.devices.reshape(fsdp_count // TEAM, NEAR, CORE, tp_count)
    cut_mesh = Mesh(cut, ("outer",) + LAYER)
    fsdp = ("outer", "near", "core")
    rows = P(fsdp + ("tp",), None)
    wide = P(fsdp, "tp")
    tall = P("tp", fsdp)
    weights = (wide, tall, wide, tall, P())
    return jax.shard_map(
        local,
        mesh=cut_mesh,
        in_specs=(rows, rows, P(), P()) + weights * 3,
        out_specs=(rows, rows, P()) + (wide,) * 4 + (tall,) * 4 + (wide,) * 4 + (tall,) * 4 + (P(),) * 3,
        check_vma=False,
    )
```

time: 820 us -> 710 us (0.87)
  Pallas kernels: 404 us -> 514 us
  waiting for transfers between devices: 104 us -> 0.26 us
  matrix products: 172 us -> 134 us
  local copies, waits for them, and re-layouts: 51.8 us -> 13.8 us
  starting transfers between devices: 22.4 us -> 0.67 us
  other arithmetic: 38.9 us -> 21.4 us
    ppermute x29 -> x0, waiting for transfers between devices: 83 us -> none  [the longest x24 67 us: team_swap(): return lax.ppermute(values, ('near', 'core'), pairs)]
    pallas_call x1, Pallas kernels: 15.3 us -> 63.1 us  [attend(): pl.pallas_call(kernel, name='attend', grid=(count,), out_shape=(jax.Shape...]
    dot_general x13 -> x8, matrix products: 172 us -> 134 us  [dot(): lax.dot_general(left, right, ((contract[0], contract[1]), ((), ())), pref...]
    pallas_call x1, Pallas kernels: 22.1 us -> 56.4 us  [attend_back(): pl.pallas_call(kernel, name='attend_back', grid=(count,), out_shape=(jax....]
    pallas_call x5 -> x9, Pallas kernels: 268 us -> 293 us  [the longest x1 102 us: norm_back_gather(): pl.pallas_call(kernel, name=name, out_shape=(jax.ShapeDtypeStruct((rows,...]
    ppermute x29 -> x0, starting transfers between devices: 21.8 us -> none  [the longest x24 17.2 us: team_swap(): return lax.ppermute(values, ('near', 'core'), pairs)]
    reduce_scatter x4, waiting for transfers between devices: 21.1 us -> 0.1 us  [sum_weight(): return lax.psum_scatter(gradient, 'outer', scatter_dimension=0, tiled=True)]
    convert_element_type x6 -> x2, other arithmetic: 21 us -> 3.8 us  [the longest x1 2.52 us: local(): activated = swish_product(gate_part, up_part).astype(jnp.bfloat16)]
  transfers between devices with their start and end apart: 37 -> 7, of which waited for: 17 -> 1; matrix products, arithmetic and copies ran while one was open for 23% -> 22% of each run, Pallas kernels for 36% -> 66%
where the time goes in v4:
time: 710 us; the launch traced here: 702 us
  Pallas kernels  514 us (72%)
  matrix products  134 us (19%)
  other arithmetic  21.4 us (3%)
  between operations  17.5 us (2%)
  local copies, waits for them, and re-layouts  13.8 us (2%)
    dot_general x8, matrix products, dot(): lax.dot_general(left, right, ((contract[0], contract[1]), ((), ())), pref...  134 us
    pallas_call x1, Pallas kernels, branch_and_norm(): pl.pallas_call(kernel, name=name, out_shape=(jax.ShapeDtypeStruct((rows,...  102 us
    pallas_call x1, Pallas kernels, norm_back_gather(): pl.pallas_call(kernel, name=name, out_shape=(jax.ShapeDtypeStruct((rows,...  102 us
    pallas_call x1, Pallas kernels, norm_back_last(): pl.pallas_call(kernel, name=name, out_shape=(jax.ShapeDtypeStruct((rows,...  72.7 us
    pallas_call x1, Pallas kernels, gather_rows(): pl.pallas_call(kernel, name=name, out_shape=(layer_rows(rows, width),) +...  65 us
    pallas_call x1, Pallas kernels, attend(): pl.pallas_call(kernel, name='attend', grid=(count,), out_shape=(jax.Shape...  63.1 us
    pallas_call x1, Pallas kernels, attend_back(): pl.pallas_call(kernel, name='attend_back', grid=(count,), out_shape=(jax....  56.4 us
    pallas_call x2, Pallas kernels, adam_rows(): pl.pallas_call(kernel, name='adam_rows', grid=(rows // height,), out_shap...  17.5 us
  transfers between devices with their start and end apart: 7, of which 1 were waited for; matrix products, arithmetic and copies ran while one was open for 22% of the time, Pallas kernels for 66%

profile of v4, /device:TPU:0, one launch (start us, length us, event | category | flops | bytes accessed | tf_op | source)
XLA Modules:
  0.0 702.2 jit_solution(6320027842968326216)
XLA Ops:
  7.2 1.3 convert_element_type.58
  8.6 1.3 copy.43
  10.0 0.9 maximum_maximum_fusion.pieces
  10.9 12.9 %exchange_first.1 = bf16[4,128,768]{2,1,0:T(8,128)(2,1)} custom-call(bf16[4,128,768]{2,1,0:T(8,128)(2,1)} %maximum_maximum_fusion.pieces), custom_call_target="tpu_custom_call" | custom-call | bytes 40800000 | tf_op jit(solution)/shard_map/exchange_first/pallas_call | solution.py:351
  23.9 0.0 all-gather.6.cloned.1.call-start
  24.0 0.4 fusion.4
  24.3 0.6 fusion.20
  24.9 0.6 copy-done.11
  25.5 1.4 fusion.6.own
  27.0 0.2 convert_element_type.60
  27.1 0.1 fusion.17
  27.3 0.1 maximum_bitcast_fusion
  27.3 0.1 maximum_bitcast_fusion.2
  27.4 1.3 pad_maximum_fusion.3.rest_0_
  28.7 65.0 %gather_inputs.1 = (bf16[2,2,2,320,2048]{4,3,2,1,0:T(8,128)(2,1)}, bf16[4,128,1536]{2,1,0:T(8,128)(2,1)}) custom-call(bf16[320,2048]{1,0:T(8,128)(2,1)} %fusion.6.own, bf16[4,128,1536]{2,1,0:T(8,128)(2,1)} %pad_maximum_fusion.3.rest_0_), custom_call_target="tpu_custom_call" | custom-call | bytes 204000000 | tf_op jit(solution)/shard_map/gather_inputs/pallas_call | solution.py:381
  93.8 0.0 all-gather.8.cloned.1.call-start
  93.9 0.3 copy.44
  94.2 0.2 select_reduce_fusion.lengths
  94.4 0.6 dynamic_slice.4
  95.0 0.7 add_compare_fusion
  95.7 1.2 fusion.9
  96.9 1.1 pad_maximum_fusion.5
  98.0 0.1 slice_bitcast_fusion.3
  98.0 1.0 pad_maximum_fusion.4.rest_0_
  99.0 0.6 slice_bitcast_fusion.8.gains
  99.6 1.2 broadcast_select_fusion.own.upstream
  100.8 63.1 %attend.1 = (f32[4,640,512]{2,1,0:T(8,128)}, bf16[4,640,256]{2,1,0:T(8,128)(2,1)}, f32[4,640,128]{2,1,0:T(8,128)}, bf16[4,640,2048]{2,1,0:T(8,128)(2,1)}, bf16[2...) custom-call(s32[4]{0:T(128)} %copy-done.19, bf16[4,640,2048]{2,1,0:T(8,128)(2,1)} %bitcast.89, ...), custom_call_target="tpu_custom_call" | custom-call | bytes 170000000 | tf_op jit(solution)/shard_map/attend/pallas_call | solution.py:743
  163.9 0.2 reduce-scatter.5.cloned.1.call-start
  164.1 102.3 %branch_and_norm.1 = (f32[320,2048]{1,0:T(8,128)}, bf16[2,2,2,320,2048]{4,3,2,1,0:T(8,128)(2,1)}) custom-call(bf16[2,2,2,320,2048]{4,3,2,1,0:T(8,128)(2,1)} %bitcast.94, bf16[320,2048]{1,0:T(8,128)(2,1)} %values.1, f32[1,2048]{1,0:T(1,128)} %bitcast.107), custom_call_target="tpu_custom_call" | custom-call | bytes 323000000 | tf_op jit(solution)/shard_map/branch_and_norm/pallas_call | solution.py:430
  266.4 22.3 %fusion.21 = f32[2560,1536]{0,1:T(8,128)S(1)} fusion(bf16[2560,2048]{1,0:T(8,128)(2,1)} %bitcast.112, bf16[2048,1536]{1,0:T(8,128)(2,1)} %all-gather.6.cloned.1.call-done), kind=kOutput, calls=%fused_computation.76 | convolution fusion | flops 16106127360 | bytes 32505856 | tf_op jit(solution)/shard_map/dot_general | solution.py:1034
  288.7 2.5 multiply_convert_fusion.1
  291.3 2.9 copy-done.1
  294.2 1.9 copy-done.5
  296.0 12.2 %convolution_convert_fusion.3 = bf16[2048,768]{1,0:T(8,128)(2,1)} fusion(bf16[2560,2048]{1,0:T(8,128)(2,1)} %bitcast.110, bf16[2560,768]{0,1:T(8,128)(2,1)S(1)} %multiply_convert_fusion.1), kind=kOutput, calls=%fused_computation.12 | convolution fusion | flops 8054636544 | bytes 17563648 | tf_op jit(solution)/shard_map/dot_general | solution.py:1034
  308.3 0.3 reduce-scatter.7.cloned.1.call-start
  308.6 20.9 %fusion.2 = (bf16[2560,768]{0,1:T(8,128)(2,1)}, bf16[2560,768]{0,1:T(8,128)(2,1)}) fusion(f32[2560,1536]{0,1:T(8,128)} %copy-done.1, bf16[2560,2048]{1,0:T(8,128)(2,1)} %bitcast.111, bf16[2048,768]{1,0:T(8,128)(2,1)} %all-gather.8.cloned.1.call-done), kind=kOutput, calls=%fused_computation.5 | convolution fusion | flops 8080588800 | bytes 37224448 | tf_op jit(solution)/shard_map/dot_general | solution.py:1034
  329.5 23.5 %convolution_convert_fusion.1 = bf16[2560,2048]{1,0:T(8,128)(2,1)} fusion(bf16[2048,1536]{1,0:T(8,128)(2,1)} %all-gather.6.cloned.1.call-done, bf16[2560,768]{0,1:T(8,128)(2,1)} %get-tuple-element.130, bf16[2560,768]{0,1:T(8,128)(2,1)} %get-tuple-element.129), kind=kOutput, calls=%fused_computation.2 | convolution fusion | flops 16127098880 | bytes 24641536 | tf_op jit(solution)/shard_map/dot_general | solution.py:1034
  353.0 22.9 %convolution_convert_fusion.2 = bf16[2048,1536]{1,0:T(8,128)(2,1)} fusion(bf16[2560,2048]{1,0:T(8,128)(2,1)} %bitcast.113, bf16[2560,768]{0,1:T(8,128)(2,1)} %get-tuple-element.130, bf16[2560,768]{0,1:T(8,128)(2,1)} %get-tuple-element.129), kind=kOutput, calls=%fused_computation.11 | convolution fusion | flops 16125001728 | bytes 24641536 | tf_op jit(solution)/shard_map/dot_general | solution.py:1034
  375.9 0.0 reduce-scatter.9.cloned.1.call-start
  376.0 101.9 %norm_back_mlp.1 = (f32[320,2048]{1,0:T(8,128)}, f32[8,2048]{1,0:T(8,128)}, bf16[2,2,2,320,2048]{4,3,2,1,0:T(8,128)(2,1)}) custom-call(bf16[2,2,2,320,2048]{4,3,2,1,0:T(8,128)(2,1)} %bitcast.93, f32[320,2048]{1,0:T(8,128)} %get-tuple-element.85.values.hidden, bf16[320,2048]{1,0:T(8,128)(2,1)} %broadcast_select_fusion.own.upstream, f32[1,2048]{1,0:T(1,128)} %bitcast.108), custom_call_target="tpu_custom_call" | custom-call | bytes 340000000 | tf_op jit(solution)/shard_map/norm_back_mlp/pallas_call | solution.py:480
  477.9 8.5 %convolution_convert_fusion.5 = bf16[2048,256]{1,0:T(8,128)(2,1)} fusion(bf16[2560,2048]{1,0:T(8,128)(2,1)} %bitcast.91, bf16[2560,256]{1,0:T(8,128)(2,1)} %bitcast.115), kind=kOutput, calls=%fused_computation.20 | convolution fusion | flops 2684878848 | bytes 12845056 | tf_op jit(solution)/shard_map/dot_general | solution.py:1034
  486.4 0.1 reduce-scatter.7.cloned.1.call-done
  486.5 0.0 reduce-scatter.11.cloned.1.call-start
  486.6 13.3 %convolution_convert_fusion = bf16[2560,2048]{1,0:T(8,128)(2,1)} fusion(bf16[2560,768]{0,1:T(8,128)(2,1)} %copy-done.5, bf16[2048,768]{1,0:T(8,128)(2,1)S(1)} %copy-done.22), kind=kOutput, calls=%fused_computation.1 | convolution fusion | flops 8058306560 | bytes 17563648 | tf_op jit(solution)/shard_map/dot_general | solution.py:1034
  499.9 56.4 %attend_back.1 = (bf16[4,640,512]{2,1,0:T(8,128)(2,1)}, f32[2,8,128]{2,1,0:T(8,128)}, bf16[4,640,2048]{2,1,0:T(8,128)(2,1)}, bf16[320,2048]{1,0:T(8,128)(2,1)}) custom-call(s32[4]{0:T(128)} %copy-done.19, f32[4,640,512]{2,1,0:T(8,128)} %get-tuple-element.76.proj, bf16[4,640,2048]{2,1,0:T(8,128)(2,1)} %bitcast.92, f32[4,640,128]{2,1,0:T(8,128)} %get-tuple-element.87.logs, ...), custom_call_target="tpu_custom_call" | custom-call | bytes 170000000 | tf_op jit(solution)/shard_map/attend_back/pallas_call | solution.py:880
  556.4 10.3 %convolution_convert_fusion.4 = bf16[2048,512]{1,0:T(8,128)(2,1)} fusion(bf16[2560,2048]{1,0:T(8,128)(2,1)} %bitcast.90, bf16[2560,512]{1,0:T(8,128)(2,1)} %bitcast.114), kind=kOutput, calls=%fused_computation.16 | convolution fusion | flops 5369757696 | bytes 15204352 | tf_op jit(solution)/shard_map/dot_general | solution.py:1034
  566.8 1.0 multiply_reduce_fusion.1
  567.9 0.3 copy-done.4
  568.2 1.4 multiply_reduce_fusion
  569.6 72.7 %norm_back_attn.1 = (bf16[320,2048]{1,0:T(8,128)(2,1)}, f32[8,2048]{1,0:T(8,128)}, bf16[4,128,768]{2,1,0:T(8,128)(2,1)}, bf16[4,128,1536]{2,1,0:T(8,128)(2,1)}, bf16[4,128,256]{2,1,0:T(8,128)(2,1)}) custom-call(bf16[2,2,2,320,2048]{4,3,2,1,0:T(8,128)(2,1)} %bitcast.96, bf16[320,2048]{1,0:T(8,128)(2,1)} %values.1, f32[320,2048]{1,0:T(8,128)} %get-tuple-element.90.upstream, ...), custom_call_target="tpu_custom_call" | custom-call | bytes 221000000 | tf_op jit(solution)/shard_map/norm_back_attn/pallas_call | solution.py:527
  642.3 0.9 reduce_sum.83
  643.2 0.7 multiply_reduce_fusion.3
  643.9 1.9 multiply_reduce_fusion.2
  648.4 0.6 fusion.10.values
  649.0 12.7 %total_everywhere.1 = (f32[48,128]{1,0:T(8,128)}, f32[8,128]{1,0:T(8,128)}, f32[8,128]{1,0:T(8,128)}, bf16[4,128,512]{2,1,0:T(8,128)(2,1)}) custom-call(f32[48,128]{1,0:T(8,128)} %fusion.10.values, bf16[4,128,512]{2,1,0:T(8,128)(2,1)} %bitcast.101), custom_call_target="tpu_custom_call" | custom-call | tf_op jit(solution)/shard_map/total_everywhere/pallas_call | solution.py:609
  661.8 1.2 slice.155
  663.0 1.2 slice.153
  664.2 4.0 adam_columns.2
  668.1 6.6 adam_rows.2
  674.8 6.0 adam_columns.3
  680.8 10.9 %adam_rows.3 = (f32[128,6144]{1,0:T(8,128)}, f32[128,6144]{1,0:T(8,128)}, f32[128,6144]{1,0:T(8,128)}, bf16[128,6144]{1,0:T(8,128)(2,1)}) custom-call(f32[128,6144]{1,0:T(8,128)} %weight.6, f32[128,6144]{1,0:T(8,128)} %moment.6, f32[128,6144]{1,0:T(8,128)} %square.26, bf16[4,128,1536]{2,1,0:T(8,128)(2,1)} %get-tuple-element.115.pieces, ...), custom_call_target="tpu_custom_call" | custom-call | bytes 22020096 | tf_op jit(solution)/shard_map/adam_rows/pallas_call | solution.py:949
  691.7 1.3 multiply_subtract_fusion
  693.0 1.1 copy.47
  694.0 1.1 copy.48
  (67 shorter events, 0.5 us)
Async XLA Ops:
  7.2 93.6 %all-gather.4.cloned.1.call-start = ((), (), s32[]{:S(2)}) async-start(), calls=%async_computation.4 | async-start | bytes 3932160 | tf_op jit(solution)/shard_map/all_gather | solution.py:1006
  8.5 15.4 %copy-start = (bf16[320,2048]{1,0:T(8,128)(2,1)S(1)}, bf16[320,2048]{1,0:T(8,128)(2,1)}, u32[]{:S(2)}) copy-start(bf16[320,2048]{1,0:T(8,128)(2,1)} %values.1) | copy-start | bytes 3932164
  8.6 15.7 %copy-start.12 = (f32[4352]{0:T(1024)S(1)}, f32[4352]{0:T(1024)}, u32[]{:S(2)}) copy-start(f32[4352]{0:T(1024)} %param.27) | copy-start | bytes 52228
  23.9 242.5 %all-gather.6.cloned.1.call-start = ((), (), s32[]{:S(2)}) async-start(), calls=%async_computation.5 | async-start | bytes 7864320 | tf_op jit(solution)/shard_map/all_gather | solution.py:1006
  23.9 3.0 copy-start.2
  24.9 0.6 copy-start.11
  27.4 66.5 %copy-start.3 = (f32[3072,128]{1,0:T(8,128)S(1)}, f32[3072,128]{1,0:T(8,128)}, u32[]{:S(2)}) copy-start(f32[3072,128]{1,0:T(8,128)} %weight.7) | copy-start | bytes 4718596
  28.7 65.4 %copy-start.20 = (s32[16]{0:T(128)S(1)}, s32[16]{0:T(128)}, u32[]{:S(2)}) copy-start(s32[16]{0:T(128)} %param.21) | copy-start | bytes 196
  28.7 65.5 %copy-start.21 = (s32[16]{0:T(128)S(1)}, s32[16]{0:T(128)}, u32[]{:S(2)}) copy-start(s32[16]{0:T(128)} %param.22) | copy-start | bytes 196
  93.8 214.7 %all-gather.8.cloned.1.call-start = ((), (), s32[]{:S(2)}) async-start(), calls=%async_computation.6 | async-start | bytes 3932160 | tf_op jit(solution)/shard_map/all_gather | solution.py:1006
  94.2 5.4 copy-start.9
  94.4 6.4 copy-start.19
  163.9 212.0 %reduce-scatter.5.cloned.1.call-start = ((), (), s32[]{:S(2)}) async-start(), calls=%async_computation.7 | async-start | bytes 3932160 | tf_op jit(solution)/shard_map/reduce_scatter | solution.py:1014
  288.7 5.5 copy-start.1
  294.2 1.9 copy-start.5
  308.3 178.2 %reduce-scatter.7.cloned.1.call-start = ((), (), s32[]{:S(2)}) async-start(), calls=%async_computation.8 | async-start | bytes 7864320 | tf_op jit(solution)/shard_map/reduce_scatter | solution.py:1014
  375.9 190.8 %reduce-scatter.9.cloned.1.call-start = ((), (), s32[]{:S(2)}) async-start(), calls=%async_computation.9 | async-start | bytes 1310720 | tf_op jit(solution)/shard_map/reduce_scatter | solution.py:1014
  477.9 8.7 %copy-start.22 = (bf16[2048,768]{1,0:T(8,128)(2,1)S(1)}, bf16[2048,768]{1,0:T(8,128)(2,1)}, u32[]{:S(2)}) copy-start(bf16[2048,768]{1,0:T(8,128)(2,1)} %all-gather.8.cloned.1.call-done) | copy-start | bytes 9437188
  486.5 157.4 %reduce-scatter.11.cloned.1.call-start = ((), (), s32[]{:S(2)}) async-start(), calls=%async_computation.10 | async-start | bytes 2621440 | tf_op jit(solution)/shard_map/reduce_scatter | solution.py:1014
  556.4 10.4 %copy-start.14 = (f32[8,2048]{1,0:T(8,128)S(1)}, f32[8,2048]{1,0:T(8,128)}, u32[]{:S(2)}) copy-start(f32[8,2048]{1,0:T(8,128)} %get-tuple-element.100) | copy-start | bytes 196612
  556.4 10.4 %copy-start.18 = (f32[2,8,128]{2,1,0:T(8,128)S(1)}, f32[2,8,128]{2,1,0:T(8,128)}, u32[]{:S(2)}) copy-start(f32[2,8,128]{2,1,0:T(8,128)} %get-tuple-element.101) | copy-start | bytes 24580
  556.4 10.5 %copy-start.6 = (bf16[512,768]{1,0:T(8,128)(2,1)S(1)}, bf16[512,768]{1,0:T(8,128)(2,1)}, u32[]{:S(2)}) copy-start(bf16[512,768]{1,0:T(8,128)(2,1)} %reduce-scatter.5.cloned.1.call-done) | copy-start | bytes 2359300
  566.7 1.4 copy-start.4
  569.6 73.6 %copy-start.10 = (bf16[512,256]{1,0:T(8,128)(2,1)S(1)}, bf16[512,256]{1,0:T(8,128)(2,1)}, u32[]{:S(2)}) copy-start(bf16[512,256]{1,0:T(8,128)(2,1)} %reduce-scatter.9.cloned.1.call-done) | copy-start | bytes 786436
  680.7 10.9 %copy-start.13 = (f32[4352]{0:T(1024)S(1)}, f32[4352]{0:T(1024)}, u32[]{:S(2)}) copy-start(f32[4352]{0:T(1024)} %param.27) | copy-start | bytes 52228
  680.7 10.9 %copy-start.15 = (f32[4352]{0:T(1024)S(1)}, f32[4352]{0:T(1024)}, u32[]{:S(2)}) copy-start(f32[4352]{0:T(1024)} %param.32) | copy-start | bytes 52228
  680.8 10.9 %copy-start.16 = (f32[4352]{0:T(1024)S(1)}, f32[4352]{0:T(1024)}, u32[]{:S(2)}) copy-start(f32[4352]{0:T(1024)} %param.37) | copy-start | bytes 52228
  680.8 10.9 %copy-start.17 = (f32[48,128]{1,0:T(8,128)S(1)}, f32[48,128]{1,0:T(8,128)}, u32[]{:S(2)}) copy-start(f32[48,128]{1,0:T(8,128)} %get-tuple-element.125) | copy-start | bytes 73732
  680.8 12.2 %copy-start.7 = (bf16[320,2048]{1,0:T(8,128)(2,1)S(1)}, bf16[320,2048]{1,0:T(8,128)(2,1)}, u32[]{:S(2)}) copy-start(bf16[320,2048]{1,0:T(8,128)(2,1)} %get-tuple-element.196) | copy-start | bytes 3932164
  680.8 13.2 %copy-start.8 = (bf16[320,2048]{1,0:T(8,128)(2,1)S(1)}, bf16[320,2048]{1,0:T(8,128)(2,1)}, u32[]{:S(2)}) copy-start(bf16[320,2048]{1,0:T(8,128)(2,1)} %get-tuple-element.197) | copy-start | bytes 3932164
Sparse Core Ops, SparseCore 0:
  24.0 64.6 all-gather.3
  93.9 115.6 all-gather.5
  211.2 61.7 all-gather.7
  308.4 60.5 reduce-scatter.4
  376.0 110.4 reduce-scatter.6
  489.2 27.6 reduce-scatter.8
  566.9 43.7 reduce-scatter.10

commit v5 on v4

--- a/solution.py
+++ b/solution.py
@@ -107,6 +107,10 @@
     ]
 
 
+def crossing(pieces, width):
+    return sum(2 * piece.shape[1] * piece.shape[2] for piece in pieces) // width
+
+
 def plan_exchanges(pieces, mixed, sems):
     copies = []
     for place, (piece, result) in enumerate(zip(pieces, mixed)):
@@ -114,10 +118,11 @@
     return copies
 
 
-def plan_gather(own, out, send, recv, own_sem, cut):
+def plan_gather(own, out, send, recv, own_sem, cut, base=0, rows=None):
     near, core, tp = spots()
-    rows = own.shape[0]
-    low, high = pl.ds(0, cut), pl.ds(cut, rows - cut)
+    rows = own.shape[0] if rows is None else rows
+    low, high = pl.ds(base, cut), pl.ds(base + cut, rows - cut)
+    all_rows = pl.ds(base, rows)
 
     def make(number, source, target, flip):
         return link(source, target, send.at[number], recv.at[number], flip)
@@ -129,8 +134,8 @@
         ref = out.at[where_near, core, where_tp, part]
         return make(number, ref, ref, flip)
 
-    keep = pltpu.make_async_copy(own, out.at[near, core, tp], own_sem)
-    twin_own = make(4, own, out.at[near, core, tp], TO_CORE)
+    keep = pltpu.make_async_copy(own.at[all_rows], out.at[near, core, tp, all_rows], own_sem)
+    twin_own = give(4, all_rows, TO_CORE)
     near_high = give(1, high, TO_NEAR)
     tp_high = give(2, high, TO_TP)
     far_high = relay(7, 1 - near, tp, high, TO_TP)
@@ -190,6 +195,10 @@
     return [begin, middle, later, finish]
 
 
+def balanced(rows, beside):
+    return max(0, (rows - beside) // 2 // CHUNK * CHUNK)
+
+
 def gather_scratch():
     return [
         pltpu.SemaphoreType.DMA((GATHER_COPIES,)),
@@ -210,31 +219,16 @@
         target[at] = total.astype(target.dtype)
 
 
-def plan_sum(part, total, scratch, cut):
-    mine, theirs, way_near, way_tp, from_tp, from_near, send, recv, local_sem = scratch
-    near, core, tp = spots()
+def plan_sum(outgoing, mine, keep, total, scratch, cut):
+    theirs, way_near, way_tp, from_tp, from_near, send, recv = scratch
     rows = total.shape[0]
     low, high = pl.ds(0, cut), pl.ds(cut, rows - cut)
-    order = [(1 - near, 1 - tp), (near, 1 - tp), (1 - near, tp), (near, tp)]
-    twin, keep = [], []
-    for number, (a, b) in enumerate(order):
-        twin.append(
-            link(
-                part.at[a, 1 - core, b],
-                theirs.at[number],
-                send.at[number],
-                recv.at[number],
-                TO_CORE,
-            )
-        )
-        keep.append(
-            pltpu.make_async_copy(part.at[a, core, b], mine.at[number], local_sem.at[number])
-        )
 
     def make(number, source, target, flip):
         return link(source, target, send.at[number], recv.at[number], flip)
 
-    far, to_tp, to_near = mine.at[0], mine.at[1], mine.at[2]
+    twin = [make(number, outgoing[number], theirs.at[number], TO_CORE) for number in range(4)]
+    far, to_tp, to_near, own = mine
     far_high = make(5, far.at[high], way_tp, TO_TP)
     tp_high = make(6, to_tp.at[high], from_tp.at[high], TO_TP)
     near_high = make(9, to_near.at[high], from_near.at[high], TO_NEAR)
@@ -243,34 +237,45 @@
         far_low = make(4, far.at[low], way_near, TO_NEAR)
         near_low = make(7, to_near.at[low], from_near.at[low], TO_NEAR)
         tp_low = make(8, to_tp.at[low], from_tp.at[low], TO_TP)
-        ways += [far_low, near_low, tp_low]
+        ways += [near_low, tp_low]
 
     def ready(number):
-        keep[number].wait()
+        if keep:
+            keep[number].wait()
         twin[number].wait_recv()
 
     def both(number):
-        return (mine.at[number], 0), (theirs.at[number], 0)
-
-    def begin():
-        for number in range(4):
+        return (mine[number], 0), (theirs.at[number], 0)
+
+    def begin(numbers=range(4)):
+        for number in numbers:
             twin[number].start()
-            keep[number].start()
-
-    def first():
+            if keep:
+                keep[number].start()
+
+    def send_far():
         ready(0)
         if cut:
             add_rows(far, 0, cut, *both(0))
             far_low.start()
         add_rows(far, cut, rows - cut, *both(0))
         far_high.start()
+
+    def send_tp():
         ready(1)
         add_rows(to_tp, cut, rows - cut, *both(1))
         tp_high.start()
+
+    def send_near():
         ready(2)
         if cut:
             add_rows(to_near, 0, cut, *both(2))
             near_low.start()
+
+    def first():
+        send_far()
+        send_tp()
+        send_near()
 
     def second():
         if cut:
@@ -285,18 +290,31 @@
 
     def finish():
         for copy in ways[1:]:
-            if not cut or copy is not far_low:
-                copy.wait_recv()
-        for copy in twin + ways:
+            copy.wait_recv()
+        for copy in twin + ways + ([far_low] if cut else []):
             copy.wait_send()
 
-    return [begin, first, second, finish], from_tp, from_near
-
-
-def sum_scratch(rows, width, cut):
+    return [begin, first, second, finish], (send_far, send_tp, send_near)
+
+
+def plan_sum_of(part, total, scratch, cut):
+    mine, local_sem, *scratch = scratch
+    near, core, tp = spots()
+    order = [(1 - near, 1 - tp), (near, 1 - tp), (1 - near, tp), (near, tp)]
+    outgoing = [part.at[a, 1 - core, b] for a, b in order]
+    keep = [
+        pltpu.make_async_copy(part.at[a, core, b], mine.at[number], local_sem.at[number])
+        for number, (a, b) in enumerate(order)
+    ]
+    blocks = [mine.at[number] for number in range(4)]
+    steps, _ = plan_sum(outgoing, blocks, keep, total, scratch, cut)
+    return steps, scratch[3], scratch[4]
+
+
+def sum_scratch(rows, width, cut, fetched=True):
     low = jnp.bfloat16
-    return [
-        pltpu.VMEM((4, rows, width), low),
+    fetch = [pltpu.VMEM((4, rows, width), low), pltpu.SemaphoreType.DMA((4,))]
+    return (fetch if fetched else []) + [
         pltpu.VMEM((4, rows, width), low),
         pltpu.VMEM((max(cut, CHUNK), width), low),
         pltpu.VMEM((rows - cut, width), low),
@@ -304,7 +322,6 @@
         pltpu.VMEM((rows, width), low),
         pltpu.SemaphoreType.DMA((SUM_COPIES,)),
         pltpu.SemaphoreType.DMA((SUM_COPIES,)),
-        pltpu.SemaphoreType.DMA((4,)),
     ]
 
 
@@ -363,11 +380,12 @@
 def gather_rows(values, extra, number, name):
     rows, width = values.shape
     extras = len(extra)
+    cut = balanced(rows, crossing(extra, width))
 
     def kernel(own, *rest):
         pieces, out, mixed = rest[:extras], rest[extras], rest[extras + 1 : 2 * extras + 1]
         sems = rest[2 * extras + 1 :]
-        begin, *steps = plan_gather(own, out, *sems[:3], cut=0)
+        begin, *steps = plan_gather(own, out, *sems[:3], cut=cut)
         copies = plan_exchanges(pieces, mixed, sems[3:])
         greet(EVERYONE_NEAR)
         begin()
@@ -411,7 +429,7 @@
 
     def kernel(part, residual, gain, hidden, out, *scratch):
         normed, sems = scratch[SUM_SCRATCH], scratch[SUM_SCRATCH + 1 :]
-        steps, from_tp, from_near = plan_sum(part, hidden, scratch[:SUM_SCRATCH], cut)
+        steps, from_tp, from_near = plan_sum_of(part, hidden, scratch[:SUM_SCRATCH], cut)
         onward = plan_gather(normed, out, *sems, cut=cut)
         greet(NEIGHBOURS)
         for step in steps:
@@ -449,62 +467,155 @@
     return scale * scaled - value * (scale * scale * scale * inner), grad * value * scale
 
 
-def norm_back_gather(part, values, upstream, gain, number, name):
+def sequence_order():
+    near, core, _ = spots()
+    return [
+        (near if place >= 2 else 1 - near) * CORE + (core if place % 2 else 1 - core)
+        for place in range(TEAM)
+    ]
+
+
+def halves_times(left, weights, target, rows):
+    for start in range(0, weights.shape[0], 512):
+        at = pl.ds(start, 512)
+        product = lax.dot_general(
+            left, weights[at, :], (((1,), (1,)), ((), ())), preferred_element_type=jnp.float32
+        ).astype(target.dtype)
+        target[0, :, at] = product[:rows]
+        target[1, :, at] = product[rows:]
+
+
+def feed_back_rest(
+    grad_gate_up, weights, active, down, values, upstream, gain, number, name
+):
     rows, width = values.shape
+    count, both_rows, units = grad_gate_up.shape
     cut = rows // 2
 
-    def kernel(part, values, upstream, gain, result, gain_grad, out, *scratch):
-        (total, low), sems = (
-            scratch[SUM_SCRATCH : SUM_SCRATCH + 2],
-            scratch[SUM_SCRATCH + 2 :],
+    def kernel(
+        grad, weights, active, down, values, upstream, gain, result, gain_grad, out, branch, *scratch
+    ):
+        (grad_v, weights_v, active_v, down_v, values_v, upstream_v, parts, total, low), rest = (
+            scratch[:9],
+            scratch[9:],
         )
-        steps, from_tp, from_near = plan_sum(part, total, scratch[:SUM_SCRATCH], cut)
+        (load_sem, store_sem), rest = rest[:2], rest[2:]
+        sums, sems = rest[:7], rest[7:]
+        from_tp, from_near = sums[3], sums[4]
+        near, core, tp = spots()
+        members = sequence_order()
+        outgoing = [parts.at[place, half] for place, half in ((0, 1 - tp), (2, 1 - tp), (0, tp), (2, tp))]
+        mine = [parts.at[place, half] for place, half in ((1, 1 - tp), (3, 1 - tp), (1, tp), (3, tp))]
+        steps, (send_far, send_tp, send_near) = plan_sum(outgoing, mine, (), total, sums, cut)
         onward = plan_gather(low, out, *sems, cut=cut)
+        fetch = [
+            pltpu.make_async_copy(grad.at[member], grad_v.at[place % 2], load_sem.at[place])
+            for place, member in enumerate(members)
+        ]
+        fetch += [
+            pltpu.make_async_copy(source, target, load_sem.at[4 + place])
+            for place, (source, target) in enumerate(
+                (
+                    (weights, weights_v),
+                    (values, values_v),
+                    (upstream, upstream_v),
+                    (active, active_v),
+                    (down, down_v),
+                )
+            )
+        ]
+        for place in (0, 4, 1, 5, 6, 7, 8):
+            fetch[place].start()
         greet(NEIGHBOURS)
-        for step in steps:
-            step()
+        fetch[4].wait()
+        for place in range(count):
+            fetch[place].wait()
+            halves_times(grad_v[place % 2], weights_v, parts.at[place], rows)
+            if place + 2 < count:
+                fetch[place + 2].start()
+            if place == 0:
+                steps[0]((0, 2))
+            elif place == 1:
+                send_far()
+                send_near()
+            elif place == 2:
+                steps[0]((1, 3))
+        send_tp()
+        steps[2]()
+        fetch[5].wait()
+        fetch[6].wait()
         gain_grad[...] = jnp.zeros_like(gain_grad)
+        steps[3]()
 
         def finish(at):
             grad = total[at] + read(from_tp, at) + read(from_near, at)
-            back, by_gain = norm_back(read(values, at), gain[...], grad)
+            back, by_gain = norm_back(values_v[at], gain[...], grad)
             gain_grad[...] += by_gain.reshape(CHUNK // 8, 8, width).sum(axis=0)
-            value = read(upstream, at) + back
-            result[at] = value
+            value = read(upstream_v, at) + back
+            total[at] = value
             low[at] = value.astype(jnp.bfloat16)
 
         row_loop(rows, finish)
-        for step in onward:
-            step()
-
-    result, gain_grad, full = pl.pallas_call(
+        onward[0]()
+        stores = [pltpu.make_async_copy(total, result, store_sem.at[count])]
+        stores[0].start()
+        fetch[7].wait()
+        fetch[8].wait()
+        for place in range(count):
+            halves_times(active_v[place], down_v, parts.at[place], rows)
+            store = pltpu.make_async_copy(parts.at[place], branch.at[place], store_sem.at[place])
+            store.start()
+            stores.append(store)
+            if place == 1:
+                onward[1]()
+        onward[2]()
+        onward[3]()
+        for store in stores:
+            store.wait()
+
+    low_type = jnp.bfloat16
+    result, gain_grad, full, branch = pl.pallas_call(
         kernel,
         name=name,
         out_shape=(
             jax.ShapeDtypeStruct((rows, width), jnp.float32),
             jax.ShapeDtypeStruct((8, width), jnp.float32),
             layer_rows(rows, width),
+            jax.ShapeDtypeStruct((count, 2, rows, width), low_type),
         ),
-        in_specs=[anywhere()] + [in_vmem()] * 3,
-        out_specs=(in_vmem(), in_vmem(), anywhere()),
-        scratch_shapes=sum_scratch(rows, width, cut)
-        + [pltpu.VMEM((rows, width), jnp.float32), pltpu.VMEM((rows, width), jnp.bfloat16)]
+        in_specs=[anywhere()] * 6 + [in_vmem()],
+        out_specs=(anywhere(), in_vmem(), anywhere(), anywhere()),
+        scratch_shapes=[
+            pltpu.VMEM((2, both_rows, units), low_type),
+            pltpu.VMEM(weights.shape, low_type),
+            pltpu.VMEM(active.shape, low_type),
+            pltpu.VMEM(down.shape, low_type),
+            pltpu.VMEM((rows, width), values.dtype),
+            pltpu.VMEM((rows, width), upstream.dtype),
+            pltpu.VMEM((count, 2, rows, width), low_type),
+            pltpu.VMEM((rows, width), jnp.float32),
+            pltpu.VMEM((rows, width), low_type),
+            pltpu.SemaphoreType.DMA((9,)),
+            pltpu.SemaphoreType.DMA((count + 1,)),
+        ]
+        + sum_scratch(rows, width, cut, fetched=False)
         + gather_scratch(),
         compiler_params=params(number),
-        cost_estimate=cost_of(100),
-    )(spread(part, rows), values, upstream, gain.reshape(1, width))
-    return result, gain_grad.sum(axis=0), full.reshape(-1, width)
+        cost_estimate=cost_of(105),
+    )(grad_gate_up, weights, active, down, values, upstream, gain.reshape(1, width))
+    return result, gain_grad.sum(axis=0), full.reshape(-1, width), branch.reshape(-1, width)
 
 
 def norm_back_last(part, values, upstream, gain, extra, number, name):
     rows, width = values.shape
     extras = len(extra)
+    cut = balanced(rows, crossing(extra, width))
 
     def kernel(part, values, upstream, gain, *rest):
         pieces, (result, gain_grad) = rest[:extras], rest[extras : extras + 2]
         mixed, rest = rest[extras + 2 : 2 * extras + 2], rest[2 * extras + 2 :]
         total, sems = rest[SUM_SCRATCH], rest[SUM_SCRATCH + 1 :]
-        steps, from_tp, from_near = plan_sum(part, total, rest[:SUM_SCRATCH], 0)
+        steps, from_tp, from_near = plan_sum_of(part, total, rest[:SUM_SCRATCH], cut)
         copies = plan_exchanges(pieces, mixed, sems)
         greet(EVERYONE_NEAR)
         steps[0]()
@@ -534,7 +645,7 @@
         + tuple(like(piece) for piece in extra),
         in_specs=[anywhere()] + [in_vmem()] * 3 + [anywhere()] * extras,
         out_specs=(in_vmem(), in_vmem()) + (anywhere(),) * extras,
-        scratch_shapes=sum_scratch(rows, width, 0)
+        scratch_shapes=sum_scratch(rows, width, cut)
         + [pltpu.VMEM((rows, width), jnp.float32)]
         + exchange_scratch() * extras,
         compiler_params=params(number),
@@ -681,18 +792,19 @@
         ).astype(out.dtype)
 
 
-def attend(normed, weights, cotangent, extra, group_length, cos_full, sin_full, gains, heads, number):
+def attend(normed, weights, cotangent, extra, group_length, cos_full, sin_full, gains, heads, early, number):
     count, rows, width = normed.shape
     wide = (heads + 2) * HD
     extras = len(extra)
     own_rows = cotangent.shape[0]
+    cut = balanced(early, crossing(extra, width))
 
     def kernel(lengths, normed, weights, cos_ref, sin_ref, gains, own, *rest):
         pieces, rest = rest[:extras], rest[extras:]
         (proj, out, logs, branch, gathered), rest = rest[:5], rest[5:]
         mixed, (queries, keys, values), sems = rest[:extras], rest[extras : extras + 3], rest[extras + 3 :]
         sequence = pl.program_id(0)
-        steps = plan_gather(own, gathered, *sems[:3], cut=own_rows // 2)
+        steps = plan_gather(own, gathered, *sems[:3], cut=cut, rows=early)
         copies = plan_exchanges(pieces, mixed, sems[3:])
 
         @pl.when(sequence == 0)
@@ -780,32 +892,50 @@
         compiler_params=params(number),
         cost_estimate=cost_of(50),
     )(group_length, normed, weights, cos_full, sin_full, gains, cotangent, *extra)
-    return outs[:4] + (outs[4].reshape(-1, width),) + tuple(outs[5:])
+    return outs
 
 
 def attend_back(
-    projected, grad_attn, logs, weights, part, hidden, group_length, cos_full, sin_full, gains, heads, number
+    projected,
+    grad_attn,
+    logs,
+    weights,
+    part,
+    hidden,
+    extra,
+    group_length,
+    cos_full,
+    sin_full,
+    gains,
+    heads,
+    number,
 ):
     count, rows, wide = projected.shape
     own_rows, width = hidden.shape
-    cut = own_rows // 2
+    extras = len(extra)
+    cut = balanced(own_rows, crossing(extra, width))
 
     def kernel(
         lengths, proj, grad, logs, weights, cos_ref, sin_ref, gains, part, hidden, *rest
     ):
+        pieces, rest = rest[:extras], rest[extras:]
         (out, gain_grad, back_part, output), rest = rest[:4], rest[4:]
+        mixed, rest = rest[:extras], rest[extras:]
         (queries, keys, values, grad_att, grad_q, grad_k, grad_v, total, held, held_sem), rest = (
             rest[:10],
             rest[10:],
         )
         sequence = pl.program_id(0)
-        steps, from_tp, from_near = plan_sum(part, total, rest, cut)
+        steps, from_tp, from_near = plan_sum_of(part, total, rest[:SUM_SCRATCH], cut)
+        copies = plan_exchanges(pieces, mixed, rest[SUM_SCRATCH:])
         fetch = pltpu.make_async_copy(hidden, held, held_sem)
 
         @pl.when(sequence == 0)
         def _():
-            greet(NEIGHBOURS)
+            greet(EVERYONE_NEAR)
             steps[0]()
+            for copy in copies:
+                copy.start()
             fetch.start()
             gain_grad[...] = jnp.zeros_like(gain_grad)
 
@@ -860,11 +990,11 @@
         settle(heads, 1, grad_k[...] * (HD ** (-0.5)))
         out[0, :, columns(heads + 1)] = grad_v[...].astype(jnp.bfloat16)
 
-        @pl.when(sequence == 2)
+        across_columns(out[0], weights, 0, wide, back_part)
+
+        @pl.when(sequence == 1)
         def _():
             steps[2]()
-
-        across_columns(out[0], weights, 0, wide, back_part)
 
         @pl.when(sequence == count - 1)
         def _():
@@ -876,6 +1006,8 @@
                 output[at] = (held[at] + value).astype(jnp.bfloat16)
 
             row_loop(own_rows, finish)
+            for copy in copies:
+                copy.wait()
 
     return pl.pallas_call(
         kernel,
@@ -886,7 +1018,8 @@
             jax.ShapeDtypeStruct((2, 8, HD), jnp.float32),
             jax.ShapeDtypeStruct((count, rows, width), jnp.bfloat16),
             jax.ShapeDtypeStruct((own_rows, width), jnp.bfloat16),
-        ),
+        )
+        + tuple(like(piece) for piece in extra),
         in_specs=[
             pl.BlockSpec(memory_space=pltpu.SMEM),
             per_sequence(rows, wide),
@@ -898,13 +1031,15 @@
             whole(2, HD),
             anywhere(),
             anywhere(),
-        ],
+        ]
+        + [anywhere()] * extras,
         out_specs=(
             per_sequence(rows, wide),
             pl.BlockSpec((2, 8, HD), lambda s: (0, 0, 0)),
             per_sequence(rows, width),
             pl.BlockSpec((own_rows, width), lambda s: (0, 0)),
-        ),
+        )
+        + (anywhere(),) * extras,
         scratch_shapes=[
             pltpu.VMEM((heads, rows, HD), jnp.bfloat16),
             pltpu.VMEM((rows, HD), jnp.bfloat16),
@@ -917,76 +1052,211 @@
             pltpu.VMEM((own_rows, width), jnp.float32),
             pltpu.SemaphoreType.DMA,
         ]
-        + sum_scratch(own_rows, width, cut),
+        + sum_scratch(own_rows, width, cut)
+        + exchange_scratch() * extras,
         compiler_params=params(number),
         cost_estimate=cost_of(50),
     )(
-        group_length, projected, grad_attn, logs, weights, cos_full, sin_full, gains, spread(part, own_rows), hidden
-    )
-
-
-def adam_rows(weight, moment, square, pieces, factor, widths):
-    rows, total = weight.shape
-    height = 16
-
-    def kernel(weight, moment, square, pieces, factor, new, one, two, low):
-        scale = factor[0:1, 0:1]
-        for member in range(TEAM):
-            first, inside = 0, 0
-            for width in widths:
-                share = width // TEAM
-                at = pl.ds(first + member * share, share)
-                gradient = pieces[member, :, inside : inside + share].astype(jnp.float32)
-                value, one[:, at], two[:, at] = adam_update(
-                    weight[:, at], gradient, moment[:, at], square[:, at], scale, weight_decay, learn_rate
-                )
-                new[:, at] = value
-                low[:, at] = value.astype(jnp.bfloat16)
-                first += width
-                inside += share
-
-    block = pl.BlockSpec((height, total), lambda s: (s, 0))
+        group_length,
+        projected,
+        grad_attn,
+        logs,
+        weights,
+        cos_full,
+        sin_full,
+        gains,
+        spread(part, own_rows),
+        hidden,
+        *extra,
+    )
+
+
+def feed(normed, weights, cotangent, gathered, early, number):
+    count, rows, width = normed.shape
+    units = weights.shape[1] // 2
+    late = cotangent.shape[0] - early
+
+    def kernel(normed, weights, own, _, product, active, out, *sems):
+        steps = plan_gather(
+            own, out, *sems, cut=balanced(late, 0), base=early, rows=late
+        )
+        sequence = pl.program_id(0)
+
+        @pl.when(sequence == 0)
+        def _():
+            greet(NEIGHBOURS)
+            steps[0]()
+
+        for start in range(0, units, 256):
+            gate_at, up_at = pl.ds(start, 256), pl.ds(units + start, 256)
+            gate = jnp.dot(normed[0], weights[:, gate_at], preferred_element_type=jnp.float32)
+            up = jnp.dot(normed[0], weights[:, up_at], preferred_element_type=jnp.float32)
+            product[0, :, gate_at] = gate
+            product[0, :, up_at] = up
+            active[0, :, gate_at] = swish_product(gate, up).astype(jnp.bfloat16)
+
+        for place in (1, 2, 3):
+
+            @pl.when(sequence == count - 4 + place)
+            def _(place=place):
+                steps[place]()
+
     return pl.pallas_call(
         kernel,
-        name="adam_rows",
-        grid=(rows // height,),
-        out_shape=(like(weight),) * 3 + (jax.ShapeDtypeStruct(weight.shape, jnp.bfloat16),),
+        name="feed",
+        grid=(count,),
+        out_shape=(
+            jax.ShapeDtypeStruct((count, rows, 2 * units), jnp.float32),
+            jax.ShapeDtypeStruct((count, rows, units), jnp.bfloat16),
+            like(gathered),
+        ),
         in_specs=[
-            block,
-            block,
-            block,
-            pl.BlockSpec((TEAM, height, pieces.shape[2]), lambda s: (0, s, 0)),
-            whole(8, HD),
+            per_sequence(rows, width),
+            whole(*weights.shape),
+            anywhere(),
+            anywhere(),
         ],
-        out_specs=(block,) * 4,
-        compiler_params=pltpu.CompilerParams(vmem_limit_bytes=VMEM_LIMIT),
-        cost_estimate=cost_of(rows * total * 28 / 3.4e6),
-    )(weight, moment, square, pieces, factor)
-
-
-def adam_columns(weight, moment, square, pieces, factor):
-    rows, total = weight.shape
-    share = rows // TEAM
-
-    def kernel(weight, moment, square, pieces, factor, new, one, two, low):
-        gradient = pieces[0].astype(jnp.float32).T
-        value, one[...], two[...] = adam_update(
-            weight[...], gradient, moment[...], square[...], factor[0:1, 0:1], weight_decay, learn_rate
-        )
-        new[...] = value
-        low[...] = value.astype(jnp.bfloat16)
-
-    block = pl.BlockSpec((share, total), lambda s: (s, 0))
+        out_specs=(per_sequence(rows, 2 * units), per_sequence(rows, units), anywhere()),
+        scratch_shapes=gather_scratch(),
+        input_output_aliases={3: 2},
+        compiler_params=params(number),
+        cost_estimate=cost_of(28),
+    )(normed, weights, cotangent, gathered)
+
+
+def feed_back(grads, weights, product):
+    count, rows, width = grads.shape
+    units = weights.shape[1]
+
+    def kernel(grads, weights, product, out):
+        for start in range(0, units, 256):
+            gate_at, up_at = pl.ds(start, 256), pl.ds(units + start, 256)
+            grad = jnp.dot(grads[0], weights[:, gate_at], preferred_element_type=jnp.float32)
+            gate, up = product[0, :, gate_at], product[0, :, up_at]
+            share = jax.nn.sigmoid(gate)
+            by_gate = grad * up * share * (1.0 + gate * (1.0 - share))
+            out[0, :, gate_at] = by_gate.astype(jnp.bfloat16)
+            out[0, :, up_at] = (grad * gate * share).astype(jnp.bfloat16)
+
     return pl.pallas_call(
         kernel,
-        name="adam_columns",
-        grid=(TEAM,),
-        out_shape=(like(weight),) * 3 + (jax.ShapeDtypeStruct(weight.shape, jnp.bfloat16),),
-        in_specs=[block, block, block, per_sequence(*pieces.shape[1:]), whole(8, HD)],
-        out_specs=(block,) * 4,
+        name="feed_back",
+        grid=(count,),
+        out_shape=jax.ShapeDtypeStruct((count, rows, 2 * units), jnp.bfloat16),
+        in_specs=[
+            per_sequence(rows, width),
+            whole(*weights.shape),
+            per_sequence(rows, 2 * units),
+        ],
+        out_specs=per_sequence(rows, 2 * units),
         compiler_params=pltpu.CompilerParams(vmem_limit_bytes=VMEM_LIMIT),
-        cost_estimate=cost_of(rows * total * 28 / 3.4e6),
-    )(weight, moment, square, pieces, factor)
+        cost_estimate=cost_of(18),
+    )(grads, weights, product)
+
+
+def adam_all(sets, factor):
+    jobs = []
+    for weight, _, _, pieces, widths in sets:
+        rows = weight.shape[0]
+        height = rows // TEAM if widths is None else max(CHUNK, rows // 4)
+        jobs.append((height, rows // height, widths))
+    count = sum(job[1] for job in jobs)
+    total = len(sets)
+
+    def kernel(*refs):
+        inputs, factor, outputs = refs[: 4 * total], refs[4 * total], refs[4 * total + 1 : 8 * total + 1]
+        held = refs[8 * total + 1 : 13 * total + 1]
+        piece_sem, in_sem, out_sem = refs[13 * total + 1 :]
+        scale = factor[0:1, 0:1]
+        loads, stores = [], []
+        for place in range(total):
+            load = pltpu.make_async_copy(
+                inputs[4 * place + 3], held[5 * place + 3], piece_sem.at[place]
+            )
+            load.start()
+            loads.append(load)
+        work, slot = [], 0
+        for place, (height, steps, widths) in enumerate(jobs):
+            for step in range(steps):
+                at = pl.ds(step * height, height)
+                arrive = []
+                for kind in range(3):
+                    copy = pltpu.make_async_copy(
+                        inputs[4 * place + kind].at[at],
+                        held[5 * place + kind].at[at],
+                        in_sem.at[3 * slot + kind],
+                    )
+                    copy.start()
+                    arrive.append(copy)
+                work.append((place, step, at, slot, arrive))
+                slot += 1
+        for place, step, at, slot, arrive in work:
+            height, _, widths = jobs[place]
+            weight, moment, square, pieces, low = held[5 * place : 5 * place + 5]
+            if step == 0:
+                loads[place].wait()
+            for copy in arrive:
+                copy.wait()
+
+            def update(rows, across, gradient):
+                where = (rows, across)
+                value, one, two = adam_update(
+                    weight[where], gradient, moment[where], square[where], scale, weight_decay, learn_rate
+                )
+                weight[where], moment[where], square[where] = value, one, two
+                low[where] = value.astype(jnp.bfloat16)
+
+            if widths is None:
+                update(at, slice(None), pieces[step].astype(jnp.float32).T)
+            else:
+
+                @pl.loop(0, height // CHUNK)
+                def _(row):
+                    rows = pl.ds(pl.multiple_of(step * height + row * CHUNK, CHUNK), CHUNK)
+                    for member in range(TEAM):
+                        first, inside = 0, 0
+                        for width in widths:
+                            share = width // TEAM
+                            update(
+                                rows,
+                                pl.ds(first + member * share, share),
+                                pieces[member, rows, pl.ds(inside, share)].astype(jnp.float32),
+                            )
+                            first += width
+                            inside += share
+
+            for kind, source in enumerate((weight, moment, square, low)):
+                copy = pltpu.make_async_copy(
+                    source.at[at], outputs[4 * place + kind].at[at], out_sem.at[4 * slot + kind]
+                )
+                copy.start()
+                stores.append(copy)
+        for copy in stores:
+            copy.wait()
+
+    args, shapes, scratch, moved = [], [], [], 0
+    for weight, moment, square, pieces, _ in sets:
+        args += [weight, moment, square, pieces]
+        low = jax.ShapeDtypeStruct(weight.shape, jnp.bfloat16)
+        shapes += [like(weight)] * 3 + [low]
+        scratch += [pltpu.VMEM(each.shape, each.dtype) for each in (weight, moment, square, pieces, low)]
+        moved += weight.size * 28
+    outs = pl.pallas_call(
+        kernel,
+        name="adam_all",
+        out_shape=tuple(shapes),
+        in_specs=[anywhere()] * (4 * total) + [in_vmem()],
+        out_specs=(anywhere(),) * (4 * total),
+        scratch_shapes=scratch
+        + [
+            pltpu.SemaphoreType.DMA((total,)),
+            pltpu.SemaphoreType.DMA((3 * count,)),
+            pltpu.SemaphoreType.DMA((4 * count,)),
+        ],
+        compiler_params=pltpu.CompilerParams(vmem_limit_bytes=VMEM_LIMIT),
+        cost_estimate=cost_of(moved / 3.4e6),
+    )(*args, factor)
+    return [outs[4 * place : 4 * place + 4] for place in range(total)]
 
 
 def split_columns(values, widths):
@@ -1112,14 +1382,24 @@
 
     residual_in = inputs.astype(jnp.float32)
     normed_attn = residual_in * rms_scale(residual_in) * attn_gain
-    normed_attn, first_mixed = lax.optimization_barrier(
-        (normed_attn.astype(jnp.bfloat16), first_mixed)
+    grad_low = jnp.where(valid_rows, cotangent, jnp.zeros_like(cotangent))
+    normed_attn, first_mixed, grad_low, down_pieces, cos_full, sin_full = (
+        lax.optimization_barrier(
+            (
+                normed_attn.astype(jnp.bfloat16),
+                first_mixed,
+                grad_low,
+                down_pieces,
+                cos_full,
+                sin_full,
+            )
+        )
     )
     normed_attn, gate_up_mixed = gather_rows(
         normed_attn, (gate_up_pieces,), 0, "gather_inputs"
     )
     gate_up_full = gather_outer(gate_up_mixed)
-    grad_low = jnp.where(valid_rows, cotangent, jnp.zeros_like(cotangent))
+    early = half_rows * 3 // 5 // CHUNK * CHUNK
     projected, attended, logs, attn_branch, grad_all, down_mixed = attend(
         normed_attn.reshape(TEAM, row_count, D),
         first_full,
@@ -1130,43 +1410,38 @@
         sin_full,
         head_gains,
         heads,
+        early,
         1,
     )
     down_full = gather_outer(down_mixed)
     attended = attended.reshape(-1, heads * HD)
     hidden, normed_mlp = branch_and_norm(attn_branch, inputs, mlp_gain, 2, "branch_and_norm")
-    gate_up = times(normed_mlp, gate_up_full)
-    gate_part = gate_up[:, :hidden_units]
-    up_part = gate_up[:, hidden_units:]
-    activated = swish_product(gate_part, up_part).astype(jnp.bfloat16)
-    mlp_part = times_across(activated, down_full).astype(jnp.bfloat16)
-
-    grad_down = over_rows(grad_all, activated).astype(jnp.bfloat16)
-    grad_all, grad_down = after(grad_all, grad_down)
+    gate_up, activated, grad_all = feed(
+        normed_mlp.reshape(TEAM, row_count, D), gate_up_full, grad_low, grad_all, early, 8
+    )
+    grad_down = over_rows(grad_all.reshape(-1, D), activated.reshape(-1, hidden_units))
+    grad_all, grad_down = after(grad_all, grad_down.astype(jnp.bfloat16))
     down_sum = sum_weight(grad_down)
-    grad_activated = times(grad_all, down_full)
-    swish_pull = jax.vjp(swish_product, gate_part, up_part)[1]
-    grad_gate, grad_up = swish_pull(grad_activated)
-    grad_gate_up = jnp.concatenate([grad_gate, grad_up], axis=1).astype(jnp.bfloat16)
-    grad_normed_mlp = times_across(grad_gate_up, gate_up_full).astype(jnp.bfloat16)
-    grad_gate_up_weight = over_rows(normed_mlp, grad_gate_up).astype(jnp.bfloat16)
-    grad_normed_mlp, grad_gate_up_weight, down_sum = lax.optimization_barrier(
-        (grad_normed_mlp, grad_gate_up_weight, down_sum)
+    grad_gate_up = feed_back(grad_all.reshape(TEAM, row_count, D), down_full, gate_up)
+    grad_gate_up_weight = over_rows(normed_mlp, grad_gate_up.reshape(-1, 2 * hidden_units))
+    grad_gate_up, grad_gate_up_weight, down_sum = lax.optimization_barrier(
+        (grad_gate_up, grad_gate_up_weight.astype(jnp.bfloat16), down_sum)
     )
     gate_up_sum = sum_weight(grad_gate_up_weight)
-    grad_hidden, grad_mlp_gain, grad_attn = norm_back_gather(
-        grad_normed_mlp, hidden, grad_low, mlp_gain, 3, "norm_back_mlp"
+    grad_hidden, grad_mlp_gain, grad_attn, mlp_part = feed_back_rest(
+        grad_gate_up, gate_up_full, activated, down_full, hidden, grad_low, mlp_gain, 3, "feed_back_rest"
     )
     grad_out_weight = over_rows(grad_attn, attended).astype(jnp.bfloat16)
     grad_out_weight, gate_up_sum = after(grad_out_weight, gate_up_sum)
     out_sum = sum_weight(grad_out_weight)
-    grad_projected, grad_head_gains, grad_normed_attn, output = attend_back(
+    grad_projected, grad_head_gains, grad_normed_attn, output, down_mixed = attend_back(
         projected,
         grad_attn.reshape(TEAM, row_count, D),
         logs,
         first_full,
         mlp_part,
         hidden,
+        (team_pieces(down_sum),),
         group_length,
         cos_full,
         sin_full,
@@ -1178,12 +1453,12 @@
     grad_qkv_weight = over_rows(normed_attn, grad_projected).astype(jnp.bfloat16)
     grad_qkv_weight, out_sum = after(grad_qkv_weight, out_sum)
     qkv_sum = sum_weight(grad_qkv_weight)
-    input_grad, grad_attn_gain, down_mixed, gate_up_mixed, out_mixed = norm_back_last(
+    input_grad, grad_attn_gain, gate_up_mixed, out_mixed = norm_back_last(
         grad_normed_attn,
         inputs,
         grad_hidden,
         attn_gain,
-        (team_pieces(down_sum), team_pieces(gate_up_sum), team_pieces(out_sum)),
+        (team_pieces(gate_up_sum), team_pieces(out_sum)),
         4,
         "norm_back_attn",
     )
@@ -1202,17 +1477,19 @@
     )
     gain_grad = packed.reshape(-1)[:gain_count]
     grad_norm, factor = norm_tile[0, 0], factor_tile[0, 0]
-    new_qkv, new_qkv_one, new_qkv_two, qkv_copy = adam_rows(
-        qkv_weight, qkv_moment, qkv_square, qkv_mixed, factor_tile, qkv_widths
-    )
-    new_out, new_out_one, new_out_two, out_copy = adam_columns(
-        out_weight, out_moment, out_square, out_mixed, factor_tile
-    )
-    new_gate_up, new_gate_up_one, new_gate_up_two, gate_up_copy = adam_rows(
-        gate_up_weight, gate_up_moment, gate_up_square, gate_up_mixed, factor_tile, gate_up_widths
-    )
-    new_down, new_down_one, new_down_two, down_copy = adam_columns(
-        down_weight, down_moment, down_square, down_mixed, factor_tile
+    (
+        (new_gate_up, new_gate_up_one, new_gate_up_two, gate_up_copy),
+        (new_down, new_down_one, new_down_two, down_copy),
+        (new_out, new_out_one, new_out_two, out_copy),
+        (new_qkv, new_qkv_one, new_qkv_two, qkv_copy),
+    ) = adam_all(
+        [
+            (gate_up_weight, gate_up_moment, gate_up_square, gate_up_mixed, gate_up_widths),
+            (down_weight, down_moment, down_square, down_mixed, None),
+            (out_weight, out_moment, out_square, out_mixed, None),
+            (qkv_weight, qkv_moment, qkv_square, qkv_mixed, qkv_widths),
+        ],
+        factor_tile,
     )
     new_gains, new_gains_one, new_gains_two = adam_update(
         norm_gains, gain_grad, gains_moment, gains_square, factor, 0.0, gain_rate

time: 710 us -> 651 us (0.917)
  matrix products: 134 us -> 54.2 us
  waiting for transfers between devices: 0.26 us -> 20.9 us
  Pallas kernels: 514 us -> 523 us
    dot_general x8 -> x4, matrix products: 134 us -> 54.2 us  [dot(): lax.dot_general(left, right, ((contract[0], contract[1]), ((), ())), pref...]
    pallas_call x5 -> x4, Pallas kernels: 129 us -> 171 us  [the longest x1 108 us: feed_back_rest(): pl.pallas_call(kernel, name=name, out_shape=(jax.ShapeDtypeStruct((rows,...]
    pallas_call x1, Pallas kernels: 63.1 us -> 40.6 us  [attend(): pl.pallas_call(kernel, name='attend', grid=(count,), out_shape=(jax.Shape...]
    reduce_scatter x4, waiting for transfers between devices: 0.1 us -> 20.7 us  [sum_weight(): return lax.psum_scatter(gradient, 'outer', scatter_dimension=0, tiled=True)]
  transfers between devices with their start and end apart: 7 -> 7, of which waited for: 1 -> 1; matrix products, arithmetic and copies ran while one was open for 22% -> 11% of each run, Pallas kernels for 66% -> 75%
where the time goes in v5:
time: 651 us; the launch traced here: 644 us
  Pallas kernels  523 us (80%)
  matrix products  54.2 us (8%)
  waiting for transfers between devices  20.9 us (3%)
  other arithmetic  19.7 us (3%)
  between operations  17.4 us (3%)
  local copies, waits for them, and re-layouts  7.99 us (1%)
    pallas_call x1, Pallas kernels, feed_back_rest(): pl.pallas_call(kernel, name=name, out_shape=(jax.ShapeDtypeStruct((rows,...  108 us
    pallas_call x1, Pallas kernels, branch_and_norm(): pl.pallas_call(kernel, name=name, out_shape=(jax.ShapeDtypeStruct((rows,...  101 us
    pallas_call x1, Pallas kernels, norm_back_last(): pl.pallas_call(kernel, name=name, out_shape=(jax.ShapeDtypeStruct((rows,...  65.6 us
    pallas_call x1, Pallas kernels, attend_back(): pl.pallas_call(kernel, name='attend_back', grid=(count,), out_shape=(jax....  60.7 us
    pallas_call x1, Pallas kernels, gather_rows(): pl.pallas_call(kernel, name=name, out_shape=(layer_rows(rows, width),) +...  58 us
    dot_general x4, matrix products, dot(): lax.dot_general(left, right, ((contract[0], contract[1]), ((), ())), pref...  54.2 us
    pallas_call x1, Pallas kernels, attend(): pl.pallas_call(kernel, name='attend', grid=(count,), out_shape=(jax.Shape...  40.6 us
    pallas_call x1, Pallas kernels, feed(): pl.pallas_call(kernel, name='feed', grid=(count,), out_shape=(jax.ShapeDt...  28.2 us
  transfers between devices with their start and end apart: 7, of which 1 were waited for; matrix products, arithmetic and copies ran while one was open for 11% of the time, Pallas kernels for 75%

profile of v5, /device:TPU:0, one launch (start us, length us, event | category | flops | bytes accessed | tf_op | source)
XLA Modules:
  0.0 644.0 jit_solution(6621039921574555464)
XLA Ops:
  7.2 0.0 all-gather.4.cloned.1.call-start
  7.2 1.3 convert_element_type.48
  8.7 0.1 copy.44
  8.9 0.9 maximum_maximum_fusion.pieces
  9.9 12.9 %exchange_first.1 = bf16[4,128,768]{2,1,0:T(8,128)(2,1)} custom-call(bf16[4,128,768]{2,1,0:T(8,128)(2,1)} %maximum_maximum_fusion.pieces), custom_call_target="tpu_custom_call" | custom-call | bytes 40800000 | tf_op jit(solution)/shard_map/exchange_first/pallas_call | solution.py:368
  22.8 0.0 all-gather.4.cloned.1.call-update
  22.8 0.0 all-gather.6.cloned.1.call-start
  22.9 0.3 copy.45
  23.2 0.2 select_reduce_fusion.lengths
  23.4 0.6 dynamic_slice.4
  24.0 0.7 add_compare_fusion
  24.6 1.2 fusion.5
  25.9 1.1 pad_maximum_fusion.2
  27.0 0.1 slice_bitcast_fusion.3
  27.0 1.0 pad_maximum_fusion.1.rest_0_
  28.0 0.4 fusion
  28.4 0.6 fusion.14
  29.0 1.2 broadcast_select_fusion.own.upstream
  30.2 1.4 fusion.2.own
  31.6 0.2 convert_element_type.51
  31.8 0.1 fusion.11
  31.9 0.1 maximum_bitcast_fusion
  32.0 0.1 maximum_bitcast_fusion.2
  32.1 1.3 pad_maximum_fusion.rest_0_
  33.4 58.0 %gather_inputs.1 = (bf16[2,2,2,320,2048]{4,3,2,1,0:T(8,128)(2,1)}, bf16[4,128,1536]{2,1,0:T(8,128)(2,1)}) custom-call(bf16[320,2048]{1,0:T(8,128)(2,1)} %fusion.2.own, bf16[4,128,1536]{2,1,0:T(8,128)(2,1)} %pad_maximum_fusion.rest_0_), custom_call_target="tpu_custom_call" | custom-call | bytes 204000000 | tf_op jit(solution)/shard_map/gather_inputs/pallas_call | solution.py:399
  91.4 0.0 all-gather.6.cloned.1.call-update
  91.4 0.0 all-gather.8.cloned.1.call-start
  91.5 0.6 slice_bitcast_fusion.8.gains
  92.0 40.6 %attend.1 = (f32[4,640,512]{2,1,0:T(8,128)}, bf16[4,640,256]{2,1,0:T(8,128)(2,1)}, f32[4,640,128]{2,1,0:T(8,128)}, bf16[4,640,2048]{2,1,0:T(8,128)(2,1)}, bf16[2...) custom-call(s32[4]{0:T(128)} %copy-done.16, bf16[4,640,2048]{2,1,0:T(8,128)(2,1)} %bitcast.92, ...), custom_call_target="tpu_custom_call" | custom-call | bytes 170000000 | tf_op jit(solution)/shard_map/attend/pallas_call | solution.py:855
  132.6 0.0 all-gather.8.cloned.1.call-update
  132.6 0.2 reduce-scatter.5.cloned.1.call-start
  132.8 101.5 %branch_and_norm.1 = (f32[320,2048]{1,0:T(8,128)}, bf16[2,2,2,320,2048]{4,3,2,1,0:T(8,128)(2,1)}) custom-call(bf16[2,2,2,320,2048]{4,3,2,1,0:T(8,128)(2,1)} %bitcast.97, bf16[320,2048]{1,0:T(8,128)(2,1)} %values.1, f32[1,2048]{1,0:T(1,128)} %bitcast.109), custom_call_target="tpu_custom_call" | custom-call | bytes 323000000 | tf_op jit(solution)/shard_map/branch_and_norm/pallas_call | solution.py:448
  234.3 0.0 all-gather.6.cloned.1.call-done.weights
  234.3 28.2 %feed.1 = (f32[4,640,1536]{2,1,0:T(8,128)}, bf16[4,640,768]{2,1,0:T(8,128)(2,1)}, bf16[2,2,2,320,2048]{4,3,2,1,0:T(8,128)(2,1)}) custom-call(bf16[4,640,2048]{2,1,0:T(8,128)(2,1)} %bitcast.89, bf16[2048,1536]{1,0:T(8,128)(2,1)} %all-gather.6.cloned.1.call-done.weights, ...), custom_call_target="tpu_custom_call", output_to_operand_aliasing={{2}: (3, {})} | custom-call | bytes 95200000 | tf_op jit(solution)/shard_map/feed/pallas_call | solution.py:1104
  262.5 13.6 %convolution_convert_fusion.1 = bf16[2048,768]{1,0:T(8,128)(2,1)} fusion(bf16[2560,2048]{1,0:T(8,128)(2,1)} %bitcast.86, bf16[2560,768]{1,0:T(8,128)(2,1)} %bitcast.99), kind=kOutput, calls=%fused_computation.1 | convolution fusion | flops 8054636544 | bytes 17563648 | tf_op jit(solution)/shard_map/dot_general | solution.py:1304
  276.1 0.0 reduce-scatter.7.cloned.1.call-start
  276.2 0.0 all-gather.8.cloned.1.call-done.weights.down
  276.2 17.6 %feed_back.1.grad = bf16[4,640,1536]{2,1,0:T(8,128)(2,1)} custom-call(bf16[4,640,2048]{2,1,0:T(8,128)(2,1)} %bitcast.87, bf16[2048,768]{1,0:T(8,128)(2,1)} %all-gather.8.cloned.1.call-done.weights.down, f32[4,640,1536]{2,1,0:T(8,128)} %get-tuple-element.97.product), custom_call_target="tpu_custom_call" | custom-call | bytes 61200000 | tf_op jit(solution)/shard_map/feed_back/pallas_call | solution.py:1141
  293.8 22.4 %convolution_convert_fusion = bf16[2048,1536]{1,0:T(8,128)(2,1)} fusion(bf16[2560,2048]{1,0:T(8,128)(2,1)} %bitcast.90, bf16[2560,1536]{1,0:T(8,128)(2,1)} %bitcast.88), kind=kOutput, calls=%fused_computation | convolution fusion | flops 16109273088 | bytes 24641536 | tf_op jit(solution)/shard_map/dot_general | solution.py:1304
  316.2 20.7 %reduce-scatter.5.cloned.1.call-done = bf16[512,768]{1,0:T(8,128)(2,1)} async-done(((bf16[2048,768]{1,0:T(8,128)(2,1)}), bf16[512,768]{1,0:T(8,128)(2,1)}) %reduce-scatter.5.cloned.1.call-update) | async-done | bytes 786448 | tf_op jit(solution)/shard_map/reduce_scatter | solution.py:1284
  337.0 0.3 reduce-scatter.9.cloned.1.call-start
  337.2 108.3 %feed_back_rest.1 = (f32[320,2048]{1,0:T(8,128)}, f32[8,2048]{1,0:T(8,128)}, bf16[2,2,2,320,2048]{4,3,2,1,0:T(8,128)(2,1)}, bf16[4,2,320,2048]{3,2,1,0:T(8,128)(2,1)}) custom-call(bf16[4,640,1536]{2,1,0:T(8,128)(2,1)} %feed_back.1.grad, bf16[2048,1536]{1,0:T(8,128)(2,1)} %all-gather.6.cloned.1.call-done.weights, ...), custom_call_target="tpu_custom_call" | custom-call | bytes 357000000 | tf_op jit(solution)/shard_map/feed_back_rest/pallas_call | solution.py:577
  445.6 8.1 %convolution_convert_fusion.3 = bf16[2048,256]{1,0:T(8,128)(2,1)} fusion(bf16[2560,2048]{1,0:T(8,128)(2,1)} %bitcast.94, bf16[2560,256]{1,0:T(8,128)(2,1)S(1)} %bitcast.113), kind=kOutput, calls=%fused_computation.9 | convolution fusion | flops 2684878848 | bytes 12845056 | tf_op jit(solution)/shard_map/dot_general | solution.py:1304
  453.7 0.0 reduce-scatter.9.cloned.1.call-update
  453.7 0.0 reduce-scatter.11.cloned.1.call-start
  453.7 60.7 %attend_back.1 = (bf16[4,640,512]{2,1,0:T(8,128)(2,1)}, f32[2,8,128]{2,1,0:T(8,128)}, bf16[4,640,2048]{2,1,0:T(8,128)(2,1)}, bf16[320,2048]{1,0:T(8,128)(2,1)}, bf16[4,128,768]{2,1,0:T(8,128)(2,1)}) custom-call(s32[4]{0:T(128)} %copy-done.16, f32[4,640,512]{2,1,0:T(8,128)} %get-tuple-element.88.proj, bf16[4,640,2048]{2,1,0:T(8,128)(2,1)} %bitcast.95, ...), custom_call_target="tpu_custom_call" | custom-call | bytes 170000000 | tf_op jit(solution)/shard_map/attend_back/pallas_call | solution.py:1012
  514.4 10.2 %convolution_convert_fusion.2 = bf16[2048,512]{1,0:T(8,128)(2,1)} fusion(bf16[2560,2048]{1,0:T(8,128)(2,1)} %bitcast.93, bf16[2560,512]{1,0:T(8,128)(2,1)} %bitcast.112), kind=kOutput, calls=%fused_computation.5 | convolution fusion | flops 5369757696 | bytes 15204352 | tf_op jit(solution)/shard_map/dot_general | solution.py:1304
  524.6 0.0 reduce-scatter.11.cloned.1.call-update
  524.7 1.0 multiply_reduce_fusion.1
  525.7 0.3 copy-done.3
  526.0 1.4 multiply_reduce_fusion
  527.4 65.6 %norm_back_attn.1 = (bf16[320,2048]{1,0:T(8,128)(2,1)}, f32[8,2048]{1,0:T(8,128)}, bf16[4,128,1536]{2,1,0:T(8,128)(2,1)}, bf16[4,128,256]{2,1,0:T(8,128)(2,1)}) custom-call(bf16[2,2,2,320,2048]{4,3,2,1,0:T(8,128)(2,1)} %bitcast.91, bf16[320,2048]{1,0:T(8,128)(2,1)} %values.1, f32[320,2048]{1,0:T(8,128)} %get-tuple-element.107.upstream, f32[1,2048]{1,0:T(1,128)} %bitcast.108, ...), custom_call_target="tpu_custom_call" | custom-call | bytes 221000000 | tf_op jit(solution)/shard_map/norm_back_attn/pallas_call | solution.py:638
  593.1 0.9 reduce_sum.83
  593.9 0.7 multiply_reduce_fusion.3
  594.7 1.9 multiply_reduce_fusion.2
  599.2 0.6 fusion.6.values
  599.8 13.3 %total_everywhere.1 = (f32[48,128]{1,0:T(8,128)}, f32[8,128]{1,0:T(8,128)}, f32[8,128]{1,0:T(8,128)}, bf16[4,128,512]{2,1,0:T(8,128)(2,1)}) custom-call(f32[48,128]{1,0:T(8,128)} %fusion.6.values, bf16[4,128,512]{2,1,0:T(8,128)(2,1)} %bitcast.103), custom_call_target="tpu_custom_call" | custom-call | tf_op jit(solution)/shard_map/total_everywhere/pallas_call | solution.py:720
  613.1 1.2 slice.147
  614.3 1.2 slice.145
  615.5 2.0 multiply_subtract_fusion
  617.5 16.6 %adam_all.1 = (f32[128,6144]{1,0:T(8,128)}, f32[128,6144]{1,0:T(8,128)}, f32[128,6144]{1,0:T(8,128)}, bf16[128,6144]{1,0:T(8,128)(2,1)}, f32[3072,128]{1,0:T(8,1...) custom-call(f32[128,6144]{1,0:T(8,128)} %refs_0_.1, ...), custom_call_target="tpu_custom_call" | custom-call | bytes 44040192 | tf_op jit(solution)/shard_map/adam_all/pallas_call | solution.py:1244
  634.1 1.1 copy.49
  635.2 0.7 copy-done.7
  635.9 1.1 copy.50
  (55 shorter events, 0.3 us)
Async XLA Ops:
  7.2 1.5 copy-start.5
  7.2 84.8 %all-gather.4.cloned.1.call-start = ((), (), s32[]{:S(2)}) async-start(), calls=%async_computation.4 | async-start | bytes 3932160 | tf_op jit(solution)/shard_map/all_gather | solution.py:1276
  8.9 14.0 %copy-start.2 = (f32[3072,128]{1,0:T(8,128)S(1)}, f32[3072,128]{1,0:T(8,128)}, u32[]{:S(2)}) copy-start(f32[3072,128]{1,0:T(8,128)} %refs_4_.1) | copy-start | bytes 4718596
  9.9 13.3 %copy-start.17 = (s32[16]{0:T(128)S(1)}, s32[16]{0:T(128)}, u32[]{:S(2)}) copy-start(s32[16]{0:T(128)} %param.21) | copy-start | bytes 196
  9.9 13.3 %copy-start.18 = (s32[16]{0:T(128)S(1)}, s32[16]{0:T(128)}, u32[]{:S(2)}) copy-start(s32[16]{0:T(128)} %param.22) | copy-start | bytes 196
  22.8 211.5 %all-gather.6.cloned.1.call-start = ((), (), s32[]{:S(2)}) async-start(), calls=%async_computation.5 | async-start | bytes 7864320 | tf_op jit(solution)/shard_map/all_gather | solution.py:1276
  23.4 4.6 copy-start.16
  25.9 2.1 copy-start
  27.0 1.4 copy-start.11
  27.0 2.0 copy-start.8
  29.0 2.6 copy-start.10
  29.0 2.6 copy-start.1
  91.4 184.8 %all-gather.8.cloned.1.call-start = ((), (), s32[]{:S(2)}) async-start(), calls=%async_computation.6 | async-start | bytes 3932160 | tf_op jit(solution)/shard_map/all_gather | solution.py:1276
  132.6 204.3 %reduce-scatter.5.cloned.1.call-start = ((), (), s32[]{:S(2)}) async-start(), calls=%async_computation.7 | async-start | bytes 3932160 | tf_op jit(solution)/shard_map/reduce_scatter | solution.py:1284
  276.1 177.5 %reduce-scatter.7.cloned.1.call-start = ((), (), s32[]{:S(2)}) async-start(), calls=%async_computation.8 | async-start | bytes 7864320 | tf_op jit(solution)/shard_map/reduce_scatter | solution.py:1284
  337.0 187.6 %reduce-scatter.9.cloned.1.call-start = ((), (), s32[]{:S(2)}) async-start(), calls=%async_computation.9 | async-start | bytes 1310720 | tf_op jit(solution)/shard_map/reduce_scatter | solution.py:1284
  337.2 108.4 %copy-start.19 = (bf16[4,640,256]{2,1,0:T(8,128)(2,1)S(1)}, bf16[4,640,256]{2,1,0:T(8,128)(2,1)}, u32[]{:S(2)}) copy-start(bf16[4,640,256]{2,1,0:T(8,128)(2,1)} %get-tuple-element.108) | copy-start | bytes 3932164
  453.7 141.0 %reduce-scatter.11.cloned.1.call-start = ((), (), s32[]{:S(2)}) async-start(), calls=%async_computation.10 | async-start | bytes 2621440 | tf_op jit(solution)/shard_map/reduce_scatter | solution.py:1284
  514.4 10.2 %copy-start.15 = (f32[2,8,128]{2,1,0:T(8,128)S(1)}, f32[2,8,128]{2,1,0:T(8,128)}, u32[]{:S(2)}) copy-start(f32[2,8,128]{2,1,0:T(8,128)} %get-tuple-element.117) | copy-start | bytes 24580
  514.4 10.2 %copy-start.12 = (f32[8,2048]{1,0:T(8,128)S(1)}, f32[8,2048]{1,0:T(8,128)}, u32[]{:S(2)}) copy-start(f32[8,2048]{1,0:T(8,128)} %get-tuple-element.116) | copy-start | bytes 196612
  514.4 10.3 %copy-start.4 = (bf16[512,768]{1,0:T(8,128)(2,1)S(1)}, bf16[512,768]{1,0:T(8,128)(2,1)}, u32[]{:S(2)}) copy-start(bf16[512,768]{1,0:T(8,128)(2,1)} %reduce-scatter.5.cloned.1.call-done) | copy-start | bytes 2359300
  524.6 1.4 copy-start.3
  527.4 66.5 %copy-start.9 = (bf16[512,256]{1,0:T(8,128)(2,1)S(1)}, bf16[512,256]{1,0:T(8,128)(2,1)}, u32[]{:S(2)}) copy-start(bf16[512,256]{1,0:T(8,128)(2,1)} %reduce-scatter.9.cloned.1.call-done) | copy-start | bytes 786436
  527.4 88.1 %copy-start.13 = (f32[4352]{0:T(1024)S(1)}, f32[4352]{0:T(1024)}, u32[]{:S(2)}) copy-start(f32[4352]{0:T(1024)} %param.32) | copy-start | bytes 52228
  527.4 88.1 %copy-start.14 = (f32[4352]{0:T(1024)S(1)}, f32[4352]{0:T(1024)}, u32[]{:S(2)}) copy-start(f32[4352]{0:T(1024)} %param.37) | copy-start | bytes 52228
  617.5 16.6 %copy-start.6 = (bf16[320,2048]{1,0:T(8,128)(2,1)S(1)}, bf16[320,2048]{1,0:T(8,128)(2,1)}, u32[]{:S(2)}) copy-start(bf16[320,2048]{1,0:T(8,128)(2,1)} %get-tuple-element.210) | copy-start | bytes 3932164
  634.1 1.8 copy-start.7
Sparse Core Ops, SparseCore 0:
  22.9 64.6 all-gather.3
  91.5 115.7 all-gather.5
  208.9 61.7 all-gather.7
  276.2 60.6 reduce-scatter.4
  339.1 110.7 reduce-scatter.6
  453.8 26.5 reduce-scatter.8
  524.7 43.5 reduce-scatter.10

commit v6 on v5

--- a/solution.py
+++ b/solution.py
@@ -326,6 +326,7 @@
 
 
 SUM_SCRATCH = 9
+COST_SHARE = 1e5
 
 
 def params(number):
@@ -336,7 +337,7 @@
 
 def cost_of(microseconds):
     return pl.CostEstimate(
-        flops=0, bytes_accessed=int(microseconds * 3.4e6), transcendentals=0
+        flops=0, bytes_accessed=int(microseconds * COST_SHARE), transcendentals=0
     )
 
 
@@ -651,13 +652,14 @@
         compiler_params=params(number),
         cost_estimate=cost_of(65),
     )(spread(part, rows), values, upstream, gain.reshape(1, width), *extra)
-    return (outs[0], outs[1].sum(axis=0)) + tuple(outs[2:])
-
-
-def total_everywhere(values, pieces, outer_count, number, name):
+    return outs
+
+
+def total_everywhere(values, first, pieces, outer_count, number, name):
     shape = values.shape
-
-    def kernel(values, pieces, out, norm, factor, mixed, layer, outers, send, recv, *sems):
+    width = first.shape[1]
+
+    def kernel(values, first, square_of, pieces, out, norm, factor, mixed, layer, outers, send, recv, *sems):
         near, core, tp = spots()
         outer = lax.axis_index("outer")
         partners = [
@@ -689,7 +691,15 @@
             return copies
 
         mine = near * (CORE * 2) + core * 2 + tp
-        layer[mine] = values[...]
+        row = lax.broadcasted_iota(jnp.int32, shape, 0)
+        column = lax.broadcasted_iota(jnp.int32, shape, 1)
+        flat = square_of[...].astype(jnp.float32)
+        squares = jnp.sum(flat * flat, keepdims=True)
+        squares = jnp.where((row == shape[0] - 8) & (column == 0), squares, 0.0)
+        layer[mine] = values[...] + squares
+        sums = jnp.sum(first[...], axis=0, keepdims=True)
+        for place in range(width // HD):
+            layer[mine, place : place + 1] = sums[:, place * HD : (place + 1) * HD]
         copies = share(layer, mine, 0, 7)
         others = plan_exchange(pieces, mixed, *sems)
         for copy in others:
@@ -706,7 +716,6 @@
         for slot in range(1, outer_count):
             total = total + outers[slot]
         out[...] = total
-        row = lax.broadcasted_iota(jnp.int32, shape, 0)
         squares = jnp.sum(jnp.where(row < shape[0] - 8, total * total, total), keepdims=True)
         root = jnp.sqrt(squares)
         norm[...] = jnp.broadcast_to(root, norm.shape)
@@ -721,7 +730,7 @@
         kernel,
         name=name,
         out_shape=(jax.ShapeDtypeStruct(shape, jnp.float32), tile, tile, like(pieces)),
-        in_specs=[in_vmem(), anywhere()],
+        in_specs=[in_vmem(), in_vmem(), in_vmem(), anywhere()],
         out_specs=(in_vmem(), in_vmem(), in_vmem(), anywhere()),
         scratch_shapes=[
             pltpu.VMEM((8,) + shape, jnp.float32),
@@ -731,7 +740,7 @@
         ]
         + exchange_scratch(),
         compiler_params=params(number),
-    )(values, pieces)
+    )(values, first, pieces.reshape(-1, pieces.shape[2]), pieces)
 
 
 def head_scale(raw, gain, cos_full, sin_full):
@@ -895,14 +904,22 @@
     return outs
 
 
+def team_split(width, outer_count):
+    split = TEAM if width // outer_count % (TEAM * HD) == 0 else 1
+    return split, width // outer_count // split
+
+
 def attend_back(
     projected,
+    normed,
+    attended,
     grad_attn,
     logs,
     weights,
     part,
     hidden,
     extra,
+    outer_count,
     group_length,
     cos_full,
     sin_full,
@@ -915,16 +932,17 @@
     extras = len(extra)
     cut = balanced(own_rows, crossing(extra, width))
 
+    every = wide + heads * HD
+    split, share = team_split(width, outer_count)
+
     def kernel(
-        lengths, proj, grad, logs, weights, cos_ref, sin_ref, gains, part, hidden, *rest
+        lengths, proj, normed, attended, grad, logs, weights, cos_ref, sin_ref, gains, part, hidden, *rest
     ):
         pieces, rest = rest[:extras], rest[extras:]
-        (out, gain_grad, back_part, output), rest = rest[:4], rest[4:]
+        (out, gain_grad, back_part, output, grad_weights), rest = rest[:5], rest[5:]
         mixed, rest = rest[:extras], rest[extras:]
-        (queries, keys, values, grad_att, grad_q, grad_k, grad_v, total, held, held_sem), rest = (
-            rest[:10],
-            rest[10:],
-        )
+        (queries, keys, values, grad_att, grad_q, grad_k, grad_v, summed), rest = rest[:8], rest[8:]
+        (total, held, held_sem), rest = rest[:3], rest[3:]
         sequence = pl.program_id(0)
         steps, from_tp, from_near = plan_sum_of(part, total, rest[:SUM_SCRATCH], cut)
         copies = plan_exchanges(pieces, mixed, rest[SUM_SCRATCH:])
@@ -938,6 +956,7 @@
                 copy.start()
             fetch.start()
             gain_grad[...] = jnp.zeros_like(gain_grad)
+            summed[...] = jnp.zeros_like(summed)
 
         length = lengths[sequence]
         grad_att[...] = jnp.dot(
@@ -996,6 +1015,16 @@
         def _():
             steps[2]()
 
+        by_projected, by_attended = out[0].T, attended[0].T
+        for start in range(0, width, 512):
+            at = pl.ds(start, 512)
+            summed[:wide, at] += jnp.dot(
+                by_projected, normed[0, :, at], preferred_element_type=jnp.float32
+            )
+            summed[wide:, at] += jnp.dot(
+                by_attended, grad[0, :, at], preferred_element_type=jnp.float32
+            )
+
         @pl.when(sequence == count - 1)
         def _():
             fetch.wait()
@@ -1006,6 +1035,12 @@
                 output[at] = (held[at] + value).astype(jnp.bfloat16)
 
             row_loop(own_rows, finish)
+            for outer in range(outer_count):
+                for member in range(split):
+                    start = (outer * split + member) * share
+                    grad_weights[outer, member] = summed[:, start : start + share].astype(
+                        jnp.bfloat16
+                    )
             for copy in copies:
                 copy.wait()
 
@@ -1018,11 +1053,14 @@
             jax.ShapeDtypeStruct((2, 8, HD), jnp.float32),
             jax.ShapeDtypeStruct((count, rows, width), jnp.bfloat16),
             jax.ShapeDtypeStruct((own_rows, width), jnp.bfloat16),
+            jax.ShapeDtypeStruct((outer_count, split, every, share), jnp.bfloat16),
         )
         + tuple(like(piece) for piece in extra),
         in_specs=[
             pl.BlockSpec(memory_space=pltpu.SMEM),
             per_sequence(rows, wide),
+            per_sequence(rows, width),
+            per_sequence(rows, heads * HD),
             per_sequence(rows, width),
             per_sequence(rows, HD),
             whole(width, wide + heads * HD),
@@ -1037,7 +1075,8 @@
             per_sequence(rows, wide),
             pl.BlockSpec((2, 8, HD), lambda s: (0, 0, 0)),
             per_sequence(rows, width),
-            pl.BlockSpec((own_rows, width), lambda s: (0, 0)),
+            whole(own_rows, width),
+            whole(outer_count, split, every, share),
         )
         + (anywhere(),) * extras,
         scratch_shapes=[
@@ -1048,6 +1087,7 @@
             pltpu.VMEM((heads, rows, HD), jnp.float32),
             pltpu.VMEM((rows, HD), jnp.float32),
             pltpu.VMEM((rows, HD), jnp.float32),
+            pltpu.VMEM((every, width), jnp.float32),
             pltpu.VMEM((own_rows, width), jnp.float32),
             pltpu.VMEM((own_rows, width), jnp.float32),
             pltpu.SemaphoreType.DMA,
@@ -1059,6 +1099,8 @@
     )(
         group_length,
         projected,
+        normed,
+        attended,
         grad_attn,
         logs,
         weights,
@@ -1154,47 +1196,50 @@
     )(grads, weights, product)
 
 
-def adam_all(sets, factor):
+def adam_all(sets, pieces, factor):
     jobs = []
-    for weight, _, _, pieces, widths in sets:
+    for weight, _, _, source, kind, detail in sets:
         rows = weight.shape[0]
-        height = rows // TEAM if widths is None else max(CHUNK, rows // 4)
-        jobs.append((height, rows // height, widths))
+        height = {"columns": max(CHUNK, rows // 4), "across": rows}.get(kind, rows // TEAM)
+        jobs.append((height, rows // height, source, kind, detail))
     count = sum(job[1] for job in jobs)
-    total = len(sets)
+    total, sources = len(sets), len(pieces)
 
     def kernel(*refs):
-        inputs, factor, outputs = refs[: 4 * total], refs[4 * total], refs[4 * total + 1 : 8 * total + 1]
-        held = refs[8 * total + 1 : 13 * total + 1]
-        piece_sem, in_sem, out_sem = refs[13 * total + 1 :]
+        inputs, refs = refs[: 3 * total], refs[3 * total :]
+        piece_refs, factor, refs = refs[:sources], refs[sources], refs[sources + 1 :]
+        outputs, refs = refs[: 4 * total], refs[4 * total :]
+        held, refs = refs[: 4 * total], refs[4 * total :]
+        held_pieces, (piece_sem, in_sem, out_sem) = refs[:sources], refs[sources:]
         scale = factor[0:1, 0:1]
-        loads, stores = [], []
-        for place in range(total):
-            load = pltpu.make_async_copy(
-                inputs[4 * place + 3], held[5 * place + 3], piece_sem.at[place]
+        loads, stores, work, slot = [], [], [], 0
+        for place in range(sources):
+            loads.append(
+                pltpu.make_async_copy(piece_refs[place], held_pieces[place], piece_sem.at[place])
             )
-            load.start()
-            loads.append(load)
-        work, slot = [], 0
-        for place, (height, steps, widths) in enumerate(jobs):
+            loads[place].start()
+        for place, (height, steps, *_) in enumerate(jobs):
             for step in range(steps):
                 at = pl.ds(step * height, height)
                 arrive = []
-                for kind in range(3):
+                for number in range(3):
                     copy = pltpu.make_async_copy(
-                        inputs[4 * place + kind].at[at],
-                        held[5 * place + kind].at[at],
-                        in_sem.at[3 * slot + kind],
+                        inputs[3 * place + number].at[at],
+                        held[4 * place + number].at[at],
+                        in_sem.at[3 * slot + number],
                     )
                     copy.start()
                     arrive.append(copy)
                 work.append((place, step, at, slot, arrive))
                 slot += 1
+        arrived = set()
         for place, step, at, slot, arrive in work:
-            height, _, widths = jobs[place]
-            weight, moment, square, pieces, low = held[5 * place : 5 * place + 5]
-            if step == 0:
-                loads[place].wait()
+            height, _, source, kind, detail = jobs[place]
+            weight, moment, square, low = held[4 * place : 4 * place + 4]
+            gradients = held_pieces[source]
+            if source not in arrived:
+                loads[source].wait()
+                arrived.add(source)
             for copy in arrive:
                 copy.wait()
 
@@ -1206,56 +1251,63 @@
                 weight[where], moment[where], square[where] = value, one, two
                 low[where] = value.astype(jnp.bfloat16)
 
-            if widths is None:
-                update(at, slice(None), pieces[step].astype(jnp.float32).T)
+            def spans(widths):
+                for member in range(TEAM):
+                    first, inside = 0, 0
+                    for width in widths:
+                        share = width // TEAM
+                        yield member, pl.ds(first + member * share, share), pl.ds(inside, share)
+                        first += width
+                        inside += share
+
+            if kind == "rows":
+                update(at, slice(None), gradients[step].astype(jnp.float32).T)
+            elif kind == "below":
+                update(
+                    at, slice(None), gradients[step, pl.ds(detail, height)].astype(jnp.float32)
+                )
+            elif kind == "across":
+                for member, across, inside in spans(detail):
+                    update(at, across, gradients[member, inside].astype(jnp.float32).T)
             else:
 
                 @pl.loop(0, height // CHUNK)
                 def _(row):
                     rows = pl.ds(pl.multiple_of(step * height + row * CHUNK, CHUNK), CHUNK)
-                    for member in range(TEAM):
-                        first, inside = 0, 0
-                        for width in widths:
-                            share = width // TEAM
-                            update(
-                                rows,
-                                pl.ds(first + member * share, share),
-                                pieces[member, rows, pl.ds(inside, share)].astype(jnp.float32),
-                            )
-                            first += width
-                            inside += share
-
-            for kind, source in enumerate((weight, moment, square, low)):
+                    for member, across, inside in spans(detail):
+                        update(rows, across, gradients[member, rows, inside].astype(jnp.float32))
+
+            for number, origin in enumerate((weight, moment, square, low)):
                 copy = pltpu.make_async_copy(
-                    source.at[at], outputs[4 * place + kind].at[at], out_sem.at[4 * slot + kind]
+                    origin.at[at], outputs[4 * place + number].at[at], out_sem.at[4 * slot + number]
                 )
                 copy.start()
                 stores.append(copy)
         for copy in stores:
             copy.wait()
 
-    args, shapes, scratch, moved = [], [], [], 0
-    for weight, moment, square, pieces, _ in sets:
-        args += [weight, moment, square, pieces]
+    args, shapes, scratch = [], [], []
+    for weight, moment, square, *_ in sets:
+        args += [weight, moment, square]
         low = jax.ShapeDtypeStruct(weight.shape, jnp.bfloat16)
         shapes += [like(weight)] * 3 + [low]
-        scratch += [pltpu.VMEM(each.shape, each.dtype) for each in (weight, moment, square, pieces, low)]
-        moved += weight.size * 28
+        scratch += [pltpu.VMEM(each.shape, each.dtype) for each in (weight, moment, square, low)]
     outs = pl.pallas_call(
         kernel,
         name="adam_all",
         out_shape=tuple(shapes),
-        in_specs=[anywhere()] * (4 * total) + [in_vmem()],
+        in_specs=[anywhere()] * (3 * total + sources) + [in_vmem()],
         out_specs=(anywhere(),) * (4 * total),
         scratch_shapes=scratch
+        + [pltpu.VMEM(piece.shape, piece.dtype) for piece in pieces]
         + [
-            pltpu.SemaphoreType.DMA((total,)),
+            pltpu.SemaphoreType.DMA((sources,)),
             pltpu.SemaphoreType.DMA((3 * count,)),
             pltpu.SemaphoreType.DMA((4 * count,)),
         ],
         compiler_params=pltpu.CompilerParams(vmem_limit_bytes=VMEM_LIMIT),
-        cost_estimate=cost_of(moved / 3.4e6),
-    )(*args, factor)
+        cost_estimate=cost_of(15),
+    )(*args, *pieces, factor)
     return [outs[4 * place : 4 * place + 4] for place in range(total)]
 
 
@@ -1414,7 +1466,6 @@
         1,
     )
     down_full = gather_outer(down_mixed)
-    attended = attended.reshape(-1, heads * HD)
     hidden, normed_mlp = branch_and_norm(attn_branch, inputs, mlp_gain, 2, "branch_and_norm")
     gate_up, activated, grad_all = feed(
         normed_mlp.reshape(TEAM, row_count, D), gate_up_full, grad_low, grad_all, early, 8
@@ -1424,24 +1475,24 @@
     down_sum = sum_weight(grad_down)
     grad_gate_up = feed_back(grad_all.reshape(TEAM, row_count, D), down_full, gate_up)
     grad_gate_up_weight = over_rows(normed_mlp, grad_gate_up.reshape(-1, 2 * hidden_units))
-    grad_gate_up, grad_gate_up_weight, down_sum = lax.optimization_barrier(
-        (grad_gate_up, grad_gate_up_weight.astype(jnp.bfloat16), down_sum)
+    grad_gate_up, grad_gate_up_weight = after(
+        grad_gate_up, grad_gate_up_weight.astype(jnp.bfloat16)
     )
     gate_up_sum = sum_weight(grad_gate_up_weight)
     grad_hidden, grad_mlp_gain, grad_attn, mlp_part = feed_back_rest(
         grad_gate_up, gate_up_full, activated, down_full, hidden, grad_low, mlp_gain, 3, "feed_back_rest"
     )
-    grad_out_weight = over_rows(grad_attn, attended).astype(jnp.bfloat16)
-    grad_out_weight, gate_up_sum = after(grad_out_weight, gate_up_sum)
-    out_sum = sum_weight(grad_out_weight)
-    grad_projected, grad_head_gains, grad_normed_attn, output, down_mixed = attend_back(
+    _, grad_head_gains, grad_normed_attn, output, grad_first, down_mixed = attend_back(
         projected,
+        normed_attn.reshape(TEAM, row_count, D),
+        attended,
         grad_attn.reshape(TEAM, row_count, D),
         logs,
         first_full,
         mlp_part,
         hidden,
         (team_pieces(down_sum),),
+        lax.axis_size("outer"),
         group_length,
         cos_full,
         sin_full,
@@ -1449,31 +1500,36 @@
         heads,
         7,
     )
-    grad_projected = grad_projected.reshape(-1, projected.shape[2])
-    grad_qkv_weight = over_rows(normed_attn, grad_projected).astype(jnp.bfloat16)
-    grad_qkv_weight, out_sum = after(grad_qkv_weight, out_sum)
-    qkv_sum = sum_weight(grad_qkv_weight)
-    input_grad, grad_attn_gain, gate_up_mixed, out_mixed = norm_back_last(
+    first_sum = sum_weight(grad_first.reshape(-1, grad_first.shape[3]))
+    if grad_first.shape[1] == TEAM:
+        first_sum = team_pieces(first_sum)
+    else:
+        first_sum = first_sum.reshape(first_sum.shape[0], TEAM, -1).transpose(1, 0, 2)
+    input_grad, attn_gain_parts, gate_up_mixed = norm_back_last(
         grad_normed_attn,
         inputs,
         grad_hidden,
         attn_gain,
-        (team_pieces(gate_up_sum), team_pieces(out_sum)),
+        (team_pieces(gate_up_sum),),
         4,
         "norm_back_attn",
     )
     gain_part = jnp.concatenate(
-        [grad_attn_gain, grad_mlp_gain, grad_head_gains.sum(axis=1).reshape(-1)]
+        [jnp.zeros_like(grad_mlp_gain), grad_mlp_gain, grad_head_gains.sum(axis=1).reshape(-1)]
     )
     square_part = sum(
-        jnp.sum(jnp.square(member.astype(jnp.float32)))
-        for member in (qkv_sum, out_sum, gate_up_sum, down_sum)
+        jnp.sum(jnp.square(member.astype(jnp.float32))) for member in (gate_up_sum, down_sum)
     )
     gain_count = gain_part.shape[0]
     packed = jnp.pad(gain_part, (0, -gain_count % PAD))
     packed = jnp.concatenate([packed, jnp.pad(square_part[None], (0, PAD - 1))])
-    packed, norm_tile, factor_tile, qkv_mixed = total_everywhere(
-        packed.reshape(-1, HD), team_pieces(qkv_sum), lax.axis_size("outer"), 5, "total_everywhere"
+    packed, norm_tile, factor_tile, first_mixed = total_everywhere(
+        packed.reshape(-1, HD),
+        attn_gain_parts,
+        first_sum,
+        lax.axis_size("outer"),
+        5,
+        "total_everywhere",
     )
     gain_grad = packed.reshape(-1)[:gain_count]
     grad_norm, factor = norm_tile[0, 0], factor_tile[0, 0]
@@ -1484,11 +1540,12 @@
         (new_qkv, new_qkv_one, new_qkv_two, qkv_copy),
     ) = adam_all(
         [
-            (gate_up_weight, gate_up_moment, gate_up_square, gate_up_mixed, gate_up_widths),
-            (down_weight, down_moment, down_square, down_mixed, None),
-            (out_weight, out_moment, out_square, out_mixed, None),
-            (qkv_weight, qkv_moment, qkv_square, qkv_mixed, qkv_widths),
+            (gate_up_weight, gate_up_moment, gate_up_square, 0, "columns", gate_up_widths),
+            (down_weight, down_moment, down_square, 1, "rows", None),
+            (out_weight, out_moment, out_square, 2, "below", (heads + 2) * HD),
+            (qkv_weight, qkv_moment, qkv_square, 2, "across", qkv_widths),
         ],
+        (gate_up_mixed, down_mixed, first_mixed),
         factor_tile,
     )
     new_gains, new_gains_one, new_gains_two = adam_update(

time: 651 us -> 618 us (0.949)
  waiting for transfers between devices: 20.9 us -> 0.17 us
  matrix products: 54.2 us -> 36 us
  Pallas kernels: 523 us -> 530 us
    reduce_scatter x4 -> x3, waiting for transfers between devices: 20.7 us -> 0.02 us  [sum_weight(): return lax.psum_scatter(gradient, 'outer', scatter_dimension=0, tiled=True)]
    dot_general x4 -> x2, matrix products: 54.2 us -> 36 us  [dot(): lax.dot_general(left, right, ((contract[0], contract[1]), ((), ())), pref...]
  transfers between devices with their start and end apart: 7 -> 6, of which waited for: 1 -> 0; matrix products, arithmetic and copies ran while one was open for 11% -> 8% of each run, Pallas kernels for 75% -> 79%
where the time goes in v6:
time: 618 us; the launch traced here: 610 us
  Pallas kernels  530 us (86%)
  matrix products  36 us (6%)
  other arithmetic  17.6 us (3%)
  between operations  16.3 us (3%)
  local copies, waits for them, and re-layouts  9.64 us (2%)
    pallas_call x1, Pallas kernels, feed_back_rest(): pl.pallas_call(kernel, name=name, out_shape=(jax.ShapeDtypeStruct((rows,...  109 us
    pallas_call x1, Pallas kernels, branch_and_norm(): pl.pallas_call(kernel, name=name, out_shape=(jax.ShapeDtypeStruct((rows,...  101 us
    pallas_call x1, Pallas kernels, attend_back(): pl.pallas_call(kernel, name='attend_back', grid=(count,), out_shape=(jax....  65.1 us
    pallas_call x1, Pallas kernels, norm_back_last(): pl.pallas_call(kernel, name=name, out_shape=(jax.ShapeDtypeStruct((rows,...  64.8 us
    pallas_call x1, Pallas kernels, gather_rows(): pl.pallas_call(kernel, name=name, out_shape=(layer_rows(rows, width),) +...  57.9 us
    pallas_call x1, Pallas kernels, attend(): pl.pallas_call(kernel, name='attend', grid=(count,), out_shape=(jax.Shape...  40.5 us
    dot_general x2, matrix products, dot(): lax.dot_general(left, right, ((contract[0], contract[1]), ((), ())), pref...  36 us
    pallas_call x1, Pallas kernels, feed(): pl.pallas_call(kernel, name='feed', grid=(count,), out_shape=(jax.ShapeDt...  28.2 us
  transfers between devices with their start and end apart: 6, of which 0 were waited for; matrix products, arithmetic and copies ran while one was open for 8% of the time, Pallas kernels for 79%

profile of v6, /device:TPU:0, one launch (start us, length us, event | category | flops | bytes accessed | tf_op | source)
XLA Modules:
  0.0 610.4 jit_solution(5509440357654601332)
XLA Ops:
  7.2 0.0 all-gather.4.cloned.1.call-start
  7.2 1.3 convert_element_type.36
  8.7 0.1 copy.44
  8.9 0.9 maximum_maximum_fusion.pieces
  9.9 12.9 %exchange_first.1 = bf16[4,128,768]{2,1,0:T(8,128)(2,1)} custom-call(bf16[4,128,768]{2,1,0:T(8,128)(2,1)} %maximum_maximum_fusion.pieces), custom_call_target="tpu_custom_call" | custom-call | bytes 1200000 | tf_op jit(solution)/shard_map/exchange_first/pallas_call | solution.py:369
  22.8 0.0 all-gather.4.cloned.1.call-update
  22.8 0.0 all-gather.6.cloned.1.call-start
  22.9 0.3 copy.45
  23.2 0.3 copy-done.15
  23.4 0.0 copy-done.16
  23.5 0.2 select_reduce_fusion.lengths
  23.6 0.6 dynamic_slice.4
  24.2 0.7 add_compare_fusion
  24.9 1.2 fusion.5
  26.1 1.1 pad_maximum_fusion.2
  27.2 0.1 slice_bitcast_fusion.3
  27.3 1.0 pad_maximum_fusion.1.rest_0_
  28.3 0.5 copy-done
  28.8 0.4 fusion
  29.2 0.6 fusion.14
  29.8 1.2 broadcast_select_fusion.own.upstream
  31.0 1.4 fusion.2.own
  32.4 0.1 copy-done.1
  32.5 0.2 convert_element_type.39
  32.7 0.1 fusion.11
  32.8 0.1 maximum_bitcast_fusion
  32.9 0.1 maximum_bitcast_fusion.2
  33.0 1.3 pad_maximum_fusion.rest_0_
  34.3 57.9 %gather_inputs.1 = (bf16[2,2,2,320,2048]{4,3,2,1,0:T(8,128)(2,1)}, bf16[4,128,1536]{2,1,0:T(8,128)(2,1)}) custom-call(bf16[320,2048]{1,0:T(8,128)(2,1)} %fusion.2.own, bf16[4,128,1536]{2,1,0:T(8,128)(2,1)} %pad_maximum_fusion.rest_0_), custom_call_target="tpu_custom_call" | custom-call | bytes 6000000 | tf_op jit(solution)/shard_map/gather_inputs/pallas_call | solution.py:400
  92.2 0.0 all-gather.6.cloned.1.call-update
  92.2 0.0 all-gather.8.cloned.1.call-start
  92.3 0.6 slice_bitcast_fusion.8.gains
  92.9 40.5 %attend.1 = (f32[4,640,512]{2,1,0:T(8,128)}, bf16[4,640,256]{2,1,0:T(8,128)(2,1)}, f32[4,640,128]{2,1,0:T(8,128)}, bf16[4,640,2048]{2,1,0:T(8,128)(2,1)}, bf16[2...) custom-call(s32[4]{0:T(128)} %copy-done.14, bf16[4,640,2048]{2,1,0:T(8,128)(2,1)} %bitcast.80, ...), custom_call_target="tpu_custom_call" | custom-call | bytes 5000000 | tf_op jit(solution)/shard_map/attend/pallas_call | solution.py:864
  133.4 0.0 all-gather.8.cloned.1.call-update
  133.4 0.3 reduce-scatter.4.cloned.1.call-start
  133.7 101.4 %branch_and_norm.1 = (f32[320,2048]{1,0:T(8,128)}, bf16[2,2,2,320,2048]{4,3,2,1,0:T(8,128)(2,1)}) custom-call(bf16[2,2,2,320,2048]{4,3,2,1,0:T(8,128)(2,1)} %bitcast.86, bf16[320,2048]{1,0:T(8,128)(2,1)} %values.1, f32[1,2048]{1,0:T(1,128)} %bitcast.100), custom_call_target="tpu_custom_call" | custom-call | bytes 9500000 | tf_op jit(solution)/shard_map/branch_and_norm/pallas_call | solution.py:449
  235.1 0.0 all-gather.6.cloned.1.call-done.weights
  235.1 28.2 %feed.1 = (f32[4,640,1536]{2,1,0:T(8,128)}, bf16[4,640,768]{2,1,0:T(8,128)(2,1)}, bf16[2,2,2,320,2048]{4,3,2,1,0:T(8,128)(2,1)}) custom-call(bf16[4,640,2048]{2,1,0:T(8,128)(2,1)} %bitcast.83, bf16[2048,1536]{1,0:T(8,128)(2,1)} %all-gather.6.cloned.1.call-done.weights, ...), custom_call_target="tpu_custom_call", output_to_operand_aliasing={{2}: (3, {})} | custom-call | bytes 2800000 | tf_op jit(solution)/shard_map/feed/pallas_call | solution.py:1146
  263.3 13.6 %convolution_convert_fusion.1 = bf16[2048,768]{1,0:T(8,128)(2,1)} fusion(bf16[2560,2048]{1,0:T(8,128)(2,1)} %bitcast.78, bf16[2560,768]{1,0:T(8,128)(2,1)} %bitcast.90), kind=kOutput, calls=%fused_computation.1 | convolution fusion | flops 8054636544 | bytes 17563648 | tf_op jit(solution)/shard_map/dot_general | solution.py:1356
  276.9 0.0 reduce-scatter.4.cloned.1.call-update
  276.9 0.4 reduce-scatter.6.cloned.1.call-start
  277.4 0.0 all-gather.8.cloned.1.call-done.weights.down
  277.4 17.6 %feed_back.1.grad = bf16[4,640,1536]{2,1,0:T(8,128)(2,1)} custom-call(bf16[4,640,2048]{2,1,0:T(8,128)(2,1)} %bitcast.79, bf16[2048,768]{1,0:T(8,128)(2,1)} %all-gather.8.cloned.1.call-done.weights.down, f32[4,640,1536]{2,1,0:T(8,128)} %get-tuple-element.92.product), custom_call_target="tpu_custom_call" | custom-call | bytes 1800000 | tf_op jit(solution)/shard_map/feed_back/pallas_call | solution.py:1183
  295.0 22.4 %convolution_convert_fusion = bf16[2048,1536]{1,0:T(8,128)(2,1)} fusion(bf16[2560,2048]{1,0:T(8,128)(2,1)} %bitcast.84, bf16[2560,1536]{1,0:T(8,128)(2,1)} %bitcast.82), kind=kOutput, calls=%fused_computation | convolution fusion | flops 16109273088 | bytes 24641536 | tf_op jit(solution)/shard_map/dot_general | solution.py:1356
  317.4 0.0 reduce-scatter.6.cloned.1.call-update
  317.5 0.0 reduce-scatter.8.cloned.1.call-start
  317.5 108.6 %feed_back_rest.1 = (f32[320,2048]{1,0:T(8,128)}, f32[8,2048]{1,0:T(8,128)}, bf16[2,2,2,320,2048]{4,3,2,1,0:T(8,128)(2,1)}, bf16[4,2,320,2048]{3,2,1,0:T(8,128)(2,1)}) custom-call(bf16[4,640,1536]{2,1,0:T(8,128)(2,1)} %feed_back.1.grad, bf16[2048,1536]{1,0:T(8,128)(2,1)} %all-gather.6.cloned.1.call-done.weights, ...), custom_call_target="tpu_custom_call" | custom-call | bytes 10500000 | tf_op jit(solution)/shard_map/feed_back_rest/pallas_call | solution.py:578
  426.1 0.0 reduce-scatter.4.cloned.1.call-done
  426.2 65.1 %attend_back.1 = (bf16[4,640,512]{2,1,0:T(8,128)(2,1)}, f32[2,8,128]{2,1,0:T(8,128)}, bf16[4,640,2048]{2,1,0:T(8,128)(2,1)}, bf16[320,2048]{1,0:T(8,128)(2,1)}, ...) custom-call(s32[4]{0:T(128)} %copy-done.14, f32[4,640,512]{2,1,0:T(8,128)} %get-tuple-element.82.proj, ...), custom_call_target="tpu_custom_call" | custom-call | bytes 5000000 | tf_op jit(solution)/shard_map/attend_back/pallas_call | solution.py:1047
  491.3 0.0 reduce-scatter.8.cloned.1.call-update
  491.4 0.8 copy-done.10
  492.2 0.3 copy-done.3
  492.5 1.0 multiply_reduce_fusion.1
  493.5 2.8 multiply_reduce_fusion
  497.6 64.8 %norm_back_attn.1 = (bf16[320,2048]{1,0:T(8,128)(2,1)}, f32[8,2048]{1,0:T(8,128)}, bf16[4,128,1536]{2,1,0:T(8,128)(2,1)}) custom-call(bf16[2,2,2,320,2048]{4,3,2,1,0:T(8,128)(2,1)} %bitcast.85, bf16[320,2048]{1,0:T(8,128)(2,1)} %values.1, f32[320,2048]{1,0:T(8,128)} %get-tuple-element.101.upstream, f32[1,2048]{1,0:T(1,128)} %bitcast.99, ...), custom_call_target="tpu_custom_call" | custom-call | bytes 6500000 | tf_op jit(solution)/shard_map/norm_back_attn/pallas_call | solution.py:639
  562.5 0.6 fusion.6.values
  563.1 16.9 %total_everywhere.1 = (f32[48,128]{1,0:T(8,128)}, f32[8,128]{1,0:T(8,128)}, f32[8,128]{1,0:T(8,128)}, bf16[4,768,128]{2,1,0:T(8,128)(2,1)}) custom-call(f32[48,128]{1,0:T(8,128)} %fusion.6.values, f32[8,2048]{1,0:T(8,128)} %get-tuple-element.106.first, bf16[3072,128]{1,0:T(8,128)(2,1)} %reduce-scatter.8.cloned.1.call-done.square_of, ...), custom_call_target="tpu_custom_call" | custom-call | tf_op jit(solution)/shard_map/total_everywhere/pallas_call | solution.py:729
  580.0 1.2 slice.147
  581.2 1.2 slice.145
  582.4 2.0 multiply_subtract_fusion
  584.4 15.9 %adam_all.1 = (f32[128,6144]{1,0:T(8,128)}, f32[128,6144]{1,0:T(8,128)}, f32[128,6144]{1,0:T(8,128)}, bf16[128,6144]{1,0:T(8,128)(2,1)}, f32[3072,128]{1,0:T(8,1...) custom-call(f32[128,6144]{1,0:T(8,128)} %refs_0_.1, ...), custom_call_target="tpu_custom_call" | custom-call | bytes 1500000 | tf_op jit(solution)/shard_map/adam_all/pallas_call | solution.py:1295
  600.3 1.1 copy.49
  601.3 0.7 copy-done.6
  602.1 1.1 copy.50
  (42 shorter events, 0.3 us)
Async XLA Ops:
  7.2 1.5 copy-start.4
  7.2 85.6 %all-gather.4.cloned.1.call-start = ((), (), s32[]{:S(2)}) async-start(), calls=%async_computation.3 | async-start | bytes 3932160 | tf_op jit(solution)/shard_map/all_gather | solution.py:1328
  9.9 13.0 %copy-start.2 = (f32[3072,128]{1,0:T(8,128)S(1)}, f32[3072,128]{1,0:T(8,128)}, u32[]{:S(2)}) copy-start(f32[3072,128]{1,0:T(8,128)} %refs_3_.1) | copy-start | bytes 4718596
  22.8 0.7 copy-start.15
  22.8 0.7 copy-start.16
  22.8 212.3 %all-gather.6.cloned.1.call-start = ((), (), s32[]{:S(2)}) async-start(), calls=%async_computation.4 | async-start | bytes 7864320 | tf_op jit(solution)/shard_map/all_gather | solution.py:1328
  23.6 3.6 copy-start.14
  27.2 1.6 copy-start
  27.3 1.9 copy-start.9
  27.3 2.5 copy-start.7
  29.8 2.6 copy-start.8
  29.8 2.8 copy-start.1
  92.2 185.2 %all-gather.8.cloned.1.call-start = ((), (), s32[]{:S(2)}) async-start(), calls=%async_computation.5 | async-start | bytes 3932160 | tf_op jit(solution)/shard_map/all_gather | solution.py:1328
  133.4 292.8 %reduce-scatter.4.cloned.1.call-start = ((), (), s32[]{:S(2)}) async-start(), calls=%async_computation.6 | async-start | bytes 3932160 | tf_op jit(solution)/shard_map/reduce_scatter | solution.py:1336
  276.9 216.6 %reduce-scatter.6.cloned.1.call-start = ((), (), s32[]{:S(2)}) async-start(), calls=%async_computation.7 | async-start | bytes 7864320 | tf_op jit(solution)/shard_map/reduce_scatter | solution.py:1336
  317.5 245.6 %reduce-scatter.8.cloned.1.call-start = ((), (), s32[]{:S(2)}) async-start(), calls=%async_computation.8 | async-start | bytes 3932160 | tf_op jit(solution)/shard_map/reduce_scatter | solution.py:1336
  491.3 0.8 copy-start.10
  491.3 0.9 copy-start.13
  491.3 1.2 copy-start.3
  562.5 19.9 %copy-start.11 = (f32[4352]{0:T(1024)S(1)}, f32[4352]{0:T(1024)}, u32[]{:S(2)}) copy-start(f32[4352]{0:T(1024)} %param.32) | copy-start | bytes 52228
  562.5 19.9 %copy-start.12 = (f32[4352]{0:T(1024)S(1)}, f32[4352]{0:T(1024)}, u32[]{:S(2)}) copy-start(f32[4352]{0:T(1024)} %param.37) | copy-start | bytes 52228
  584.4 15.9 %copy-start.5 = (bf16[320,2048]{1,0:T(8,128)(2,1)S(1)}, bf16[320,2048]{1,0:T(8,128)(2,1)}, u32[]{:S(2)}) copy-start(bf16[320,2048]{1,0:T(8,128)(2,1)} %get-tuple-element.198) | copy-start | bytes 3932164
  600.3 1.8 copy-start.6
Sparse Core Ops, SparseCore 0:
  23.0 64.6 all-gather.3
  92.4 115.8 all-gather.5
  209.8 61.7 all-gather.7
  277.0 60.6 reduce-scatter.3
  339.9 110.7 reduce-scatter.5
  491.5 60.6 reduce-scatter.7

commit v7 on v6

--- a/solution.py
+++ b/solution.py
@@ -48,6 +48,7 @@
 VMEM_LIMIT = 60 * 1024 * 1024
 CHUNK = 16
 GATHER_COPIES = 13
+AHEAD = 4
 SUM_COPIES = 10
 NEIGHBOURS = ((1, 0, 0), (0, 1, 0), (0, 0, 1))
 MATES = ((0, 1, 0), (1, 0, 0), (1, 1, 0))
@@ -118,7 +119,7 @@
     return copies
 
 
-def plan_gather(own, out, send, recv, own_sem, cut, base=0, rows=None):
+def plan_gather(own, out, send, recv, own_sem, cut, base=0, rows=None, parts=False):
     near, core, tp = spots()
     rows = own.shape[0] if rows is None else rows
     low, high = pl.ds(base, cut), pl.ds(base + cut, rows - cut)
@@ -180,18 +181,39 @@
             near_low.wait_recv()
             twin_beside_low.start()
 
-    def finish():
+    def own_there():
+        keep.wait()
+
+    def twin_there():
+        twin_own.wait_recv()
+        twin_across.wait_recv()
+        if cut:
+            twin_across_low.wait_recv()
+
+    def far_there():
         if cut:
             far_low.wait_recv()
             twin_far_low.start()
         far_high.wait_recv()
         twin_far.start()
-        for copy in twins:
-            copy.wait_recv()
+
+    def rest_there():
+        twin_beside.wait_recv()
+        twin_far.wait_recv()
+        if cut:
+            twin_beside_low.wait_recv()
+            twin_far_low.wait_recv()
         for copy in ways + twins:
             copy.wait_send()
-        keep.wait()
-
+
+    def finish():
+        own_there()
+        twin_there()
+        far_there()
+        rest_there()
+
+    if parts:
+        return [begin, middle, later, own_there, twin_there, far_there, rest_there]
     return [begin, middle, later, finish]
 
 
@@ -476,45 +498,46 @@
     ]
 
 
-def halves_times(left, weights, target, rows):
+def times_turned(left, weights, target):
     for start in range(0, weights.shape[0], 512):
         at = pl.ds(start, 512)
-        product = lax.dot_general(
+        target[:, at] = lax.dot_general(
             left, weights[at, :], (((1,), (1,)), ((), ())), preferred_element_type=jnp.float32
         ).astype(target.dtype)
-        target[0, :, at] = product[:rows]
-        target[1, :, at] = product[rows:]
 
 
 def feed_back_rest(
-    grad_gate_up, weights, active, down, values, upstream, gain, number, name
+    grad_gate, grad_up, weights, active, down, normed, values, upstream, gain, outer_count, number, name
 ):
     rows, width = values.shape
-    count, both_rows, units = grad_gate_up.shape
+    count, both_rows, units = grad_gate.shape
+    all_rows = count * both_rows
+    past = all_rows - width
     cut = rows // 2
+    split, share = team_split(width, outer_count)
+    turns = width // 512
 
     def kernel(
-        grad, weights, active, down, values, upstream, gain, result, gain_grad, out, branch, *scratch
+        gate, ups, weights, active, down, normed, values, upstream, gain,
+        result, gain_grad, low, branch, grad_weight, *scratch
     ):
-        (grad_v, weights_v, active_v, down_v, values_v, upstream_v, parts, total, low), rest = (
-            scratch[:9],
-            scratch[9:],
+        (grad_v, weights_v, active_v, down_v, values_v, upstream_v, parts, total), rest = (
+            scratch[:8],
+            scratch[8:],
         )
-        (load_sem, store_sem), rest = rest[:2], rest[2:]
-        sums, sems = rest[:7], rest[7:]
+        (shares, staged, load_sem, store_sem, chunk_sem, piece_sem), sums = rest[:6], rest[6:]
         from_tp, from_near = sums[3], sums[4]
         near, core, tp = spots()
         members = sequence_order()
         outgoing = [parts.at[place, half] for place, half in ((0, 1 - tp), (2, 1 - tp), (0, tp), (2, tp))]
         mine = [parts.at[place, half] for place, half in ((1, 1 - tp), (3, 1 - tp), (1, tp), (3, tp))]
         steps, (send_far, send_tp, send_near) = plan_sum(outgoing, mine, (), total, sums, cut)
-        onward = plan_gather(low, out, *sems, cut=cut)
+        stores = [
+            pltpu.make_async_copy(shares.at[place % 2], branch.at[place], store_sem.at[place])
+            for place in range(count)
+        ]
         fetch = [
-            pltpu.make_async_copy(grad.at[member], grad_v.at[place % 2], load_sem.at[place])
-            for place, member in enumerate(members)
-        ]
-        fetch += [
-            pltpu.make_async_copy(source, target, load_sem.at[4 + place])
+            pltpu.make_async_copy(source, target, load_sem.at[place])
             for place, (source, target) in enumerate(
                 (
                     (weights, weights_v),
@@ -522,144 +545,284 @@
                     (upstream, upstream_v),
                     (active, active_v),
                     (down, down_v),
+                    (ups, active_v),
                 )
             )
         ]
-        for place in (0, 4, 1, 5, 6, 7, 8):
+        grads = []
+        for place, member in enumerate(members):
+            for side, source in enumerate((gate, ups)):
+                grads.append(
+                    pltpu.make_async_copy(
+                        source.at[member],
+                        grad_v.at[place % 2, :, :, pl.ds(side * units, units)],
+                        load_sem.at[6 + 2 * place + side],
+                    )
+                )
+
+        def bring(place):
+            grads[2 * place].start()
+            grads[2 * place + 1].start()
+
+        def brought(place):
+            grads[2 * place].wait()
+            grads[2 * place + 1].wait()
+
+        def back(place, half):
+            times_turned(grad_v[place % 2, half], weights_v, parts.at[place, half])
+
+        def chunk(turn):
+            at, slot = pl.ds(turn * 512, 512), turn % 2
+            return [
+                pltpu.make_async_copy(
+                    normed.at[pl.ds(0, width), at],
+                    weights_v.at[:, pl.ds(slot * 1024, 512)],
+                    chunk_sem.at[slot, 0],
+                ),
+                pltpu.make_async_copy(
+                    normed.at[pl.ds(width, past), at],
+                    weights_v.at[pl.ds(slot * past, past), pl.ds(512, 512)],
+                    chunk_sem.at[slot, 1],
+                ),
+            ]
+
+        def pieces(turn):
+            slot = turn % 2
+            return [
+                pltpu.make_async_copy(
+                    staged.at[slot, :, pl.ds(place * share, share)],
+                    grad_weight.at[turn * (512 // share) + place],
+                    piece_sem.at[slot, place],
+                )
+                for place in range(512 // share)
+            ]
+
+        fetch[0].start()
+        bring(0)
+        bring(1)
+        greet(NEIGHBOURS)
+        fetch[0].wait()
+        brought(0)
+        back(0, 1 - tp)
+        steps[0]((0,))
+        brought(1)
+        back(1, 1 - tp)
+        send_far()
+        back(0, tp)
+        steps[0]((2,))
+        bring(2)
+        for place in (3, 4, 1, 2):
             fetch[place].start()
-        greet(NEIGHBOURS)
+        back(1, tp)
+        send_near()
+        bring(3)
+        brought(2)
+        back(2, 1 - tp)
+        steps[0]((1,))
+        brought(3)
+        back(3, 1 - tp)
+        send_tp()
+        back(2, tp)
+        steps[0]((3,))
+        back(3, tp)
+        for turn in (0, 1):
+            for copy in chunk(turn):
+                copy.start()
+        fetch[3].wait()
         fetch[4].wait()
         for place in range(count):
-            fetch[place].wait()
-            halves_times(grad_v[place % 2], weights_v, parts.at[place], rows)
-            if place + 2 < count:
-                fetch[place + 2].start()
-            if place == 0:
-                steps[0]((0, 2))
-            elif place == 1:
-                send_far()
-                send_near()
-            elif place == 2:
-                steps[0]((1, 3))
-        send_tp()
+            if place >= 2:
+                stores[place - 2].wait()
+            for half in range(2):
+                times_turned(active_v[place, half], down_v, shares.at[place % 2, half])
+            stores[place].start()
+        fetch[5].start()
         steps[2]()
         fetch[5].wait()
-        fetch[6].wait()
+        for turn in range(turns):
+            slot = turn % 2
+            for copy in chunk(turn):
+                copy.wait()
+            left = active_v[...].reshape(all_rows, units)
+            product = lax.dot_general(
+                left[:width],
+                weights_v[:, slot * 1024 : slot * 1024 + 512],
+                (((0,), (0,)), ((), ())),
+                preferred_element_type=jnp.float32,
+            ) + lax.dot_general(
+                left[width:],
+                weights_v[slot * past : (slot + 1) * past, 512:1024],
+                (((0,), (0,)), ((), ())),
+                preferred_element_type=jnp.float32,
+            )
+            if turn >= 2:
+                for copy in pieces(turn - 2):
+                    copy.wait()
+            staged[slot] = product.astype(staged.dtype)
+            for copy in pieces(turn):
+                copy.start()
+            if turn + 2 < turns:
+                for copy in chunk(turn + 2):
+                    copy.start()
+        fetch[1].wait()
+        fetch[2].wait()
         gain_grad[...] = jnp.zeros_like(gain_grad)
         steps[3]()
 
         def finish(at):
             grad = total[at] + read(from_tp, at) + read(from_near, at)
-            back, by_gain = norm_back(values_v[at], gain[...], grad)
+            turned, by_gain = norm_back(values_v[at], gain[...], grad)
             gain_grad[...] += by_gain.reshape(CHUNK // 8, 8, width).sum(axis=0)
-            value = read(upstream_v, at) + back
+            value = read(upstream_v, at) + turned
             total[at] = value
             low[at] = value.astype(jnp.bfloat16)
 
         row_loop(rows, finish)
-        onward[0]()
-        stores = [pltpu.make_async_copy(total, result, store_sem.at[count])]
-        stores[0].start()
-        fetch[7].wait()
-        fetch[8].wait()
-        for place in range(count):
-            halves_times(active_v[place], down_v, parts.at[place], rows)
-            store = pltpu.make_async_copy(parts.at[place], branch.at[place], store_sem.at[place])
-            store.start()
-            stores.append(store)
-            if place == 1:
-                onward[1]()
-        onward[2]()
-        onward[3]()
-        for store in stores:
-            store.wait()
+        store = pltpu.make_async_copy(total, result, store_sem.at[count])
+        store.start()
+        for turn in range(max(0, turns - 2), turns):
+            for copy in pieces(turn):
+                copy.wait()
+        for copy in [store] + stores[2:]:
+            copy.wait()
 
     low_type = jnp.bfloat16
-    result, gain_grad, full, branch = pl.pallas_call(
+    halves = (count, 2, rows, units)
+    result, gain_grad, rounded, branch, grad_weight = pl.pallas_call(
         kernel,
         name=name,
         out_shape=(
             jax.ShapeDtypeStruct((rows, width), jnp.float32),
             jax.ShapeDtypeStruct((8, width), jnp.float32),
-            layer_rows(rows, width),
+            jax.ShapeDtypeStruct((rows, width), low_type),
             jax.ShapeDtypeStruct((count, 2, rows, width), low_type),
+            jax.ShapeDtypeStruct((outer_count * split, units, share), low_type),
         ),
-        in_specs=[anywhere()] * 6 + [in_vmem()],
-        out_specs=(anywhere(), in_vmem(), anywhere(), anywhere()),
+        in_specs=[anywhere()] * 8 + [in_vmem()],
+        out_specs=(anywhere(), in_vmem(), in_vmem(), anywhere(), anywhere()),
         scratch_shapes=[
-            pltpu.VMEM((2, both_rows, units), low_type),
+            pltpu.VMEM((2, 2, rows, 2 * units), low_type),
             pltpu.VMEM(weights.shape, low_type),
-            pltpu.VMEM(active.shape, low_type),
+            pltpu.VMEM(halves, low_type),
             pltpu.VMEM(down.shape, low_type),
             pltpu.VMEM((rows, width), values.dtype),
             pltpu.VMEM((rows, width), upstream.dtype),
             pltpu.VMEM((count, 2, rows, width), low_type),
             pltpu.VMEM((rows, width), jnp.float32),
-            pltpu.VMEM((rows, width), low_type),
-            pltpu.SemaphoreType.DMA((9,)),
+            pltpu.VMEM((2, 2, rows, width), low_type),
+            pltpu.VMEM((2, units, 512), low_type),
+            pltpu.SemaphoreType.DMA((6 + 2 * count,)),
             pltpu.SemaphoreType.DMA((count + 1,)),
+            pltpu.SemaphoreType.DMA((2, 2)),
+            pltpu.SemaphoreType.DMA((2, 512 // share)),
         ]
-        + sum_scratch(rows, width, cut, fetched=False)
-        + gather_scratch(),
+        + sum_scratch(rows, width, cut, fetched=False),
         compiler_params=params(number),
-        cost_estimate=cost_of(105),
-    )(grad_gate_up, weights, active, down, values, upstream, gain.reshape(1, width))
-    return result, gain_grad.sum(axis=0), full.reshape(-1, width), branch.reshape(-1, width)
-
-
-def norm_back_last(part, values, upstream, gain, extra, number, name):
+        cost_estimate=cost_of(60),
+    )(
+        grad_gate.reshape(halves),
+        grad_up.reshape(halves),
+        weights,
+        active.reshape(halves),
+        down,
+        normed,
+        values,
+        upstream,
+        gain.reshape(1, width),
+    )
+    return result, gain_grad.sum(axis=0), rounded, branch.reshape(-1, width), grad_weight
+
+
+def square_sum(values):
+    values = values.reshape(-1, values.shape[-1]).astype(jnp.float32)
+    return jnp.sum(values * values, keepdims=True)
+
+
+def corner(value):
+    row = lax.broadcasted_iota(jnp.int32, (8, HD), 0)
+    column = lax.broadcasted_iota(jnp.int32, (8, HD), 1)
+    return jnp.where((row == 0) & (column == 0), value, 0.0)
+
+
+def norm_back_last(part, values, upstream, gain, extra, squared, number, name):
     rows, width = values.shape
-    extras = len(extra)
+    extras, count = len(extra), len(squared)
     cut = balanced(rows, crossing(extra, width))
 
     def kernel(part, values, upstream, gain, *rest):
-        pieces, (result, gain_grad) = rest[:extras], rest[extras : extras + 2]
-        mixed, rest = rest[extras + 2 : 2 * extras + 2], rest[2 * extras + 2 :]
-        total, sems = rest[SUM_SCRATCH], rest[SUM_SCRATCH + 1 :]
-        steps, from_tp, from_near = plan_sum_of(part, total, rest[:SUM_SCRATCH], cut)
+        pieces, rest = rest[:extras], rest[extras:]
+        squared, (result, gain_grad, squares), rest = (
+            rest[:count],
+            rest[count : count + 3],
+            rest[count + 3 :],
+        )
+        mixed, rest = rest[:extras], rest[extras:]
+        sums, rest = rest[:SUM_SCRATCH], rest[SUM_SCRATCH:]
+        (total, values_v, upstream_v, load_sem), rest = rest[:4], rest[4:]
+        squared_v, sems = rest[:count], rest[count:]
+        steps, from_tp, from_near = plan_sum_of(part, total, sums, cut)
         copies = plan_exchanges(pieces, mixed, sems)
+        fetch = [
+            pltpu.make_async_copy(source, target, load_sem.at[place])
+            for place, (source, target) in enumerate(
+                zip((values, upstream) + tuple(squared), (values_v, upstream_v) + tuple(squared_v))
+            )
+        ]
         greet(EVERYONE_NEAR)
         steps[0]()
         for copy in copies:
             copy.start()
-        for step in steps[1:]:
-            step()
+        for copy in fetch:
+            copy.start()
+        steps[1]()
+        for copy in fetch:
+            copy.wait()
+        squares[...] = corner(sum(square_sum(ref[...]) for ref in squared_v))
+        steps[2]()
         gain_grad[...] = jnp.zeros_like(gain_grad)
+        steps[3]()
 
         def finish(at):
             grad = total[at] + read(from_tp, at) + read(from_near, at)
-            back, by_gain = norm_back(read(values, at), gain[...], grad)
+            back, by_gain = norm_back(read(values_v, at), gain[...], grad)
             gain_grad[...] += by_gain.reshape(CHUNK // 8, 8, width).sum(axis=0)
-            result[at] = (read(upstream, at) + back).astype(jnp.bfloat16)
+            result[at] = (upstream_v[at] + back).astype(jnp.bfloat16)
 
         row_loop(rows, finish)
         for copy in copies:
             copy.wait()
 
-    outs = pl.pallas_call(
+    return pl.pallas_call(
         kernel,
         name=name,
         out_shape=(
             jax.ShapeDtypeStruct((rows, width), jnp.bfloat16),
             jax.ShapeDtypeStruct((8, width), jnp.float32),
+            jax.ShapeDtypeStruct((8, HD), jnp.float32),
         )
         + tuple(like(piece) for piece in extra),
-        in_specs=[anywhere()] + [in_vmem()] * 3 + [anywhere()] * extras,
-        out_specs=(in_vmem(), in_vmem()) + (anywhere(),) * extras,
+        in_specs=[anywhere()] * 3 + [in_vmem()] * (1 + extras) + [anywhere()] * count,
+        out_specs=(in_vmem(), in_vmem(), in_vmem()) + (anywhere(),) * extras,
         scratch_shapes=sum_scratch(rows, width, cut)
-        + [pltpu.VMEM((rows, width), jnp.float32)]
+        + [
+            pltpu.VMEM((rows, width), jnp.float32),
+            pltpu.VMEM((rows, width), values.dtype),
+            pltpu.VMEM((rows, width), upstream.dtype),
+            pltpu.SemaphoreType.DMA((2 + count,)),
+        ]
+        + [pltpu.VMEM(each.shape, each.dtype) for each in squared]
         + exchange_scratch() * extras,
         compiler_params=params(number),
         cost_estimate=cost_of(65),
-    )(spread(part, rows), values, upstream, gain.reshape(1, width), *extra)
-    return outs
-
-
-def total_everywhere(values, first, pieces, outer_count, number, name):
-    shape = values.shape
+    )(spread(part, rows), values, upstream, gain.reshape(1, width), *extra, *squared)
+
+
+def total_everywhere(values, first, squares, pieces, outer_count, number, name):
+    gains = values.shape[0]
+    shape = (gains + 8, HD)
     width = first.shape[1]
 
-    def kernel(values, first, square_of, pieces, out, norm, factor, mixed, layer, outers, send, recv, *sems):
+    def kernel(values, first, squares, pieces, out, norm, factor, mixed, layer, outers, send, recv, *sems):
         near, core, tp = spots()
         outer = lax.axis_index("outer")
         partners = [
@@ -691,12 +854,8 @@
             return copies
 
         mine = near * (CORE * 2) + core * 2 + tp
-        row = lax.broadcasted_iota(jnp.int32, shape, 0)
-        column = lax.broadcasted_iota(jnp.int32, shape, 1)
-        flat = square_of[...].astype(jnp.float32)
-        squares = jnp.sum(flat * flat, keepdims=True)
-        squares = jnp.where((row == shape[0] - 8) & (column == 0), squares, 0.0)
-        layer[mine] = values[...] + squares
+        layer[mine, :gains] = values[...]
+        layer[mine, gains:] = squares[...] + corner(square_sum(pieces[...]))
         sums = jnp.sum(first[...], axis=0, keepdims=True)
         for place in range(width // HD):
             layer[mine, place : place + 1] = sums[:, place * HD : (place + 1) * HD]
@@ -716,8 +875,10 @@
         for slot in range(1, outer_count):
             total = total + outers[slot]
         out[...] = total
-        squares = jnp.sum(jnp.where(row < shape[0] - 8, total * total, total), keepdims=True)
-        root = jnp.sqrt(squares)
+        gain_part = total[:gains]
+        root = jnp.sqrt(
+            jnp.sum(gain_part * gain_part, keepdims=True) + jnp.sum(total[gains:], keepdims=True)
+        )
         norm[...] = jnp.broadcast_to(root, norm.shape)
         factor[...] = jnp.broadcast_to(
             jnp.minimum(1.0, clip_norm / (root + 1e-06)), factor.shape
@@ -730,7 +891,7 @@
         kernel,
         name=name,
         out_shape=(jax.ShapeDtypeStruct(shape, jnp.float32), tile, tile, like(pieces)),
-        in_specs=[in_vmem(), in_vmem(), in_vmem(), anywhere()],
+        in_specs=[in_vmem()] * 4,
         out_specs=(in_vmem(), in_vmem(), in_vmem(), anywhere()),
         scratch_shapes=[
             pltpu.VMEM((8,) + shape, jnp.float32),
@@ -740,7 +901,7 @@
         ]
         + exchange_scratch(),
         compiler_params=params(number),
-    )(values, first, pieces.reshape(-1, pieces.shape[2]), pieces)
+    )(values, first, squares, pieces)
 
 
 def head_scale(raw, gain, cos_full, sin_full):
@@ -880,9 +1041,9 @@
             whole(rows, HD),
             whole(rows, HD),
             whole(2, HD),
-            anywhere(),
+            whole(own_rows, width),
         ]
-        + [anywhere()] * extras,
+        + [whole(*piece.shape) for piece in extra],
         out_specs=(
             per_sequence(rows, wide),
             per_sequence(rows, heads * HD),
@@ -909,11 +1070,21 @@
     return split, width // outer_count // split
 
 
+def local_first(place):
+    near, core, _ = spots()
+    other_near, other_core = place // 2, place % 2
+    return (near + other_near * (1 - 2 * near)) * CORE + core + other_core * (1 - 2 * core)
+
+
+def ordered(*shape):
+    return pl.BlockSpec((1,) + shape, lambda s: (local_first(s),) + (0,) * len(shape))
+
+
 def attend_back(
     projected,
     normed,
     attended,
-    grad_attn,
+    own_grad,
     logs,
     weights,
     part,
@@ -936,39 +1107,61 @@
     split, share = team_split(width, outer_count)
 
     def kernel(
-        lengths, proj, normed, attended, grad, logs, weights, cos_ref, sin_ref, gains, part, hidden, *rest
+        lengths, proj, normed, attended, own_grad, logs, weights_any, cos_ref, sin_ref, gains, part, hidden, *rest
     ):
         pieces, rest = rest[:extras], rest[extras:]
-        (out, gain_grad, back_part, output, grad_weights), rest = rest[:5], rest[5:]
+        (gathered, gain_grad, back_part, output, grad_weights), rest = rest[:5], rest[5:]
         mixed, rest = rest[:extras], rest[extras:]
-        (queries, keys, values, grad_att, grad_q, grad_k, grad_v, summed), rest = rest[:8], rest[8:]
-        (total, held, held_sem), rest = rest[:3], rest[3:]
-        sequence = pl.program_id(0)
-        steps, from_tp, from_near = plan_sum_of(part, total, rest[:SUM_SCRATCH], cut)
-        copies = plan_exchanges(pieces, mixed, rest[SUM_SCRATCH:])
+        (queries, keys, values, grad_att, grad_q, grad_k, grad_v_sum, summed), rest = rest[:8], rest[8:]
+        (total, held, held_sem, out, grad_v, grad_sem), rest = rest[:6], rest[6:]
+        (weights, staged, weights_sem, store_sem), rest = rest[:4], rest[4:]
+        sums, sems, rest = rest[:SUM_SCRATCH], rest[SUM_SCRATCH : SUM_SCRATCH + 3], rest[SUM_SCRATCH + 3 :]
+        place = pl.program_id(0)
+        sequence = local_first(place)
+        steps, from_tp, from_near = plan_sum_of(part, total, sums, cut)
+        gather = plan_gather(own_grad, gathered, *sems, cut=own_rows // 2, parts=True)
+        copies = plan_exchanges(pieces, mixed, rest)
+        fetch_weights = pltpu.make_async_copy(weights_any, weights, weights_sem)
+        store = pltpu.make_async_copy(staged, grad_weights, store_sem)
+
+        def arrival(which):
+            member = local_first(which)
+            return pltpu.make_async_copy(
+                gathered.at[member // CORE, member % CORE],
+                grad_v.at[which % 2],
+                grad_sem.at[which % 2],
+            )
+
         fetch = pltpu.make_async_copy(hidden, held, held_sem)
 
-        @pl.when(sequence == 0)
+        @pl.when(place == 0)
         def _():
             greet(EVERYONE_NEAR)
+            gather[0]()
             steps[0]()
-            for copy in copies:
-                copy.start()
             fetch.start()
+            fetch_weights.start()
             gain_grad[...] = jnp.zeros_like(gain_grad)
             summed[...] = jnp.zeros_like(summed)
-
+            gather[1]()
+            gather[2]()
+            gather[3]()
+            arrival(0).start()
+            fetch_weights.wait()
+
+        @pl.when(place == 2)
+        def _():
+            arrival(3).start()
+
+        head_inputs(proj, gains, cos_ref, sin_ref, queries, keys, values, heads)
+        grad_k[...] = jnp.zeros_like(grad_k)
+        grad_v_sum[...] = jnp.zeros_like(grad_v_sum)
+        arrival(place).wait()
+        grad = grad_v[place % 2].reshape(rows, width)
         length = lengths[sequence]
         grad_att[...] = jnp.dot(
-            grad[0], weights[:, wide:], preferred_element_type=jnp.float32
+            grad, weights[:, wide:], preferred_element_type=jnp.float32
         ).astype(jnp.bfloat16)
-        head_inputs(proj, gains, cos_ref, sin_ref, queries, keys, values, heads)
-        grad_k[...] = jnp.zeros_like(grad_k)
-        grad_v[...] = jnp.zeros_like(grad_v)
-
-        @pl.when(sequence == 0)
-        def _():
-            steps[1]()
 
         for step in range(rows // BLOCK):
             at = pl.ds(step * BLOCK, BLOCK)
@@ -990,7 +1183,7 @@
             grad_k[seen] += lax.dot_general(
                 grad_scores, stacked, (((0,), (0,)), ((), ())), preferred_element_type=jnp.float32
             )
-            grad_v[seen] += lax.dot_general(
+            grad_v_sum[seen] += lax.dot_general(
                 probs.astype(jnp.bfloat16),
                 above,
                 (((0,), (0,)), ((), ())),
@@ -1001,32 +1194,48 @@
             back, by_gain = head_back(
                 proj[0, :, columns(column)], gains[gain : gain + 1, :], value, cos_ref[...], sin_ref[...]
             )
-            out[0, :, columns(column)] = back.astype(jnp.bfloat16)
+            out[:, columns(column)] = back.astype(jnp.bfloat16)
             gain_grad[gain] += by_gain.reshape(rows // 8, 8, HD).sum(axis=0)
 
         for head in range(heads):
             settle(head, 0, grad_q[head])
         settle(heads, 1, grad_k[...] * (HD ** (-0.5)))
-        out[0, :, columns(heads + 1)] = grad_v[...].astype(jnp.bfloat16)
-
-        across_columns(out[0], weights, 0, wide, back_part)
-
-        @pl.when(sequence == 1)
-        def _():
-            steps[2]()
-
-        by_projected, by_attended = out[0].T, attended[0].T
+        out[:, columns(heads + 1)] = grad_v_sum[...].astype(jnp.bfloat16)
+
+        across_columns(out[...], weights, 0, wide, back_part)
+
+        by_projected, by_attended = out[...].T, attended[0].T
         for start in range(0, width, 512):
             at = pl.ds(start, 512)
             summed[:wide, at] += jnp.dot(
                 by_projected, normed[0, :, at], preferred_element_type=jnp.float32
             )
             summed[wide:, at] += jnp.dot(
-                by_attended, grad[0, :, at], preferred_element_type=jnp.float32
+                by_attended, grad[:, start : start + 512], preferred_element_type=jnp.float32
             )
 
-        @pl.when(sequence == count - 1)
+        @pl.when(place == 0)
         def _():
+            gather[5]()
+            steps[1]()
+            for copy in copies:
+                copy.start()
+            gather[4]()
+            arrival(1).start()
+
+        @pl.when(place == 1)
+        def _():
+            steps[2]()
+            gather[6]()
+            arrival(2).start()
+
+        @pl.when(place == count - 1)
+        def _():
+            for outer in range(outer_count):
+                for member in range(split):
+                    start = (outer * split + member) * share
+                    staged[outer, member] = summed[:, start : start + share].astype(jnp.bfloat16)
+            store.start()
             fetch.wait()
             steps[3]()
 
@@ -1035,12 +1244,7 @@
                 output[at] = (held[at] + value).astype(jnp.bfloat16)
 
             row_loop(own_rows, finish)
-            for outer in range(outer_count):
-                for member in range(split):
-                    start = (outer * split + member) * share
-                    grad_weights[outer, member] = summed[:, start : start + share].astype(
-                        jnp.bfloat16
-                    )
+            store.wait()
             for copy in copies:
                 copy.wait()
 
@@ -1049,7 +1253,7 @@
         name="attend_back",
         grid=(count,),
         out_shape=(
-            jax.ShapeDtypeStruct((count, rows, wide), jnp.bfloat16),
+            layer_rows(own_rows, width),
             jax.ShapeDtypeStruct((2, 8, HD), jnp.float32),
             jax.ShapeDtypeStruct((count, rows, width), jnp.bfloat16),
             jax.ShapeDtypeStruct((own_rows, width), jnp.bfloat16),
@@ -1058,25 +1262,25 @@
         + tuple(like(piece) for piece in extra),
         in_specs=[
             pl.BlockSpec(memory_space=pltpu.SMEM),
-            per_sequence(rows, wide),
-            per_sequence(rows, width),
-            per_sequence(rows, heads * HD),
-            per_sequence(rows, width),
-            per_sequence(rows, HD),
-            whole(width, wide + heads * HD),
+            ordered(rows, wide),
+            ordered(rows, width),
+            ordered(rows, heads * HD),
+            whole(own_rows, width),
+            ordered(rows, HD),
+            anywhere(),
             whole(rows, HD),
             whole(rows, HD),
             whole(2, HD),
             anywhere(),
             anywhere(),
         ]
-        + [anywhere()] * extras,
+        + [whole(*piece.shape) for piece in extra],
         out_specs=(
-            per_sequence(rows, wide),
+            anywhere(),
             pl.BlockSpec((2, 8, HD), lambda s: (0, 0, 0)),
-            per_sequence(rows, width),
+            ordered(rows, width),
             whole(own_rows, width),
-            whole(outer_count, split, every, share),
+            anywhere(),
         )
         + (anywhere(),) * extras,
         scratch_shapes=[
@@ -1091,8 +1295,16 @@
             pltpu.VMEM((own_rows, width), jnp.float32),
             pltpu.VMEM((own_rows, width), jnp.float32),
             pltpu.SemaphoreType.DMA,
+            pltpu.VMEM((rows, wide), jnp.bfloat16),
+            pltpu.VMEM((2, 2, own_rows, width), jnp.bfloat16),
+            pltpu.SemaphoreType.DMA((2,)),
+            pltpu.VMEM(weights.shape, weights.dtype),
+            pltpu.VMEM((outer_count, split, every, share), jnp.bfloat16),
+            pltpu.SemaphoreType.DMA,
+            pltpu.SemaphoreType.DMA,
         ]
         + sum_scratch(own_rows, width, cut)
+        + gather_scratch()
         + exchange_scratch() * extras,
         compiler_params=params(number),
         cost_estimate=cost_of(50),
@@ -1101,7 +1313,7 @@
         projected,
         normed,
         attended,
-        grad_attn,
+        own_grad,
         logs,
         weights,
         cos_full,
@@ -1155,7 +1367,7 @@
         in_specs=[
             per_sequence(rows, width),
             whole(*weights.shape),
-            anywhere(),
+            whole(*cotangent.shape),
             anywhere(),
         ],
         out_specs=(per_sequence(rows, 2 * units), per_sequence(rows, units), anywhere()),
@@ -1170,124 +1382,186 @@
     count, rows, width = grads.shape
     units = weights.shape[1]
 
-    def kernel(grads, weights, product, out):
+    def kernel(grads, weights, product, by_gate, by_up):
         for start in range(0, units, 256):
             gate_at, up_at = pl.ds(start, 256), pl.ds(units + start, 256)
             grad = jnp.dot(grads[0], weights[:, gate_at], preferred_element_type=jnp.float32)
             gate, up = product[0, :, gate_at], product[0, :, up_at]
             share = jax.nn.sigmoid(gate)
-            by_gate = grad * up * share * (1.0 + gate * (1.0 - share))
-            out[0, :, gate_at] = by_gate.astype(jnp.bfloat16)
-            out[0, :, up_at] = (grad * gate * share).astype(jnp.bfloat16)
+            slope = grad * up * share * (1.0 + gate * (1.0 - share))
+            by_gate[0, :, gate_at] = slope.astype(jnp.bfloat16)
+            by_up[0, :, gate_at] = (grad * gate * share).astype(jnp.bfloat16)
 
     return pl.pallas_call(
         kernel,
         name="feed_back",
         grid=(count,),
-        out_shape=jax.ShapeDtypeStruct((count, rows, 2 * units), jnp.bfloat16),
+        out_shape=(jax.ShapeDtypeStruct((count, rows, units), jnp.bfloat16),) * 2,
         in_specs=[
             per_sequence(rows, width),
             whole(*weights.shape),
             per_sequence(rows, 2 * units),
         ],
-        out_specs=per_sequence(rows, 2 * units),
+        out_specs=(per_sequence(rows, units),) * 2,
         compiler_params=pltpu.CompilerParams(vmem_limit_bytes=VMEM_LIMIT),
         cost_estimate=cost_of(18),
     )(grads, weights, product)
 
 
-def adam_all(sets, pieces, factor):
-    jobs = []
-    for weight, _, _, source, kind, detail in sets:
-        rows = weight.shape[0]
-        height = {"columns": max(CHUNK, rows // 4), "across": rows}.get(kind, rows // TEAM)
-        jobs.append((height, rows // height, source, kind, detail))
-    count = sum(job[1] for job in jobs)
-    total, sources = len(sets), len(pieces)
+def spans(widths, base=0):
+    for member in range(TEAM):
+        first, inside = base, 0
+        for width in widths:
+            share = width // TEAM
+            yield member, pl.ds(first + member * share, share), pl.ds(inside, share)
+            first += width
+            inside += share
+
+
+def by_columns(start, height, widths, source):
+    def run(pieces, update):
+        @pl.loop(0, height // CHUNK)
+        def _(row):
+            rows = pl.ds(pl.multiple_of(start + row * CHUNK, CHUNK), CHUNK)
+            for member, across, inside in spans(widths):
+                update(rows, across, pieces[member, rows, inside])
+
+    return source, pl.ds(start, height), pl.ds(0, sum(widths)), run
+
+
+def by_turned(height, base, widths, source, members=range(TEAM)):
+    parts = [part for part in spans(widths, base) if part[0] in members]
+
+    def run(pieces, update):
+        for member, across, inside in parts:
+            update(pl.ds(0, height), across, pieces[member, inside].astype(jnp.float32).T)
+
+    if len(members) == 1:
+        columns = parts[0][1]
+    else:
+        columns = pl.ds(base, sum(widths))
+    return source, pl.ds(0, height), columns, run
+
+
+def by_rows(member, height, width, inside, source):
+    at, across = pl.ds(member * height, height), pl.ds(0, width)
+
+    def run(pieces, update):
+        if inside is None:
+            update(at, across, pieces[member].astype(jnp.float32).T)
+        else:
+            update(at, across, pieces[member, pl.ds(inside, height)])
+
+    return source, at, across, run
+
+
+def adam_all(sets, pieces, factor, gain_grad, gains, passed):
+    jobs = [(place,) + job for place, group in enumerate(sets) for job in group[3]]
+    count, total, sources, others = len(jobs), len(sets), len(pieces), len(passed)
 
     def kernel(*refs):
         inputs, refs = refs[: 3 * total], refs[3 * total :]
         piece_refs, factor, refs = refs[:sources], refs[sources], refs[sources + 1 :]
+        (gain_grad, *gains), refs = refs[:4], refs[4:]
+        passed, refs = refs[:others], refs[others:]
         outputs, refs = refs[: 4 * total], refs[4 * total :]
+        new_gains, refs = refs[:3], refs[3:]
+        onward, refs = refs[:others], refs[others:]
         held, refs = refs[: 4 * total], refs[4 * total :]
-        held_pieces, (piece_sem, in_sem, out_sem) = refs[:sources], refs[sources:]
+        held_pieces, refs = refs[:sources], refs[sources:]
+        between, (piece_sem, in_sem, out_sem, pass_sem) = refs[:others], refs[others:]
         scale = factor[0:1, 0:1]
-        loads, stores, work, slot = [], [], [], 0
-        for place in range(sources):
-            loads.append(
-                pltpu.make_async_copy(piece_refs[place], held_pieces[place], piece_sem.at[place])
-            )
-            loads[place].start()
-        for place, (height, steps, *_) in enumerate(jobs):
-            for step in range(steps):
-                at = pl.ds(step * height, height)
-                arrive = []
-                for number in range(3):
-                    copy = pltpu.make_async_copy(
-                        inputs[3 * place + number].at[at],
-                        held[4 * place + number].at[at],
+        loads = [
+            pltpu.make_async_copy(piece_refs[place], held_pieces[place], piece_sem.at[place])
+            for place in range(sources)
+        ]
+        arrivals, stores = [], []
+        kept = [
+            pltpu.make_async_copy(source, target, pass_sem.at[0, place])
+            for place, (source, target) in enumerate(zip(passed, between))
+        ]
+        kept_on = [
+            pltpu.make_async_copy(source, target, pass_sem.at[1, place])
+            for place, (source, target) in enumerate(zip(between, onward))
+        ]
+        for slot, (place, source, at, across, _) in enumerate(jobs):
+            arrivals.append(
+                [
+                    pltpu.make_async_copy(
+                        inputs[3 * place + number].at[at, across],
+                        held[4 * place + number].at[at, across],
                         in_sem.at[3 * slot + number],
                     )
+                    for number in range(3)
+                ]
+            )
+        first_use = {}
+        for slot, job in enumerate(jobs):
+            first_use.setdefault(job[1], slot)
+
+        def bring(slot):
+            if slot < count:
+                if first_use[jobs[slot][1]] == slot:
+                    loads[jobs[slot][1]].start()
+                for copy in arrivals[slot]:
                     copy.start()
-                    arrive.append(copy)
-                work.append((place, step, at, slot, arrive))
-                slot += 1
-        arrived = set()
-        for place, step, at, slot, arrive in work:
-            height, _, source, kind, detail = jobs[place]
+
+        for slot in range(AHEAD):
+            bring(slot)
+        gain_step = adam_update(
+            gains[0][...],
+            gain_grad[: gains[0].shape[0]],
+            gains[1][...],
+            gains[2][...],
+            scale,
+            0.0,
+            gain_rate,
+        )
+        for target, value in zip(new_gains, gain_step):
+            target[...] = value
+        for slot, (place, source, at, across, run) in enumerate(jobs):
             weight, moment, square, low = held[4 * place : 4 * place + 4]
-            gradients = held_pieces[source]
-            if source not in arrived:
+            if first_use[source] == slot:
                 loads[source].wait()
-                arrived.add(source)
-            for copy in arrive:
+            for copy in arrivals[slot]:
                 copy.wait()
-
-            def update(rows, across, gradient):
-                where = (rows, across)
+            bring(slot + AHEAD)
+            if slot == 0:
+                for copy in kept:
+                    copy.start()
+
+            def update(rows, columns, gradient):
+                where = (rows, columns)
                 value, one, two = adam_update(
-                    weight[where], gradient, moment[where], square[where], scale, weight_decay, learn_rate
+                    weight[where],
+                    gradient.astype(jnp.float32),
+                    moment[where],
+                    square[where],
+                    scale,
+                    weight_decay,
+                    learn_rate,
                 )
                 weight[where], moment[where], square[where] = value, one, two
                 low[where] = value.astype(jnp.bfloat16)
 
-            def spans(widths):
-                for member in range(TEAM):
-                    first, inside = 0, 0
-                    for width in widths:
-                        share = width // TEAM
-                        yield member, pl.ds(first + member * share, share), pl.ds(inside, share)
-                        first += width
-                        inside += share
-
-            if kind == "rows":
-                update(at, slice(None), gradients[step].astype(jnp.float32).T)
-            elif kind == "below":
-                update(
-                    at, slice(None), gradients[step, pl.ds(detail, height)].astype(jnp.float32)
-                )
-            elif kind == "across":
-                for member, across, inside in spans(detail):
-                    update(at, across, gradients[member, inside].astype(jnp.float32).T)
-            else:
-
-                @pl.loop(0, height // CHUNK)
-                def _(row):
-                    rows = pl.ds(pl.multiple_of(step * height + row * CHUNK, CHUNK), CHUNK)
-                    for member, across, inside in spans(detail):
-                        update(rows, across, gradients[member, rows, inside].astype(jnp.float32))
-
+            run(held_pieces[source], update)
             for number, origin in enumerate((weight, moment, square, low)):
                 copy = pltpu.make_async_copy(
-                    origin.at[at], outputs[4 * place + number].at[at], out_sem.at[4 * slot + number]
+                    origin.at[at, across],
+                    outputs[4 * place + number].at[at, across],
+                    out_sem.at[4 * slot + number],
                 )
                 copy.start()
                 stores.append(copy)
-        for copy in stores:
+            if slot == 4:
+                for arrived, copy in zip(kept, kept_on):
+                    arrived.wait()
+                    copy.start()
+        for copy in stores + kept_on:
             copy.wait()
 
     args, shapes, scratch = [], [], []
-    for weight, moment, square, *_ in sets:
+    for weight, moment, square, _ in sets:
         args += [weight, moment, square]
         low = jax.ShapeDtypeStruct(weight.shape, jnp.bfloat16)
         shapes += [like(weight)] * 3 + [low]
@@ -1295,20 +1569,22 @@
     outs = pl.pallas_call(
         kernel,
         name="adam_all",
-        out_shape=tuple(shapes),
-        in_specs=[anywhere()] * (3 * total + sources) + [in_vmem()],
-        out_specs=(anywhere(),) * (4 * total),
+        out_shape=tuple(shapes) + (like(gains[0]),) * 3 + tuple(like(each) for each in passed),
+        in_specs=[anywhere()] * (3 * total + sources) + [in_vmem()] * 5 + [anywhere()] * others,
+        out_specs=(anywhere(),) * (4 * total) + (in_vmem(),) * 3 + (anywhere(),) * others,
         scratch_shapes=scratch
-        + [pltpu.VMEM(piece.shape, piece.dtype) for piece in pieces]
+        + [pltpu.VMEM(each.shape, each.dtype) for each in tuple(pieces) + tuple(passed)]
         + [
             pltpu.SemaphoreType.DMA((sources,)),
             pltpu.SemaphoreType.DMA((3 * count,)),
             pltpu.SemaphoreType.DMA((4 * count,)),
+            pltpu.SemaphoreType.DMA((2, others)),
         ],
         compiler_params=pltpu.CompilerParams(vmem_limit_bytes=VMEM_LIMIT),
         cost_estimate=cost_of(15),
-    )(*args, *pieces, factor)
-    return [outs[4 * place : 4 * place + 4] for place in range(total)]
+    )(*args, *pieces, factor, gain_grad, *gains, *passed)
+    steps = [outs[4 * place : 4 * place + 4] for place in range(total)]
+    return steps + [outs[4 * total : 4 * total + 3], outs[4 * total + 3 :]]
 
 
 def split_columns(values, widths):
@@ -1330,6 +1606,12 @@
 
 def team_pieces(summed):
     return summed.reshape(TEAM, -1, summed.shape[-1])
+
+
+def turned_pieces(summed):
+    if summed.shape[1] * TEAM * lax.axis_size("outer") == D:
+        return team_pieces(summed)
+    return summed.reshape(summed.shape[0], TEAM, -1).transpose(1, 0, 2)
 
 
 def sum_weight(gradient):
@@ -1398,6 +1680,7 @@
     hidden_units = FF // tp_count // TEAM
     qkv_widths = (H * HD // tp_count, KV * HD // tp_count, KV * HD // tp_count)
     out_widths = (H * HD // tp_count,)
+    part_rows = qkv_weight.shape[0]
     gate_up_widths = (FF // tp_count, FF // tp_count)
     down_widths = (FF // tp_count,)
 
@@ -1451,7 +1734,7 @@
         normed_attn, (gate_up_pieces,), 0, "gather_inputs"
     )
     gate_up_full = gather_outer(gate_up_mixed)
-    early = half_rows * 3 // 5 // CHUNK * CHUNK
+    early = half_rows * 2 // 5 // CHUNK * CHUNK
     projected, attended, logs, attn_branch, grad_all, down_mixed = attend(
         normed_attn.reshape(TEAM, row_count, D),
         first_full,
@@ -1473,20 +1756,32 @@
     grad_down = over_rows(grad_all.reshape(-1, D), activated.reshape(-1, hidden_units))
     grad_all, grad_down = after(grad_all, grad_down.astype(jnp.bfloat16))
     down_sum = sum_weight(grad_down)
-    grad_gate_up = feed_back(grad_all.reshape(TEAM, row_count, D), down_full, gate_up)
-    grad_gate_up_weight = over_rows(normed_mlp, grad_gate_up.reshape(-1, 2 * hidden_units))
-    grad_gate_up, grad_gate_up_weight = after(
-        grad_gate_up, grad_gate_up_weight.astype(jnp.bfloat16)
-    )
-    gate_up_sum = sum_weight(grad_gate_up_weight)
-    grad_hidden, grad_mlp_gain, grad_attn, mlp_part = feed_back_rest(
-        grad_gate_up, gate_up_full, activated, down_full, hidden, grad_low, mlp_gain, 3, "feed_back_rest"
-    )
+    grad_gate, grad_up = feed_back(
+        grad_all.reshape(TEAM, row_count, D), down_full, gate_up
+    )
+    grad_gate_weight = over_rows(normed_mlp, grad_gate.reshape(-1, hidden_units))
+    grad_gate, grad_gate_weight = after(grad_gate, grad_gate_weight.astype(jnp.bfloat16))
+    gate_sum = sum_weight(grad_gate_weight)
+    grad_hidden, grad_mlp_gain, own_grad, mlp_part, grad_up_weight = feed_back_rest(
+        grad_gate,
+        grad_up,
+        gate_up_full,
+        activated,
+        down_full,
+        normed_mlp,
+        hidden,
+        grad_low,
+        mlp_gain,
+        lax.axis_size("outer"),
+        3,
+        "feed_back_rest",
+    )
+    up_sum = turned_pieces(sum_weight(grad_up_weight.reshape(-1, grad_up_weight.shape[2])))
     _, grad_head_gains, grad_normed_attn, output, grad_first, down_mixed = attend_back(
         projected,
         normed_attn.reshape(TEAM, row_count, D),
         attended,
-        grad_attn.reshape(TEAM, row_count, D),
+        own_grad,
         logs,
         first_full,
         mlp_part,
@@ -1500,57 +1795,84 @@
         heads,
         7,
     )
-    first_sum = sum_weight(grad_first.reshape(-1, grad_first.shape[3]))
-    if grad_first.shape[1] == TEAM:
-        first_sum = team_pieces(first_sum)
-    else:
-        first_sum = first_sum.reshape(first_sum.shape[0], TEAM, -1).transpose(1, 0, 2)
-    input_grad, attn_gain_parts, gate_up_mixed = norm_back_last(
+    grad_first, gate_sum = after(grad_first, gate_sum)
+    first_sum = turned_pieces(sum_weight(grad_first.reshape(-1, grad_first.shape[3])))
+    input_grad, attn_gain_parts, squares, gate_mixed, up_mixed = norm_back_last(
         grad_normed_attn,
         inputs,
         grad_hidden,
         attn_gain,
-        (team_pieces(gate_up_sum),),
+        (team_pieces(gate_sum), up_sum),
+        (gate_sum, up_sum, down_sum),
         4,
         "norm_back_attn",
     )
     gain_part = jnp.concatenate(
         [jnp.zeros_like(grad_mlp_gain), grad_mlp_gain, grad_head_gains.sum(axis=1).reshape(-1)]
     )
-    square_part = sum(
-        jnp.sum(jnp.square(member.astype(jnp.float32))) for member in (gate_up_sum, down_sum)
-    )
     gain_count = gain_part.shape[0]
     packed = jnp.pad(gain_part, (0, -gain_count % PAD))
-    packed = jnp.concatenate([packed, jnp.pad(square_part[None], (0, PAD - 1))])
     packed, norm_tile, factor_tile, first_mixed = total_everywhere(
         packed.reshape(-1, HD),
         attn_gain_parts,
+        squares,
         first_sum,
         lax.axis_size("outer"),
         5,
         "total_everywhere",
     )
-    gain_grad = packed.reshape(-1)[:gain_count]
-    grad_norm, factor = norm_tile[0, 0], factor_tile[0, 0]
+    grad_norm = norm_tile[0, 0]
     (
         (new_gate_up, new_gate_up_one, new_gate_up_two, gate_up_copy),
         (new_down, new_down_one, new_down_two, down_copy),
         (new_out, new_out_one, new_out_two, out_copy),
         (new_qkv, new_qkv_one, new_qkv_two, qkv_copy),
+        new_gains,
+        (output, input_grad),
     ) = adam_all(
         [
-            (gate_up_weight, gate_up_moment, gate_up_square, 0, "columns", gate_up_widths),
-            (down_weight, down_moment, down_square, 1, "rows", None),
-            (out_weight, out_moment, out_square, 2, "below", (heads + 2) * HD),
-            (qkv_weight, qkv_moment, qkv_square, 2, "across", qkv_widths),
+            (
+                gate_up_weight,
+                gate_up_moment,
+                gate_up_square,
+                [
+                    by_columns(start, max(CHUNK, part_rows // 4), gate_up_widths[:1], 0)
+                    for start in range(0, part_rows, max(CHUNK, part_rows // 4))
+                ]
+                + [
+                    by_turned(part_rows, gate_up_widths[0], gate_up_widths[1:], 1, (member,))
+                    for member in range(TEAM)
+                ],
+            ),
+            (
+                down_weight,
+                down_moment,
+                down_square,
+                [by_rows(member, hidden_units, part_rows, None, 2) for member in range(TEAM)],
+            ),
+            (
+                out_weight,
+                out_moment,
+                out_square,
+                [
+                    by_rows(member, heads * HD, part_rows, (heads + 2) * HD, 3)
+                    for member in range(TEAM)
+                ],
+            ),
+            (
+                qkv_weight,
+                qkv_moment,
+                qkv_square,
+                [by_turned(part_rows, 0, qkv_widths, 3)],
+            ),
         ],
-        (gate_up_mixed, down_mixed, first_mixed),
+        (gate_mixed, up_mixed, down_mixed, first_mixed),
         factor_tile,
-    )
-    new_gains, new_gains_one, new_gains_two = adam_update(
-        norm_gains, gain_grad, gains_moment, gains_square, factor, 0.0, gain_rate
-    )
+        packed,
+        [each.reshape(-1, HD) for each in (norm_gains, gains_moment, gains_square)],
+        (output, input_grad),
+    )
+    new_gains, new_gains_one, new_gains_two = (each.reshape(-1) for each in new_gains)
     return (
         output,
         input_grad,

time: 618 us -> 590 us (0.955)
  matrix products: 36 us -> 27.2 us
  Pallas kernels: 530 us -> 522 us
    pallas_call x1, Pallas kernels: 109 us -> 59.5 us  [feed_back_rest(): pl.pallas_call(kernel, name=name, out_shape=(jax.ShapeDtypeStruct((rows,...]
    pallas_call x3, Pallas kernels: 98.6 us -> 140 us  [the longest x1 100 us: attend_back(): pl.pallas_call(kernel, name='attend_back', grid=(count,), out_shape=(laye...]
    pallas_call x1, Pallas kernels: 28.2 us -> 37.1 us  [feed(): pl.pallas_call(kernel, name='feed', grid=(count,), out_shape=(jax.ShapeDt...]
    dot_general x2, matrix products: 36 us -> 27.2 us  [dot(): lax.dot_general(left, right, ((contract[0], contract[1]), ((), ())), pref...]
    pallas_call x1, Pallas kernels: 40.5 us -> 32.1 us  [attend(): pl.pallas_call(kernel, name='attend', grid=(count,), out_shape=(jax.Shape...]
  transfers between devices with their start and end apart: 6 -> 7, of which waited for: 0 -> 0; matrix products, arithmetic and copies ran while one was open for 8% -> 7% of each run, Pallas kernels for 79% -> 81%
where the time goes in v7:
time: 590 us; the launch traced here: 582 us
  Pallas kernels  522 us (88%)
  matrix products  27.2 us (5%)
  between operations  14.9 us (3%)
  other arithmetic  11.7 us (2%)
    pallas_call x1, Pallas kernels, branch_and_norm(): pl.pallas_call(kernel, name=name, out_shape=(jax.ShapeDtypeStruct((rows,...  102 us
    pallas_call x1, Pallas kernels, attend_back(): pl.pallas_call(kernel, name='attend_back', grid=(count,), out_shape=(laye...  100 us
    pallas_call x1, Pallas kernels, norm_back_last(): pl.pallas_call(kernel, name=name, out_shape=(jax.ShapeDtypeStruct((rows,...  63.3 us
    pallas_call x1, Pallas kernels, feed_back_rest(): pl.pallas_call(kernel, name=name, out_shape=(jax.ShapeDtypeStruct((rows,...  59.5 us
    pallas_call x1, Pallas kernels, gather_rows(): pl.pallas_call(kernel, name=name, out_shape=(layer_rows(rows, width),) +...  57.9 us
    pallas_call x1, Pallas kernels, feed(): pl.pallas_call(kernel, name='feed', grid=(count,), out_shape=(jax.ShapeDt...  37.1 us
    pallas_call x1, Pallas kernels, attend(): pl.pallas_call(kernel, name='attend', grid=(count,), out_shape=(jax.Shape...  32.1 us
    dot_general x2, matrix products, dot(): lax.dot_general(left, right, ((contract[0], contract[1]), ((), ())), pref...  27.2 us
  transfers between devices with their start and end apart: 7, of which 0 were waited for; matrix products, arithmetic and copies ran while one was open for 7% of the time, Pallas kernels for 81%

profile of v7, /device:TPU:0, one launch (start us, length us, event | category | flops | bytes accessed | tf_op | source)
XLA Modules:
  0.0 582.3 jit_solution(17016968981526339054)
XLA Ops:
  7.2 0.0 copy-start.4
  7.2 0.0 all-gather.4.cloned.1.call-start
  7.2 1.3 convert_element_type.28
  8.7 0.1 copy.44
  8.9 0.0 copy-start.2
  8.9 0.9 maximum_maximum_fusion.pieces
  9.9 12.9 %exchange_first.1 = bf16[4,128,768]{2,1,0:T(8,128)(2,1)} custom-call(bf16[4,128,768]{2,1,0:T(8,128)(2,1)} %maximum_maximum_fusion.pieces), custom_call_target="tpu_custom_call" | custom-call | bytes 1200000 | tf_op jit(solution)/shard_map/exchange_first/pallas_call | solution.py:391
  22.8 0.0 all-gather.4.cloned.1.call-update
  22.8 0.0 all-gather.6.cloned.1.call-start
  22.9 0.0 copy-done.2
  22.9 1.2 copy.45
  24.1 0.0 copy-done.11
  24.1 0.2 select_reduce_fusion.lengths
  24.2 0.6 dynamic_slice.4
  24.8 0.7 add_compare_fusion
  25.5 1.2 fusion.5
  26.7 0.0 copy-start
  26.8 1.1 pad_maximum_fusion.2
  27.8 0.1 slice_bitcast_fusion.3
  27.9 1.0 pad_maximum_fusion.1.rest_0_
  28.9 0.0 copy-done.10
  28.9 0.4 fusion
  29.2 0.6 fusion.10
  29.9 1.2 broadcast_select_fusion.own.upstream
  31.1 1.4 fusion.2.own
  32.5 0.0 copy-done.6
  32.5 0.1 copy-done.1
  32.6 0.2 convert_element_type.31
  32.8 0.1 fusion.7
  32.9 0.1 maximum_bitcast_fusion
  33.0 0.1 maximum_bitcast_fusion.2
  33.0 1.3 pad_maximum_fusion.rest_0_
  34.4 57.9 %gather_inputs.1 = (bf16[2,2,2,320,2048]{4,3,2,1,0:T(8,128)(2,1)}, bf16[4,128,1536]{2,1,0:T(8,128)(2,1)}) custom-call(bf16[320,2048]{1,0:T(8,128)(2,1)} %fusion.2.own, bf16[4,128,1536]{2,1,0:T(8,128)(2,1)} %pad_maximum_fusion.rest_0_), custom_call_target="tpu_custom_call" | custom-call | bytes 6000000 | tf_op jit(solution)/shard_map/gather_inputs/pallas_call | solution.py:422
  92.3 0.0 all-gather.6.cloned.1.call-update
  92.3 0.0 all-gather.8.cloned.1.call-start
  92.3 0.6 slice_bitcast_fusion.8.gains
  92.9 32.1 %attend.1 = (f32[4,640,512]{2,1,0:T(8,128)}, bf16[4,640,256]{2,1,0:T(8,128)(2,1)}, f32[4,640,128]{2,1,0:T(8,128)}, bf16[4,640,2048]{2,1,0:T(8,128)(2,1)}, bf16[2...) custom-call(s32[4]{0:T(128)} %copy-done.10, bf16[4,640,2048]{2,1,0:T(8,128)(2,1)} %bitcast.84, ...), custom_call_target="tpu_custom_call" | custom-call | bytes 5000000 | tf_op jit(solution)/shard_map/attend/pallas_call | solution.py:1025
  125.0 0.0 all-gather.8.cloned.1.call-update
  125.1 0.3 reduce-scatter.5.cloned.1.call-start
  125.3 102.1 %branch_and_norm.1 = (f32[320,2048]{1,0:T(8,128)}, bf16[2,2,2,320,2048]{4,3,2,1,0:T(8,128)(2,1)}) custom-call(bf16[2,2,2,320,2048]{4,3,2,1,0:T(8,128)(2,1)} %bitcast.86, bf16[320,2048]{1,0:T(8,128)(2,1)} %values.1, f32[1,2048]{1,0:T(1,128)} %bitcast.107), custom_call_target="tpu_custom_call" | custom-call | bytes 9500000 | tf_op jit(solution)/shard_map/branch_and_norm/pallas_call | solution.py:471
  227.5 0.0 all-gather.6.cloned.1.call-done.weights
  227.5 37.1 %feed.1 = (f32[4,640,1536]{2,1,0:T(8,128)}, bf16[4,640,768]{2,1,0:T(8,128)(2,1)}, bf16[2,2,2,320,2048]{4,3,2,1,0:T(8,128)(2,1)}) custom-call(bf16[4,640,2048]{2,1,0:T(8,128)(2,1)} %bitcast.79, bf16[2048,1536]{1,0:T(8,128)(2,1)} %all-gather.6.cloned.1.call-done.weights, ...), custom_call_target="tpu_custom_call", output_to_operand_aliasing={{2}: (3, {})} | custom-call | bytes 2800000 | tf_op jit(solution)/shard_map/feed/pallas_call | solution.py:1358
  264.6 13.6 %convolution_convert_fusion.1 = bf16[2048,768]{1,0:T(8,128)(2,1)} fusion(bf16[2560,2048]{1,0:T(8,128)(2,1)} %bitcast.82, bf16[2560,768]{1,0:T(8,128)(2,1)} %bitcast.89), kind=kOutput, calls=%fused_computation.1 | convolution fusion | flops 8054636544 | bytes 17563648 | tf_op jit(solution)/shard_map/dot_general | solution.py:1638
  278.2 0.0 reduce-scatter.5.cloned.1.call-update
  278.2 0.3 reduce-scatter.7.cloned.1.call-start
  278.5 0.0 all-gather.8.cloned.1.call-done.weights.down
  278.5 17.6 %feed_back.1 = (bf16[4,640,768]{2,1,0:T(8,128)(2,1)}, bf16[4,640,768]{2,1,0:T(8,128)(2,1)}) custom-call(bf16[4,640,2048]{2,1,0:T(8,128)(2,1)} %bitcast.83, bf16[2048,768]{1,0:T(8,128)(2,1)} %all-gather.8.cloned.1.call-done.weights.down, f32[4,640,1536]{2,1,0:T(8,128)} %get-tuple-element.104.product), custom_call_target="tpu_custom_call" | custom-call | bytes 1800000 | tf_op jit(solution)/shard_map/feed_back/pallas_call | solution.py:1395
  296.2 13.6 %convolution_convert_fusion = bf16[2048,768]{1,0:T(8,128)(2,1)} fusion(bf16[2560,2048]{1,0:T(8,128)(2,1)} %bitcast.80, bf16[2560,768]{1,0:T(8,128)(2,1)} %bitcast.91), kind=kOutput, calls=%fused_computation | convolution fusion | flops 8054636544 | bytes 17563648 | tf_op jit(solution)/shard_map/dot_general | solution.py:1638
  309.8 0.0 reduce-scatter.7.cloned.1.call-update
  309.8 0.5 reduce-scatter.9.cloned.1.call-start
  310.3 59.5 %feed_back_rest.1 = (f32[320,2048]{1,0:T(8,128)}, f32[8,2048]{1,0:T(8,128)}, bf16[320,2048]{1,0:T(8,128)(2,1)}, bf16[4,2,320,2048]{3,2,1,0:T(8,128)(2,1)}, bf16[16,768,128]{2,1,0:T(8,128)(2,1)}) custom-call(bf16[4,2,320,768]{3,2,1,0:T(8,128)(2,1)} %bitcast.92, bf16[4,2,320,768]{3,2,1,0:T(8,128)(2,1)} %bitcast.93, ...), custom_call_target="tpu_custom_call" | custom-call | bytes 6000000 | tf_op jit(solution)/shard_map/feed_back_rest/pallas_call | solution.py:691
  369.8 0.0 reduce-scatter.9.cloned.1.call-update
  369.8 0.0 reduce-scatter.11.cloned.1.call-start
  369.9 0.0 reduce-scatter.5.cloned.1.call-done.rest_4_
  369.9 100.4 %attend_back.1 = (bf16[2,2,2,320,2048]{4,3,2,1,0:T(8,128)(2,1)}, f32[2,8,128]{2,1,0:T(8,128)}, bf16[4,640,2048]{2,1,0:T(8,128)(2,1)}, bf16[320,2048]{1,0:T(8,128...) custom-call(s32[4]{0:T(128)} %copy-done.10, f32[4,640,512]{2,1,0:T(8,128)} %get-tuple-element.94.proj, ...), custom_call_target="tpu_custom_call" | custom-call | bytes 5000000 | tf_op jit(solution)/shard_map/attend_back/pallas_call | solution.py:1251
  470.4 0.0 reduce-scatter.7.cloned.1.call-done.rest_2_
  470.4 0.0 reduce-scatter.11.cloned.1.call-update
  470.4 0.8 copy-done.8
  471.2 0.0 reduce-scatter.9.cloned.1.call-done
  471.3 63.3 %norm_back_attn.1 = (bf16[320,2048]{1,0:T(8,128)(2,1)}, f32[8,2048]{1,0:T(8,128)}, f32[8,128]{1,0:T(8,128)}, bf16[4,128,768]{2,1,0:T(8,128)(2,1)}, bf16[4,768,128]{2,1,0:T(8,128)(2,1)}) custom-call(bf16[2,2,2,320,2048]{4,3,2,1,0:T(8,128)(2,1)} %bitcast.87, bf16[320,2048]{1,0:T(8,128)(2,1)} %values.1, f32[320,2048]{1,0:T(8,128)} %get-tuple-element.114.upstream, ...), custom_call_target="tpu_custom_call" | custom-call | bytes 6500000 | tf_op jit(solution)/shard_map/norm_back_attn/pallas_call | solution.py:795
  534.6 0.6 fusion.6.values
  535.2 16.8 %total_everywhere.1 = (f32[48,128]{1,0:T(8,128)}, f32[8,128]{1,0:T(8,128)}, f32[8,128]{1,0:T(8,128)}, bf16[4,768,128]{2,1,0:T(8,128)(2,1)}) custom-call(f32[40,128]{1,0:T(8,128)} %fusion.6.values, f32[8,2048]{1,0:T(8,128)} %get-tuple-element.124.first, f32[8,128]{1,0:T(8,128)} %get-tuple-element.125.squares, bf16[4,768,128]{2,1,0:T(8,128)(2,1)} %bitcast.105), custom_call_target="tpu_custom_call" | custom-call | tf_op jit(solution)/shard_map/total_everywhere/pallas_call | solution.py:890
  552.0 1.2 slice.138
  553.2 21.8 %adam_all.1 = (f32[128,6144]{1,0:T(8,128)}, f32[128,6144]{1,0:T(8,128)}, f32[128,6144]{1,0:T(8,128)}, bf16[128,6144]{1,0:T(8,128)(2,1)}, f32[3072,128]{1,0:T(8,1...) custom-call(f32[128,6144]{1,0:T(8,128)} %refs_0_.1, ...), custom_call_target="tpu_custom_call" | custom-call | bytes 1500000 | tf_op jit(solution)/shard_map/adam_all/pallas_call | solution.py:1569
  (30 shorter events, 0.2 us)
Async XLA Ops:
  7.2 1.5 copy-start.4
  7.2 85.7 %all-gather.4.cloned.1.call-start = ((), (), s32[]{:S(2)}) async-start(), calls=%async_computation.4 | async-start | bytes 3932160 | tf_op jit(solution)/shard_map/all_gather | solution.py:1604
  8.9 14.0 %copy-start.2 = (f32[3072,128]{1,0:T(8,128)S(1)}, f32[3072,128]{1,0:T(8,128)}, u32[]{:S(2)}) copy-start(f32[3072,128]{1,0:T(8,128)} %refs_3_.1) | copy-start | bytes 4718596
  9.9 14.2 %copy-start.11 = (s32[16]{0:T(128)S(1)}, s32[16]{0:T(128)}, u32[]{:S(2)}) copy-start(s32[16]{0:T(128)} %param.21) | copy-start | bytes 196
  9.9 14.2 %copy-start.12 = (s32[16]{0:T(128)S(1)}, s32[16]{0:T(128)}, u32[]{:S(2)}) copy-start(s32[16]{0:T(128)} %param.22) | copy-start | bytes 196
  22.8 204.7 %all-gather.6.cloned.1.call-start = ((), (), s32[]{:S(2)}) async-start(), calls=%async_computation.5 | async-start | bytes 7864320 | tf_op jit(solution)/shard_map/all_gather | solution.py:1604
  24.0 3.8 copy-start.3
  24.2 4.6 copy-start.10
  26.7 2.1 copy-start
  27.8 1.4 copy-start.7
  27.8 2.0 copy-start.5
  29.9 2.6 copy-start.6
  29.9 2.8 copy-start.1
  92.3 186.2 %all-gather.8.cloned.1.call-start = ((), (), s32[]{:S(2)}) async-start(), calls=%async_computation.6 | async-start | bytes 3932160 | tf_op jit(solution)/shard_map/all_gather | solution.py:1604
  125.1 244.8 %reduce-scatter.5.cloned.1.call-start = ((), (), s32[]{:S(2)}) async-start(), calls=%async_computation.7 | async-start | bytes 3932160 | tf_op jit(solution)/shard_map/reduce_scatter | solution.py:1618
  278.2 192.2 %reduce-scatter.7.cloned.1.call-start = ((), (), s32[]{:S(2)}) async-start(), calls=%async_computation.8 | async-start | bytes 3932160 | tf_op jit(solution)/shard_map/reduce_scatter | solution.py:1618
  309.8 161.5 %reduce-scatter.9.cloned.1.call-start = ((), (), s32[]{:S(2)}) async-start(), calls=%async_computation.9 | async-start | bytes 3932160 | tf_op jit(solution)/shard_map/reduce_scatter | solution.py:1618
  369.8 165.4 %reduce-scatter.11.cloned.1.call-start = ((), (), s32[]{:S(2)}) async-start(), calls=%async_computation.10 | async-start | bytes 3932160 | tf_op jit(solution)/shard_map/reduce_scatter | solution.py:1618
  470.4 0.8 copy-start.8
  470.4 0.9 copy-start.9
Sparse Core Ops, SparseCore 0:
  22.9 64.6 all-gather.3
  92.4 115.8 all-gather.5
  209.9 61.7 all-gather.7
  278.3 60.6 reduce-scatter.4
  341.8 60.2 reduce-scatter.6
  404.3 60.2 reduce-scatter.8
  470.5 60.5 reduce-scatter.10

commit v8 on v7

--- a/solution.py
+++ b/solution.py
@@ -1,5 +1,8 @@
+from functools import partial
+
 import jax
 import jax.numpy as jnp
+import numpy as np
 from jax import lax
 from jax.experimental import pallas as pl
 from jax.experimental.pallas import tpu as pltpu
@@ -40,15 +43,11 @@
     return jax.nn.silu(gate_part) * up_part
 
 
-def pick(values, index):
-    return lax.dynamic_index_in_dim(values, index, 0, keepdims=False)
-
-
 MESH_ID = pl.DeviceIdType.MESH
 VMEM_LIMIT = 60 * 1024 * 1024
 CHUNK = 16
-GATHER_COPIES = 13
-AHEAD = 4
+GATHER_COPIES = 16
+AHEAD = 1000
 SUM_COPIES = 10
 NEIGHBOURS = ((1, 0, 0), (0, 1, 0), (0, 0, 1))
 MATES = ((0, 1, 0), (1, 0, 0), (1, 1, 0))
@@ -119,7 +118,7 @@
     return copies
 
 
-def plan_gather(own, out, send, recv, own_sem, cut, base=0, rows=None, parts=False):
+def plan_gather(own, out, send, recv, own_sem, cut, base=0, rows=None, parts=False, apart=False):
     near, core, tp = spots()
     rows = own.shape[0] if rows is None else rows
     low, high = pl.ds(base, cut), pl.ds(base + cut, rows - cut)
@@ -137,14 +136,19 @@
 
     keep = pltpu.make_async_copy(own.at[all_rows], out.at[near, core, tp, all_rows], own_sem)
     twin_own = give(4, all_rows, TO_CORE)
-    near_high = give(1, high, TO_NEAR)
+    first_rows = (rows - cut) // 2 // CHUNK * CHUNK
+    high_parts = [
+        (pl.ds(base + cut, first_rows), 1, 7, 8),
+        (pl.ds(base + cut + first_rows, rows - cut - first_rows), 13, 14, 15),
+    ]
+    near_high = [give(number, part, TO_NEAR) for part, number, _, _ in high_parts]
     tp_high = give(2, high, TO_TP)
-    far_high = relay(7, 1 - near, tp, high, TO_TP)
-    twin_beside = relay(8, 1 - near, tp, high, TO_CORE)
+    far_high = [relay(number, 1 - near, tp, part, TO_TP) for part, _, number, _ in high_parts]
+    twin_beside = [relay(number, 1 - near, tp, part, TO_CORE) for part, _, _, number in high_parts]
     twin_across = relay(9, near, 1 - tp, high, TO_CORE)
     twin_far = relay(12, 1 - near, 1 - tp, high, TO_CORE)
-    twins = [twin_own, twin_beside, twin_across, twin_far]
-    ways = [near_high, tp_high, far_high]
+    twins = [twin_own, twin_across, twin_far] + twin_beside
+    ways = near_high + far_high + [tp_high]
     if cut:
         tp_low = give(0, low, TO_TP)
         near_low = give(3, low, TO_NEAR)
@@ -155,24 +159,36 @@
         twins += [twin_across_low, twin_beside_low, twin_far_low]
         ways += [tp_low, near_low, far_low]
 
-    def begin():
+    def begin_tp():
         if cut:
             tp_low.start()
-        near_high.start()
         tp_high.start()
+        twin_own.start()
+        keep.start()
+
+    def begin_near():
+        for copy in near_high:
+            copy.start()
         if cut:
             near_low.start()
-        twin_own.start()
-        keep.start()
+
+    def begin():
+        begin_near()
+        begin_tp()
+
+    def pass_on(part):
+        near_high[part].wait_recv()
+        far_high[part].start()
+        twin_beside[part].start()
 
     def middle():
         if cut:
             tp_low.wait_recv()
             far_low.start()
             twin_across_low.start()
-        near_high.wait_recv()
-        far_high.start()
-        twin_beside.start()
+        pass_on(0)
+        if not apart:
+            pass_on(1)
 
     def later():
         tp_high.wait_recv()
@@ -194,11 +210,13 @@
         if cut:
             far_low.wait_recv()
             twin_far_low.start()
-        far_high.wait_recv()
+        for copy in far_high:
+            copy.wait_recv()
         twin_far.start()
 
     def rest_there():
-        twin_beside.wait_recv()
+        for copy in twin_beside:
+            copy.wait_recv()
         twin_far.wait_recv()
         if cut:
             twin_beside_low.wait_recv()
@@ -214,6 +232,8 @@
 
     if parts:
         return [begin, middle, later, own_there, twin_there, far_there, rest_there]
+    if apart:
+        return [begin_tp, begin_near, middle, partial(pass_on, 1), later, finish]
     return [begin, middle, later, finish]
 
 
@@ -379,63 +399,228 @@
     return jax.ShapeDtypeStruct((NEAR, CORE, 2, rows, width), jnp.bfloat16)
 
 
-def exchange(pieces, number, name):
-    def kernel(pieces, out, *sems):
-        greet(MATES)
-        copies = plan_exchange(pieces, out, *sems)
-        for copy in copies:
-            copy.start()
-        for copy in copies:
-            copy.wait()
-
-    return pl.pallas_call(
-        kernel,
-        name=name,
-        out_shape=like(pieces),
-        in_specs=[anywhere()],
-        out_specs=anywhere(),
-        scratch_shapes=exchange_scratch(),
-        compiler_params=params(number),
-        cost_estimate=cost_of(12),
-    )(pieces)
-
-
-def gather_rows(values, extra, number, name):
-    rows, width = values.shape
-    extras = len(extra)
-    cut = balanced(rows, crossing(extra, width))
-
-    def kernel(own, *rest):
-        pieces, out, mixed = rest[:extras], rest[extras], rest[extras + 1 : 2 * extras + 1]
-        sems = rest[2 * extras + 1 :]
-        begin, *steps = plan_gather(own, out, *sems[:3], cut=cut)
-        copies = plan_exchanges(pieces, mixed, sems[3:])
-        greet(EVERYONE_NEAR)
-        begin()
-        for copy in copies:
-            copy.start()
-        for step in steps:
-            step()
-        for copy in copies:
-            copy.wait()
-
-    outs = pl.pallas_call(
-        kernel,
-        name=name,
-        out_shape=(layer_rows(rows, width),) + tuple(like(piece) for piece in extra),
-        in_specs=[anywhere()] * (1 + extras),
-        out_specs=(anywhere(),) * (1 + extras),
-        scratch_shapes=gather_scratch() + exchange_scratch() * extras,
-        compiler_params=params(number),
-        cost_estimate=cost_of(60),
-    )(values, *extra)
-    return (outs[0].reshape(-1, width),) + tuple(outs[1:])
-
-
 def row_loop(rows, body):
     @pl.loop(0, rows // CHUNK)
     def _(step):
         body(pl.ds(pl.multiple_of(step * CHUNK, CHUNK), CHUNK))
+
+
+def plan_line(blocks, send, recv, count):
+    own = lax.axis_index("outer")
+
+    def message(side, number):
+        block = blocks.at[own - number if side == 0 else own + number]
+        return pltpu.make_async_remote_copy(
+            src_ref=block,
+            dst_ref=block,
+            send_sem=send.at[side, number],
+            recv_sem=recv.at[side, number],
+            device_id={"outer": own + 1 if side == 0 else own - 1},
+            device_id_type=MESH_ID,
+        )
+
+    def arrival(side, number):
+        block = blocks.at[own - 1 - number if side == 0 else own + 1 + number]
+        return pltpu.make_async_remote_copy(
+            src_ref=block,
+            dst_ref=block,
+            send_sem=send.at[side, number],
+            recv_sem=recv.at[side, number],
+            device_id={"outer": own + 1 if side == 0 else own - 1},
+            device_id_type=MESH_ID,
+        )
+
+    def sends(side, number):
+        if side == 0:
+            return (own < count - 1) & (own >= number)
+        return (own > 0) & (own + number < count)
+
+    def gets(side, number):
+        return own >= number + 1 if side == 0 else own + 1 + number < count
+
+    def push(number):
+        for side in range(2):
+
+            @pl.when(sends(side, number))
+            def _(side=side):
+                message(side, number).start()
+
+    def take(number):
+        for side in range(2):
+
+            @pl.when(gets(side, number))
+            def _(side=side):
+                arrival(side, number).wait_recv()
+
+            if number + 2 < count:
+
+                @pl.when(sends(side, number + 1))
+                def _(side=side):
+                    message(side, number + 1).start()
+
+    def settle():
+        for number in range(count - 1):
+            for side in range(2):
+
+                @pl.when(sends(side, number))
+                def _(side=side, number=number):
+                    message(side, number).wait_send()
+
+    return push, take, settle
+
+
+def greet_all(flips, count):
+    barrier = pltpu.get_barrier_semaphore()
+    own = lax.axis_index("outer")
+    for flip in flips:
+        pl.semaphore_signal(barrier, inc=1, device_id=flipped(*flip), device_id_type=MESH_ID)
+    for there, neighbour in ((own < count - 1, own + 1), (own > 0, own - 1)):
+
+        @pl.when(there)
+        def _(neighbour=neighbour):
+            pl.semaphore_signal(
+                barrier, inc=1, device_id={"outer": neighbour}, device_id_type=MESH_ID
+            )
+
+    beside = jnp.where(own < count - 1, 1, 0) + jnp.where(own > 0, 1, 0)
+    pl.semaphore_wait(barrier, len(flips) + beside)
+
+
+def sequence_length(lengths, owners, group):
+    total = jnp.int32(0)
+    for place in range(lengths.shape[0]):
+        total += jnp.where(owners[place] == group, lengths[place], 0)
+    return total
+
+
+def opening(
+    qkv, out_weight, gate_up, down, inputs, gain, cotangent, lengths, owners, outer_count, number
+):
+    rows, width = inputs.shape
+    part_rows, wide = qkv.shape
+    tall, units = out_weight.shape[0], down.shape[0]
+    widths = (wide // 2, wide // 4, wide // 4)
+    first_shape = jax.ShapeDtypeStruct((TEAM, part_rows, (wide + tall) // TEAM), jnp.bfloat16)
+    gate_up_shape = jax.ShapeDtypeStruct((TEAM, part_rows, 2 * units // TEAM), jnp.bfloat16)
+    down_shape = jax.ShapeDtypeStruct((TEAM, part_rows, units // TEAM), jnp.bfloat16)
+    cut = balanced(rows, crossing((first_shape, gate_up_shape), width))
+
+    def kernel(
+        lengths, owners, qkv, out_weight, inputs, gain, gate_up, down, cotangent,
+        out, mixed, full, low, down_pieces,
+        normed, first, pieces, gate_up_v, down_v, cotangent_v, load_sem, line_send, line_recv, *sems
+    ):
+        near, core, tp = spots()
+        outer = lax.axis_index("outer")
+        begin_tp, begin_near, middle, middle_rest, later, finish = plan_gather(
+            normed, out, *sems[:3], cut=cut, apart=True
+        )
+        team = plan_exchange(first, full.at[outer], *sems[3:6])
+        others = plan_exchange(pieces, mixed, *sems[6:9])
+        push, take, settle = plan_line(full, line_send, line_recv, outer_count)
+        fetch = [
+            pltpu.make_async_copy(source, target, load_sem.at[place])
+            for place, (source, target) in enumerate(
+                ((cotangent, cotangent_v), (gate_up, gate_up_v), (down, down_v))
+            )
+        ]
+        for copy in fetch:
+            copy.start()
+        for member, across, inside in spans(widths):
+            first[member, :, inside] = qkv[:, across].astype(jnp.bfloat16)
+        for member in range(TEAM):
+            at = pl.ds(member * (tall // TEAM), tall // TEAM)
+            first[member, :, wide // TEAM :] = out_weight[at].astype(jnp.bfloat16).T
+        greet_all(EVERYONE_NEAR, outer_count)
+        for copy in team:
+            copy.start()
+
+        def prepare(at):
+            value = inputs[at].astype(jnp.float32)
+            normed[at] = (value * rms_scale(value) * gain[...]).astype(jnp.bfloat16)
+
+        row_loop(rows, prepare)
+        begin_tp()
+        fetch[1].wait()
+        for member, across, inside in spans((units, units)):
+            pieces[member, :, inside] = gate_up_v[:, across].astype(jnp.bfloat16)
+        for copy in team:
+            copy.wait()
+        push(0)
+        begin_near()
+        length = sequence_length(lengths, owners, outer * TEAM + near * CORE + core)
+        fetch[0].wait()
+
+        def mask(at):
+            row = lax.broadcasted_iota(jnp.int32, (CHUNK, width), 0) + at.start + tp * rows
+            value = jnp.where(row < length, cotangent_v[at].astype(jnp.float32), 0.0)
+            low[at] = value.astype(jnp.bfloat16)
+
+        row_loop(rows, mask)
+        fetch[2].wait()
+        for member in range(TEAM):
+            at = pl.ds(member * (units // TEAM), units // TEAM)
+            down_pieces[member] = down_v[at].astype(jnp.bfloat16).T
+        middle()
+        take(0)
+        middle_rest()
+        for copy in others:
+            copy.start()
+        later()
+        for step in range(1, outer_count - 1):
+            take(step)
+        finish()
+        settle()
+        for copy in others:
+            copy.wait()
+
+    scalars = pl.BlockSpec(memory_space=pltpu.SMEM)
+    outs = pl.pallas_call(
+        kernel,
+        name="opening",
+        out_shape=(
+            layer_rows(rows, width),
+            gate_up_shape,
+            jax.ShapeDtypeStruct((outer_count,) + first_shape.shape, jnp.bfloat16),
+            jax.ShapeDtypeStruct((rows, width), jnp.bfloat16),
+            down_shape,
+        ),
+        in_specs=[scalars] * 2 + [in_vmem()] * 4 + [anywhere()] * 3,
+        out_specs=(anywhere(),) * 3 + (in_vmem(),) * 2,
+        scratch_shapes=[
+            pltpu.VMEM((rows, width), jnp.bfloat16),
+            pltpu.VMEM(first_shape.shape, jnp.bfloat16),
+            pltpu.VMEM(gate_up_shape.shape, jnp.bfloat16),
+            pltpu.VMEM(gate_up.shape, gate_up.dtype),
+            pltpu.VMEM(down.shape, down.dtype),
+            pltpu.VMEM(cotangent.shape, cotangent.dtype),
+            pltpu.SemaphoreType.DMA((3,)),
+            pltpu.SemaphoreType.DMA((2, outer_count)),
+            pltpu.SemaphoreType.DMA((2, outer_count)),
+        ]
+        + gather_scratch()
+        + exchange_scratch() * 2,
+        compiler_params=params(number),
+        cost_estimate=cost_of(60),
+    )(
+        lengths,
+        owners,
+        qkv,
+        out_weight,
+        inputs,
+        gain.reshape(1, width),
+        gate_up,
+        down,
+        cotangent,
+    )
+    gathered, mixed, full, low, down_pieces = outs
+    return (
+        gathered.reshape(-1, width),
+        mixed,
+        full.reshape(-1, first_shape.shape[2]),
+        low,
+        down_pieces,
+    )
 
 
 def spread(part, rows):
@@ -962,14 +1147,14 @@
         ).astype(out.dtype)
 
 
-def attend(normed, weights, cotangent, extra, group_length, cos_full, sin_full, gains, heads, early, number):
+def attend(normed, weights, cotangent, extra, lengths, owners, cos_full, sin_full, gains, heads, early, number):
     count, rows, width = normed.shape
     wide = (heads + 2) * HD
     extras = len(extra)
     own_rows = cotangent.shape[0]
     cut = balanced(early, crossing(extra, width))
 
-    def kernel(lengths, normed, weights, cos_ref, sin_ref, gains, own, *rest):
+    def kernel(lengths, owners, normed, weights, cos_ref, sin_ref, gains, own, *rest):
         pieces, rest = rest[:extras], rest[extras:]
         (proj, out, logs, branch, gathered), rest = rest[:5], rest[5:]
         mixed, (queries, keys, values), sems = rest[:extras], rest[extras : extras + 3], rest[extras + 3 :]
@@ -984,7 +1169,8 @@
             for copy in copies:
                 copy.start()
 
-        length = lengths[sequence]
+        group = lax.axis_index("outer") * TEAM + sequence
+        length = sequence_length(lengths, owners, group)
         proj[0] = jnp.dot(
             normed[0], weights[:, :wide], preferred_element_type=jnp.float32
         )
@@ -1035,6 +1221,7 @@
         )
         + tuple(like(piece) for piece in extra),
         in_specs=[
+            pl.BlockSpec(memory_space=pltpu.SMEM),
             pl.BlockSpec(memory_space=pltpu.SMEM),
             per_sequence(rows, width),
             whole(width, wide + heads * HD),
@@ -1061,7 +1248,7 @@
         + exchange_scratch() * extras,
         compiler_params=params(number),
         cost_estimate=cost_of(50),
-    )(group_length, normed, weights, cos_full, sin_full, gains, cotangent, *extra)
+    )(lengths, owners, normed, weights, cos_full, sin_full, gains, cotangent, *extra)
     return outs
 
 
@@ -1091,7 +1278,8 @@
     hidden,
     extra,
     outer_count,
-    group_length,
+    lengths,
+    owners,
     cos_full,
     sin_full,
     gains,
@@ -1107,7 +1295,7 @@
     split, share = team_split(width, outer_count)
 
     def kernel(
-        lengths, proj, normed, attended, own_grad, logs, weights_any, cos_ref, sin_ref, gains, part, hidden, *rest
+        lengths, owners, proj, normed, attended, own_grad, logs, weights_any, cos_ref, sin_ref, gains, part, hidden, *rest
     ):
         pieces, rest = rest[:extras], rest[extras:]
         (gathered, gain_grad, back_part, output, grad_weights), rest = rest[:5], rest[5:]
@@ -1158,7 +1346,8 @@
         grad_v_sum[...] = jnp.zeros_like(grad_v_sum)
         arrival(place).wait()
         grad = grad_v[place % 2].reshape(rows, width)
-        length = lengths[sequence]
+        group = lax.axis_index("outer") * TEAM + sequence
+        length = sequence_length(lengths, owners, group)
         grad_att[...] = jnp.dot(
             grad, weights[:, wide:], preferred_element_type=jnp.float32
         ).astype(jnp.bfloat16)
@@ -1261,6 +1450,7 @@
         )
         + tuple(like(piece) for piece in extra),
         in_specs=[
+            pl.BlockSpec(memory_space=pltpu.SMEM),
             pl.BlockSpec(memory_space=pltpu.SMEM),
             ordered(rows, wide),
             ordered(rows, width),
@@ -1309,7 +1499,8 @@
         compiler_params=params(number),
         cost_estimate=cost_of(50),
     )(
-        group_length,
+        lengths,
+        owners,
         projected,
         normed,
         attended,
@@ -1434,7 +1625,7 @@
 
     def run(pieces, update):
         for member, across, inside in parts:
-            update(pl.ds(0, height), across, pieces[member, inside].astype(jnp.float32).T)
+            update(pl.ds(0, height), across, pieces[member, inside].T)
 
     if len(members) == 1:
         columns = parts[0][1]
@@ -1448,7 +1639,7 @@
 
     def run(pieces, update):
         if inside is None:
-            update(at, across, pieces[member].astype(jnp.float32).T)
+            update(at, across, pieces[member].T)
         else:
             update(at, across, pieces[member, pl.ds(inside, height)])
 
@@ -1587,17 +1778,12 @@
     return steps + [outs[4 * total : 4 * total + 3], outs[4 * total + 3 :]]
 
 
-def split_columns(values, widths):
-    members = []
-    for member in range(TEAM):
-        start, parts = 0, []
-        for width in widths:
-            share = width // TEAM
-            first = start + member * share
-            parts.append(values[:, first : first + share])
-            start += width
-        members.append(jnp.concatenate(parts, axis=1))
-    return jnp.stack(members)
+def rotary(count):
+    frequency = rope_base ** (-(np.arange(HD // 2) * 2.0 / HD))
+    angles = np.arange(count)[:, None] * frequency[None, :]
+    cosine, sine = np.cos(angles), np.sin(angles)
+    full = [np.concatenate(pair, axis=1) for pair in ((cosine, cosine), (-sine, sine))]
+    return [jnp.asarray(table, jnp.float32) for table in full]
 
 
 def gather_outer(mixed):
@@ -1626,11 +1812,10 @@
     clipped = gradient * factor
     moment_one = beta_first * moment_one + (1.0 - beta_first) * clipped
     moment_two = beta_second * moment_two + (1.0 - beta_second) * clipped * clipped
-    first_fixed = moment_one / (1.0 - beta_first**STEP)
-    second_fixed = moment_two / (1.0 - beta_second**STEP)
-    weight = weight - rate_value * (
-        first_fixed / (jnp.sqrt(second_fixed) + adam_epsilon) + decay_rate * weight
-    )
+    first_fixed = moment_one * (rate_value / (1.0 - beta_first**STEP))
+    root_fixed = jnp.sqrt(moment_two) * (1.0 - beta_second**STEP) ** (-0.5)
+    kept = weight * (1.0 - rate_value * decay_rate) if decay_rate else weight
+    weight = kept - first_fixed / (root_fixed + adam_epsilon)
     return (weight, moment_one, moment_two)
 
 
@@ -1684,54 +1869,23 @@
     gate_up_widths = (FF // tp_count, FF // tp_count)
     down_widths = (FF // tp_count,)
 
-    first_group = lax.axis_index("outer") * TEAM
-    group_ids = first_group + jnp.arange(TEAM)
-    group_length = jnp.sum(
-        jnp.where(owners[None, :] == group_ids[:, None], lengths[None, :], 0), axis=1
-    )
-    own_group = lax.axis_index("near") * CORE + lax.axis_index("core")
-    own_rows = lax.axis_index("tp") * half_rows + jnp.arange(half_rows)
-    valid_rows = (own_rows < pick(group_length, own_group))[:, None]
-    half_width = HD // 2
-    frequency = rope_base ** (-(jnp.arange(half_width, dtype=jnp.float32) * 2.0 / HD))
-    angles = jnp.arange(row_count, dtype=jnp.float32)[:, None] * frequency[None, :]
-    cosine, sine = jnp.cos(angles), jnp.sin(angles)
-    cos_full = jnp.concatenate([cosine, cosine], axis=1)
-    sin_full = jnp.concatenate([-sine, sine], axis=1)
+    cos_full, sin_full = rotary(row_count)
     attn_gain = norm_gains[:D]
     mlp_gain = norm_gains[D : 2 * D]
     head_gains = norm_gains[2 * D :].reshape(2, HD)
 
-    first_pieces = jnp.concatenate(
-        [
-            split_columns(qkv_weight.astype(jnp.bfloat16), qkv_widths),
-            split_columns(out_weight.astype(jnp.bfloat16).T, out_widths),
-        ],
-        axis=2,
-    )
-    gate_up_pieces = split_columns(gate_up_weight.astype(jnp.bfloat16), gate_up_widths)
-    down_pieces = split_columns(down_weight.astype(jnp.bfloat16).T, down_widths)
-    first_mixed = exchange(first_pieces, 6, "exchange_first")
-    first_full = gather_outer(first_mixed)
-    qkv_full = first_full[:, : (heads + 2) * HD]
-
-    residual_in = inputs.astype(jnp.float32)
-    normed_attn = residual_in * rms_scale(residual_in) * attn_gain
-    grad_low = jnp.where(valid_rows, cotangent, jnp.zeros_like(cotangent))
-    normed_attn, first_mixed, grad_low, down_pieces, cos_full, sin_full = (
-        lax.optimization_barrier(
-            (
-                normed_attn.astype(jnp.bfloat16),
-                first_mixed,
-                grad_low,
-                down_pieces,
-                cos_full,
-                sin_full,
-            )
-        )
-    )
-    normed_attn, gate_up_mixed = gather_rows(
-        normed_attn, (gate_up_pieces,), 0, "gather_inputs"
+    normed_attn, gate_up_mixed, first_full, grad_low, down_pieces = opening(
+        qkv_weight,
+        out_weight,
+        gate_up_weight,
+        down_weight,
+        inputs,
+        attn_gain,
+        cotangent,
+        lengths,
+        owners,
+        lax.axis_size("outer"),
+        0,
     )
     gate_up_full = gather_outer(gate_up_mixed)
     early = half_rows * 2 // 5 // CHUNK * CHUNK
@@ -1740,7 +1894,8 @@
         first_full,
         grad_low,
         (down_pieces,),
-        group_length,
+        lengths,
+        owners,
         cos_full,
         sin_full,
         head_gains,
@@ -1788,7 +1943,8 @@
         hidden,
         (team_pieces(down_sum),),
         lax.axis_size("outer"),
-        group_length,
+        lengths,
+        owners,
         cos_full,
         sin_full,
         head_gains,

time: 590 us -> 580 us (0.983)
  other arithmetic: 11.7 us -> 0.65 us
    pallas_call x2 -> x1, Pallas kernels: 70.8 us -> 78.9 us  [opening(): pl.pallas_call(kernel, name='opening', out_shape=(layer_rows(rows, width)...]
  transfers between devices with their start and end apart: 7 -> 6, of which waited for: 0 -> 0; matrix products, arithmetic and copies ran while one was open for 7% -> 5% of each run, Pallas kernels for 81% -> 72%
where the time goes in v8:
time: 580 us; the launch traced here: 575 us
  Pallas kernels  527 us (91%)
  matrix products  27.2 us (5%)
  between operations  14.7 us (3%)
    pallas_call x1, Pallas kernels, branch_and_norm(): pl.pallas_call(kernel, name=name, out_shape=(jax.ShapeDtypeStruct((rows,...  102 us
    pallas_call x1, Pallas kernels, attend_back(): pl.pallas_call(kernel, name='attend_back', grid=(count,), out_shape=(laye...  99.9 us
    pallas_call x1, Pallas kernels, opening(): pl.pallas_call(kernel, name='opening', out_shape=(layer_rows(rows, width)...  78.9 us
    pallas_call x1, Pallas kernels, norm_back_last(): pl.pallas_call(kernel, name=name, out_shape=(jax.ShapeDtypeStruct((rows,...  63.3 us
    pallas_call x1, Pallas kernels, feed_back_rest(): pl.pallas_call(kernel, name=name, out_shape=(jax.ShapeDtypeStruct((rows,...  60.1 us
    pallas_call x1, Pallas kernels, feed(): pl.pallas_call(kernel, name='feed', grid=(count,), out_shape=(jax.ShapeDt...  37.1 us
    pallas_call x1, Pallas kernels, attend(): pl.pallas_call(kernel, name='attend', grid=(count,), out_shape=(jax.Shape...  32.6 us
    dot_general x2, matrix products, dot(): lax.dot_general(left, right, ((contract[0], contract[1]), ((), ())), pref...  27.2 us
  transfers between devices with their start and end apart: 6, of which 0 were waited for; matrix products, arithmetic and copies ran while one was open for 5% of the time, Pallas kernels for 72%

profile of v8, /device:TPU:0, one launch (start us, length us, event | category | flops | bytes accessed | tf_op | source)
XLA Modules:
  0.0 575.1 jit_solution(6077613835108963826)
XLA Ops:
  7.2 0.0 all-gather.3.cloned.1.call-start
  7.2 1.3 fusion.1
  8.6 78.9 %opening.1 = (bf16[2,2,2,320,2048]{4,3,2,1,0:T(8,128)(2,1)}, bf16[4,128,1536]{2,1,0:T(8,128)(2,1)}, bf16[4,4,128,768]{3,2,1,0:T(8,128)(2,1)}, bf16[320,2048]{1,0:T(8,128)(2,1)}, bf16[4,128,768]{2,1,0:T(8,128)(2,1)}) custom-call(s32[16]{0:T(128)} %lengths.5, s32[16]{0:T(128)} %owners.5, f32[128,2048]{1,0:T(8,128)} %refs_9_.1, f32[1024,128]{1,0:T(8,128)} %refs_6_.1, ...), custom_call_target="tpu_custom_call" | custom-call | bytes 6000000 | tf_op jit(solution)/shard_map/opening/pallas_call | solution.py:578
  87.4 0.0 all-gather.3.cloned.1.call-update
  87.5 0.0 all-gather.5.cloned.1.call-start
  87.5 1.3 slice_bitcast_fusion.gains
  88.8 32.6 %attend.1 = (f32[4,640,512]{2,1,0:T(8,128)}, bf16[4,640,256]{2,1,0:T(8,128)(2,1)}, f32[4,640,128]{2,1,0:T(8,128)}, bf16[4,640,2048]{2,1,0:T(8,128)(2,1)}, bf16[2...) custom-call(s32[16]{0:T(128)} %lengths.5, s32[16]{0:T(128)} %owners.5, bf16[4,640,2048]{2,1,0:T(8,128)(2,1)} %bitcast.45, ...), custom_call_target="tpu_custom_call" | custom-call | bytes 5000000 | tf_op jit(solution)/shard_map/attend/pallas_call | solution.py:1211
  121.4 0.0 all-gather.5.cloned.1.call-update
  121.4 0.3 reduce-scatter.5.cloned.1.call-start
  121.7 101.5 %branch_and_norm.1 = (f32[320,2048]{1,0:T(8,128)}, bf16[2,2,2,320,2048]{4,3,2,1,0:T(8,128)(2,1)}) custom-call(bf16[2,2,2,320,2048]{4,3,2,1,0:T(8,128)(2,1)} %bitcast.50, bf16[320,2048]{1,0:T(8,128)(2,1)} %values.1, f32[1,2048]{1,0:T(1,128)} %bitcast.66), custom_call_target="tpu_custom_call" | custom-call | bytes 9500000 | tf_op jit(solution)/shard_map/branch_and_norm/pallas_call | solution.py:656
  223.2 0.0 all-gather.3.cloned.1.call-done.weights
  223.2 37.1 %feed.1 = (f32[4,640,1536]{2,1,0:T(8,128)}, bf16[4,640,768]{2,1,0:T(8,128)(2,1)}, bf16[2,2,2,320,2048]{4,3,2,1,0:T(8,128)(2,1)}) custom-call(bf16[4,640,2048]{2,1,0:T(8,128)(2,1)} %bitcast.40, bf16[2048,1536]{1,0:T(8,128)(2,1)} %all-gather.3.cloned.1.call-done.weights, ...), custom_call_target="tpu_custom_call", output_to_operand_aliasing={{2}: (3, {})} | custom-call | bytes 2800000 | tf_op jit(solution)/shard_map/feed/pallas_call | solution.py:1549
  260.4 13.6 %convolution_convert_fusion.1 = bf16[2048,768]{1,0:T(8,128)(2,1)} fusion(bf16[2560,2048]{1,0:T(8,128)(2,1)} %bitcast.43, bf16[2560,768]{1,0:T(8,128)(2,1)} %bitcast.52), kind=kOutput, calls=%fused_computation.1 | convolution fusion | flops 8054636544 | bytes 17563648 | tf_op jit(solution)/shard_map/dot_general | solution.py:1823
  273.9 0.0 reduce-scatter.5.cloned.1.call-update
  274.0 0.3 reduce-scatter.7.cloned.1.call-start
  274.3 0.0 all-gather.5.cloned.1.call-done.weights.down
  274.3 18.2 %feed_back.1 = (bf16[4,640,768]{2,1,0:T(8,128)(2,1)}, bf16[4,640,768]{2,1,0:T(8,128)(2,1)}) custom-call(bf16[4,640,2048]{2,1,0:T(8,128)(2,1)} %bitcast.44, bf16[2048,768]{1,0:T(8,128)(2,1)} %all-gather.5.cloned.1.call-done.weights.down, f32[4,640,1536]{2,1,0:T(8,128)} %get-tuple-element.100.product), custom_call_target="tpu_custom_call" | custom-call | bytes 1800000 | tf_op jit(solution)/shard_map/feed_back/pallas_call | solution.py:1586
  292.5 13.6 %convolution_convert_fusion = bf16[2048,768]{1,0:T(8,128)(2,1)} fusion(bf16[2560,2048]{1,0:T(8,128)(2,1)} %bitcast.41, bf16[2560,768]{1,0:T(8,128)(2,1)} %bitcast.54), kind=kOutput, calls=%fused_computation | convolution fusion | flops 8054636544 | bytes 17563648 | tf_op jit(solution)/shard_map/dot_general | solution.py:1823
  306.1 0.0 reduce-scatter.7.cloned.1.call-update
  306.1 0.5 reduce-scatter.9.cloned.1.call-start
  306.6 60.1 %feed_back_rest.1 = (f32[320,2048]{1,0:T(8,128)}, f32[8,2048]{1,0:T(8,128)}, bf16[320,2048]{1,0:T(8,128)(2,1)}, bf16[4,2,320,2048]{3,2,1,0:T(8,128)(2,1)}, bf16[16,768,128]{2,1,0:T(8,128)(2,1)}) custom-call(bf16[4,2,320,768]{3,2,1,0:T(8,128)(2,1)} %bitcast.55, bf16[4,2,320,768]{3,2,1,0:T(8,128)(2,1)} %bitcast.56, ...), custom_call_target="tpu_custom_call" | custom-call | bytes 6000000 | tf_op jit(solution)/shard_map/feed_back_rest/pallas_call | solution.py:876
  366.7 0.0 reduce-scatter.9.cloned.1.call-update
  366.7 0.0 reduce-scatter.11.cloned.1.call-start
  366.8 0.0 reduce-scatter.5.cloned.1.call-done.rest_4_
  366.8 99.9 %attend_back.1 = (bf16[2,2,2,320,2048]{4,3,2,1,0:T(8,128)(2,1)}, f32[2,8,128]{2,1,0:T(8,128)}, bf16[4,640,2048]{2,1,0:T(8,128)(2,1)}, bf16[320,2048]{1,0:T(8,128...) custom-call(s32[16]{0:T(128)} %lengths.5, s32[16]{0:T(128)} %owners.5, ...), custom_call_target="tpu_custom_call" | custom-call | bytes 5000000 | tf_op jit(solution)/shard_map/attend_back/pallas_call | solution.py:1440
  466.7 0.0 copy-start
  466.7 0.0 copy-start.1
  466.7 0.0 reduce-scatter.7.cloned.1.call-done.rest_2_
  466.8 0.0 reduce-scatter.11.cloned.1.call-update
  466.8 0.8 copy-done
  467.6 0.0 copy-done.1
  467.6 0.0 reduce-scatter.9.cloned.1.call-done
  467.6 63.3 %norm_back_attn.1 = (bf16[320,2048]{1,0:T(8,128)(2,1)}, f32[8,2048]{1,0:T(8,128)}, f32[8,128]{1,0:T(8,128)}, bf16[4,128,768]{2,1,0:T(8,128)(2,1)}, bf16[4,768,128]{2,1,0:T(8,128)(2,1)}) custom-call(bf16[2,2,2,320,2048]{4,3,2,1,0:T(8,128)(2,1)} %bitcast.51, bf16[320,2048]{1,0:T(8,128)(2,1)} %values.1, f32[320,2048]{1,0:T(8,128)} %get-tuple-element.110.upstream, ...), custom_call_target="tpu_custom_call" | custom-call | bytes 6500000 | tf_op jit(solution)/shard_map/norm_back_attn/pallas_call | solution.py:980
  531.0 0.6 fusion.values
  531.6 0.0 reduce-scatter.11.cloned.1.call-done
  531.6 16.6 %total_everywhere.1 = (f32[48,128]{1,0:T(8,128)}, f32[8,128]{1,0:T(8,128)}, f32[8,128]{1,0:T(8,128)}, bf16[4,768,128]{2,1,0:T(8,128)(2,1)}) custom-call(f32[40,128]{1,0:T(8,128)} %fusion.values, f32[8,2048]{1,0:T(8,128)} %get-tuple-element.120.first, f32[8,128]{1,0:T(8,128)} %get-tuple-element.121.squares, bf16[4,768,128]{2,1,0:T(8,128)(2,1)} %bitcast.65), custom_call_target="tpu_custom_call" | custom-call | tf_op jit(solution)/shard_map/total_everywhere/pallas_call | solution.py:1075
  548.2 1.2 slice.26
  549.4 18.3 %adam_all.1 = (f32[128,6144]{1,0:T(8,128)}, f32[128,6144]{1,0:T(8,128)}, f32[128,6144]{1,0:T(8,128)}, bf16[128,6144]{1,0:T(8,128)(2,1)}, f32[3072,128]{1,0:T(8,1...) custom-call(f32[128,6144]{1,0:T(8,128)} %refs_0_.1, ...), custom_call_target="tpu_custom_call" | custom-call | bytes 1500000 | tf_op jit(solution)/shard_map/adam_all/pallas_call | solution.py:1760
  (3 shorter events, 0.0 us)
Async XLA Ops:
  7.2 216.0 %all-gather.3.cloned.1.call-start = ((), (), s32[]{:S(2)}) async-start(), calls=%async_computation.4 | async-start | bytes 7864320 | tf_op jit(solution)/shard_map/all_gather | solution.py:1790
  87.5 186.8 %all-gather.5.cloned.1.call-start = ((), (), s32[]{:S(2)}) async-start(), calls=%async_computation.5 | async-start | bytes 3932160 | tf_op jit(solution)/shard_map/all_gather | solution.py:1790
  121.4 245.4 %reduce-scatter.5.cloned.1.call-start = ((), (), s32[]{:S(2)}) async-start(), calls=%async_computation.6 | async-start | bytes 3932160 | tf_op jit(solution)/shard_map/reduce_scatter | solution.py:1804
  274.0 192.8 %reduce-scatter.7.cloned.1.call-start = ((), (), s32[]{:S(2)}) async-start(), calls=%async_computation.7 | async-start | bytes 3932160 | tf_op jit(solution)/shard_map/reduce_scatter | solution.py:1804
  306.1 161.5 %reduce-scatter.9.cloned.1.call-start = ((), (), s32[]{:S(2)}) async-start(), calls=%async_computation.8 | async-start | bytes 3932160 | tf_op jit(solution)/shard_map/reduce_scatter | solution.py:1804
  366.7 164.8 %reduce-scatter.11.cloned.1.call-start = ((), (), s32[]{:S(2)}) async-start(), calls=%async_computation.9 | async-start | bytes 3932160 | tf_op jit(solution)/shard_map/reduce_scatter | solution.py:1804
  466.7 0.8 copy-start
  466.7 0.9 copy-start.1
Sparse Core Ops, SparseCore 0:
  87.6 113.1 all-gather.2
  202.3 61.7 all-gather.4
  274.1 57.7 reduce-scatter.4
  334.6 60.2 reduce-scatter.6
  397.0 60.2 reduce-scatter.8
  466.9 57.4 reduce-scatter.10

commit v9 on v8

--- a/solution.py
+++ b/solution.py
@@ -48,7 +48,8 @@
 CHUNK = 16
 GATHER_COPIES = 16
 AHEAD = 1000
-SUM_COPIES = 10
+PART = TEAM // 2
+SUM_COPIES = 12
 NEIGHBOURS = ((1, 0, 0), (0, 1, 0), (0, 0, 1))
 MATES = ((0, 1, 0), (1, 0, 0), (1, 1, 0))
 EVERYONE_NEAR = NEIGHBOURS + ((1, 1, 0),)
@@ -261,6 +262,11 @@
         target[at] = total.astype(target.dtype)
 
 
+def halved(start, count):
+    half = count // 2 // CHUNK * CHUNK
+    return (start, half), (start + half, count - half)
+
+
 def plan_sum(outgoing, mine, keep, total, scratch, cut):
     theirs, way_near, way_tp, from_tp, from_near, send, recv = scratch
     rows = total.shape[0]
@@ -271,15 +277,24 @@
 
     twin = [make(number, outgoing[number], theirs.at[number], TO_CORE) for number in range(4)]
     far, to_tp, to_near, own = mine
+    low_parts = halved(0, cut)
+    high_parts = halved(cut, rows - cut)
     far_high = make(5, far.at[high], way_tp, TO_TP)
     tp_high = make(6, to_tp.at[high], from_tp.at[high], TO_TP)
-    near_high = make(9, to_near.at[high], from_near.at[high], TO_NEAR)
-    ways = [far_high, tp_high, near_high]
+    near_high = [
+        make(9 + 2 * place, to_near.at[pl.ds(*part)], from_near.at[pl.ds(*part)], TO_NEAR)
+        for place, part in enumerate(high_parts)
+    ]
+    ways = [far_high, tp_high] + near_high
+    tp_low = []
     if cut:
         far_low = make(4, far.at[low], way_near, TO_NEAR)
         near_low = make(7, to_near.at[low], from_near.at[low], TO_NEAR)
-        tp_low = make(8, to_tp.at[low], from_tp.at[low], TO_TP)
-        ways += [near_low, tp_low]
+        tp_low = [
+            make(8 + 2 * place, to_tp.at[pl.ds(*part)], from_tp.at[pl.ds(*part)], TO_TP)
+            for place, part in enumerate(low_parts)
+        ]
+        ways += [far_low, near_low] + tp_low
 
     def ready(number):
         if keep:
@@ -322,18 +337,27 @@
     def second():
         if cut:
             far_low.wait_recv()
-            add_rows(to_tp, 0, cut, *both(1), (way_near, 0))
-            tp_low.start()
         far_high.wait_recv()
-        add_rows(to_near, cut, rows - cut, *both(2), (way_tp, cut))
-        near_high.start()
+        for place, part in enumerate(high_parts):
+            if cut:
+                add_rows(to_tp, *low_parts[place], *both(1), (way_near, 0))
+                tp_low[place].start()
+            add_rows(to_near, *part, *both(2), (way_tp, cut))
+            near_high[place].start()
         ready(3)
         add_rows(total, 0, rows, *both(3))
 
-    def finish():
-        for copy in ways[1:]:
-            copy.wait_recv()
-        for copy in twin + ways + ([far_low] if cut else []):
+    def finish(body):
+        tp_high.wait_recv()
+        if cut:
+            near_low.wait_recv()
+        for place, part in enumerate(high_parts):
+            if cut:
+                tp_low[place].wait_recv()
+                row_loop(*low_parts[place], body)
+            near_high[place].wait_recv()
+            row_loop(*part, body)
+        for copy in twin + ways:
             copy.wait_send()
 
     return [begin, first, second, finish], (send_far, send_tp, send_near)
@@ -399,36 +423,31 @@
     return jax.ShapeDtypeStruct((NEAR, CORE, 2, rows, width), jnp.bfloat16)
 
 
-def row_loop(rows, body):
-    @pl.loop(0, rows // CHUNK)
+def row_loop(start, count, body):
+    @pl.loop(0, count // CHUNK)
     def _(step):
-        body(pl.ds(pl.multiple_of(step * CHUNK, CHUNK), CHUNK))
+        body(pl.ds(pl.multiple_of(start + step * CHUNK, CHUNK), CHUNK))
 
 
 def plan_line(blocks, send, recv, count):
     own = lax.axis_index("outer")
 
-    def message(side, number):
-        block = blocks.at[own - number if side == 0 else own + number]
+    def handle(side, number, half, there):
+        block = blocks.at[there, pl.ds(half * PART, PART)]
         return pltpu.make_async_remote_copy(
             src_ref=block,
             dst_ref=block,
-            send_sem=send.at[side, number],
-            recv_sem=recv.at[side, number],
+            send_sem=send.at[side, number, half],
+            recv_sem=recv.at[side, number, half],
             device_id={"outer": own + 1 if side == 0 else own - 1},
             device_id_type=MESH_ID,
         )
 
-    def arrival(side, number):
-        block = blocks.at[own - 1 - number if side == 0 else own + 1 + number]
-        return pltpu.make_async_remote_copy(
-            src_ref=block,
-            dst_ref=block,
-            send_sem=send.at[side, number],
-            recv_sem=recv.at[side, number],
-            device_id={"outer": own + 1 if side == 0 else own - 1},
-            device_id_type=MESH_ID,
-        )
+    def message(side, number, half):
+        return handle(side, number, half, own - number if side == 0 else own + number)
+
+    def arrival(side, number, half):
+        return handle(side, number, half, own - 1 - number if side == 0 else own + 1 + number)
 
     def sends(side, number):
         if side == 0:
@@ -443,20 +462,22 @@
 
             @pl.when(sends(side, number))
             def _(side=side):
-                message(side, number).start()
+                for half in range(2):
+                    message(side, number, half).start()
 
     def take(number):
-        for side in range(2):
-
-            @pl.when(gets(side, number))
-            def _(side=side):
-                arrival(side, number).wait_recv()
-
-            if number + 2 < count:
-
-                @pl.when(sends(side, number + 1))
-                def _(side=side):
-                    message(side, number + 1).start()
+        for half in range(2):
+            for side in range(2):
+
+                @pl.when(gets(side, number))
+                def _(side=side, half=half):
+                    arrival(side, number, half).wait_recv()
+
+                if number + 2 < count:
+
+                    @pl.when(sends(side, number + 1))
+                    def _(side=side, half=half):
+                        message(side, number + 1, half).start()
 
     def settle():
         for number in range(count - 1):
@@ -464,7 +485,8 @@
 
                 @pl.when(sends(side, number))
                 def _(side=side, number=number):
-                    message(side, number).wait_send()
+                    for half in range(2):
+                        message(side, number, half).wait_send()
 
     return push, take, settle
 
@@ -539,7 +561,7 @@
             value = inputs[at].astype(jnp.float32)
             normed[at] = (value * rms_scale(value) * gain[...]).astype(jnp.bfloat16)
 
-        row_loop(rows, prepare)
+        row_loop(0, rows, prepare)
         begin_tp()
         fetch[1].wait()
         for member, across, inside in spans((units, units)):
@@ -556,7 +578,7 @@
             value = jnp.where(row < length, cotangent_v[at].astype(jnp.float32), 0.0)
             low[at] = value.astype(jnp.bfloat16)
 
-        row_loop(rows, mask)
+        row_loop(0, rows, mask)
         fetch[2].wait()
         for member in range(TEAM):
             at = pl.ds(member * (units // TEAM), units // TEAM)
@@ -595,8 +617,8 @@
             pltpu.VMEM(down.shape, down.dtype),
             pltpu.VMEM(cotangent.shape, cotangent.dtype),
             pltpu.SemaphoreType.DMA((3,)),
-            pltpu.SemaphoreType.DMA((2, outer_count)),
-            pltpu.SemaphoreType.DMA((2, outer_count)),
+            pltpu.SemaphoreType.DMA((2, outer_count, 2)),
+            pltpu.SemaphoreType.DMA((2, outer_count, 2)),
         ]
         + gather_scratch()
         + exchange_scratch() * 2,
@@ -640,7 +662,7 @@
         steps, from_tp, from_near = plan_sum_of(part, hidden, scratch[:SUM_SCRATCH], cut)
         onward = plan_gather(normed, out, *sems, cut=cut)
         greet(NEIGHBOURS)
-        for step in steps:
+        for step in steps[:3]:
             step()
 
         def finish(at):
@@ -649,7 +671,7 @@
             hidden[at] = value
             normed[at] = (value * rms_scale(value) * gain[...]).astype(jnp.bfloat16)
 
-        row_loop(rows, finish)
+        steps[3](finish)
         for step in onward:
             step()
 
@@ -852,7 +874,6 @@
         fetch[1].wait()
         fetch[2].wait()
         gain_grad[...] = jnp.zeros_like(gain_grad)
-        steps[3]()
 
         def finish(at):
             grad = total[at] + read(from_tp, at) + read(from_near, at)
@@ -862,7 +883,7 @@
             total[at] = value
             low[at] = value.astype(jnp.bfloat16)
 
-        row_loop(rows, finish)
+        steps[3](finish)
         store = pltpu.make_async_copy(total, result, store_sem.at[count])
         store.start()
         for turn in range(max(0, turns - 2), turns):
@@ -965,7 +986,6 @@
         squares[...] = corner(sum(square_sum(ref[...]) for ref in squared_v))
         steps[2]()
         gain_grad[...] = jnp.zeros_like(gain_grad)
-        steps[3]()
 
         def finish(at):
             grad = total[at] + read(from_tp, at) + read(from_near, at)
@@ -973,7 +993,7 @@
             gain_grad[...] += by_gain.reshape(CHUNK // 8, 8, width).sum(axis=0)
             result[at] = (upstream_v[at] + back).astype(jnp.bfloat16)
 
-        row_loop(rows, finish)
+        steps[3](finish)
         for copy in copies:
             copy.wait()
 
@@ -1154,20 +1174,24 @@
     own_rows = cotangent.shape[0]
     cut = balanced(early, crossing(extra, width))
 
-    def kernel(lengths, owners, normed, weights, cos_ref, sin_ref, gains, own, *rest):
+    def kernel(lengths, owners, normed, weights_any, cos_ref, sin_ref, gains, own, *rest):
         pieces, rest = rest[:extras], rest[extras:]
         (proj, out, logs, branch, gathered), rest = rest[:5], rest[5:]
-        mixed, (queries, keys, values), sems = rest[:extras], rest[extras : extras + 3], rest[extras + 3 :]
+        mixed, rest = rest[:extras], rest[extras:]
+        (queries, keys, values, weights, weights_sem), sems = rest[:5], rest[5:]
+        fetch = pltpu.make_async_copy(weights_any, weights, weights_sem)
         sequence = pl.program_id(0)
         steps = plan_gather(own, gathered, *sems[:3], cut=cut, rows=early)
         copies = plan_exchanges(pieces, mixed, sems[3:])
 
         @pl.when(sequence == 0)
         def _():
+            fetch.start()
             greet(EVERYONE_NEAR)
             steps[0]()
             for copy in copies:
                 copy.start()
+            fetch.wait()
 
         group = lax.axis_index("outer") * TEAM + sequence
         length = sequence_length(lengths, owners, group)
@@ -1224,7 +1248,7 @@
             pl.BlockSpec(memory_space=pltpu.SMEM),
             pl.BlockSpec(memory_space=pltpu.SMEM),
             per_sequence(rows, width),
-            whole(width, wide + heads * HD),
+            anywhere(),
             whole(rows, HD),
             whole(rows, HD),
             whole(2, HD),
@@ -1243,6 +1267,8 @@
             pltpu.VMEM((heads, rows, HD), jnp.bfloat16),
             pltpu.VMEM((rows, HD), jnp.bfloat16),
             pltpu.VMEM((rows, HD), jnp.bfloat16),
+            pltpu.VMEM(weights.shape, weights.dtype),
+            pltpu.SemaphoreType.DMA,
         ]
         + gather_scratch()
         + exchange_scratch() * extras,
@@ -1426,13 +1452,12 @@
                     staged[outer, member] = summed[:, start : start + share].astype(jnp.bfloat16)
             store.start()
             fetch.wait()
-            steps[3]()
 
             def finish(at):
                 value = total[at] + read(from_tp, at) + read(from_near, at)
                 output[at] = (held[at] + value).astype(jnp.bfloat16)
 
-            row_loop(own_rows, finish)
+            steps[3](finish)
             store.wait()
             for copy in copies:
                 copy.wait()
@@ -1521,7 +1546,8 @@
     units = weights.shape[1] // 2
     late = cotangent.shape[0] - early
 
-    def kernel(normed, weights, own, _, product, active, out, *sems):
+    def kernel(normed, weights_any, own, _, product, active, out, weights, weights_sem, *sems):
+        fetch = pltpu.make_async_copy(weights_any, weights, weights_sem)
         steps = plan_gather(
             own, out, *sems, cut=balanced(late, 0), base=early, rows=late
         )
@@ -1529,8 +1555,10 @@
 
         @pl.when(sequence == 0)
         def _():
+            fetch.start()
             greet(NEIGHBOURS)
             steps[0]()
+            fetch.wait()
 
         for start in range(0, units, 256):
             gate_at, up_at = pl.ds(start, 256), pl.ds(units + start, 256)
@@ -1557,12 +1585,13 @@
         ),
         in_specs=[
             per_sequence(rows, width),
-            whole(*weights.shape),
+            anywhere(),
             whole(*cotangent.shape),
             anywhere(),
         ],
         out_specs=(per_sequence(rows, 2 * units), per_sequence(rows, units), anywhere()),
-        scratch_shapes=gather_scratch(),
+        scratch_shapes=[pltpu.VMEM(weights.shape, weights.dtype), pltpu.SemaphoreType.DMA]
+        + gather_scratch(),
         input_output_aliases={3: 2},
         compiler_params=params(number),
         cost_estimate=cost_of(28),
@@ -1888,7 +1917,7 @@
         0,
     )
     gate_up_full = gather_outer(gate_up_mixed)
-    early = half_rows * 2 // 5 // CHUNK * CHUNK
+    early = half_rows // 2 // CHUNK * CHUNK
     projected, attended, logs, attn_branch, grad_all, down_mixed = attend(
         normed_attn.reshape(TEAM, row_count, D),
         first_full,
@@ -1912,8 +1941,12 @@
     grad_all, grad_down = after(grad_all, grad_down.astype(jnp.bfloat16))
     down_sum = sum_weight(grad_down)
     grad_gate, grad_up = feed_back(
-        grad_all.reshape(TEAM, row_count, D), down_full, gate_up
+        grad_all.reshape(-1, half_rows, D),
+        down_full,
+        gate_up.reshape(-1, half_rows, 2 * hidden_units),
     )
+    grad_gate = grad_gate.reshape(TEAM, row_count, hidden_units)
+    grad_up = grad_up.reshape(TEAM, row_count, hidden_units)
     grad_gate_weight = over_rows(normed_mlp, grad_gate.reshape(-1, hidden_units))
     grad_gate, grad_gate_weight = after(grad_gate, grad_gate_weight.astype(jnp.bfloat16))
     gate_sum = sum_weight(grad_gate_weight)

time: 580 us -> 570 us (0.983)
  Pallas kernels: 527 us -> 516 us
    pallas_call x1, Pallas kernels: 37.1 us -> 30.9 us  [feed(): pl.pallas_call(kernel, name='feed', grid=(count,), out_shape=(jax.ShapeDt...]
where the time goes in v9:
time: 570 us; the launch traced here: 565 us
  Pallas kernels  516 us (91%)
  matrix products  27.2 us (5%)
  between operations  14.8 us (3%)
    pallas_call x1, Pallas kernels, branch_and_norm(): pl.pallas_call(kernel, name=name, out_shape=(jax.ShapeDtypeStruct((rows,...  100 us
    pallas_call x1, Pallas kernels, attend_back(): pl.pallas_call(kernel, name='attend_back', grid=(count,), out_shape=(laye...  99.9 us
    pallas_call x1, Pallas kernels, opening(): pl.pallas_call(kernel, name='opening', out_shape=(layer_rows(rows, width)...  73.2 us
    pallas_call x1, Pallas kernels, norm_back_last(): pl.pallas_call(kernel, name=name, out_shape=(jax.ShapeDtypeStruct((rows,...  62.3 us
    pallas_call x1, Pallas kernels, feed_back_rest(): pl.pallas_call(kernel, name=name, out_shape=(jax.ShapeDtypeStruct((rows,...  59.1 us
    pallas_call x1, Pallas kernels, attend(): pl.pallas_call(kernel, name='attend', grid=(count,), out_shape=(jax.Shape...  36.9 us
    pallas_call x1, Pallas kernels, feed(): pl.pallas_call(kernel, name='feed', grid=(count,), out_shape=(jax.ShapeDt...  30.9 us
    dot_general x2, matrix products, dot(): lax.dot_general(left, right, ((contract[0], contract[1]), ((), ())), pref...  27.2 us
  transfers between devices with their start and end apart: 6, of which 0 were waited for; matrix products, arithmetic and copies ran while one was open for 5% of the time, Pallas kernels for 72%

profile of v9, /device:TPU:0, one launch (start us, length us, event | category | flops | bytes accessed | tf_op | source)
XLA Modules:
  0.0 564.6 jit_solution(13401261276993357255)
XLA Ops:
  7.2 0.0 all-gather.3.cloned.1.call-start
  7.2 1.3 fusion.1
  8.6 73.2 %opening.1 = (bf16[2,2,2,320,2048]{4,3,2,1,0:T(8,128)(2,1)}, bf16[4,128,1536]{2,1,0:T(8,128)(2,1)}, bf16[4,4,128,768]{3,2,1,0:T(8,128)(2,1)}, bf16[320,2048]{1,0:T(8,128)(2,1)}, bf16[4,128,768]{2,1,0:T(8,128)(2,1)}) custom-call(s32[16]{0:T(128)} %lengths.5, s32[16]{0:T(128)} %owners.5, f32[128,2048]{1,0:T(8,128)} %refs_9_.1, f32[1024,128]{1,0:T(8,128)} %refs_6_.1, ...), custom_call_target="tpu_custom_call" | custom-call | bytes 6000000 | tf_op jit(solution)/shard_map/opening/pallas_call | solution.py:600
  81.7 0.0 all-gather.3.cloned.1.call-update
  81.8 0.0 all-gather.5.cloned.1.call-start
  81.8 1.3 slice_bitcast_fusion.gains
  83.1 36.9 %attend.1 = (f32[4,640,512]{2,1,0:T(8,128)}, bf16[4,640,256]{2,1,0:T(8,128)(2,1)}, f32[4,640,128]{2,1,0:T(8,128)}, bf16[4,640,2048]{2,1,0:T(8,128)(2,1)}, bf16[2...) custom-call(s32[16]{0:T(128)} %lengths.5, s32[16]{0:T(128)} %owners.5, bf16[4,640,2048]{2,1,0:T(8,128)(2,1)} %bitcast.47, ...), custom_call_target="tpu_custom_call" | custom-call | bytes 5000000 | tf_op jit(solution)/shard_map/attend/pallas_call | solution.py:1235
  120.0 0.0 all-gather.5.cloned.1.call-update
  120.0 0.3 reduce-scatter.5.cloned.1.call-start
  120.3 100.1 %branch_and_norm.1 = (f32[320,2048]{1,0:T(8,128)}, bf16[2,2,2,320,2048]{4,3,2,1,0:T(8,128)(2,1)}) custom-call(bf16[2,2,2,320,2048]{4,3,2,1,0:T(8,128)(2,1)} %bitcast.53, bf16[320,2048]{1,0:T(8,128)(2,1)} %values.1, f32[1,2048]{1,0:T(1,128)} %bitcast.69), custom_call_target="tpu_custom_call" | custom-call | bytes 9500000 | tf_op jit(solution)/shard_map/branch_and_norm/pallas_call | solution.py:678
  220.4 0.0 all-gather.3.cloned.1.call-done.weights_any.weights
  220.4 30.9 %feed.1 = (f32[4,640,1536]{2,1,0:T(8,128)}, bf16[4,640,768]{2,1,0:T(8,128)(2,1)}, bf16[2,2,2,320,2048]{4,3,2,1,0:T(8,128)(2,1)}) custom-call(bf16[4,640,2048]{2,1,0:T(8,128)(2,1)} %bitcast.42, bf16[2048,1536]{1,0:T(8,128)(2,1)} %all-gather.3.cloned.1.call-done.weights_any.weights, ...), custom_call_target="tpu_custom_call", output_to_operand_aliasing={{2}: (3, {})} | custom-call | bytes 2800000 | tf_op jit(solution)/shard_map/feed/pallas_call | solution.py:1577
  251.3 13.6 %convolution_convert_fusion.1 = bf16[2048,768]{1,0:T(8,128)(2,1)} fusion(bf16[2560,2048]{1,0:T(8,128)(2,1)} %bitcast.45, bf16[2560,768]{1,0:T(8,128)(2,1)} %bitcast.55), kind=kOutput, calls=%fused_computation.1 | convolution fusion | flops 8054636544 | bytes 17563648 | tf_op jit(solution)/shard_map/dot_general | solution.py:1852
  264.9 0.0 reduce-scatter.5.cloned.1.call-update
  264.9 0.3 reduce-scatter.7.cloned.1.call-start
  265.2 0.0 all-gather.5.cloned.1.call-done.weights.down
  265.2 18.7 %feed_back.1 = (bf16[8,320,768]{2,1,0:T(8,128)(2,1)}, bf16[8,320,768]{2,1,0:T(8,128)(2,1)}) custom-call(bf16[8,320,2048]{2,1,0:T(8,128)(2,1)} %bitcast.46, bf16[2048,768]{1,0:T(8,128)(2,1)} %all-gather.5.cloned.1.call-done.weights.down, f32[8,320,1536]{2,1,0:T(8,128)} %bitcast.49), custom_call_target="tpu_custom_call" | custom-call | bytes 1800000 | tf_op jit(solution)/shard_map/feed_back/pallas_call | solution.py:1615
  283.9 13.6 %convolution_convert_fusion = bf16[2048,768]{1,0:T(8,128)(2,1)} fusion(bf16[2560,2048]{1,0:T(8,128)(2,1)} %bitcast.43, bf16[2560,768]{1,0:T(8,128)(2,1)} %bitcast.57), kind=kOutput, calls=%fused_computation | convolution fusion | flops 8054636544 | bytes 17563648 | tf_op jit(solution)/shard_map/dot_general | solution.py:1852
  297.5 0.0 reduce-scatter.7.cloned.1.call-update
  297.6 0.5 reduce-scatter.9.cloned.1.call-start
  298.1 59.1 %feed_back_rest.1 = (f32[320,2048]{1,0:T(8,128)}, f32[8,2048]{1,0:T(8,128)}, bf16[320,2048]{1,0:T(8,128)(2,1)}, bf16[4,2,320,2048]{3,2,1,0:T(8,128)(2,1)}, bf16[16,768,128]{2,1,0:T(8,128)(2,1)}) custom-call(bf16[4,2,320,768]{3,2,1,0:T(8,128)(2,1)} %bitcast.58, bf16[4,2,320,768]{3,2,1,0:T(8,128)(2,1)} %bitcast.59, ...), custom_call_target="tpu_custom_call" | custom-call | bytes 6000000 | tf_op jit(solution)/shard_map/feed_back_rest/pallas_call | solution.py:897
  357.2 0.0 reduce-scatter.9.cloned.1.call-update
  357.2 0.0 reduce-scatter.11.cloned.1.call-start
  357.3 0.0 reduce-scatter.5.cloned.1.call-done.rest_4_
  357.3 99.9 %attend_back.1 = (bf16[2,2,2,320,2048]{4,3,2,1,0:T(8,128)(2,1)}, f32[2,8,128]{2,1,0:T(8,128)}, bf16[4,640,2048]{2,1,0:T(8,128)(2,1)}, bf16[320,2048]{1,0:T(8,128...) custom-call(s32[16]{0:T(128)} %lengths.5, s32[16]{0:T(128)} %owners.5, ...), custom_call_target="tpu_custom_call" | custom-call | bytes 5000000 | tf_op jit(solution)/shard_map/attend_back/pallas_call | solution.py:1465
  457.2 0.0 copy-start
  457.2 0.0 copy-start.1
  457.2 0.0 reduce-scatter.7.cloned.1.call-done.rest_2_
  457.2 0.0 reduce-scatter.11.cloned.1.call-update
  457.2 0.8 copy-done
  458.0 0.0 copy-done.1
  458.1 0.0 reduce-scatter.9.cloned.1.call-done
  458.1 62.3 %norm_back_attn.1 = (bf16[320,2048]{1,0:T(8,128)(2,1)}, f32[8,2048]{1,0:T(8,128)}, f32[8,128]{1,0:T(8,128)}, bf16[4,128,768]{2,1,0:T(8,128)(2,1)}, bf16[4,768,128]{2,1,0:T(8,128)(2,1)}) custom-call(bf16[2,2,2,320,2048]{4,3,2,1,0:T(8,128)(2,1)} %bitcast.54, bf16[320,2048]{1,0:T(8,128)(2,1)} %values.1, f32[320,2048]{1,0:T(8,128)} %get-tuple-element.110.upstream, ...), custom_call_target="tpu_custom_call" | custom-call | bytes 6500000 | tf_op jit(solution)/shard_map/norm_back_attn/pallas_call | solution.py:1000
  520.4 0.6 fusion.values
  521.0 0.0 reduce-scatter.11.cloned.1.call-done
  521.0 16.2 %total_everywhere.1 = (f32[48,128]{1,0:T(8,128)}, f32[8,128]{1,0:T(8,128)}, f32[8,128]{1,0:T(8,128)}, bf16[4,768,128]{2,1,0:T(8,128)(2,1)}) custom-call(f32[40,128]{1,0:T(8,128)} %fusion.values, f32[8,2048]{1,0:T(8,128)} %get-tuple-element.120.first, f32[8,128]{1,0:T(8,128)} %get-tuple-element.121.squares, bf16[4,768,128]{2,1,0:T(8,128)(2,1)} %bitcast.68), custom_call_target="tpu_custom_call" | custom-call | tf_op jit(solution)/shard_map/total_everywhere/pallas_call | solution.py:1095
  537.2 1.2 slice.26
  538.4 18.9 %adam_all.1 = (f32[128,6144]{1,0:T(8,128)}, f32[128,6144]{1,0:T(8,128)}, f32[128,6144]{1,0:T(8,128)}, bf16[128,6144]{1,0:T(8,128)(2,1)}, f32[3072,128]{1,0:T(8,1...) custom-call(f32[128,6144]{1,0:T(8,128)} %refs_0_.1, ...), custom_call_target="tpu_custom_call" | custom-call | bytes 1500000 | tf_op jit(solution)/shard_map/adam_all/pallas_call | solution.py:1789
  (3 shorter events, 0.0 us)
Async XLA Ops:
  7.2 213.2 %all-gather.3.cloned.1.call-start = ((), (), s32[]{:S(2)}) async-start(), calls=%async_computation.4 | async-start | bytes 7864320 | tf_op jit(solution)/shard_map/all_gather | solution.py:1819
  81.8 183.5 %all-gather.5.cloned.1.call-start = ((), (), s32[]{:S(2)}) async-start(), calls=%async_computation.5 | async-start | bytes 3932160 | tf_op jit(solution)/shard_map/all_gather | solution.py:1819
  120.0 237.3 %reduce-scatter.5.cloned.1.call-start = ((), (), s32[]{:S(2)}) async-start(), calls=%async_computation.6 | async-start | bytes 3932160 | tf_op jit(solution)/shard_map/reduce_scatter | solution.py:1833
  264.9 192.3 %reduce-scatter.7.cloned.1.call-start = ((), (), s32[]{:S(2)}) async-start(), calls=%async_computation.7 | async-start | bytes 3932160 | tf_op jit(solution)/shard_map/reduce_scatter | solution.py:1833
  297.6 160.5 %reduce-scatter.9.cloned.1.call-start = ((), (), s32[]{:S(2)}) async-start(), calls=%async_computation.8 | async-start | bytes 3932160 | tf_op jit(solution)/shard_map/reduce_scatter | solution.py:1833
  357.2 163.8 %reduce-scatter.11.cloned.1.call-start = ((), (), s32[]{:S(2)}) async-start(), calls=%async_computation.9 | async-start | bytes 3932160 | tf_op jit(solution)/shard_map/reduce_scatter | solution.py:1833
  457.2 0.8 copy-start
  457.2 0.9 copy-start.1
Sparse Core Ops, SparseCore 0:
  81.9 115.7 all-gather.2
  199.3 61.7 all-gather.4
  265.0 59.3 reduce-scatter.4
  327.2 60.2 reduce-scatter.6
  389.6 60.2 reduce-scatter.8
  457.4 59.3 reduce-scatter.10

commit v10 on v9

--- a/solution.py
+++ b/solution.py
@@ -46,7 +46,7 @@
 MESH_ID = pl.DeviceIdType.MESH
 VMEM_LIMIT = 60 * 1024 * 1024
 CHUNK = 16
-GATHER_COPIES = 16
+GATHER_COPIES = 17
 AHEAD = 1000
 PART = TEAM // 2
 SUM_COPIES = 12
@@ -147,8 +147,11 @@
     far_high = [relay(number, 1 - near, tp, part, TO_TP) for part, _, number, _ in high_parts]
     twin_beside = [relay(number, 1 - near, tp, part, TO_CORE) for part, _, _, number in high_parts]
     twin_across = relay(9, near, 1 - tp, high, TO_CORE)
-    twin_far = relay(12, 1 - near, 1 - tp, high, TO_CORE)
-    twins = [twin_own, twin_across, twin_far] + twin_beside
+    twin_far = [
+        relay(number, 1 - near, 1 - tp, part, TO_CORE)
+        for (part, *_), number in zip(high_parts, (12, 16))
+    ]
+    twins = [twin_own, twin_across] + twin_far + twin_beside
     ways = near_high + far_high + [tp_high]
     if cut:
         tp_low = give(0, low, TO_TP)
@@ -211,14 +214,13 @@
         if cut:
             far_low.wait_recv()
             twin_far_low.start()
-        for copy in far_high:
+        for copy, twin in zip(far_high, twin_far):
             copy.wait_recv()
-        twin_far.start()
+            twin.start()
 
     def rest_there():
-        for copy in twin_beside:
+        for copy in twin_beside + twin_far:
             copy.wait_recv()
-        twin_far.wait_recv()
         if cut:
             twin_beside_low.wait_recv()
             twin_far_low.wait_recv()
@@ -457,16 +459,18 @@
     def gets(side, number):
         return own >= number + 1 if side == 0 else own + 1 + number < count
 
-    def push(number):
+    near = lax.axis_index("near")
+    halves = (near, 1 - near)
+
+    def push(number, place):
         for side in range(2):
 
             @pl.when(sends(side, number))
             def _(side=side):
-                for half in range(2):
-                    message(side, number, half).start()
+                message(side, number, halves[place]).start()
 
     def take(number):
-        for half in range(2):
+        for half in halves:
             for side in range(2):
 
                 @pl.when(gets(side, number))
@@ -491,7 +495,7 @@
     return push, take, settle
 
 
-def greet_all(flips, count):
+def greet_all(flips, count, work):
     barrier = pltpu.get_barrier_semaphore()
     own = lax.axis_index("outer")
     for flip in flips:
@@ -504,6 +508,7 @@
                 barrier, inc=1, device_id={"outer": neighbour}, device_id_type=MESH_ID
             )
 
+    work()
     beside = jnp.where(own < count - 1, 1, 0) + jnp.where(own > 0, 1, 0)
     pl.semaphore_wait(barrier, len(flips) + beside)
 
@@ -548,28 +553,33 @@
         ]
         for copy in fetch:
             copy.start()
-        for member, across, inside in spans(widths):
-            first[member, :, inside] = qkv[:, across].astype(jnp.bfloat16)
-        for member in range(TEAM):
-            at = pl.ds(member * (tall // TEAM), tall // TEAM)
-            first[member, :, wide // TEAM :] = out_weight[at].astype(jnp.bfloat16).T
-        greet_all(EVERYONE_NEAR, outer_count)
-        for copy in team:
-            copy.start()
-
         def prepare(at):
             value = inputs[at].astype(jnp.float32)
             normed[at] = (value * rms_scale(value) * gain[...]).astype(jnp.bfloat16)
 
-        row_loop(0, rows, prepare)
+        def work():
+            for member, across, inside in spans(widths):
+                first[member, :, inside] = qkv[:, across].astype(jnp.bfloat16)
+            for member in range(TEAM):
+                at = pl.ds(member * (tall // TEAM), tall // TEAM)
+                first[member, :, wide // TEAM :] = out_weight[at].astype(jnp.bfloat16).T
+            row_loop(0, rows, prepare)
+
+        greet_all(EVERYONE_NEAR, outer_count, work)
+        for copy in team:
+            copy.start()
         begin_tp()
+        team[0].wait()
+        team[3].wait()
+        push(0, 0)
         fetch[1].wait()
         for member, across, inside in spans((units, units)):
             pieces[member, :, inside] = gate_up_v[:, across].astype(jnp.bfloat16)
-        for copy in team:
+        for copy in team[1:3]:
             copy.wait()
-        push(0)
+        push(0, 1)
         begin_near()
+        take(0)
         length = sequence_length(lengths, owners, outer * TEAM + near * CORE + core)
         fetch[0].wait()
 
@@ -584,12 +594,13 @@
             at = pl.ds(member * (units // TEAM), units // TEAM)
             down_pieces[member] = down_v[at].astype(jnp.bfloat16).T
         middle()
-        take(0)
+        if outer_count > 2:
+            take(1)
         middle_rest()
         for copy in others:
             copy.start()
         later()
-        for step in range(1, outer_count - 1):
+        for step in range(2, outer_count - 1):
             take(step)
         finish()
         settle()
@@ -1059,13 +1070,13 @@
             return copies
 
         mine = near * (CORE * 2) + core * 2 + tp
+        others = plan_exchange(pieces, mixed, *sems)
         layer[mine, :gains] = values[...]
         layer[mine, gains:] = squares[...] + corner(square_sum(pieces[...]))
         sums = jnp.sum(first[...], axis=0, keepdims=True)
         for place in range(width // HD):
             layer[mine, place : place + 1] = sums[:, place * HD : (place + 1) * HD]
         copies = share(layer, mine, 0, 7)
-        others = plan_exchange(pieces, mixed, *sems)
         for copy in others:
             copy.start()
         for copy in copies:
@@ -1106,6 +1117,7 @@
         ]
         + exchange_scratch(),
         compiler_params=params(number),
+        cost_estimate=cost_of(16),
     )(values, first, squares, pieces)
 
 
@@ -1189,8 +1201,6 @@
             fetch.start()
             greet(EVERYONE_NEAR)
             steps[0]()
-            for copy in copies:
-                copy.start()
             fetch.wait()
 
         group = lax.axis_index("outer") * TEAM + sequence
@@ -1221,6 +1231,8 @@
         @pl.when(sequence == 1)
         def _():
             steps[1]()
+            for copy in copies:
+                copy.start()
 
         @pl.when(sequence == 2)
         def _():
@@ -1433,14 +1445,14 @@
         def _():
             gather[5]()
             steps[1]()
-            for copy in copies:
-                copy.start()
             gather[4]()
             arrival(1).start()
 
         @pl.when(place == 1)
         def _():
             steps[2]()
+            for copy in copies:
+                copy.start()
             gather[6]()
             arrival(2).start()
 
@@ -1598,34 +1610,65 @@
     )(normed, weights, cotangent, gathered)
 
 
-def feed_back(grads, weights, product):
+def feed_back(grads, weights, product, normed, outer_count):
     count, rows, width = grads.shape
     units = weights.shape[1]
-
-    def kernel(grads, weights, product, by_gate, by_up):
-        for start in range(0, units, 256):
-            gate_at, up_at = pl.ds(start, 256), pl.ds(units + start, 256)
-            grad = jnp.dot(grads[0], weights[:, gate_at], preferred_element_type=jnp.float32)
-            gate, up = product[0, :, gate_at], product[0, :, up_at]
-            share = jax.nn.sigmoid(gate)
-            slope = grad * up * share * (1.0 + gate * (1.0 - share))
-            by_gate[0, :, gate_at] = slope.astype(jnp.bfloat16)
-            by_up[0, :, gate_at] = (grad * gate * share).astype(jnp.bfloat16)
+    split, share = team_split(width, outer_count)
+    turns = width // 512
+
+    def kernel(grads, weights, product, normed, by_gate, by_up, grad_weight, kept):
+        step = pl.program_id(0)
+
+        @pl.when(step < count)
+        def _():
+            for start in range(0, units, 256):
+                gate_at, up_at = pl.ds(start, 256), pl.ds(units + start, 256)
+                grad = jnp.dot(grads[0], weights[:, gate_at], preferred_element_type=jnp.float32)
+                gate, up = product[0, :, gate_at], product[0, :, up_at]
+                part = jax.nn.sigmoid(gate)
+                slope = grad * up * part * (1.0 + gate * (1.0 - part))
+                by_gate[0, :, gate_at] = slope.astype(jnp.bfloat16)
+                by_up[0, :, gate_at] = (grad * gate * part).astype(jnp.bfloat16)
+            kept[step] = by_gate[0]
+
+        @pl.when(step >= count)
+        def _():
+            turned = lax.dot_general(
+                kept[...].reshape(count * rows, units),
+                normed[...],
+                (((0,), (0,)), ((), ())),
+                preferred_element_type=jnp.float32,
+            ).astype(jnp.bfloat16)
+            for place in range(512 // share):
+                grad_weight[place] = turned[:, place * share : (place + 1) * share]
+
+    def early(*shape):
+        return pl.BlockSpec((1,) + shape, lambda s: (jnp.minimum(s, count - 1), 0, 0))
+
+    def late(s):
+        return jnp.maximum(s - count, 0)
 
     return pl.pallas_call(
         kernel,
         name="feed_back",
-        grid=(count,),
-        out_shape=(jax.ShapeDtypeStruct((count, rows, units), jnp.bfloat16),) * 2,
+        grid=(count + turns,),
+        out_shape=(jax.ShapeDtypeStruct((count, rows, units), jnp.bfloat16),) * 2
+        + (jax.ShapeDtypeStruct((width // share, units, share), jnp.bfloat16),),
         in_specs=[
-            per_sequence(rows, width),
+            early(rows, width),
             whole(*weights.shape),
-            per_sequence(rows, 2 * units),
+            early(rows, 2 * units),
+            pl.BlockSpec((count * rows, 512), lambda s: (0, late(s))),
         ],
-        out_specs=(per_sequence(rows, units),) * 2,
+        out_specs=(
+            early(rows, units),
+            early(rows, units),
+            pl.BlockSpec((512 // share, units, share), lambda s: (late(s), 0, 0)),
+        ),
+        scratch_shapes=[pltpu.VMEM((count, rows, units), jnp.bfloat16)],
         compiler_params=pltpu.CompilerParams(vmem_limit_bytes=VMEM_LIMIT),
-        cost_estimate=cost_of(18),
-    )(grads, weights, product)
+        cost_estimate=cost_of(28),
+    )(grads, weights, product, normed)
 
 
 def spans(widths, base=0):
@@ -1636,17 +1679,6 @@
             yield member, pl.ds(first + member * share, share), pl.ds(inside, share)
             first += width
             inside += share
-
-
-def by_columns(start, height, widths, source):
-    def run(pieces, update):
-        @pl.loop(0, height // CHUNK)
-        def _(row):
-            rows = pl.ds(pl.multiple_of(start + row * CHUNK, CHUNK), CHUNK)
-            for member, across, inside in spans(widths):
-                update(rows, across, pieces[member, rows, inside])
-
-    return source, pl.ds(start, height), pl.ds(0, sum(widths)), run
 
 
 def by_turned(height, base, widths, source, members=range(TEAM)):
@@ -1940,16 +1972,16 @@
     grad_down = over_rows(grad_all.reshape(-1, D), activated.reshape(-1, hidden_units))
     grad_all, grad_down = after(grad_all, grad_down.astype(jnp.bfloat16))
     down_sum = sum_weight(grad_down)
-    grad_gate, grad_up = feed_back(
-        grad_all.reshape(-1, half_rows, D),
+    grad_gate, grad_up, grad_gate_weight = feed_back(
+        grad_all.reshape(TEAM, row_count, D),
         down_full,
-        gate_up.reshape(-1, half_rows, 2 * hidden_units),
+        gate_up,
+        normed_mlp,
+        lax.axis_size("outer"),
     )
-    grad_gate = grad_gate.reshape(TEAM, row_count, hidden_units)
-    grad_up = grad_up.reshape(TEAM, row_count, hidden_units)
-    grad_gate_weight = over_rows(normed_mlp, grad_gate.reshape(-1, hidden_units))
-    grad_gate, grad_gate_weight = after(grad_gate, grad_gate_weight.astype(jnp.bfloat16))
-    gate_sum = sum_weight(grad_gate_weight)
+    gate_sum = turned_pieces(
+        sum_weight(grad_gate_weight.reshape(-1, grad_gate_weight.shape[2]))
+    )
     grad_hidden, grad_mlp_gain, own_grad, mlp_part, grad_up_weight = feed_back_rest(
         grad_gate,
         grad_up,
@@ -1991,7 +2023,7 @@
         inputs,
         grad_hidden,
         attn_gain,
-        (team_pieces(gate_sum), up_sum),
+        (gate_sum, up_sum),
         (gate_sum, up_sum, down_sum),
         4,
         "norm_back_attn",
@@ -2025,11 +2057,8 @@
                 gate_up_moment,
                 gate_up_square,
                 [
-                    by_columns(start, max(CHUNK, part_rows // 4), gate_up_widths[:1], 0)
-                    for start in range(0, part_rows, max(CHUNK, part_rows // 4))
-                ]
-                + [
-                    by_turned(part_rows, gate_up_widths[0], gate_up_widths[1:], 1, (member,))
+                    by_turned(part_rows, base, gate_up_widths[:1], source, (member,))
+                    for source, base in enumerate((0, gate_up_widths[0]))
                     for member in range(TEAM)
                 ],
             ),

time: 570 us -> 558 us (0.979)
  matrix products: 27.2 us -> 13.6 us
    dot_general x2 -> x1, matrix products: 27.2 us -> 13.6 us  [dot(): lax.dot_general(left, right, ((contract[0], contract[1]), ((), ())), pref...]
    pallas_call x1, Pallas kernels: 18.7 us -> 28.2 us  [feed_back(): pl.pallas_call(kernel, name='feed_back', grid=(count + turns,), out_shape...]
    pallas_call x1, Pallas kernels: 73.2 us -> 67.1 us  [opening(): pl.pallas_call(kernel, name='opening', out_shape=(layer_rows(rows, width)...]
  transfers between devices with their start and end apart: 6 -> 6, of which waited for: 0 -> 0; matrix products, arithmetic and copies ran while one was open for 5% -> 3% of each run, Pallas kernels for 72% -> 75%
where the time goes in v10:
time: 558 us; the launch traced here: 553 us
  Pallas kernels  519 us (93%)
  between operations  14.6 us (3%)
  matrix products  13.6 us (2%)
    pallas_call x1, Pallas kernels, branch_and_norm(): pl.pallas_call(kernel, name=name, out_shape=(jax.ShapeDtypeStruct((rows,...  101 us
    pallas_call x1, Pallas kernels, attend_back(): pl.pallas_call(kernel, name='attend_back', grid=(count,), out_shape=(laye...  100 us
    pallas_call x1, Pallas kernels, opening(): pl.pallas_call(kernel, name='opening', out_shape=(layer_rows(rows, width)...  67.1 us
    pallas_call x1, Pallas kernels, norm_back_last(): pl.pallas_call(kernel, name=name, out_shape=(jax.ShapeDtypeStruct((rows,...  62.2 us
    pallas_call x1, Pallas kernels, feed_back_rest(): pl.pallas_call(kernel, name=name, out_shape=(jax.ShapeDtypeStruct((rows,...  57.9 us
    pallas_call x1, Pallas kernels, attend(): pl.pallas_call(kernel, name='attend', grid=(count,), out_shape=(jax.Shape...  35.3 us
    pallas_call x1, Pallas kernels, feed(): pl.pallas_call(kernel, name='feed', grid=(count,), out_shape=(jax.ShapeDt...  31 us
    pallas_call x1, Pallas kernels, feed_back(): pl.pallas_call(kernel, name='feed_back', grid=(count + turns,), out_shape...  28.2 us
  transfers between devices with their start and end apart: 6, of which 0 were waited for; matrix products, arithmetic and copies ran while one was open for 3% of the time, Pallas kernels for 75%

profile of v10, /device:TPU:0, one launch (start us, length us, event | category | flops | bytes accessed | tf_op | source)
XLA Modules:
  0.0 552.8 jit_solution(14319472775360341414)
XLA Ops:
  7.2 0.0 all-gather.3.cloned.1.call-start
  7.2 1.3 fusion.1
  8.6 67.1 %opening.1 = (bf16[2,2,2,320,2048]{4,3,2,1,0:T(8,128)(2,1)}, bf16[4,128,1536]{2,1,0:T(8,128)(2,1)}, bf16[4,4,128,768]{3,2,1,0:T(8,128)(2,1)}, bf16[320,2048]{1,0:T(8,128)(2,1)}, bf16[4,128,768]{2,1,0:T(8,128)(2,1)}) custom-call(s32[16]{0:T(128)} %lengths.5, s32[16]{0:T(128)} %owners.5, f32[128,2048]{1,0:T(8,128)} %refs_9_.1, f32[1024,128]{1,0:T(8,128)} %refs_6_.1, ...), custom_call_target="tpu_custom_call" | custom-call | bytes 6000000 | tf_op jit(solution)/shard_map/opening/pallas_call | solution.py:611
  75.7 0.0 all-gather.3.cloned.1.call-update
  75.7 0.0 all-gather.5.cloned.1.call-start
  75.7 1.3 slice_bitcast_fusion.gains
  77.0 35.3 %attend.1 = (f32[4,640,512]{2,1,0:T(8,128)}, bf16[4,640,256]{2,1,0:T(8,128)(2,1)}, f32[4,640,128]{2,1,0:T(8,128)}, bf16[4,640,2048]{2,1,0:T(8,128)(2,1)}, bf16[2...) custom-call(s32[16]{0:T(128)} %lengths.5, s32[16]{0:T(128)} %owners.5, bf16[4,640,2048]{2,1,0:T(8,128)(2,1)} %bitcast.41, ...), custom_call_target="tpu_custom_call" | custom-call | bytes 5000000 | tf_op jit(solution)/shard_map/attend/pallas_call | solution.py:1247
  112.3 0.0 all-gather.5.cloned.1.call-update
  112.3 0.2 reduce-scatter.5.cloned.1.call-start
  112.5 100.9 %branch_and_norm.1 = (f32[320,2048]{1,0:T(8,128)}, bf16[2,2,2,320,2048]{4,3,2,1,0:T(8,128)(2,1)}) custom-call(bf16[2,2,2,320,2048]{4,3,2,1,0:T(8,128)(2,1)} %bitcast.48, bf16[320,2048]{1,0:T(8,128)(2,1)} %values.1, f32[1,2048]{1,0:T(1,128)} %bitcast.65), custom_call_target="tpu_custom_call" | custom-call | bytes 9500000 | tf_op jit(solution)/shard_map/branch_and_norm/pallas_call | solution.py:689
  213.4 0.0 all-gather.3.cloned.1.call-done.weights_any.weights
  213.4 31.0 %feed.1 = (f32[4,640,1536]{2,1,0:T(8,128)}, bf16[4,640,768]{2,1,0:T(8,128)(2,1)}, bf16[2,2,2,320,2048]{4,3,2,1,0:T(8,128)(2,1)}) custom-call(bf16[4,640,2048]{2,1,0:T(8,128)(2,1)} %bitcast.38, bf16[2048,1536]{1,0:T(8,128)(2,1)} %all-gather.3.cloned.1.call-done.weights_any.weights, ...), custom_call_target="tpu_custom_call", output_to_operand_aliasing={{2}: (3, {})} | custom-call | bytes 2800000 | tf_op jit(solution)/shard_map/feed/pallas_call | solution.py:1589
  244.4 13.6 %convolution_convert_fusion = bf16[2048,768]{1,0:T(8,128)(2,1)} fusion(bf16[2560,2048]{1,0:T(8,128)(2,1)} %bitcast.43, bf16[2560,768]{1,0:T(8,128)(2,1)} %bitcast.50), kind=kOutput, calls=%fused_computation | convolution fusion | flops 8054636544 | bytes 17563648 | tf_op jit(solution)/shard_map/dot_general | solution.py:1884
  258.0 0.0 reduce-scatter.5.cloned.1.call-update
  258.0 0.0 reduce-scatter.7.cloned.1.call-start
  258.1 0.0 all-gather.5.cloned.1.call-done.weights.down
  258.1 28.2 %feed_back.1 = (bf16[4,640,768]{2,1,0:T(8,128)(2,1)}, bf16[4,640,768]{2,1,0:T(8,128)(2,1)}, bf16[16,768,128]{2,1,0:T(8,128)(2,1)}) custom-call(bf16[4,640,2048]{2,1,0:T(8,128)(2,1)} %bitcast.44, bf16[2048,768]{1,0:T(8,128)(2,1)} %all-gather.5.cloned.1.call-done.weights.down, f32[4,640,1536]{2,1,0:T(8,128)} %get-tuple-element.99.product, ...), custom_call_target="tpu_custom_call" | custom-call | bytes 2800000 | tf_op jit(solution)/shard_map/feed_back/pallas_call | solution.py:1651
  286.3 0.0 reduce-scatter.7.cloned.1.call-update
  286.3 0.3 reduce-scatter.9.cloned.1.call-start
  286.6 57.9 %feed_back_rest.1 = (f32[320,2048]{1,0:T(8,128)}, f32[8,2048]{1,0:T(8,128)}, bf16[320,2048]{1,0:T(8,128)(2,1)}, bf16[4,2,320,2048]{3,2,1,0:T(8,128)(2,1)}, bf16[16,768,128]{2,1,0:T(8,128)(2,1)}) custom-call(bf16[4,2,320,768]{3,2,1,0:T(8,128)(2,1)} %bitcast.52, bf16[4,2,320,768]{3,2,1,0:T(8,128)(2,1)} %bitcast.53, ...), custom_call_target="tpu_custom_call" | custom-call | bytes 6000000 | tf_op jit(solution)/shard_map/feed_back_rest/pallas_call | solution.py:908
  344.5 0.0 reduce-scatter.9.cloned.1.call-update
  344.5 0.0 reduce-scatter.11.cloned.1.call-start
  344.6 0.0 reduce-scatter.5.cloned.1.call-done.rest_4_
  344.6 100.4 %attend_back.1 = (bf16[2,2,2,320,2048]{4,3,2,1,0:T(8,128)(2,1)}, f32[2,8,128]{2,1,0:T(8,128)}, bf16[4,640,2048]{2,1,0:T(8,128)(2,1)}, bf16[320,2048]{1,0:T(8,128...) custom-call(s32[16]{0:T(128)} %lengths.5, s32[16]{0:T(128)} %owners.5, ...), custom_call_target="tpu_custom_call" | custom-call | bytes 5000000 | tf_op jit(solution)/shard_map/attend_back/pallas_call | solution.py:1477
  445.0 0.0 copy-start
  445.0 0.0 copy-start.1
  445.0 0.0 reduce-scatter.7.cloned.1.call-done
  445.0 0.0 reduce-scatter.11.cloned.1.call-update
  445.1 0.8 copy-done
  445.8 0.0 copy-done.1
  445.9 0.0 reduce-scatter.9.cloned.1.call-done
  445.9 62.2 %norm_back_attn.1 = (bf16[320,2048]{1,0:T(8,128)(2,1)}, f32[8,2048]{1,0:T(8,128)}, f32[8,128]{1,0:T(8,128)}, bf16[4,768,128]{2,1,0:T(8,128)(2,1)}, bf16[4,768,128]{2,1,0:T(8,128)(2,1)}) custom-call(bf16[2,2,2,320,2048]{4,3,2,1,0:T(8,128)(2,1)} %bitcast.49, bf16[320,2048]{1,0:T(8,128)(2,1)} %values.1, f32[320,2048]{1,0:T(8,128)} %get-tuple-element.108.upstream, ...), custom_call_target="tpu_custom_call" | custom-call | bytes 6500000 | tf_op jit(solution)/shard_map/norm_back_attn/pallas_call | solution.py:1011
  508.1 0.6 fusion.values
  508.8 0.0 reduce-scatter.11.cloned.1.call-done
  508.8 16.9 %total_everywhere.1 = (f32[48,128]{1,0:T(8,128)}, f32[8,128]{1,0:T(8,128)}, f32[8,128]{1,0:T(8,128)}, bf16[4,768,128]{2,1,0:T(8,128)(2,1)}) custom-call(f32[40,128]{1,0:T(8,128)} %fusion.values, f32[8,2048]{1,0:T(8,128)} %get-tuple-element.118.first, f32[8,128]{1,0:T(8,128)} %get-tuple-element.119.squares, bf16[4,768,128]{2,1,0:T(8,128)(2,1)} %bitcast.64), custom_call_target="tpu_custom_call" | custom-call | bytes 1600000 | tf_op jit(solution)/shard_map/total_everywhere/pallas_call | solution.py:1106
  525.7 1.2 slice.26
  526.8 18.8 %adam_all.1 = (f32[128,6144]{1,0:T(8,128)}, f32[128,6144]{1,0:T(8,128)}, f32[128,6144]{1,0:T(8,128)}, bf16[128,6144]{1,0:T(8,128)(2,1)}, f32[3072,128]{1,0:T(8,1...) custom-call(f32[128,6144]{1,0:T(8,128)} %refs_0_.1, ...), custom_call_target="tpu_custom_call" | custom-call | bytes 1500000 | tf_op jit(solution)/shard_map/adam_all/pallas_call | solution.py:1821
  (3 shorter events, 0.0 us)
Async XLA Ops:
  7.2 206.2 %all-gather.3.cloned.1.call-start = ((), (), s32[]{:S(2)}) async-start(), calls=%async_computation.4 | async-start | bytes 7864320 | tf_op jit(solution)/shard_map/all_gather | solution.py:1851
  75.7 182.4 %all-gather.5.cloned.1.call-start = ((), (), s32[]{:S(2)}) async-start(), calls=%async_computation.5 | async-start | bytes 3932160 | tf_op jit(solution)/shard_map/all_gather | solution.py:1851
  112.3 232.3 %reduce-scatter.5.cloned.1.call-start = ((), (), s32[]{:S(2)}) async-start(), calls=%async_computation.6 | async-start | bytes 3932160 | tf_op jit(solution)/shard_map/reduce_scatter | solution.py:1865
  258.0 187.0 %reduce-scatter.7.cloned.1.call-start = ((), (), s32[]{:S(2)}) async-start(), calls=%async_computation.7 | async-start | bytes 3932160 | tf_op jit(solution)/shard_map/reduce_scatter | solution.py:1865
  286.3 159.6 %reduce-scatter.9.cloned.1.call-start = ((), (), s32[]{:S(2)}) async-start(), calls=%async_computation.8 | async-start | bytes 3932160 | tf_op jit(solution)/shard_map/reduce_scatter | solution.py:1865
  344.5 164.2 %reduce-scatter.11.cloned.1.call-start = ((), (), s32[]{:S(2)}) async-start(), calls=%async_computation.9 | async-start | bytes 3932160 | tf_op jit(solution)/shard_map/reduce_scatter | solution.py:1865
  445.0 0.8 copy-start
  445.0 0.9 copy-start.1
Sparse Core Ops, SparseCore 0:
  75.8 115.7 all-gather.2
  193.2 61.7 all-gather.4
  258.1 60.4 reduce-scatter.4
  321.4 60.2 reduce-scatter.6
  383.8 60.2 reduce-scatter.8
  446.3 60.2 reduce-scatter.10

commit v11 on v10

--- a/solution.py
+++ b/solution.py
@@ -49,6 +49,7 @@
 GATHER_COPIES = 17
 AHEAD = 1000
 PART = TEAM // 2
+HEAD_GAINS = 2 * D // HD
 SUM_COPIES = 12
 NEIGHBOURS = ((1, 0, 0), (0, 1, 0), (0, 0, 1))
 MATES = ((0, 1, 0), (1, 0, 0), (1, 1, 0))
@@ -425,6 +426,13 @@
     return jax.ShapeDtypeStruct((NEAR, CORE, 2, rows, width), jnp.bfloat16)
 
 
+def wide_gain(gains, place, width):
+    first = place * (width // HD)
+    return jnp.concatenate(
+        [gains[first + part : first + part + 1] for part in range(width // HD)], axis=1
+    )
+
+
 def row_loop(start, count, body):
     @pl.loop(0, count // CHUNK)
     def _(step):
@@ -521,7 +529,7 @@
 
 
 def opening(
-    qkv, out_weight, gate_up, down, inputs, gain, cotangent, lengths, owners, outer_count, number
+    qkv, out_weight, gate_up, down, inputs, gains, cotangent, lengths, owners, outer_count, number
 ):
     rows, width = inputs.shape
     part_rows, wide = qkv.shape
@@ -533,7 +541,7 @@
     cut = balanced(rows, crossing((first_shape, gate_up_shape), width))
 
     def kernel(
-        lengths, owners, qkv, out_weight, inputs, gain, gate_up, down, cotangent,
+        lengths, owners, qkv, out_weight, inputs, gains, gate_up, down, cotangent,
         out, mixed, full, low, down_pieces,
         normed, first, pieces, gate_up_v, down_v, cotangent_v, load_sem, line_send, line_recv, *sems
     ):
@@ -553,9 +561,11 @@
         ]
         for copy in fetch:
             copy.start()
+        gain = wide_gain(gains, 0, width)
+
         def prepare(at):
             value = inputs[at].astype(jnp.float32)
-            normed[at] = (value * rms_scale(value) * gain[...]).astype(jnp.bfloat16)
+            normed[at] = (value * rms_scale(value) * gain).astype(jnp.bfloat16)
 
         def work():
             for member, across, inside in spans(widths):
@@ -641,7 +651,7 @@
         qkv,
         out_weight,
         inputs,
-        gain.reshape(1, width),
+        gains,
         gate_up,
         down,
         cotangent,
@@ -664,11 +674,12 @@
     return ref[at].astype(jnp.float32)
 
 
-def branch_and_norm(part, residual, gain, number, name):
+def branch_and_norm(part, residual, gains, number, name):
     rows, width = residual.shape
     cut = rows // 2
 
-    def kernel(part, residual, gain, hidden, out, *scratch):
+    def kernel(part, residual, gains, hidden, out, *scratch):
+        gain = wide_gain(gains, 1, width)
         normed, sems = scratch[SUM_SCRATCH], scratch[SUM_SCRATCH + 1 :]
         steps, from_tp, from_near = plan_sum_of(part, hidden, scratch[:SUM_SCRATCH], cut)
         onward = plan_gather(normed, out, *sems, cut=cut)
@@ -680,7 +691,7 @@
             value = hidden[at] + read(from_tp, at) + read(from_near, at)
             value = read(residual, at) + value
             hidden[at] = value
-            normed[at] = (value * rms_scale(value) * gain[...]).astype(jnp.bfloat16)
+            normed[at] = (value * rms_scale(value) * gain).astype(jnp.bfloat16)
 
         steps[3](finish)
         for step in onward:
@@ -697,7 +708,7 @@
         + gather_scratch(),
         compiler_params=params(number),
         cost_estimate=cost_of(95),
-    )(spread(part, rows), residual, gain.reshape(1, width))
+    )(spread(part, rows), residual, gains)
     return hidden, full.reshape(-1, width)
 
 
@@ -725,7 +736,7 @@
 
 
 def feed_back_rest(
-    grad_gate, grad_up, weights, active, down, normed, values, upstream, gain, outer_count, number, name
+    grad_gate, grad_up, weights, active, down, normed, values, upstream, gains, outer_count, number, name
 ):
     rows, width = values.shape
     count, both_rows, units = grad_gate.shape
@@ -736,7 +747,7 @@
     turns = width // 512
 
     def kernel(
-        gate, ups, weights, active, down, normed, values, upstream, gain,
+        gate, ups, weights, active, down, normed, values, upstream, gains,
         result, gain_grad, low, branch, grad_weight, *scratch
     ):
         (grad_v, weights_v, active_v, down_v, values_v, upstream_v, parts, total), rest = (
@@ -745,6 +756,7 @@
         )
         (shares, staged, load_sem, store_sem, chunk_sem, piece_sem), sums = rest[:6], rest[6:]
         from_tp, from_near = sums[3], sums[4]
+        gain = wide_gain(gains, 1, width)
         near, core, tp = spots()
         members = sequence_order()
         outgoing = [parts.at[place, half] for place, half in ((0, 1 - tp), (2, 1 - tp), (0, tp), (2, tp))]
@@ -888,7 +900,7 @@
 
         def finish(at):
             grad = total[at] + read(from_tp, at) + read(from_near, at)
-            turned, by_gain = norm_back(values_v[at], gain[...], grad)
+            turned, by_gain = norm_back(values_v[at], gain, grad)
             gain_grad[...] += by_gain.reshape(CHUNK // 8, 8, width).sum(axis=0)
             value = read(upstream_v, at) + turned
             total[at] = value
@@ -945,9 +957,9 @@
         normed,
         values,
         upstream,
-        gain.reshape(1, width),
+        gains,
     )
-    return result, gain_grad.sum(axis=0), rounded, branch.reshape(-1, width), grad_weight
+    return result, gain_grad, rounded, branch.reshape(-1, width), grad_weight
 
 
 def square_sum(values):
@@ -961,12 +973,13 @@
     return jnp.where((row == 0) & (column == 0), value, 0.0)
 
 
-def norm_back_last(part, values, upstream, gain, extra, squared, number, name):
+def norm_back_last(part, values, upstream, gains, extra, squared, number, name):
     rows, width = values.shape
     extras, count = len(extra), len(squared)
     cut = balanced(rows, crossing(extra, width))
 
-    def kernel(part, values, upstream, gain, *rest):
+    def kernel(part, values, upstream, gains, *rest):
+        gain = wide_gain(gains, 0, width)
         pieces, rest = rest[:extras], rest[extras:]
         squared, (result, gain_grad, squares), rest = (
             rest[:count],
@@ -1000,7 +1013,7 @@
 
         def finish(at):
             grad = total[at] + read(from_tp, at) + read(from_near, at)
-            back, by_gain = norm_back(read(values_v, at), gain[...], grad)
+            back, by_gain = norm_back(read(values_v, at), gain, grad)
             gain_grad[...] += by_gain.reshape(CHUNK // 8, 8, width).sum(axis=0)
             result[at] = (upstream_v[at] + back).astype(jnp.bfloat16)
 
@@ -1030,15 +1043,16 @@
         + exchange_scratch() * extras,
         compiler_params=params(number),
         cost_estimate=cost_of(65),
-    )(spread(part, rows), values, upstream, gain.reshape(1, width), *extra, *squared)
-
-
-def total_everywhere(values, first, squares, pieces, outer_count, number, name):
-    gains = values.shape[0]
+    )(spread(part, rows), values, upstream, gains, *extra, *squared)
+
+
+def total_everywhere(first, second, heads, squares, pieces, outer_count, number, name):
+    used = 2 * first.shape[1] // HD + heads.shape[0]
+    gains = used + -used % 8
     shape = (gains + 8, HD)
     width = first.shape[1]
 
-    def kernel(values, first, squares, pieces, out, norm, factor, mixed, layer, outers, send, recv, *sems):
+    def kernel(first, second, heads, squares, pieces, out, norm, factor, mixed, layer, outers, send, recv, *sems):
         near, core, tp = spots()
         outer = lax.axis_index("outer")
         partners = [
@@ -1052,6 +1066,18 @@
         barrier = pltpu.get_barrier_semaphore()
         for partner in partners:
             pl.semaphore_signal(barrier, inc=1, device_id=partner, device_id_type=MESH_ID)
+        mine = near * (CORE * 2) + core * 2 + tp
+        layer[mine, gains - 8 : gains] = jnp.zeros((8, HD), jnp.float32)
+        layer[mine, gains:] = squares[...] + corner(square_sum(pieces[...]))
+        place = 0
+        for source in (first, second):
+            sums = jnp.sum(source[...], axis=0, keepdims=True)
+            for start in range(0, width, HD):
+                layer[mine, place : place + 1] = sums[:, start : start + HD]
+                place += 1
+        for head in range(heads.shape[0]):
+            layer[mine, place : place + 1] = jnp.sum(heads[head], axis=0, keepdims=True)
+            place += 1
         pl.semaphore_wait(barrier, len(partners))
 
         def share(slots, mine, first, count):
@@ -1069,13 +1095,7 @@
                 copies.append(copy)
             return copies
 
-        mine = near * (CORE * 2) + core * 2 + tp
         others = plan_exchange(pieces, mixed, *sems)
-        layer[mine, :gains] = values[...]
-        layer[mine, gains:] = squares[...] + corner(square_sum(pieces[...]))
-        sums = jnp.sum(first[...], axis=0, keepdims=True)
-        for place in range(width // HD):
-            layer[mine, place : place + 1] = sums[:, place * HD : (place + 1) * HD]
         copies = share(layer, mine, 0, 7)
         for copy in others:
             copy.start()
@@ -1095,7 +1115,7 @@
         root = jnp.sqrt(
             jnp.sum(gain_part * gain_part, keepdims=True) + jnp.sum(total[gains:], keepdims=True)
         )
-        norm[...] = jnp.broadcast_to(root, norm.shape)
+        norm[...] = root
         factor[...] = jnp.broadcast_to(
             jnp.minimum(1.0, clip_norm / (root + 1e-06)), factor.shape
         )
@@ -1106,8 +1126,13 @@
     return pl.pallas_call(
         kernel,
         name=name,
-        out_shape=(jax.ShapeDtypeStruct(shape, jnp.float32), tile, tile, like(pieces)),
-        in_specs=[in_vmem()] * 4,
+        out_shape=(
+            jax.ShapeDtypeStruct(shape, jnp.float32),
+            jax.ShapeDtypeStruct((1, 1), jnp.float32),
+            tile,
+            like(pieces),
+        ),
+        in_specs=[in_vmem()] * 5,
         out_specs=(in_vmem(), in_vmem(), in_vmem(), anywhere()),
         scratch_shapes=[
             pltpu.VMEM((8,) + shape, jnp.float32),
@@ -1118,7 +1143,7 @@
         + exchange_scratch(),
         compiler_params=params(number),
         cost_estimate=cost_of(16),
-    )(values, first, squares, pieces)
+    )(first, second, heads, squares, pieces)
 
 
 def head_scale(raw, gain, cos_full, sin_full):
@@ -1138,10 +1163,10 @@
 def head_inputs(proj, gains, cos_ref, sin_ref, queries, keys, values, heads):
     for head in range(heads):
         queries[head] = head_scale(
-            proj[0, :, columns(head)], gains[0:1, :], cos_ref[...], sin_ref[...]
+            proj[0, :, columns(head)], gains[HEAD_GAINS : HEAD_GAINS + 1, :], cos_ref[...], sin_ref[...]
         )
     keys[...] = head_scale(
-        proj[0, :, columns(heads)], gains[1:2, :], cos_ref[...], sin_ref[...]
+        proj[0, :, columns(heads)], gains[HEAD_GAINS + 1 : HEAD_GAINS + 2, :], cos_ref[...], sin_ref[...]
     )
     values[...] = proj[0, :, columns(heads + 1)].astype(jnp.bfloat16)
 
@@ -1263,7 +1288,7 @@
             anywhere(),
             whole(rows, HD),
             whole(rows, HD),
-            whole(2, HD),
+            whole(*gains.shape),
             whole(own_rows, width),
         ]
         + [whole(*piece.shape) for piece in extra],
@@ -1419,7 +1444,7 @@
 
         def settle(column, gain, value):
             back, by_gain = head_back(
-                proj[0, :, columns(column)], gains[gain : gain + 1, :], value, cos_ref[...], sin_ref[...]
+                proj[0, :, columns(column)], gains[HEAD_GAINS + gain : HEAD_GAINS + gain + 1, :], value, cos_ref[...], sin_ref[...]
             )
             out[:, columns(column)] = back.astype(jnp.bfloat16)
             gain_grad[gain] += by_gain.reshape(rows // 8, 8, HD).sum(axis=0)
@@ -1497,7 +1522,7 @@
             anywhere(),
             whole(rows, HD),
             whole(rows, HD),
-            whole(2, HD),
+            whole(*gains.shape),
             anywhere(),
             anywhere(),
         ]
@@ -1931,9 +1956,7 @@
     down_widths = (FF // tp_count,)
 
     cos_full, sin_full = rotary(row_count)
-    attn_gain = norm_gains[:D]
-    mlp_gain = norm_gains[D : 2 * D]
-    head_gains = norm_gains[2 * D :].reshape(2, HD)
+    gains = norm_gains.reshape(-1, HD)
 
     normed_attn, gate_up_mixed, first_full, grad_low, down_pieces = opening(
         qkv_weight,
@@ -1941,7 +1964,7 @@
         gate_up_weight,
         down_weight,
         inputs,
-        attn_gain,
+        gains,
         cotangent,
         lengths,
         owners,
@@ -1959,13 +1982,13 @@
         owners,
         cos_full,
         sin_full,
-        head_gains,
+        gains,
         heads,
         early,
         1,
     )
     down_full = gather_outer(down_mixed)
-    hidden, normed_mlp = branch_and_norm(attn_branch, inputs, mlp_gain, 2, "branch_and_norm")
+    hidden, normed_mlp = branch_and_norm(attn_branch, inputs, gains, 2, "branch_and_norm")
     gate_up, activated, grad_all = feed(
         normed_mlp.reshape(TEAM, row_count, D), gate_up_full, grad_low, grad_all, early, 8
     )
@@ -1991,7 +2014,7 @@
         normed_mlp,
         hidden,
         grad_low,
-        mlp_gain,
+        gains,
         lax.axis_size("outer"),
         3,
         "feed_back_rest",
@@ -2012,7 +2035,7 @@
         owners,
         cos_full,
         sin_full,
-        head_gains,
+        gains,
         heads,
         7,
     )
@@ -2022,27 +2045,23 @@
         grad_normed_attn,
         inputs,
         grad_hidden,
-        attn_gain,
+        gains,
         (gate_sum, up_sum),
         (gate_sum, up_sum, down_sum),
         4,
         "norm_back_attn",
     )
-    gain_part = jnp.concatenate(
-        [jnp.zeros_like(grad_mlp_gain), grad_mlp_gain, grad_head_gains.sum(axis=1).reshape(-1)]
-    )
-    gain_count = gain_part.shape[0]
-    packed = jnp.pad(gain_part, (0, -gain_count % PAD))
-    packed, norm_tile, factor_tile, first_mixed = total_everywhere(
-        packed.reshape(-1, HD),
+    packed, norm_value, factor_tile, first_mixed = total_everywhere(
         attn_gain_parts,
+        grad_mlp_gain,
+        grad_head_gains,
         squares,
         first_sum,
         lax.axis_size("outer"),
         5,
         "total_everywhere",
     )
-    grad_norm = norm_tile[0, 0]
+    grad_norm = norm_value.reshape(())
     (
         (new_gate_up, new_gate_up_one, new_gate_up_two, gate_up_copy),
         (new_down, new_down_one, new_down_two, down_copy),
@@ -2087,7 +2106,7 @@
         (gate_mixed, up_mixed, down_mixed, first_mixed),
         factor_tile,
         packed,
-        [each.reshape(-1, HD) for each in (norm_gains, gains_moment, gains_square)],
+        [gains] + [each.reshape(-1, HD) for each in (gains_moment, gains_square)],
         (output, input_grad),
     )
     new_gains, new_gains_one, new_gains_two = (each.reshape(-1) for each in new_gains)

time: 558 us -> 555 us (level)
  transfers between devices with their start and end apart: 6 -> 6, of which waited for: 0 -> 0; matrix products, arithmetic and copies ran while one was open for 3% -> 2% of each run, Pallas kernels for 75% -> 76%
where the time goes in v11:
time: 555 us; the launch traced here: 549 us
  Pallas kernels  519 us (94%)
  between operations  16.3 us (3%)
  matrix products  13.6 us (2%)
    pallas_call x1, Pallas kernels, branch_and_norm(): pl.pallas_call(kernel, name=name, out_shape=(jax.ShapeDtypeStruct((rows,...  101 us
    pallas_call x1, Pallas kernels, attend_back(): pl.pallas_call(kernel, name='attend_back', grid=(count,), out_shape=(laye...  100 us
    pallas_call x1, Pallas kernels, opening(): pl.pallas_call(kernel, name='opening', out_shape=(layer_rows(rows, width)...  67.2 us
    pallas_call x1, Pallas kernels, norm_back_last(): pl.pallas_call(kernel, name=name, out_shape=(jax.ShapeDtypeStruct((rows,...  62.4 us
    pallas_call x1, Pallas kernels, feed_back_rest(): pl.pallas_call(kernel, name=name, out_shape=(jax.ShapeDtypeStruct((rows,...  57.9 us
    pallas_call x1, Pallas kernels, attend(): pl.pallas_call(kernel, name='attend', grid=(count,), out_shape=(jax.Shape...  35.3 us
    pallas_call x1, Pallas kernels, feed(): pl.pallas_call(kernel, name='feed', grid=(count,), out_shape=(jax.ShapeDt...  30.9 us
    pallas_call x1, Pallas kernels, feed_back(): pl.pallas_call(kernel, name='feed_back', grid=(count + turns,), out_shape...  28.2 us
  transfers between devices with their start and end apart: 6, of which 0 were waited for; matrix products, arithmetic and copies ran while one was open for 2% of the time, Pallas kernels for 76%

profile of v11, /device:TPU:0, one launch (start us, length us, event | category | flops | bytes accessed | tf_op | source)
XLA Modules:
  0.0 549.5 jit_solution(7998975254444207828)
XLA Ops:
  7.2 0.0 all-gather.3.cloned.1.call-start
  7.2 67.2 %opening.1 = (bf16[2,2,2,320,2048]{4,3,2,1,0:T(8,128)(2,1)}, bf16[4,128,1536]{2,1,0:T(8,128)(2,1)}, bf16[4,4,128,768]{3,2,1,0:T(8,128)(2,1)}, bf16[320,2048]{1,0:T(8,128)(2,1)}, bf16[4,128,768]{2,1,0:T(8,128)(2,1)}) custom-call(s32[16]{0:T(128)} %lengths.5, s32[16]{0:T(128)} %owners.5, f32[128,2048]{1,0:T(8,128)} %refs_9_.1, f32[1024,128]{1,0:T(8,128)} %refs_6_.1, ...), custom_call_target="tpu_custom_call" | custom-call | bytes 6000000 | tf_op jit(solution)/shard_map/opening/pallas_call | solution.py:621
  74.4 0.0 all-gather.3.cloned.1.call-update
  74.5 0.0 all-gather.5.cloned.1.call-start
  74.5 35.3 %attend.1 = (f32[4,640,512]{2,1,0:T(8,128)}, bf16[4,640,256]{2,1,0:T(8,128)(2,1)}, f32[4,640,128]{2,1,0:T(8,128)}, bf16[4,640,2048]{2,1,0:T(8,128)(2,1)}, bf16[2...) custom-call(s32[16]{0:T(128)} %lengths.5, s32[16]{0:T(128)} %owners.5, bf16[4,640,2048]{2,1,0:T(8,128)(2,1)} %bitcast.36, ...), custom_call_target="tpu_custom_call" | custom-call | bytes 5000000 | tf_op jit(solution)/shard_map/attend/pallas_call | solution.py:1272
  109.9 0.0 all-gather.5.cloned.1.call-update
  109.9 0.2 reduce-scatter.5.cloned.1.call-start
  110.1 100.9 %branch_and_norm.1 = (f32[320,2048]{1,0:T(8,128)}, bf16[2,2,2,320,2048]{4,3,2,1,0:T(8,128)(2,1)}) custom-call(bf16[2,2,2,320,2048]{4,3,2,1,0:T(8,128)(2,1)} %bitcast.40, bf16[320,2048]{1,0:T(8,128)(2,1)} %values.1, f32[34,128]{1,0:T(8,128)} %bitcast.58), custom_call_target="tpu_custom_call" | custom-call | bytes 9500000 | tf_op jit(solution)/shard_map/branch_and_norm/pallas_call | solution.py:700
  211.0 0.0 all-gather.3.cloned.1.call-done.weights_any.weights
  211.0 30.9 %feed.1 = (f32[4,640,1536]{2,1,0:T(8,128)}, bf16[4,640,768]{2,1,0:T(8,128)(2,1)}, bf16[2,2,2,320,2048]{4,3,2,1,0:T(8,128)(2,1)}) custom-call(bf16[4,640,2048]{2,1,0:T(8,128)(2,1)} %bitcast.31, bf16[2048,1536]{1,0:T(8,128)(2,1)} %all-gather.3.cloned.1.call-done.weights_any.weights, ...), custom_call_target="tpu_custom_call", output_to_operand_aliasing={{2}: (3, {})} | custom-call | bytes 2800000 | tf_op jit(solution)/shard_map/feed/pallas_call | solution.py:1614
  242.0 13.6 %convolution_convert_fusion = bf16[2048,768]{1,0:T(8,128)(2,1)} fusion(bf16[2560,2048]{1,0:T(8,128)(2,1)} %bitcast.34, bf16[2560,768]{1,0:T(8,128)(2,1)} %bitcast.43), kind=kOutput, calls=%fused_computation | convolution fusion | flops 8054636544 | bytes 17563648 | tf_op jit(solution)/shard_map/dot_general | solution.py:1909
  255.5 0.0 reduce-scatter.5.cloned.1.call-update
  255.6 0.0 reduce-scatter.7.cloned.1.call-start
  255.6 0.0 all-gather.5.cloned.1.call-done.weights.down
  255.6 28.2 %feed_back.1 = (bf16[4,640,768]{2,1,0:T(8,128)(2,1)}, bf16[4,640,768]{2,1,0:T(8,128)(2,1)}, bf16[16,768,128]{2,1,0:T(8,128)(2,1)}) custom-call(bf16[4,640,2048]{2,1,0:T(8,128)(2,1)} %bitcast.35, bf16[2048,768]{1,0:T(8,128)(2,1)} %all-gather.5.cloned.1.call-done.weights.down, f32[4,640,1536]{2,1,0:T(8,128)} %get-tuple-element.99.product, ...), custom_call_target="tpu_custom_call" | custom-call | bytes 2800000 | tf_op jit(solution)/shard_map/feed_back/pallas_call | solution.py:1676
  283.8 0.0 reduce-scatter.7.cloned.1.call-update
  283.9 0.3 reduce-scatter.9.cloned.1.call-start
  284.1 57.9 %feed_back_rest.1 = (f32[320,2048]{1,0:T(8,128)}, f32[8,2048]{1,0:T(8,128)}, bf16[320,2048]{1,0:T(8,128)(2,1)}, bf16[4,2,320,2048]{3,2,1,0:T(8,128)(2,1)}, bf16[16,768,128]{2,1,0:T(8,128)(2,1)}) custom-call(bf16[4,2,320,768]{3,2,1,0:T(8,128)(2,1)} %bitcast.45, bf16[4,2,320,768]{3,2,1,0:T(8,128)(2,1)} %bitcast.46, ...), custom_call_target="tpu_custom_call" | custom-call | bytes 6000000 | tf_op jit(solution)/shard_map/feed_back_rest/pallas_call | solution.py:920
  342.1 0.0 reduce-scatter.9.cloned.1.call-update
  342.1 0.0 reduce-scatter.11.cloned.1.call-start
  342.1 0.0 reduce-scatter.5.cloned.1.call-done.rest_4_
  342.2 100.3 %attend_back.1 = (bf16[2,2,2,320,2048]{4,3,2,1,0:T(8,128)(2,1)}, f32[2,8,128]{2,1,0:T(8,128)}, bf16[4,640,2048]{2,1,0:T(8,128)(2,1)}, bf16[320,2048]{1,0:T(8,128...) custom-call(s32[16]{0:T(128)} %lengths.5, s32[16]{0:T(128)} %owners.5, ...), custom_call_target="tpu_custom_call" | custom-call | bytes 5000000 | tf_op jit(solution)/shard_map/attend_back/pallas_call | solution.py:1502
  442.4 0.0 reduce-scatter.7.cloned.1.call-done
  442.5 0.0 reduce-scatter.11.cloned.1.call-update
  442.5 0.0 reduce-scatter.9.cloned.1.call-done
  442.5 62.4 %norm_back_attn.1 = (bf16[320,2048]{1,0:T(8,128)(2,1)}, f32[8,2048]{1,0:T(8,128)}, f32[8,128]{1,0:T(8,128)}, bf16[4,768,128]{2,1,0:T(8,128)(2,1)}, bf16[4,768,128]{2,1,0:T(8,128)(2,1)}) custom-call(bf16[2,2,2,320,2048]{4,3,2,1,0:T(8,128)(2,1)} %bitcast.41, bf16[320,2048]{1,0:T(8,128)(2,1)} %values.1, f32[320,2048]{1,0:T(8,128)} %get-tuple-element.108.upstream, ...), custom_call_target="tpu_custom_call" | custom-call | bytes 6500000 | tf_op jit(solution)/shard_map/norm_back_attn/pallas_call | solution.py:1024
  504.9 0.0 reduce-scatter.11.cloned.1.call-done
  504.9 16.5 %total_everywhere.1 = (f32[48,128]{1,0:T(8,128)}, f32[1,1]{1,0:T(1,128)}, f32[8,128]{1,0:T(8,128)}, bf16[4,768,128]{2,1,0:T(8,128)(2,1)}) custom-call(f32[8,2048]{1,0:T(8,128)} %get-tuple-element.116.first, f32[8,2048]{1,0:T(8,128)} %get-tuple-element.117.second, f32[2,8,128]{2,1,0:T(8,128)} %get-tuple-element.118.heads, ...), custom_call_target="tpu_custom_call" | custom-call | bytes 1600000 | tf_op jit(solution)/shard_map/total_everywhere/pallas_call | solution.py:1126
  521.4 19.1 %adam_all.1 = (f32[128,6144]{1,0:T(8,128)}, f32[128,6144]{1,0:T(8,128)}, f32[128,6144]{1,0:T(8,128)}, bf16[128,6144]{1,0:T(8,128)(2,1)}, f32[3072,128]{1,0:T(8,1...) custom-call(f32[128,6144]{1,0:T(8,128)} %refs_0_.1, ...), custom_call_target="tpu_custom_call" | custom-call | bytes 1500000 | tf_op jit(solution)/shard_map/adam_all/pallas_call | solution.py:1846
Async XLA Ops:
  7.2 203.8 %all-gather.3.cloned.1.call-start = ((), (), s32[]{:S(2)}) async-start(), calls=%async_computation.4 | async-start | bytes 7864320 | tf_op jit(solution)/shard_map/all_gather | solution.py:1876
  74.5 181.2 %all-gather.5.cloned.1.call-start = ((), (), s32[]{:S(2)}) async-start(), calls=%async_computation.5 | async-start | bytes 3932160 | tf_op jit(solution)/shard_map/all_gather | solution.py:1876
  109.9 232.3 %reduce-scatter.5.cloned.1.call-start = ((), (), s32[]{:S(2)}) async-start(), calls=%async_computation.6 | async-start | bytes 3932160 | tf_op jit(solution)/shard_map/reduce_scatter | solution.py:1890
  255.6 186.9 %reduce-scatter.7.cloned.1.call-start = ((), (), s32[]{:S(2)}) async-start(), calls=%async_computation.7 | async-start | bytes 3932160 | tf_op jit(solution)/shard_map/reduce_scatter | solution.py:1890
  283.9 158.6 %reduce-scatter.9.cloned.1.call-start = ((), (), s32[]{:S(2)}) async-start(), calls=%async_computation.8 | async-start | bytes 3932160 | tf_op jit(solution)/shard_map/reduce_scatter | solution.py:1890
  342.1 162.8 %reduce-scatter.11.cloned.1.call-start = ((), (), s32[]{:S(2)}) async-start(), calls=%async_computation.9 | async-start | bytes 3932160 | tf_op jit(solution)/shard_map/reduce_scatter | solution.py:1890
Sparse Core Ops, SparseCore 0:
  74.6 115.8 all-gather.2
  192.0 61.7 all-gather.4
  256.7 59.4 reduce-scatter.4
  318.9 60.2 reduce-scatter.6
  381.4 60.2 reduce-scatter.8
  443.8 60.2 reduce-scatter.10

commit v12 on v11

--- a/solution.py
+++ b/solution.py
@@ -1578,12 +1578,17 @@
     )
 
 
-def feed(normed, weights, cotangent, gathered, early, number):
+def feed(normed, weights, cotangent, gathered, early, outer_count, number):
     count, rows, width = normed.shape
     units = weights.shape[1] // 2
     late = cotangent.shape[0] - early
-
-    def kernel(normed, weights_any, own, _, product, active, out, weights, weights_sem, *sems):
+    split, share = team_split(width, outer_count)
+    turns = width // 512
+
+    def kernel(
+        normed, weights_any, own, _, product, active, out, grad_weight,
+        weights, kept, columns_v, staged, weights_sem, column_sem, piece_sem, *sems
+    ):
         fetch = pltpu.make_async_copy(weights_any, weights, weights_sem)
         steps = plan_gather(
             own, out, *sems, cut=balanced(late, 0), base=early, rows=late
@@ -1604,12 +1609,55 @@
             product[0, :, gate_at] = gate
             product[0, :, up_at] = up
             active[0, :, gate_at] = swish_product(gate, up).astype(jnp.bfloat16)
+        kept[sequence] = active[0]
 
         for place in (1, 2, 3):
 
             @pl.when(sequence == count - 4 + place)
             def _(place=place):
                 steps[place]()
+
+        @pl.when(sequence == count - 1)
+        def _():
+            def bring(turn):
+                return pltpu.make_async_copy(
+                    out.at[:, :, :, :, pl.ds(turn * 512, 512)],
+                    columns_v.at[turn % 2],
+                    column_sem.at[turn % 2],
+                )
+
+            def pieces(turn):
+                slot = turn % 2
+                return [
+                    pltpu.make_async_copy(
+                        staged.at[slot, :, pl.ds(place * share, share)],
+                        grad_weight.at[turn * (512 // share) + place],
+                        piece_sem.at[slot, place],
+                    )
+                    for place in range(512 // share)
+                ]
+
+            for turn in range(min(2, turns)):
+                bring(turn).start()
+            for turn in range(turns):
+                bring(turn).wait()
+                turned = lax.dot_general(
+                    kept[...].reshape(count * rows, units),
+                    columns_v[turn % 2].reshape(count * rows, 512),
+                    (((0,), (0,)), ((), ())),
+                    preferred_element_type=jnp.float32,
+                )
+                if turn >= 2:
+                    for copy in pieces(turn - 2):
+                        copy.wait()
+                staged[turn % 2] = turned.astype(jnp.bfloat16)
+                for copy in pieces(turn):
+                    copy.start()
+                if turn + 2 < turns:
+                    bring(turn + 2).start()
+            for turn in range(max(0, turns - 2), turns):
+                for copy in pieces(turn):
+                    copy.wait()
 
     return pl.pallas_call(
         kernel,
@@ -1619,6 +1667,7 @@
             jax.ShapeDtypeStruct((count, rows, 2 * units), jnp.float32),
             jax.ShapeDtypeStruct((count, rows, units), jnp.bfloat16),
             like(gathered),
+            jax.ShapeDtypeStruct((outer_count * split, units, share), jnp.bfloat16),
         ),
         in_specs=[
             per_sequence(rows, width),
@@ -1626,8 +1675,21 @@
             whole(*cotangent.shape),
             anywhere(),
         ],
-        out_specs=(per_sequence(rows, 2 * units), per_sequence(rows, units), anywhere()),
-        scratch_shapes=[pltpu.VMEM(weights.shape, weights.dtype), pltpu.SemaphoreType.DMA]
+        out_specs=(
+            per_sequence(rows, 2 * units),
+            per_sequence(rows, units),
+            anywhere(),
+            anywhere(),
+        ),
+        scratch_shapes=[
+            pltpu.VMEM(weights.shape, weights.dtype),
+            pltpu.VMEM((count, rows, units), jnp.bfloat16),
+            pltpu.VMEM((2,) + gathered.shape[:4] + (512,), jnp.bfloat16),
+            pltpu.VMEM((2, units, 512), jnp.bfloat16),
+            pltpu.SemaphoreType.DMA,
+            pltpu.SemaphoreType.DMA((2,)),
+            pltpu.SemaphoreType.DMA((2, 512 // share)),
+        ]
         + gather_scratch(),
         input_output_aliases={3: 2},
         compiler_params=params(number),
@@ -1989,12 +2051,16 @@
     )
     down_full = gather_outer(down_mixed)
     hidden, normed_mlp = branch_and_norm(attn_branch, inputs, gains, 2, "branch_and_norm")
-    gate_up, activated, grad_all = feed(
-        normed_mlp.reshape(TEAM, row_count, D), gate_up_full, grad_low, grad_all, early, 8
+    gate_up, activated, grad_all, grad_down = feed(
+        normed_mlp.reshape(TEAM, row_count, D),
+        gate_up_full,
+        grad_low,
+        grad_all,
+        early,
+        lax.axis_size("outer"),
+        8,
     )
-    grad_down = over_rows(grad_all.reshape(-1, D), activated.reshape(-1, hidden_units))
-    grad_all, grad_down = after(grad_all, grad_down.astype(jnp.bfloat16))
-    down_sum = sum_weight(grad_down)
+    down_sum = turned_pieces(sum_weight(grad_down.reshape(-1, grad_down.shape[2])))
     grad_gate, grad_up, grad_gate_weight = feed_back(
         grad_all.reshape(TEAM, row_count, D),
         down_full,
@@ -2029,7 +2095,7 @@
         first_full,
         mlp_part,
         hidden,
-        (team_pieces(down_sum),),
+        (down_sum,),
         lax.axis_size("outer"),
         lengths,
         owners,
@@ -2085,7 +2151,7 @@
                 down_weight,
                 down_moment,
                 down_square,
-                [by_rows(member, hidden_units, part_rows, None, 2) for member in range(TEAM)],
+                [by_rows(member, hidden_units, part_rows, 0, 2) for member in range(TEAM)],
             ),
             (
                 out_weight,

time: 555 us -> 553 us (level)
  matrix products: 13.6 us -> 0 us
  Pallas kernels: 519 us -> 531 us
    dot_general x1 -> x0, matrix products: 13.6 us -> none  [dot(): lax.dot_general(left, right, ((contract[0], contract[1]), ((), ())), pref...]
    pallas_call x1, Pallas kernels: 30.9 us -> 42.7 us  [feed(): pl.pallas_call(kernel, name='feed', grid=(count,), out_shape=(jax.ShapeDt...]
  transfers between devices with their start and end apart: 6 -> 6, of which waited for: 0 -> 0; matrix products, arithmetic and copies ran while one was open for 2% -> 0% of each run, Pallas kernels for 76% -> 78%
where the time goes in v12:
time: 553 us; the launch traced here: 548 us
  Pallas kernels  531 us (96%)
  between operations  16.4 us (3%)
    pallas_call x1, Pallas kernels, branch_and_norm(): pl.pallas_call(kernel, name=name, out_shape=(jax.ShapeDtypeStruct((rows,...  101 us
    pallas_call x1, Pallas kernels, attend_back(): pl.pallas_call(kernel, name='attend_back', grid=(count,), out_shape=(laye...  100 us
    pallas_call x1, Pallas kernels, opening(): pl.pallas_call(kernel, name='opening', out_shape=(layer_rows(rows, width)...  67.1 us
    pallas_call x1, Pallas kernels, norm_back_last(): pl.pallas_call(kernel, name=name, out_shape=(jax.ShapeDtypeStruct((rows,...  62.4 us
    pallas_call x1, Pallas kernels, feed_back_rest(): pl.pallas_call(kernel, name=name, out_shape=(jax.ShapeDtypeStruct((rows,...  58 us
    pallas_call x1, Pallas kernels, feed(): pl.pallas_call(kernel, name='feed', grid=(count,), out_shape=(jax.ShapeDt...  42.7 us
    pallas_call x1, Pallas kernels, attend(): pl.pallas_call(kernel, name='attend', grid=(count,), out_shape=(jax.Shape...  35.3 us
    pallas_call x1, Pallas kernels, feed_back(): pl.pallas_call(kernel, name='feed_back', grid=(count + turns,), out_shape...  28.2 us
  transfers between devices with their start and end apart: 6, of which 0 were waited for; matrix products, arithmetic and copies ran while one was open for 0% of the time, Pallas kernels for 78%

profile of v12, /device:TPU:0, one launch (start us, length us, event | category | flops | bytes accessed | tf_op | source)
XLA Modules:
  0.0 548.1 jit_solution(13971187388954217556)
XLA Ops:
  7.2 0.0 all-gather.3.cloned.1.call-start
  7.2 67.1 %opening.1 = (bf16[2,2,2,320,2048]{4,3,2,1,0:T(8,128)(2,1)}, bf16[4,128,1536]{2,1,0:T(8,128)(2,1)}, bf16[4,4,128,768]{3,2,1,0:T(8,128)(2,1)}, bf16[320,2048]{1,0:T(8,128)(2,1)}, bf16[4,128,768]{2,1,0:T(8,128)(2,1)}) custom-call(s32[16]{0:T(128)} %lengths.5, s32[16]{0:T(128)} %owners.5, f32[128,2048]{1,0:T(8,128)} %refs_9_.1, f32[1024,128]{1,0:T(8,128)} %refs_6_.1, ...), custom_call_target="tpu_custom_call" | custom-call | bytes 6000000 | tf_op jit(solution)/shard_map/opening/pallas_call | solution.py:621
  74.4 0.0 all-gather.3.cloned.1.call-update
  74.4 0.0 all-gather.5.cloned.1.call-start
  74.5 35.3 %attend.1 = (f32[4,640,512]{2,1,0:T(8,128)}, bf16[4,640,256]{2,1,0:T(8,128)(2,1)}, f32[4,640,128]{2,1,0:T(8,128)}, bf16[4,640,2048]{2,1,0:T(8,128)(2,1)}, bf16[2...) custom-call(s32[16]{0:T(128)} %lengths.5, s32[16]{0:T(128)} %owners.5, bf16[4,640,2048]{2,1,0:T(8,128)(2,1)} %bitcast.32, ...), custom_call_target="tpu_custom_call" | custom-call | bytes 5000000 | tf_op jit(solution)/shard_map/attend/pallas_call | solution.py:1272
  109.8 0.0 all-gather.5.cloned.1.call-update
  109.8 0.3 reduce-scatter.5.cloned.1.call-start
  110.1 100.9 %branch_and_norm.1 = (f32[320,2048]{1,0:T(8,128)}, bf16[2,2,2,320,2048]{4,3,2,1,0:T(8,128)(2,1)}) custom-call(bf16[2,2,2,320,2048]{4,3,2,1,0:T(8,128)(2,1)} %bitcast.36, bf16[320,2048]{1,0:T(8,128)(2,1)} %values.1, f32[34,128]{1,0:T(8,128)} %bitcast.55), custom_call_target="tpu_custom_call" | custom-call | bytes 9500000 | tf_op jit(solution)/shard_map/branch_and_norm/pallas_call | solution.py:700
  211.0 0.0 all-gather.3.cloned.1.call-done.weights_any.weights
  211.1 42.7 %feed.1 = (f32[4,640,1536]{2,1,0:T(8,128)}, bf16[4,640,768]{2,1,0:T(8,128)(2,1)}, bf16[2,2,2,320,2048]{4,3,2,1,0:T(8,128)(2,1)}, bf16[16,768,128]{2,1,0:T(8,128)(2,1)}) custom-call(bf16[4,640,2048]{2,1,0:T(8,128)(2,1)} %bitcast.28, bf16[2048,1536]{1,0:T(8,128)(2,1)} %all-gather.3.cloned.1.call-done.weights_any.weights, ...), custom_call_target="tpu_custom_call", output_to_operand_aliasing={{2}: (3, {})} | custom-call | bytes 2800000 | tf_op jit(solution)/shard_map/feed/pallas_call | solution.py:1662
  253.8 0.0 reduce-scatter.5.cloned.1.call-update
  253.9 0.4 reduce-scatter.7.cloned.1.call-start
  254.3 0.0 all-gather.5.cloned.1.call-done.weights.down
  254.3 28.2 %feed_back.1 = (bf16[4,640,768]{2,1,0:T(8,128)(2,1)}, bf16[4,640,768]{2,1,0:T(8,128)(2,1)}, bf16[16,768,128]{2,1,0:T(8,128)(2,1)}) custom-call(bf16[4,640,2048]{2,1,0:T(8,128)(2,1)} %bitcast.31, bf16[2048,768]{1,0:T(8,128)(2,1)} %all-gather.5.cloned.1.call-done.weights.down, f32[4,640,1536]{2,1,0:T(8,128)} %get-tuple-element.96.product, ...), custom_call_target="tpu_custom_call" | custom-call | bytes 2800000 | tf_op jit(solution)/shard_map/feed_back/pallas_call | solution.py:1738
  282.5 0.0 reduce-scatter.7.cloned.1.call-update
  282.6 0.0 reduce-scatter.9.cloned.1.call-start
  282.6 58.0 %feed_back_rest.1 = (f32[320,2048]{1,0:T(8,128)}, f32[8,2048]{1,0:T(8,128)}, bf16[320,2048]{1,0:T(8,128)(2,1)}, bf16[4,2,320,2048]{3,2,1,0:T(8,128)(2,1)}, bf16[16,768,128]{2,1,0:T(8,128)(2,1)}) custom-call(bf16[4,2,320,768]{3,2,1,0:T(8,128)(2,1)} %bitcast.40, bf16[4,2,320,768]{3,2,1,0:T(8,128)(2,1)} %bitcast.41, ...), custom_call_target="tpu_custom_call" | custom-call | bytes 6000000 | tf_op jit(solution)/shard_map/feed_back_rest/pallas_call | solution.py:920
  340.7 0.0 reduce-scatter.9.cloned.1.call-update
  340.7 0.0 reduce-scatter.11.cloned.1.call-start
  340.7 0.0 reduce-scatter.5.cloned.1.call-done
  340.8 100.4 %attend_back.1 = (bf16[2,2,2,320,2048]{4,3,2,1,0:T(8,128)(2,1)}, f32[2,8,128]{2,1,0:T(8,128)}, bf16[4,640,2048]{2,1,0:T(8,128)(2,1)}, bf16[320,2048]{1,0:T(8,128...) custom-call(s32[16]{0:T(128)} %lengths.5, s32[16]{0:T(128)} %owners.5, ...), custom_call_target="tpu_custom_call" | custom-call | bytes 5000000 | tf_op jit(solution)/shard_map/attend_back/pallas_call | solution.py:1502
  441.2 0.0 reduce-scatter.7.cloned.1.call-done
  441.2 0.0 reduce-scatter.11.cloned.1.call-update
  441.3 0.0 reduce-scatter.9.cloned.1.call-done
  441.3 62.4 %norm_back_attn.1 = (bf16[320,2048]{1,0:T(8,128)(2,1)}, f32[8,2048]{1,0:T(8,128)}, f32[8,128]{1,0:T(8,128)}, bf16[4,768,128]{2,1,0:T(8,128)(2,1)}, bf16[4,768,128]{2,1,0:T(8,128)(2,1)}) custom-call(bf16[2,2,2,320,2048]{4,3,2,1,0:T(8,128)(2,1)} %bitcast.37, bf16[320,2048]{1,0:T(8,128)(2,1)} %values.1, f32[320,2048]{1,0:T(8,128)} %get-tuple-element.106.upstream, ...), custom_call_target="tpu_custom_call" | custom-call | bytes 6500000 | tf_op jit(solution)/shard_map/norm_back_attn/pallas_call | solution.py:1024
  503.7 0.0 reduce-scatter.11.cloned.1.call-done
  503.7 16.3 %total_everywhere.1 = (f32[48,128]{1,0:T(8,128)}, f32[1,1]{1,0:T(1,128)}, f32[8,128]{1,0:T(8,128)}, bf16[4,768,128]{2,1,0:T(8,128)(2,1)}) custom-call(f32[8,2048]{1,0:T(8,128)} %get-tuple-element.114.first, f32[8,2048]{1,0:T(8,128)} %get-tuple-element.115.second, f32[2,8,128]{2,1,0:T(8,128)} %get-tuple-element.116.heads, ...), custom_call_target="tpu_custom_call" | custom-call | bytes 1600000 | tf_op jit(solution)/shard_map/total_everywhere/pallas_call | solution.py:1126
  520.1 19.0 %adam_all.1 = (f32[128,6144]{1,0:T(8,128)}, f32[128,6144]{1,0:T(8,128)}, f32[128,6144]{1,0:T(8,128)}, bf16[128,6144]{1,0:T(8,128)(2,1)}, f32[3072,128]{1,0:T(8,1...) custom-call(f32[128,6144]{1,0:T(8,128)} %refs_0_.1, ...), custom_call_target="tpu_custom_call" | custom-call | bytes 1500000 | tf_op jit(solution)/shard_map/adam_all/pallas_call | solution.py:1908
Async XLA Ops:
  7.2 203.9 %all-gather.3.cloned.1.call-start = ((), (), s32[]{:S(2)}) async-start(), calls=%async_computation.4 | async-start | bytes 7864320 | tf_op jit(solution)/shard_map/all_gather | solution.py:1938
  74.4 179.9 %all-gather.5.cloned.1.call-start = ((), (), s32[]{:S(2)}) async-start(), calls=%async_computation.5 | async-start | bytes 3932160 | tf_op jit(solution)/shard_map/all_gather | solution.py:1938
  109.8 230.9 %reduce-scatter.5.cloned.1.call-start = ((), (), s32[]{:S(2)}) async-start(), calls=%async_computation.6 | async-start | bytes 3932160 | tf_op jit(solution)/shard_map/reduce_scatter | solution.py:1952
  253.9 187.4 %reduce-scatter.7.cloned.1.call-start = ((), (), s32[]{:S(2)}) async-start(), calls=%async_computation.7 | async-start | bytes 3932160 | tf_op jit(solution)/shard_map/reduce_scatter | solution.py:1952
  282.6 158.7 %reduce-scatter.9.cloned.1.call-start = ((), (), s32[]{:S(2)}) async-start(), calls=%async_computation.8 | async-start | bytes 3932160 | tf_op jit(solution)/shard_map/reduce_scatter | solution.py:1952
  340.7 163.1 %reduce-scatter.11.cloned.1.call-start = ((), (), s32[]{:S(2)}) async-start(), calls=%async_computation.9 | async-start | bytes 3932160 | tf_op jit(solution)/shard_map/reduce_scatter | solution.py:1952
Sparse Core Ops, SparseCore 0:
  74.5 115.8 all-gather.2
  191.9 61.7 all-gather.4
  256.0 58.9 reduce-scatter.4
  317.7 60.2 reduce-scatter.6
  380.1 60.2 reduce-scatter.8
  442.6 60.2 reduce-scatter.10

commit v13 on v12

--- a/solution.py
+++ b/solution.py
@@ -541,9 +541,11 @@
     cut = balanced(rows, crossing((first_shape, gate_up_shape), width))
 
     def kernel(
-        lengths, owners, qkv, out_weight, inputs, gains, gate_up, down, cotangent,
-        out, mixed, full, low, down_pieces,
-        normed, first, pieces, gate_up_v, down_v, cotangent_v, load_sem, line_send, line_recv, *sems
+        lengths, owners, qkv_any, out_any, inputs_any, gains, gate_up, down, cotangent,
+        out, mixed, full, low_any, down_any,
+        normed, first, pieces, gate_up_v, down_v, cotangent_v,
+        qkv, out_weight, inputs, low, down_pieces,
+        store_sem, load_sem, line_send, line_recv, *sems
     ):
         near, core, tp = spots()
         outer = lax.axis_index("outer")
@@ -556,11 +558,22 @@
         fetch = [
             pltpu.make_async_copy(source, target, load_sem.at[place])
             for place, (source, target) in enumerate(
-                ((cotangent, cotangent_v), (gate_up, gate_up_v), (down, down_v))
+                (
+                    (cotangent, cotangent_v),
+                    (gate_up, gate_up_v),
+                    (down, down_v),
+                    (qkv_any, qkv),
+                    (out_any, out_weight),
+                    (inputs_any, inputs),
+                )
             )
         ]
-        for copy in fetch:
-            copy.start()
+        for place in (3, 4, 5, 1, 0, 2):
+            fetch[place].start()
+        stores = [
+            pltpu.make_async_copy(low, low_any, store_sem.at[0]),
+            pltpu.make_async_copy(down_pieces, down_any, store_sem.at[1]),
+        ]
         gain = wide_gain(gains, 0, width)
 
         def prepare(at):
@@ -568,6 +581,8 @@
             normed[at] = (value * rms_scale(value) * gain).astype(jnp.bfloat16)
 
         def work():
+            for copy in fetch[3:]:
+                copy.wait()
             for member, across, inside in spans(widths):
                 first[member, :, inside] = qkv[:, across].astype(jnp.bfloat16)
             for member in range(TEAM):
@@ -599,10 +614,12 @@
             low[at] = value.astype(jnp.bfloat16)
 
         row_loop(0, rows, mask)
+        stores[0].start()
         fetch[2].wait()
         for member in range(TEAM):
             at = pl.ds(member * (units // TEAM), units // TEAM)
             down_pieces[member] = down_v[at].astype(jnp.bfloat16).T
+        stores[1].start()
         middle()
         if outer_count > 2:
             take(1)
@@ -614,7 +631,7 @@
             take(step)
         finish()
         settle()
-        for copy in others:
+        for copy in others + stores:
             copy.wait()
 
     scalars = pl.BlockSpec(memory_space=pltpu.SMEM)
@@ -628,8 +645,8 @@
             jax.ShapeDtypeStruct((rows, width), jnp.bfloat16),
             down_shape,
         ),
-        in_specs=[scalars] * 2 + [in_vmem()] * 4 + [anywhere()] * 3,
-        out_specs=(anywhere(),) * 3 + (in_vmem(),) * 2,
+        in_specs=[scalars] * 2 + [anywhere()] * 3 + [in_vmem()] + [anywhere()] * 3,
+        out_specs=(anywhere(),) * 5,
         scratch_shapes=[
             pltpu.VMEM((rows, width), jnp.bfloat16),
             pltpu.VMEM(first_shape.shape, jnp.bfloat16),
@@ -637,7 +654,13 @@
             pltpu.VMEM(gate_up.shape, gate_up.dtype),
             pltpu.VMEM(down.shape, down.dtype),
             pltpu.VMEM(cotangent.shape, cotangent.dtype),
-            pltpu.SemaphoreType.DMA((3,)),
+            pltpu.VMEM(qkv.shape, qkv.dtype),
+            pltpu.VMEM(out_weight.shape, out_weight.dtype),
+            pltpu.VMEM(inputs.shape, inputs.dtype),
+            pltpu.VMEM((rows, width), jnp.bfloat16),
+            pltpu.VMEM(down_shape.shape, jnp.bfloat16),
+            pltpu.SemaphoreType.DMA((2,)),
+            pltpu.SemaphoreType.DMA((6,)),
             pltpu.SemaphoreType.DMA((2, outer_count, 2)),
             pltpu.SemaphoreType.DMA((2, outer_count, 2)),
         ]

time: 553 us -> 553 us (level)
  no operation moved by 1% of the time
where the time goes in v13:
time: 553 us; the launch traced here: 548 us
  Pallas kernels  530 us (96%)
  between operations  16.4 us (3%)
    pallas_call x1, Pallas kernels, branch_and_norm(): pl.pallas_call(kernel, name=name, out_shape=(jax.ShapeDtypeStruct((rows,...  101 us
    pallas_call x1, Pallas kernels, attend_back(): pl.pallas_call(kernel, name='attend_back', grid=(count,), out_shape=(laye...  100 us
    pallas_call x1, Pallas kernels, opening(): pl.pallas_call(kernel, name='opening', out_shape=(layer_rows(rows, width)...  66.5 us
    pallas_call x1, Pallas kernels, norm_back_last(): pl.pallas_call(kernel, name=name, out_shape=(jax.ShapeDtypeStruct((rows,...  62.4 us
    pallas_call x1, Pallas kernels, feed_back_rest(): pl.pallas_call(kernel, name=name, out_shape=(jax.ShapeDtypeStruct((rows,...  58.1 us
    pallas_call x1, Pallas kernels, feed(): pl.pallas_call(kernel, name='feed', grid=(count,), out_shape=(jax.ShapeDt...  42.7 us
    pallas_call x1, Pallas kernels, attend(): pl.pallas_call(kernel, name='attend', grid=(count,), out_shape=(jax.Shape...  35.3 us
    pallas_call x1, Pallas kernels, feed_back(): pl.pallas_call(kernel, name='feed_back', grid=(count + turns,), out_shape...  28.2 us
  transfers between devices with their start and end apart: 6, of which 0 were waited for; matrix products, arithmetic and copies ran while one was open for 0% of the time, Pallas kernels for 78%

profile of v13, /device:TPU:0, one launch (start us, length us, event | category | flops | bytes accessed | tf_op | source)
XLA Modules:
  0.0 547.5 jit_solution(1120775376564050762)
XLA Ops:
  7.2 0.0 all-gather.3.cloned.1.call-start
  7.2 66.5 %opening.1 = (bf16[2,2,2,320,2048]{4,3,2,1,0:T(8,128)(2,1)}, bf16[4,128,1536]{2,1,0:T(8,128)(2,1)}, bf16[4,4,128,768]{3,2,1,0:T(8,128)(2,1)}, bf16[320,2048]{1,0:T(8,128)(2,1)}, bf16[4,128,768]{2,1,0:T(8,128)(2,1)}) custom-call(s32[16]{0:T(128)} %lengths.5, s32[16]{0:T(128)} %owners.5, f32[128,2048]{1,0:T(8,128)} %refs_9_.1, f32[1024,128]{1,0:T(8,128)} %refs_6_.1, ...), custom_call_target="tpu_custom_call" | custom-call | bytes 6000000 | tf_op jit(solution)/shard_map/opening/pallas_call | solution.py:638
  73.8 0.0 all-gather.3.cloned.1.call-update
  73.8 0.0 all-gather.5.cloned.1.call-start
  73.9 35.3 %attend.1 = (f32[4,640,512]{2,1,0:T(8,128)}, bf16[4,640,256]{2,1,0:T(8,128)(2,1)}, f32[4,640,128]{2,1,0:T(8,128)}, bf16[4,640,2048]{2,1,0:T(8,128)(2,1)}, bf16[2...) custom-call(s32[16]{0:T(128)} %lengths.5, s32[16]{0:T(128)} %owners.5, bf16[4,640,2048]{2,1,0:T(8,128)(2,1)} %bitcast.32, ...), custom_call_target="tpu_custom_call" | custom-call | bytes 5000000 | tf_op jit(solution)/shard_map/attend/pallas_call | solution.py:1295
  109.2 0.0 all-gather.5.cloned.1.call-update
  109.2 0.3 reduce-scatter.5.cloned.1.call-start
  109.5 100.9 %branch_and_norm.1 = (f32[320,2048]{1,0:T(8,128)}, bf16[2,2,2,320,2048]{4,3,2,1,0:T(8,128)(2,1)}) custom-call(bf16[2,2,2,320,2048]{4,3,2,1,0:T(8,128)(2,1)} %bitcast.36, bf16[320,2048]{1,0:T(8,128)(2,1)} %values.1, f32[34,128]{1,0:T(8,128)} %bitcast.55), custom_call_target="tpu_custom_call" | custom-call | bytes 9500000 | tf_op jit(solution)/shard_map/branch_and_norm/pallas_call | solution.py:723
  210.5 0.0 all-gather.3.cloned.1.call-done.weights_any.weights
  210.5 42.7 %feed.1 = (f32[4,640,1536]{2,1,0:T(8,128)}, bf16[4,640,768]{2,1,0:T(8,128)(2,1)}, bf16[2,2,2,320,2048]{4,3,2,1,0:T(8,128)(2,1)}, bf16[16,768,128]{2,1,0:T(8,128)(2,1)}) custom-call(bf16[4,640,2048]{2,1,0:T(8,128)(2,1)} %bitcast.28, bf16[2048,1536]{1,0:T(8,128)(2,1)} %all-gather.3.cloned.1.call-done.weights_any.weights, ...), custom_call_target="tpu_custom_call", output_to_operand_aliasing={{2}: (3, {})} | custom-call | bytes 2800000 | tf_op jit(solution)/shard_map/feed/pallas_call | solution.py:1685
  253.2 0.0 reduce-scatter.5.cloned.1.call-update
  253.3 0.4 reduce-scatter.7.cloned.1.call-start
  253.7 0.0 all-gather.5.cloned.1.call-done.weights.down
  253.7 28.2 %feed_back.1 = (bf16[4,640,768]{2,1,0:T(8,128)(2,1)}, bf16[4,640,768]{2,1,0:T(8,128)(2,1)}, bf16[16,768,128]{2,1,0:T(8,128)(2,1)}) custom-call(bf16[4,640,2048]{2,1,0:T(8,128)(2,1)} %bitcast.31, bf16[2048,768]{1,0:T(8,128)(2,1)} %all-gather.5.cloned.1.call-done.weights.down, f32[4,640,1536]{2,1,0:T(8,128)} %get-tuple-element.96.product, ...), custom_call_target="tpu_custom_call" | custom-call | bytes 2800000 | tf_op jit(solution)/shard_map/feed_back/pallas_call | solution.py:1761
  281.9 0.0 reduce-scatter.7.cloned.1.call-update
  282.0 0.0 reduce-scatter.9.cloned.1.call-start
  282.0 58.1 %feed_back_rest.1 = (f32[320,2048]{1,0:T(8,128)}, f32[8,2048]{1,0:T(8,128)}, bf16[320,2048]{1,0:T(8,128)(2,1)}, bf16[4,2,320,2048]{3,2,1,0:T(8,128)(2,1)}, bf16[16,768,128]{2,1,0:T(8,128)(2,1)}) custom-call(bf16[4,2,320,768]{3,2,1,0:T(8,128)(2,1)} %bitcast.40, bf16[4,2,320,768]{3,2,1,0:T(8,128)(2,1)} %bitcast.41, ...), custom_call_target="tpu_custom_call" | custom-call | bytes 6000000 | tf_op jit(solution)/shard_map/feed_back_rest/pallas_call | solution.py:943
  340.1 0.0 reduce-scatter.9.cloned.1.call-update
  340.1 0.0 reduce-scatter.11.cloned.1.call-start
  340.2 0.0 reduce-scatter.5.cloned.1.call-done
  340.2 100.4 %attend_back.1 = (bf16[2,2,2,320,2048]{4,3,2,1,0:T(8,128)(2,1)}, f32[2,8,128]{2,1,0:T(8,128)}, bf16[4,640,2048]{2,1,0:T(8,128)(2,1)}, bf16[320,2048]{1,0:T(8,128...) custom-call(s32[16]{0:T(128)} %lengths.5, s32[16]{0:T(128)} %owners.5, ...), custom_call_target="tpu_custom_call" | custom-call | bytes 5000000 | tf_op jit(solution)/shard_map/attend_back/pallas_call | solution.py:1525
  440.6 0.0 reduce-scatter.7.cloned.1.call-done
  440.7 0.0 reduce-scatter.11.cloned.1.call-update
  440.7 0.0 reduce-scatter.9.cloned.1.call-done
  440.7 62.4 %norm_back_attn.1 = (bf16[320,2048]{1,0:T(8,128)(2,1)}, f32[8,2048]{1,0:T(8,128)}, f32[8,128]{1,0:T(8,128)}, bf16[4,768,128]{2,1,0:T(8,128)(2,1)}, bf16[4,768,128]{2,1,0:T(8,128)(2,1)}) custom-call(bf16[2,2,2,320,2048]{4,3,2,1,0:T(8,128)(2,1)} %bitcast.37, bf16[320,2048]{1,0:T(8,128)(2,1)} %values.1, f32[320,2048]{1,0:T(8,128)} %get-tuple-element.106.upstream, ...), custom_call_target="tpu_custom_call" | custom-call | bytes 6500000 | tf_op jit(solution)/shard_map/norm_back_attn/pallas_call | solution.py:1047
  503.1 0.0 reduce-scatter.11.cloned.1.call-done
  503.2 16.3 %total_everywhere.1 = (f32[48,128]{1,0:T(8,128)}, f32[1,1]{1,0:T(1,128)}, f32[8,128]{1,0:T(8,128)}, bf16[4,768,128]{2,1,0:T(8,128)(2,1)}) custom-call(f32[8,2048]{1,0:T(8,128)} %get-tuple-element.114.first, f32[8,2048]{1,0:T(8,128)} %get-tuple-element.115.second, f32[2,8,128]{2,1,0:T(8,128)} %get-tuple-element.116.heads, ...), custom_call_target="tpu_custom_call" | custom-call | bytes 1600000 | tf_op jit(solution)/shard_map/total_everywhere/pallas_call | solution.py:1149
  519.5 19.0 %adam_all.1 = (f32[128,6144]{1,0:T(8,128)}, f32[128,6144]{1,0:T(8,128)}, f32[128,6144]{1,0:T(8,128)}, bf16[128,6144]{1,0:T(8,128)(2,1)}, f32[3072,128]{1,0:T(8,1...) custom-call(f32[128,6144]{1,0:T(8,128)} %refs_0_.1, ...), custom_call_target="tpu_custom_call" | custom-call | bytes 1500000 | tf_op jit(solution)/shard_map/adam_all/pallas_call | solution.py:1931
Async XLA Ops:
  7.2 203.3 %all-gather.3.cloned.1.call-start = ((), (), s32[]{:S(2)}) async-start(), calls=%async_computation.4 | async-start | bytes 7864320 | tf_op jit(solution)/shard_map/all_gather | solution.py:1961
  73.8 179.9 %all-gather.5.cloned.1.call-start = ((), (), s32[]{:S(2)}) async-start(), calls=%async_computation.5 | async-start | bytes 3932160 | tf_op jit(solution)/shard_map/all_gather | solution.py:1961
  109.2 230.9 %reduce-scatter.5.cloned.1.call-start = ((), (), s32[]{:S(2)}) async-start(), calls=%async_computation.6 | async-start | bytes 3932160 | tf_op jit(solution)/shard_map/reduce_scatter | solution.py:1975
  253.3 187.4 %reduce-scatter.7.cloned.1.call-start = ((), (), s32[]{:S(2)}) async-start(), calls=%async_computation.7 | async-start | bytes 3932160 | tf_op jit(solution)/shard_map/reduce_scatter | solution.py:1975
  282.0 158.7 %reduce-scatter.9.cloned.1.call-start = ((), (), s32[]{:S(2)}) async-start(), calls=%async_computation.8 | async-start | bytes 3932160 | tf_op jit(solution)/shard_map/reduce_scatter | solution.py:1975
  340.1 163.0 %reduce-scatter.11.cloned.1.call-start = ((), (), s32[]{:S(2)}) async-start(), calls=%async_computation.9 | async-start | bytes 3932160 | tf_op jit(solution)/shard_map/reduce_scatter | solution.py:1975
Sparse Core Ops, SparseCore 0:
  73.9 115.8 all-gather.2
  191.3 61.7 all-gather.4
  255.4 58.8 reduce-scatter.4
  317.1 60.2 reduce-scatter.6
  379.6 60.2 reduce-scatter.8
  442.0 60.2 reduce-scatter.10
